TPU v7x, 32 devices: a whole 2x2x4 slice. The times are simulated.
32 devices in a mesh: dp: 16 (over z, y, core), tensor: 2 (over x).
Axes of the slice: x: 2, y: 2, z: 4, core: 2. Of those that a mesh axis runs over, the one named last changes fastest.
Arguments:
- tokens: bfloat16 [20480, 768], P(('dp', 'tensor')), may hold values from -6 to 6
- conditioning: bfloat16 [80, 768], P('dp'), may hold values from -6 to 6
- segment_ids: int32 [20480], P('dp'), may hold values from 0 to 4, as said below
- kept_rows: int32 [10240], P('dp'), may hold values from 0 to 1279, as said below
- cotangent: bfloat16 [20480, 768], P(('dp', 'tensor')), may hold values from -6 to 6
- mod_first: bfloat16 [768, 4608], replicated, may hold values from -0.21875 to 0.21875
- qkv_first: bfloat16 [768, 3, 768], P(None, None, 'tensor'), may hold values from -0.21875 to 0.21875
- proj_first: bfloat16 [768, 768], P('tensor'), may hold values from -3 to 3
- up_first: bfloat16 [768, 3072], P(None, 'tensor'), may hold values from -0.21875 to 0.21875
- down_first: bfloat16 [3072, 768], P('tensor'), may hold values from -0.109375 to 0.109375
- mod_second: bfloat16 [768, 4608], replicated, may hold values from -0.21875 to 0.21875
- qkv_second: bfloat16 [768, 3, 768], P(None, None, 'tensor'), may hold values from -0.21875 to 0.21875
- proj_second: bfloat16 [768, 768], P('tensor'), may hold values from -3 to 3
- up_second: bfloat16 [768, 3072], P(None, 'tensor'), may hold values from -0.21875 to 0.21875
- down_second: bfloat16 [3072, 768], P('tensor'), may hold values from -0.109375 to 0.109375
Outputs:
- first_out: bfloat16 [20480, 768], P(('dp', 'tensor'))
- routed_out: bfloat16 [20480, 768], P(('dp', 'tensor'))
- input_grad: float32 [20480, 768], P(('dp', 'tensor'))
- grad_mod_first: float32 [768, 4608], P(('dp', 'tensor'))
- grad_qkv_first: float32 [768, 3, 768], P('dp', None, 'tensor')
- grad_proj_first: float32 [768, 768], P('tensor', 'dp')
- grad_up_first: float32 [768, 3072], P('dp', 'tensor')
- grad_down_first: float32 [3072, 768], P('tensor', 'dp')
- grad_mod_second: float32 [768, 4608], P(('dp', 'tensor'))
- grad_qkv_second: float32 [768, 3, 768], P('dp', None, 'tensor')
- grad_proj_second: float32 [768, 768], P('tensor', 'dp')
- grad_up_second: float32 [768, 3072], P('dp', 'tensor')
- grad_down_second: float32 [3072, 768], P('tensor', 'dp')
Inputs may be any that keep to these rules, and one draw needn't show every extreme that they name: `segment_ids`: in each aligned block of 1280 tokens (one packed group) the ids number its sequences from 0 and never fall; a group is either one sequence of 1024 and one of 256 tokens, in either order, or five sequences of 256 tokens. `kept_rows`: each aligned block of 640 entries lists, in ascending order, distinct positions within one packed group: exactly half of the positions of each of its sequences.
All inputs are finite; a program needn't handle non-finite values.
Results may differ from a plain program's by a relative error of at most 0.035.
Values may be sent and summed in bfloat16 or wider, within the bound.
No kernel may reach another device: no remote copies, remote signals or barrier semaphores. Data moves between devices by JAX's collectives and lax.ppermute only.
A program may use at most 320 MiB of HBM per device.

v0:
```python
import jax
import jax.numpy as jnp
from jax import lax
from jax.sharding import PartitionSpec as P

HEAD_DIM = 64
SLOTS = 5
GROUP = 1280
KEEP = 640


NORM_EPS = 1e-06
HIGHEST = lax.Precision.HIGHEST
MASK_FILL = -1e30


def modulate(value_rows, shift_rows, scale_rows):
    centre = value_rows - jnp.mean(value_rows, axis=-1, keepdims=True)
    spread_sq = jnp.mean(centre * centre, axis=-1, keepdims=True)
    return centre * lax.rsqrt(spread_sq + NORM_EPS) * (1.0 + scale_rows) + shift_rows


def one_hot(slot_ids, count_slots):
    return (slot_ids[:, None] == jnp.arange(count_slots, dtype=jnp.int32)[None, :]).astype(
        jnp.float32
    )


def spread_rows(slot_hot, mod_rows):
    return jnp.dot(slot_hot, mod_rows, precision=HIGHEST)


def contract_rows(left, right):
    return lax.dot_general(
        left, right, (((0,), (0,)), ((), ())), preferred_element_type=jnp.float32
    )


def contract_cols(left, right):
    return lax.dot_general(
        left, right, (((1,), (1,)), ((), ())), preferred_element_type=jnp.float32
    )


def contract_high(left, right):
    return lax.dot_general(left, right, (((0,), (0,)), ((), ())), precision=HIGHEST)


def gather_rows(rows_in):
    return lax.all_gather(rows_in, "tensor", axis=0, tiled=True)


def scatter_rows(left, weight):
    own_rows = left.shape[0] // lax.axis_size("tensor")

    def row_term(row_start, row_count):
        return jnp.dot(left, weight, preferred_element_type=jnp.float32)

    return lax.psum_scatter(
        row_term(jnp.int32(0), lax.axis_size("tensor") * own_rows).astype(jnp.bfloat16),
        "tensor",
        scatter_dimension=0,
        tiled=True,
    ).astype(jnp.float32)


def gather_grads(rows_in):
    return lax.all_gather(rows_in, "tensor", axis=0, tiled=True)


def scatter_back(left, weight):
    own_rows = left.shape[0] // lax.axis_size("tensor")

    def row_term(row_start, row_count):
        return contract_cols(left, weight)

    return lax.psum_scatter(
        row_term(jnp.int32(0), lax.axis_size("tensor") * own_rows).astype(jnp.bfloat16),
        "tensor",
        scatter_dimension=0,
        tiled=True,
    ).astype(jnp.float32)


def keep_rows(rows_in):
    return rows_in


def pair_total(partial_value):
    return lax.psum(partial_value.astype(jnp.bfloat16), "tensor").astype(jnp.float32)


def kept_total(left, weight):
    return pair_total(jnp.dot(left, weight, preferred_element_type=jnp.float32))


def kept_total_back(left, weight):
    return pair_total(contract_cols(left, weight))


def attend(qkv_rows, segment_index, blocks):
    row_count, triple, head_count, head_dim = qkv_rows.shape
    scaling = head_dim ** (-0.5)
    keys_all = qkv_rows[:, 1]
    values_all = qkv_rows[:, 2]
    size_block = row_count // blocks
    queries = qkv_rows[:, 0].reshape(blocks, size_block, head_count, head_dim)
    seg_blocks = segment_index.reshape(blocks, size_block)

    def one_block(block_item):
        query_part, seg_part = block_item
        scores = (
            jnp.einsum("qhd,khd->hqk", query_part, keys_all, preferred_element_type=jnp.float32)
            * scaling
        )
        same_seq = seg_part[:, None] == segment_index[None, :]
        scores = jnp.where(same_seq[None], scores, MASK_FILL)
        highest = jnp.max(scores, axis=-1, keepdims=True)
        shifted = jnp.exp(scores - highest)
        summed = jnp.sum(shifted, axis=-1, keepdims=True)
        att_weights = (shifted / summed).astype(jnp.bfloat16)
        mixed_rows = jnp.einsum(
            "hqk,khd->qhd", att_weights, values_all, preferred_element_type=jnp.float32
        )
        log_total = highest[..., 0] + jnp.log(summed[..., 0])
        return (mixed_rows, log_total)

    mixed_rows, log_total = lax.map(one_block, (queries, seg_blocks))
    return (mixed_rows.reshape(row_count, head_count * head_dim), log_total)


def attend_back(qkv_rows, segment_index, log_total, d_mixed, blocks):
    row_count, triple, head_count, head_dim = qkv_rows.shape
    scaling = head_dim ** (-0.5)
    keys_all = qkv_rows[:, 1]
    values_all = qkv_rows[:, 2]
    size_block = row_count // blocks
    queries = qkv_rows[:, 0].reshape(blocks, size_block, head_count, head_dim)
    seg_blocks = segment_index.reshape(blocks, size_block)
    d_blocks = d_mixed.reshape(blocks, size_block, head_count, head_dim)

    def one_block(carry, block_item):
        acc_keys, acc_values = carry
        query_part, seg_part, lse_part, d_part = block_item
        scores = (
            jnp.einsum("qhd,khd->hqk", query_part, keys_all, preferred_element_type=jnp.float32)
            * scaling
        )
        same_seq = seg_part[:, None] == segment_index[None, :]
        scores = jnp.where(same_seq[None], scores, MASK_FILL)
        prob_rows = jnp.exp(scores - lse_part[:, :, None])
        d_probs = jnp.einsum("qhd,khd->hqk", d_part, values_all, preferred_element_type=jnp.float32)
        d_scores = (
            prob_rows * (d_probs - jnp.sum(prob_rows * d_probs, axis=-1, keepdims=True))
        ).astype(jnp.bfloat16)
        d_query = (
            jnp.einsum("hqk,khd->qhd", d_scores, keys_all, preferred_element_type=jnp.float32)
            * scaling
        )
        acc_keys = (
            acc_keys
            + jnp.einsum("hqk,qhd->khd", d_scores, query_part, preferred_element_type=jnp.float32)
            * scaling
        )
        acc_values = acc_values + jnp.einsum(
            "hqk,qhd->khd",
            prob_rows.astype(jnp.bfloat16),
            d_part,
            preferred_element_type=jnp.float32,
        )
        return ((acc_keys, acc_values), d_query)

    zero_rows = jnp.zeros((row_count, head_count, head_dim), jnp.float32)
    (d_keys, d_values), d_query = lax.scan(
        one_block, (zero_rows, zero_rows), (queries, seg_blocks, log_total, d_blocks)
    )
    d_query = d_query.reshape(row_count, head_count, head_dim)
    return (
        jnp.stack([d_query, d_keys, d_values], axis=1).reshape(row_count, -1).astype(jnp.bfloat16)
    )


def block_forward(
    value_rows, slot_hot, seg_groups, mod_table, weight_set, collect, combine, blocks
):
    w_qkv, w_proj, w_up, w_down = weight_set
    spans = [spread_rows(slot_hot, mod_table[:, column]) for column in range(6)]
    normed = modulate(value_rows, spans[0], spans[1]).astype(jnp.bfloat16)
    normed_all = collect(normed)
    qkv_rows = jnp.dot(
        normed_all, w_qkv.reshape(w_qkv.shape[0], -1), preferred_element_type=jnp.float32
    ).astype(jnp.bfloat16)
    groups, group_rows = seg_groups.shape
    head_count = w_qkv.shape[2] // HEAD_DIM
    qkv_groups = qkv_rows.reshape(groups, group_rows, 3, head_count, HEAD_DIM)
    mixed_rows, log_total = lax.map(
        lambda group_item: attend(group_item[0], group_item[1], blocks), (qkv_groups, seg_groups)
    )
    mixed_low = mixed_rows.reshape(groups * group_rows, -1).astype(jnp.bfloat16)
    attn_out = combine(mixed_low, w_proj)
    middle = value_rows + spans[2] * attn_out
    normed_two = modulate(middle, spans[3], spans[4]).astype(jnp.bfloat16)
    normed_two_all = collect(normed_two)
    up_proj = jnp.dot(normed_two_all, w_up, preferred_element_type=jnp.float32)
    activated = jax.nn.gelu(up_proj, approximate=True).astype(jnp.bfloat16)
    mlp_out = combine(activated, w_down)
    saved = (
        normed_all,
        qkv_groups,
        log_total,
        mixed_low,
        attn_out,
        middle,
        normed_two_all,
        up_proj,
        activated,
        mlp_out,
    )
    return (middle + spans[5] * mlp_out, saved)


def block_backward(
    grad_out,
    value_rows,
    slot_hot,
    sum_hot,
    seg_groups,
    mod_table,
    weight_set,
    saved,
    collect,
    combine,
    blocks,
):
    w_qkv, w_proj, w_up, w_down = weight_set
    (
        normed_all,
        qkv_groups,
        log_total,
        mixed_low,
        attn_out,
        middle,
        normed_two_all,
        up_proj,
        activated,
        mlp_out,
    ) = saved
    spans = [spread_rows(slot_hot, mod_table[:, column]) for column in range(6)]
    d_mlp = (grad_out * spans[5]).astype(jnp.bfloat16)
    d_gate_two = grad_out * mlp_out
    d_mlp_all = collect(d_mlp)
    d_activated = contract_cols(d_mlp_all, w_down)
    grad_down = contract_rows(activated, d_mlp_all)
    gelu_value, gelu_back = jax.vjp(lambda pre_act: jax.nn.gelu(pre_act, approximate=True), up_proj)
    d_up = gelu_back(d_activated)[0].astype(jnp.bfloat16)
    grad_up = contract_rows(normed_two_all, d_up)
    d_normed_two = combine(d_up, w_up)
    norm_value, norm_back = jax.vjp(modulate, middle, spans[3], spans[4])
    d_middle, d_shift_two, d_scale_two = norm_back(d_normed_two)
    d_middle = d_middle + grad_out
    d_attn = (d_middle * spans[2]).astype(jnp.bfloat16)
    d_gate_one = d_middle * attn_out
    d_attn_all = collect(d_attn)
    d_mixed = contract_cols(d_attn_all, w_proj).astype(jnp.bfloat16)
    grad_proj = contract_rows(mixed_low, d_attn_all)
    groups, group_rows = seg_groups.shape
    head_count = w_qkv.shape[2] // HEAD_DIM
    d_mixed_groups = d_mixed.reshape(groups, group_rows, head_count, HEAD_DIM)
    d_qkv = lax.map(
        lambda group_item: attend_back(
            group_item[0], group_item[1], group_item[2], group_item[3], blocks
        ),
        (qkv_groups, seg_groups, log_total, d_mixed_groups),
    )
    d_qkv = d_qkv.reshape(groups * group_rows, -1)
    w_qkv_flat = w_qkv.reshape(w_qkv.shape[0], -1)
    grad_qkv = contract_rows(normed_all, d_qkv).reshape(w_qkv.shape)
    d_normed = combine(d_qkv, w_qkv_flat)
    norm_value_one, norm_back_one = jax.vjp(modulate, value_rows, spans[0], spans[1])
    d_values, d_shift_one, d_scale_one = norm_back_one(d_normed)
    d_values = d_values + d_middle
    per_token = jnp.stack(
        [d_shift_one, d_scale_one, d_gate_one, d_shift_two, d_scale_two, d_gate_two], axis=1
    )
    d_table = jnp.einsum("rs,rcd->scd", sum_hot, per_token, precision=HIGHEST)
    return (
        d_values,
        (grad_qkv, grad_proj, grad_up, grad_down),
        d_table.reshape(d_table.shape[0], -1),
    )


def on_device(
    tokens,
    conditioning,
    segment_ids,
    kept_rows,
    cotangent,
    mod_first,
    qkv_first,
    proj_first,
    up_first,
    down_first,
    mod_second,
    qkv_second,
    proj_second,
    up_second,
    down_second,
):
    tensor_count = lax.axis_size("tensor")
    tensor_pos = lax.axis_index("tensor")
    own_rows = tokens.shape[0]
    all_rows = segment_ids.shape[0]
    groups = all_rows // GROUP
    slot_count = conditioning.shape[0]
    row_start = tensor_pos * own_rows
    slot_all = jnp.arange(all_rows, dtype=jnp.int32) // GROUP * SLOTS + segment_ids
    slot_hot = one_hot(lax.dynamic_slice_in_dim(slot_all, row_start, own_rows), slot_count)
    kept_count = kept_rows.shape[0]
    kept_all = kept_rows + jnp.arange(kept_count, dtype=jnp.int32) // KEEP * GROUP
    kept_hot = one_hot(slot_all[kept_all], slot_count)
    kept_share = kept_count // tensor_count
    kept_mine = (jnp.arange(kept_count, dtype=jnp.int32) // kept_share == tensor_pos).astype(
        jnp.float32
    )
    kept_sum_hot = kept_hot * kept_mine[:, None]
    cond_act = jax.nn.silu(conditioning.astype(jnp.float32)).astype(jnp.bfloat16)
    table_first = jnp.dot(cond_act, mod_first, preferred_element_type=jnp.float32).reshape(
        slot_count, 6, -1
    )
    table_second = jnp.dot(cond_act, mod_second, preferred_element_type=jnp.float32).reshape(
        slot_count, 6, -1
    )
    seg_first = segment_ids.reshape(groups, GROUP)
    seg_second = segment_ids[kept_all].reshape(groups, KEEP)
    weights_first = (qkv_first, proj_first, up_first, down_first)
    weights_second = (qkv_second, proj_second, up_second, down_second)
    values_first = tokens.astype(jnp.float32)
    leading_rows, saved_first = block_forward(
        values_first, slot_hot, seg_first, table_first, weights_first, gather_rows, scatter_rows, 2
    )
    first_out = leading_rows.astype(jnp.bfloat16)
    first_all, cot_all = (
        lax.all_gather(first_out, "tensor", axis=0, tiled=True),
        lax.all_gather(cotangent, "tensor", axis=0, tiled=True),
    )
    first_wide = first_all.astype(jnp.float32)
    routed_in = first_wide[kept_all]
    second_rows, saved_second = block_forward(
        routed_in, kept_hot, seg_second, table_second, weights_second, keep_rows, kept_total, 1
    )
    routed_all = first_wide.at[kept_all].set(second_rows)
    routed_out = lax.dynamic_slice_in_dim(routed_all, row_start, own_rows).astype(jnp.bfloat16)
    cot_wide = cot_all.astype(jnp.float32)
    d_routed, grads_second, d_table_second = block_backward(
        cot_wide[kept_all],
        routed_in,
        kept_hot,
        kept_sum_hot,
        seg_second,
        table_second,
        weights_second,
        saved_second,
        keep_rows,
        kept_total_back,
        1,
    )
    d_first_all = cot_wide.at[kept_all].set(d_routed)
    d_first = lax.dynamic_slice_in_dim(d_first_all, row_start, own_rows)
    input_grad, grads_first, d_table_first = block_backward(
        d_first,
        values_first,
        slot_hot,
        slot_hot,
        seg_first,
        table_first,
        weights_first,
        saved_first,
        gather_grads,
        scatter_back,
        2,
    )
    qkv_grad_one, proj_grad_one, up_grad_one, down_grad_one = grads_first
    qkv_grad_two, proj_grad_two, up_grad_two, down_grad_two = grads_second
    summed = (
        lax.psum_scatter(qkv_grad_one, "dp", scatter_dimension=0, tiled=True),
        lax.psum_scatter(proj_grad_one, "dp", scatter_dimension=1, tiled=True),
        lax.psum_scatter(up_grad_one, "dp", scatter_dimension=0, tiled=True),
        lax.psum_scatter(down_grad_one, "dp", scatter_dimension=1, tiled=True),
        lax.psum_scatter(qkv_grad_two, "dp", scatter_dimension=0, tiled=True),
        lax.psum_scatter(proj_grad_two, "dp", scatter_dimension=1, tiled=True),
        lax.psum_scatter(up_grad_two, "dp", scatter_dimension=0, tiled=True),
        lax.psum_scatter(down_grad_two, "dp", scatter_dimension=1, tiled=True),
    )
    cond_wide = cond_act.astype(jnp.float32)
    slot_one, slot_two = (
        lax.psum(d_table_first.astype(jnp.bfloat16), "tensor").astype(jnp.float32),
        lax.psum(d_table_second.astype(jnp.bfloat16), "tensor").astype(jnp.float32),
    )
    cond_every, slot_every_one, slot_every_two = (
        lax.all_gather(cond_wide.astype(jnp.bfloat16), "dp", axis=0, tiled=True).astype(
            cond_wide.dtype
        ),
        lax.all_gather(slot_one.astype(jnp.bfloat16), "dp", axis=0, tiled=True).astype(
            slot_one.dtype
        ),
        lax.all_gather(slot_two.astype(jnp.bfloat16), "dp", axis=0, tiled=True).astype(
            slot_two.dtype
        ),
    )
    mod_rows = mod_first.shape[0] // (lax.axis_size("dp") * tensor_count)
    first_mod_row = (lax.axis_index("dp") * tensor_count + tensor_pos) * mod_rows
    cond_cols = lax.dynamic_slice_in_dim(cond_every, first_mod_row, mod_rows, 1)
    mod_done_one = contract_high(cond_cols, slot_every_one)
    mod_done_two = contract_high(cond_cols, slot_every_two)
    return (
        first_out,
        routed_out,
        input_grad,
        mod_done_one,
        summed[0],
        summed[1],
        summed[2],
        summed[3],
        mod_done_two,
        summed[4],
        summed[5],
        summed[6],
        summed[7],
    )


def solution(mesh):
    return jax.shard_map(
        on_device,
        mesh=mesh,
        in_specs=(
            P(("dp", "tensor"), None),
            P("dp", None),
            P("dp"),
            P("dp"),
            P(("dp", "tensor"), None),
            P(),
            P(None, None, "tensor"),
            P("tensor", None),
            P(None, "tensor"),
            P("tensor", None),
            P(),
            P(None, None, "tensor"),
            P("tensor", None),
            P(None, "tensor"),
            P("tensor", None),
        ),
        out_specs=(
            P(("dp", "tensor"), None),
            P(("dp", "tensor"), None),
            P(("dp", "tensor"), None),
            P(("dp", "tensor"), None),
            P("dp", None, "tensor"),
            P("tensor", "dp"),
            P("dp", "tensor"),
            P("tensor", "dp"),
            P(("dp", "tensor"), None),
            P("dp", None, "tensor"),
            P("tensor", "dp"),
            P("dp", "tensor"),
            P("tensor", "dp"),
        ),
        check_vma=False,
    )
```

profile of v0, /device:TPU:0, one launch (start us, length us, event | category | flops | bytes accessed | tf_op | source)
XLA Modules:
  0.0 1482.4 jit_solution(18381671540896182002)
XLA Ops:
  26.0 30.3 %all-gather.10.cloned.1.call-done = bf16[1280,768]{1,0:T(8,128)(2,1)} async-done(((bf16[640,768]{1,0:T(8,128)(2,1)}), bf16[1280,768]{1,0:T(8,128)(2,1)}) %all-gather.10.cloned.1.call-update) | async-done | bytes 1966096 | tf_op jit(solution)/shard_map/all_gather | solution.py:50
  56.3 4.6 convolution_convert_fusion
  67.9 31.1 %while.48 = (s32[]{:T(128)}, bf16[2,640,6,64]{1,3,2,0:T(8,128)(2,1)}, f32[2,6,640]{2,1,0:T(8,128)S(1)}, s32[2,640]{1,0:T(2,128)S(1)}, s32[1280]{0:T(1024)S(1)}, ...) while((s32[]{:T(128)}, ...), condition=%wide.region_5.6_spmd, body=%wide.region_2.5_spmd.sunk | while | flops 1298428160 | bytes 64212596 | solution.py:128
  68.4 5.0 fusion.283
  77.1 6.1 fusion.285
  83.9 5.0 fusion.283
  92.6 6.1 fusion.285
  108.0 27.5 %reduce-scatter.13.cloned.1.call-done = bf16[640,768]{1,0:T(8,128)(2,1)} async-done(((bf16[1280,768]{1,0:T(8,128)(2,1)}), bf16[640,768]{1,0:T(8,128)(2,1)}) %reduce-scatter.13.cloned.1.call-update) | async-done | bytes 983056 | tf_op jit(solution)/shard_map/reduce_scatter | solution.py:59
  144.3 31.7 %all-gather.12.cloned.1.call-done = bf16[1280,768]{1,0:T(8,128)(2,1)} async-done(((bf16[640,768]{1,0:T(8,128)(2,1)}), bf16[1280,768]{1,0:T(8,128)(2,1)}) %all-gather.12.cloned.1.call-update) | async-done | bytes 1966096 | tf_op jit(solution)/shard_map/all_gather | solution.py:50
  176.1 5.5 fusion.198
  184.6 5.8 convolution_convert_fusion.3
  190.5 30.5 %reduce-scatter.15.cloned.1.call-done = bf16[640,768]{1,0:T(8,128)(2,1)} async-done(((bf16[1280,768]{1,0:T(8,128)(2,1)}), bf16[640,768]{1,0:T(8,128)(2,1)}) %reduce-scatter.15.cloned.1.call-update) | async-done | bytes 983056 | tf_op jit(solution)/shard_map/reduce_scatter | solution.py:59
  221.0 4.5 fusion.61
  244.9 12.3 all-gather.14.cloned.1.call-done
  261.0 6.1 gather_fusion
  298.2 6.4 gather_fusion.3
  313.2 18.7 %all-reduce.7.cloned.1.call-done = bf16[640,768]{1,0:T(8,128)(2,1)} async-done(((bf16[640,768]{1,0:T(8,128)(2,1)}), bf16[640,768]{1,0:T(8,128)(2,1)}) %all-reduce.7.cloned.1.call-update) | async-done | bytes 983056 | tf_op jit(solution)/shard_map/psum | solution.py:90
  331.9 4.5 fusion.191
  340.3 5.1 fusion.50
  349.7 6.2 convolution_convert_fusion.9
  355.9 32.3 %all-reduce.9.cloned.1.call-done = bf16[640,768]{1,0:T(8,128)(2,1)} async-done(((bf16[640,768]{1,0:T(8,128)(2,1)}), bf16[640,768]{1,0:T(8,128)(2,1)}) %all-reduce.9.cloned.1.call-update) | async-done | bytes 983056 | tf_op jit(solution)/shard_map/psum | solution.py:90
  398.7 6.7 multiply_reduce_fusion.1
  405.5 10.6 multiply_convert_fusion.1
  416.1 4.4 fusion.94
  427.4 60.3 %all-reduce.13.cloned.1.call-done = (bf16[640,768]{1,0:T(8,128)(2,1)}, bf16[640,768]{1,0:T(8,128)(2,1)}) async-done(((bf16[640,768]{1,0:T(8,128)(2,1)}, bf16[640,768]{1,0:T(8,128)(2,1)}), (bf16[640,768]{1,0:T(8,128)(2,1)}, bf16[640,768]{1,0:T(8,128)(2,1)})) %all-reduce.13.cloned.1.call-update) | async-done | bytes 1966096 | tf_op jit(solution)/shard_map/psum | solution.py:90
  493.7 13.7 scatter_custom_fusion.1
  510.7 31.7 %all-gather.18.cloned.1.call-done = bf16[1280,768]{1,0:T(8,128)(2,1)} async-done(((bf16[640,768]{1,0:T(8,128)(2,1)}), bf16[1280,768]{1,0:T(8,128)(2,1)}) %all-gather.18.cloned.1.call-update) | async-done | bytes 1966096 | tf_op jit(solution)/shard_map/all_gather | solution.py:68
  542.5 10.4 fusion.38
  554.8 4.4 convolution_convert_fusion.2
  559.4 30.5 %reduce-scatter.17.cloned.1.call-done = bf16[640,768]{1,0:T(8,128)(2,1)} async-done(((bf16[1280,768]{1,0:T(8,128)(2,1)}), bf16[640,768]{1,0:T(8,128)(2,1)}) %reduce-scatter.17.cloned.1.call-update) | async-done | bytes 983056 | tf_op jit(solution)/shard_map/reduce_scatter | solution.py:77
  597.5 31.5 %all-gather.20.cloned.1.call-done = bf16[1280,768]{1,0:T(8,128)(2,1)} async-done(((bf16[640,768]{1,0:T(8,128)(2,1)}), bf16[1280,768]{1,0:T(8,128)(2,1)}) %all-gather.20.cloned.1.call-update) | async-done | bytes 1966096 | tf_op jit(solution)/shard_map/all_gather | solution.py:68
  635.9 166.6 %while.49 = (s32[]{:T(128)}, f32[1280,6,64]{0,2,1:T(8,128)}, f32[1280,6,64]{0,2,1:T(8,128)}, bf16[2,640,6,64]{1,0,3,2:T(2,128)(2,1)}, bf16[2,640,6,64]{1,3,2,0:T...) while((s32[]{:T(128)}, f32[1280,6,64]{0,2,1:T(8,128)}, ...), condition=%wide.region_32.33_spmd.clone, body=%wide.region_30.32_spmd.clone.sunk | while | flops 3193729280 | bytes 294187808 | solution.py:174
  636.5 10.7 fusion.295
  647.2 17.7 %multiply_reduce_fusion.9 = (f32[6,640]{1,0:T(8,128)S(1)}, f32[6,640,1280]{2,1,0:T(8,128)}) fusion(f32[6,640,1280]{2,1,0:T(8,128)} %fusion.295, f32[6,640]{1,0:T(8,128)S(1)} %dynamic-slice_bitcast_fusion.2, bf16[1280,6,64]{0,2,1:T(8,128)(2,1)S(1)} %get-tuple-element.620, bf16[2,640,6,64]{1,3,2,0:T(8,128)(2,1)S(1)} %copy-done.21, s32[]{:T(128)S(6)} %copy.189, ...), kind=kOutput, calls=%fused_computation.20.clone.1 | convolution fusion | flops 653717760 | bytes 41651204 | tf_op jit(solution)/shard_map/while/body/eval_jaxpr/while/body/eval_jaxpr/qhd,khd->hqk/dot_general | solution.py:146
  664.9 17.4 %multiply_convert_fusion.13 = bf16[6,640,1280]{2,1,0:T(8,128)(2,1)} fusion(f32[6,640,1280]{2,1,0:T(8,128)} %get-tuple-element.558, f32[6,640,1280]{2,1,0:T(8,128)} %fusion.295, f32[6,640]{1,0:T(8,128)S(1)} %get-tuple-element.559), kind=kLoop, calls=%fused_computation.19.clone.1 | loop fusion | flops 14745600 | bytes 49167360 | tf_op jit(solution)/shard_map/while/body/eval_jaxpr/while/body/eval_jaxpr/convert_element_type | solution.py:155
  689.8 7.0 fusion.298
  700.6 17.1 %dynamic_update_slice.48 = bf16[2,640,6,64]{1,0,3,2:T(2,128)(2,1)} dynamic-update-slice(bf16[2,640,6,64]{1,0,3,2:T(2,128)(2,1)} %get-tuple-element.603, bf16[1,640,6,64]{1,0,3,2:T(2,128)(2,1)S(1)} %copy.166, s32[]{:T(128)S(6)} %copy.189, s32[]{:T(128)} %constant.225.clone.1..sunk, s32[]{:T(128)} %constant.225.clone.1..sunk, s32[]{:T(128)} %constant.225.clone.1..sunk) | dynamic-update-slice | bytes 983044 | tf_op jit(solution)/shard_map/while/body/eval_jaxpr/while/body/jit(dynamic_update_index_in_dim)/dynamic_update_slice | solution.py:128
  718.3 10.7 fusion.295
  729.0 17.7 %multiply_reduce_fusion.9 = (f32[6,640]{1,0:T(8,128)S(1)}, f32[6,640,1280]{2,1,0:T(8,128)}) fusion(f32[6,640,1280]{2,1,0:T(8,128)} %fusion.295, f32[6,640]{1,0:T(8,128)S(1)} %dynamic-slice_bitcast_fusion.2, bf16[1280,6,64]{0,2,1:T(8,128)(2,1)S(1)} %get-tuple-element.620, bf16[2,640,6,64]{1,3,2,0:T(8,128)(2,1)S(1)} %copy-done.21, s32[]{:T(128)S(6)} %copy.189, ...), kind=kOutput, calls=%fused_computation.20.clone.1 | convolution fusion | flops 653717760 | bytes 41651204 | tf_op jit(solution)/shard_map/while/body/eval_jaxpr/while/body/eval_jaxpr/qhd,khd->hqk/dot_general | solution.py:146
  746.7 17.4 %multiply_convert_fusion.13 = bf16[6,640,1280]{2,1,0:T(8,128)(2,1)} fusion(f32[6,640,1280]{2,1,0:T(8,128)} %get-tuple-element.558, f32[6,640,1280]{2,1,0:T(8,128)} %fusion.295, f32[6,640]{1,0:T(8,128)S(1)} %get-tuple-element.559), kind=kLoop, calls=%fused_computation.19.clone.1 | loop fusion | flops 14745600 | bytes 49167360 | tf_op jit(solution)/shard_map/while/body/eval_jaxpr/while/body/eval_jaxpr/convert_element_type | solution.py:155
  768.3 4.8 fusion.297
  773.1 7.0 fusion.298
  780.1 4.6 fusion.296
  785.4 17.1 %dynamic_update_slice.48 = bf16[2,640,6,64]{1,0,3,2:T(2,128)(2,1)} dynamic-update-slice(bf16[2,640,6,64]{1,0,3,2:T(2,128)(2,1)} %get-tuple-element.603, bf16[1,640,6,64]{1,0,3,2:T(2,128)(2,1)S(1)} %copy.166, s32[]{:T(128)S(6)} %copy.189, s32[]{:T(128)} %constant.225.clone.1..sunk, s32[]{:T(128)} %constant.225.clone.1..sunk, s32[]{:T(128)} %constant.225.clone.1..sunk) | dynamic-update-slice | bytes 983044 | tf_op jit(solution)/shard_map/while/body/eval_jaxpr/while/body/jit(dynamic_update_index_in_dim)/dynamic_update_slice | solution.py:128
  823.0 6.3 convolution_convert_fusion.12
  829.3 15.1 %reduce-scatter.19.cloned.1.call-done = bf16[640,768]{1,0:T(8,128)(2,1)} async-done(((bf16[1280,768]{1,0:T(8,128)(2,1)}), bf16[640,768]{1,0:T(8,128)(2,1)}) %reduce-scatter.19.cloned.1.call-update) | async-done | bytes 983056 | tf_op jit(solution)/shard_map/reduce_scatter | solution.py:77
  853.5 4.6 convolution_convert_fusion.13
  860.1 5.2 fusion.97
  866.5 6.5 fusion.185
  874.2 5.8 fusion.203
  881.6 9.0 fusion.186
  892.2 7.0 fusion.201
  904.4 7.0 fusion.86
  912.1 22.0 %all-gather = bf16[16,5,768]{2,1,0:T(8,128)(2,1)S(1)} all-gather(bf16[1,5,768]{2,1,0:T(8,128)(2,1)S(1)} %fusion.180), channel_id=1, replica_groups=mesh['dp'=16,'tensor'=2] {'dp'}, dimensions={0}, use_global_device_ids=true | all-gather | bytes 130560 | tf_op jit(solution)/shard_map/all_gather | solution.py:401
  934.9 11.2 scatter_custom_fusion
  953.7 21.3 %all-gather.2 = bf16[16,5,4608]{2,1,0:T(8,128)(2,1)S(1)} all-gather(bf16[1,5,4608]{2,1,0:T(8,128)(2,1)} %bitcast.341), channel_id=1, replica_groups=mesh['dp'=16,'tensor'=2] {'dp'}, dimensions={0}, use_global_device_ids=true | all-gather | bytes 783360 | tf_op jit(solution)/shard_map/all_gather | solution.py:407
  976.3 30.1 %all-gather.1 = bf16[16,5,4608]{2,1,0:T(8,128)(2,1)S(1)} all-gather(bf16[1,5,4608]{2,1,0:T(8,128)(2,1)} %bitcast.340), channel_id=1, replica_groups=mesh['dp'=16,'tensor'=2] {'dp'}, dimensions={0}, use_global_device_ids=true | all-gather | bytes 783360 | tf_op jit(solution)/shard_map/all_gather | solution.py:404
  1012.1 12.9 reduce-scatter.29.cloned.1.call-done
  1025.0 79.3 %reduce-scatter.35.cloned.1.call-done = f32[1536,48]{0,1:T(8,128)} async-done(((f32[1536,768]{0,1:T(8,128)}), f32[1536,48]{0,1:T(8,128)}) %reduce-scatter.35.cloned.1.call-update) | async-done | bytes 294928 | tf_op jit(solution)/shard_map/reduce_scatter | solution.py:393
  1104.3 78.9 %reduce-scatter.33.cloned.1.call-done = f32[48,1536]{1,0:T(8,128)} async-done(((f32[768,1536]{1,0:T(8,128)}), f32[48,1536]{1,0:T(8,128)}) %reduce-scatter.33.cloned.1.call-update) | async-done | bytes 294928 | tf_op jit(solution)/shard_map/reduce_scatter | solution.py:392
  1183.2 79.6 %reduce-scatter.27.cloned.1.call-done = f32[1536,48]{0,1:T(8,128)} async-done(((f32[1536,768]{0,1:T(8,128)}), f32[1536,48]{0,1:T(8,128)}) %reduce-scatter.27.cloned.1.call-update) | async-done | bytes 294928 | tf_op jit(solution)/shard_map/reduce_scatter | solution.py:389
  1262.7 78.9 %reduce-scatter.25.cloned.1.call-done = f32[48,1536]{1,0:T(8,128)} async-done(((f32[768,1536]{1,0:T(8,128)}), f32[48,1536]{1,0:T(8,128)}) %reduce-scatter.25.cloned.1.call-update) | async-done | bytes 294928 | tf_op jit(solution)/shard_map/reduce_scatter | solution.py:388
  1341.6 61.8 %reduce-scatter.23.cloned.1.call-done = f32[384,48]{0,1:T(8,128)} async-done(((f32[384,768]{0,1:T(8,128)}), f32[384,48]{0,1:T(8,128)}) %reduce-scatter.23.cloned.1.call-update) | async-done | bytes 73744 | tf_op jit(solution)/shard_map/reduce_scatter | solution.py:387
  1403.4 71.9 %reduce-scatter.21.cloned.1.call-done = f32[48,3,384]{2,0,1:T(8,128)} async-done(((f32[768,3,384]{2,0,1:T(8,128)}), f32[48,3,384]{2,0,1:T(8,128)}) %reduce-scatter.21.cloned.1.call-update) | async-done | bytes 221200 | tf_op jit(solution)/shard_map/reduce_scatter | solution.py:386
  (438 shorter events, 244.2 us)
Async XLA Ops:
  7.2 177.4 %copy-start = (bf16[1536,768]{1,0:T(8,128)(2,1)S(1)}, bf16[1536,768]{1,0:T(8,128)(2,1)}, u32[]{:S(2)}) copy-start(bf16[1536,768]{1,0:T(8,128)(2,1)} %param.28) | copy-start | bytes 7077892
  7.2 49.1 %all-gather.10.cloned.1.call-start = ((), (), s32[]{:S(2)}) async-start(), calls=%async_computation.12 | async-start | bytes 2949120 | tf_op jit(solution)/shard_map/all_gather | solution.py:50
  8.8 8.1 copy-start.85
  10.5 6.4 copy-start.94
  11.1 4.8 copy-start.4
  15.9 5.9 copy-start.69
  21.8 113.7 %reduce-scatter.13.cloned.1.call-start = ((), (), s32[]{:S(2)}) async-start(), calls=%async_computation.13 | async-start | bytes 2949120 | tf_op jit(solution)/shard_map/reduce_scatter | solution.py:59
  104.9 30.6 %copy-start.92 = (f32[5,1,768]{2,1,0:T(1,128)S(1)}, f32[5,1,768]{2,1,0:T(1,128)}, u32[]{:S(2)}) copy-start(f32[5,1,768]{2,1,0:T(1,128)} %get-tuple-element.423) | copy-start | bytes 46084
  104.9 71.1 %all-gather.12.cloned.1.call-start = ((), (), s32[]{:S(2)}) async-start(), calls=%async_computation.14 | async-start | bytes 2949120 | tf_op jit(solution)/shard_map/all_gather | solution.py:50
  144.3 76.7 %reduce-scatter.15.cloned.1.call-start = ((), (), s32[]{:S(2)}) async-start(), calls=%async_computation.15 | async-start | bytes 2949120 | tf_op jit(solution)/shard_map/reduce_scatter | solution.py:59
  190.4 30.6 %copy-start.90 = (f32[5,1,768]{2,1,0:T(1,128)S(1)}, f32[5,1,768]{2,1,0:T(1,128)}, u32[]{:S(2)}) copy-start(f32[5,1,768]{2,1,0:T(1,128)} %get-tuple-element.420) | copy-start | bytes 46084
  190.4 66.8 %all-gather.14.cloned.1.call-start = ((), (), s32[]{:S(2)}) async-start(), calls=%async_computation.16 | async-start | bytes 2949120 | tf_op jit(solution)/shard_map/all_gather | solution.py:344
  225.5 68.9 %all-gather.16.cloned.1.call-start = ((), (), s32[]{:S(2)}) async-start(), calls=%async_computation.18 | async-start | bytes 2949120 | tf_op jit(solution)/shard_map/all_gather | solution.py:345
  226.1 105.8 %all-reduce.7.cloned.1.call-start = ((), (), s32[]{:S(2)}) async-start(), calls=%async_computation.17 | async-start | bytes 1966080 | tf_op jit(solution)/shard_map/psum | solution.py:90
  226.1 267.5 %copy-start.107 = (s32[640]{0:T(1024)}, s32[640]{0:T(1024)S(1)}, u32[]{:S(2)}) copy-start(s32[640]{0:T(1024)S(1)} %compare_select_fusion) | copy-start | bytes 7684
  234.2 102.6 %copy-start.72 = (s32[640]{0:T(1024)}, s32[640]{0:T(1024)S(1)}, u32[]{:S(2)}) copy-start(s32[640]{0:T(1024)S(1)} %gather_fusion.1) | copy-start | bytes 7684
  269.0 221.9 %copy-start.81 = (f32[640]{0:T(1024)}, f32[640]{0:T(1024)S(1)}, u32[]{:S(2)}) copy-start(f32[640]{0:T(1024)S(1)} %broadcast_multiply_fusion.1) | copy-start | bytes 7684
  271.0 219.9 %copy-start.99 = (f32[640]{0:T(1024)}, f32[640]{0:T(1024)S(1)}, u32[]{:S(2)}) copy-start(f32[640]{0:T(1024)S(1)} %fusion.175) | copy-start | bytes 7684
  292.0 96.2 %all-reduce.9.cloned.1.call-start = ((), (), s32[]{:S(2)}) async-start(), calls=%async_computation.19 | async-start | bytes 1966080 | tf_op jit(solution)/shard_map/psum | solution.py:90
  304.6 5.0 copy-start.110
  331.9 8.2 copy-start.118
  336.4 54.9 %copy-start.83 = (f32[640]{0:T(1024)}, f32[640]{0:T(1024)S(1)}, u32[]{:S(2)}) copy-start(f32[640]{0:T(1024)S(1)} %broadcast_multiply_fusion) | copy-start | bytes 7684
  336.7 54.5 %copy-start.101 = (f32[640]{0:T(1024)}, f32[640]{0:T(1024)S(1)}, u32[]{:S(2)}) copy-start(f32[640]{0:T(1024)S(1)} %fusion.176) | copy-start | bytes 7684
  340.3 5.1 copy-start.66
  349.4 138.4 %all-reduce.13.cloned.1.call-start = ((), (), s32[]{:S(2)}) async-start(), calls=%async_computation.33 | async-start | bytes 3932160 | tf_op jit(solution)/shard_map/psum | solution.py:90
  388.2 5.9 copy-start.29
  388.2 5.9 copy-start.47
  391.4 5.3 slice-start
  391.4 5.3 slice-start.1
  427.4 115.1 %all-gather.18.cloned.1.call-start = ((), (), s32[]{:S(2)}) async-start(), calls=%async_computation.20 | async-start | bytes 2949120 | tf_op jit(solution)/shard_map/all_gather | solution.py:68
  510.7 79.2 %reduce-scatter.17.cloned.1.call-start = ((), (), s32[]{:S(2)}) async-start(), calls=%async_computation.21 | async-start | bytes 2949120 | tf_op jit(solution)/shard_map/reduce_scatter | solution.py:77
  542.5 12.4 copy-start.111
  554.8 35.0 %copy-start.79 = (f32[640]{0:T(1024)S(1)}, f32[640]{0:T(1024)}, u32[]{:S(2)}) copy-start(f32[640]{0:T(1024)} %copy-done.78) | copy-start | bytes 7684
  559.3 30.6 %copy-start.15 = (f32[640,768]{1,0:T(8,128)S(1)}, f32[640,768]{1,0:T(8,128)}, u32[]{:S(2)}) copy-start(f32[640,768]{1,0:T(8,128)} %copy-done.14) | copy-start | bytes 5898244
  559.3 33.0 %copy-start.106 = (f32[640]{0:T(1024)S(1)}, f32[640]{0:T(1024)}, u32[]{:S(2)}) copy-start(f32[640]{0:T(1024)} %copy-done.105) | copy-start | bytes 7684
  559.3 33.0 %copy-start.97 = (f32[640]{0:T(1024)S(1)}, f32[640]{0:T(1024)}, u32[]{:S(2)}) copy-start(f32[640]{0:T(1024)} %copy-done.96) | copy-start | bytes 7684
  559.3 69.7 %all-gather.20.cloned.1.call-start = ((), (), s32[]{:S(2)}) async-start(), calls=%async_computation.22 | async-start | bytes 2949120 | tf_op jit(solution)/shard_map/all_gather | solution.py:68
  595.2 33.8 %copy-start.115 = (bf16[384,768]{1,0:T(8,128)(2,1)S(1)}, bf16[384,768]{1,0:T(8,128)(2,1)}, u32[]{:S(2)}) copy-start(bf16[384,768]{1,0:T(8,128)(2,1)} %param.26) | copy-start | bytes 1769476
  597.2 247.2 %reduce-scatter.19.cloned.1.call-start = ((), (), s32[]{:S(2)}) async-start(), calls=%async_computation.23 | async-start | bytes 2949120 | tf_op jit(solution)/shard_map/reduce_scatter | solution.py:77
  636.5 10.8 copy-start.21
  664.9 21.4 %copy-start.2 = (f32[6,640,1280]{2,1,0:T(8,128)S(1)}, f32[6,640,1280]{2,1,0:T(8,128)}, u32[]{:S(2)}) copy-start(f32[6,640,1280]{2,1,0:T(8,128)} %get-tuple-element.558) | copy-start | bytes 58982404 | tf_op jit(solution)/shard_map/while/body/eval_jaxpr/while
  664.9 21.6 %copy-start.26 = (bf16[2,640,6,64]{1,3,2,0:T(8,128)(2,1)S(1)}, bf16[2,640,6,64]{1,3,2,0:T(8,128)(2,1)}, u32[]{:S(2)}) copy-start(bf16[2,640,6,64]{1,3,2,0:T(8,128)(2,1)} %get-tuple-element.622) | copy-start | bytes 2949124 | tf_op jit(solution)/shard_map/while/body/eval_jaxpr/while
  689.8 7.0 copy-start.6
  689.8 7.0 copy-start.22
  718.2 10.8 copy-start.21
  746.7 21.4 %copy-start.2 = (f32[6,640,1280]{2,1,0:T(8,128)S(1)}, f32[6,640,1280]{2,1,0:T(8,128)}, u32[]{:S(2)}) copy-start(f32[6,640,1280]{2,1,0:T(8,128)} %get-tuple-element.558) | copy-start | bytes 58982404 | tf_op jit(solution)/shard_map/while/body/eval_jaxpr/while
  746.7 21.6 %copy-start.26 = (bf16[2,640,6,64]{1,3,2,0:T(8,128)(2,1)S(1)}, bf16[2,640,6,64]{1,3,2,0:T(8,128)(2,1)}, u32[]{:S(2)}) copy-start(bf16[2,640,6,64]{1,3,2,0:T(8,128)(2,1)} %get-tuple-element.622) | copy-start | bytes 2949124 | tf_op jit(solution)/shard_map/while/body/eval_jaxpr/while
  773.1 7.0 copy-start.6
  773.1 7.0 copy-start.22
  813.9 139.8 %all-reduce.11.cloned.1.call-start = ((), (), s32[]{:S(2)}) async-start(), calls=%async_computation.32 | async-start | bytes 294912 | tf_op jit(solution)/shard_map/psum | solution.py:397
  829.3 16.5 %copy-start.25 = (bf16[640,768]{1,0:T(8,128)(2,1)S(1)}, bf16[640,768]{1,0:T(8,128)(2,1)}, u32[]{:S(2)}) copy-start(bf16[640,768]{1,0:T(8,128)(2,1)} %param.19) | copy-start | bytes 2949124
  829.3 16.6 %copy-start.86 = (f32[640]{0:T(1024)S(1)}, f32[640]{0:T(1024)}, u32[]{:S(2)}) copy-start(f32[640]{0:T(1024)} %copy-done.85) | copy-start | bytes 7684
  829.3 16.6 %copy-start.95 = (f32[640]{0:T(1024)S(1)}, f32[640]{0:T(1024)}, u32[]{:S(2)}) copy-start(f32[640]{0:T(1024)} %copy-done.94) | copy-start | bytes 7684
  853.5 4.7 copy-start.56
  858.2 153.9 %reduce-scatter.31.cloned.1.call-start = ((), (), s32[]{:S(2)}) async-start(), calls=%async_computation.29 | async-start | bytes 1253376 | tf_op jit(solution)/shard_map/reduce_scatter | solution.py:391
  860.1 164.9 %reduce-scatter.29.cloned.1.call-start = ((), (), s32[]{:S(2)}) async-start(), calls=%async_computation.28 | async-start | bytes 3760128 | tf_op jit(solution)/shard_map/reduce_scatter | solution.py:390
  865.3 238.9 %reduce-scatter.35.cloned.1.call-start = ((), (), s32[]{:S(2)}) async-start(), calls=%async_computation.31 | async-start | bytes 5013504 | tf_op jit(solution)/shard_map/reduce_scatter | solution.py:393
  873.0 310.1 %reduce-scatter.33.cloned.1.call-start = ((), (), s32[]{:S(2)}) async-start(), calls=%async_computation.30 | async-start | bytes 5013504 | tf_op jit(solution)/shard_map/reduce_scatter | solution.py:392
  880.0 382.7 %reduce-scatter.27.cloned.1.call-start = ((), (), s32[]{:S(2)}) async-start(), calls=%async_computation.27 | async-start | bytes 5013504 | tf_op jit(solution)/shard_map/reduce_scatter | solution.py:389
  890.6 451.0 %reduce-scatter.25.cloned.1.call-start = ((), (), s32[]{:S(2)}) async-start(), calls=%async_computation.26 | async-start | bytes 5013504 | tf_op jit(solution)/shard_map/reduce_scatter | solution.py:388
  899.2 504.2 %reduce-scatter.23.cloned.1.call-start = ((), (), s32[]{:S(2)}) async-start(), calls=%async_computation.25 | async-start | bytes 1253376 | tf_op jit(solution)/shard_map/reduce_scatter | solution.py:387
  904.3 571.0 %reduce-scatter.21.cloned.1.call-start = ((), (), s32[]{:S(2)}) async-start(), calls=%async_computation.24 | async-start | bytes 3760128 | tf_op jit(solution)/shard_map/reduce_scatter | solution.py:386
  911.4 23.5 %copy-start.20 = (f32[640,768]{1,0:T(8,128)S(1)}, f32[640,768]{1,0:T(8,128)}, u32[]{:S(2)}) copy-start(f32[640,768]{1,0:T(8,128)} %copy-done.17) | copy-start | bytes 5898244
  976.3 499.0 %copy-start.1 = (bf16[1536,768]{1,0:T(8,128)(2,1)S(1)}, bf16[1536,768]{1,0:T(8,128)(2,1)}, u32[]{:S(2)}) copy-start(bf16[1536,768]{1,0:T(8,128)(2,1)} %param.28) | copy-start | bytes 7077892
  (86 other events, 193.0 us)
Sparse Core Ops, SparseCore 0:
  21.9 34.3 all-gather.9
  105.1 30.3 reduce-scatter.12
  144.4 31.6 all-gather.11
  190.6 30.3 reduce-scatter.14
  225.6 31.6 all-gather.13
  258.7 31.6 all-gather.15
  293.2 38.6 all-reduce.6
  349.5 38.6 all-reduce.8
  427.5 60.2 all-reduce.12
  510.8 31.6 all-gather.17
  559.4 30.3 reduce-scatter.16
  597.3 31.6 all-gather.19
  814.0 30.3 reduce-scatter.18
  858.3 21.8 all-reduce.10
  884.6 58.5 reduce-scatter.30
  948.0 76.9 reduce-scatter.28
  1029.8 74.4 reduce-scatter.34
  1108.6 74.5 reduce-scatter.32
  1188.1 74.5 reduce-scatter.26
  1267.0 74.5 reduce-scatter.24
  1346.3 57.1 reduce-scatter.22
  1408.4 66.9 reduce-scatter.20
where the time goes:
time: 1490 us; the launch traced here: 1480 us
  waiting for transfers between devices  817 us (55%)
  matrix products  301 us (20%)
  local copies, waits for them, and re-layouts  145 us (10%)
  other arithmetic  129 us (9%)
  blocking collectives  73.4 us (5%)
  between operations  15.7 us (1%)
    psum x3, waiting for transfers between devices, pair_total(): lax.psum(partial_value.astype(jnp.bfloat16), 'tensor').astype(jnp.float32)  111 us
    reduce_scatter x1, waiting for transfers between devices, on_device(): lax.psum_scatter(down_grad_one, 'dp', scatter_dimension=1, tiled=True)  79.6 us
    reduce_scatter x1, waiting for transfers between devices, on_device(): lax.psum_scatter(down_grad_two, 'dp', scatter_dimension=1, tiled=True)  79.3 us
    reduce_scatter x1, waiting for transfers between devices, on_device(): lax.psum_scatter(up_grad_two, 'dp', scatter_dimension=0, tiled=True)  78.9 us
    reduce_scatter x1, waiting for transfers between devices, on_device(): lax.psum_scatter(up_grad_one, 'dp', scatter_dimension=0, tiled=True)  78.9 us
    reduce_scatter x1, waiting for transfers between devices, on_device(): lax.psum_scatter(qkv_grad_one, 'dp', scatter_dimension=0, tiled=True)  71.9 us
    all_gather x2, waiting for transfers between devices, gather_grads(): return lax.all_gather(rows_in, 'tensor', axis=0, tiled=True)  63.3 us
    all_gather x2, waiting for transfers between devices, gather_rows(): return lax.all_gather(rows_in, 'tensor', axis=0, tiled=True)  62.1 us
  transfers between devices with their start and end apart: 22, of which 19 were waited for; matrix products, arithmetic and copies ran while one was open for 11% of the time, Pallas kernels for 0%

commit v1 on v0

v1 whole, which is shorter than its diff:
```python
import functools

import jax
import jax.numpy as jnp
from jax import lax
from jax.experimental import pallas as pl
from jax.experimental.pallas import tpu as pltpu
from jax.sharding import PartitionSpec as P

D = 768
HEAD_DIM = 64
SLOTS = 5
GROUP = 1280
KEEP = 640
BLOCKS = 5
SPAN = GROUP // BLOCKS
HALF = D // 2
TILE = 768
NORM_EPS = 1e-06
f32 = jnp.float32
bf16 = jnp.bfloat16
ALL = ("dp", "tensor")
VMEM_BYTES = 60 * 1024 * 1024


def dot(left, right):
    return jnp.dot(left, right, preferred_element_type=f32)


def dot_cols(left, right):
    return lax.dot_general(left, right, (((1,), (1,)), ((), ())), preferred_element_type=f32)


def dot_rows(left, right):
    return lax.dot_general(left, right, (((0,), (0,)), ((), ())), preferred_element_type=f32)


def unit_rows(rows):
    centre = rows - jnp.mean(rows, axis=-1, keepdims=True)
    inverse = lax.rsqrt(jnp.mean(centre * centre, axis=-1, keepdims=True) + NORM_EPS)
    return centre * inverse, inverse


def norm_back(d_normed, unit, inverse, scale_row):
    e = d_normed * (1.0 + scale_row)
    return inverse * (
        e
        - jnp.mean(e, axis=-1, keepdims=True)
        - unit * jnp.mean(e * unit, axis=-1, keepdims=True)
    )


def col_sum(rows):
    return jnp.sum(rows, axis=0, keepdims=True)


def flat(ref):
    value = ref[...]
    return value.reshape(-1, value.shape[-1])


def whole(shape):
    return pl.BlockSpec(shape, lambda *_: (0,) * len(shape))


def run(body, grid, ins, outs, scratch=(), scalars=(), flops=0):
    in_specs = [whole(a.shape) if s is None else s for a, s in ins]
    out_specs = [whole(sh) if s is None else s for sh, _, s in outs]
    moved = sum(a.size * a.dtype.itemsize for a, _ in ins)
    moved += sum(jnp.dtype(d).itemsize * functools.reduce(lambda p, q: p * q, sh, 1) for sh, d, _ in outs)
    return pl.pallas_call(
        body,
        grid_spec=pltpu.PrefetchScalarGridSpec(
            num_scalar_prefetch=len(scalars),
            grid=grid,
            in_specs=in_specs,
            out_specs=out_specs,
            scratch_shapes=list(scratch),
        ),
        out_shape=[jax.ShapeDtypeStruct(sh, d) for sh, d, _ in outs],
        compiler_params=pltpu.CompilerParams(
            vmem_limit_bytes=VMEM_BYTES, dimension_semantics=("arbitrary",) * len(grid)
        ),
        cost_estimate=pl.CostEstimate(flops=int(flops), bytes_accessed=int(moved), transcendentals=0),
    )(*scalars, *[a for a, _ in ins])


def qkv_body(own, oth, tab, w, normed, q, k, v):
    rows = own.shape[1]
    step = pl.program_id(0)

    @pl.when(step == 0)
    def _():
        for side, src in ((0, own), (1, oth)):
            for i in range(BLOCKS):
                unit, _ = unit_rows(src[i].astype(f32))
                normed[side, i] = (unit * (1.0 + tab[i, 1:2]) + tab[i, 0:1]).astype(bf16)

    qkv_steps(step, normed, w, q, k, v, rows)


def qkv_next_body(normed, w, q, k, v):
    qkv_steps(pl.program_id(0), normed, w, q, k, v, normed.shape[2])


def qkv_steps(step, normed, w, q, k, v, rows):
    @pl.when(step == 0)
    def _():
        mine = normed[0].reshape(BLOCKS * rows, D)
        q[...] = dot(mine, w[0]).astype(bf16).reshape(q.shape)

    for index, out in ((1, k), (2, v)):

        @pl.when(step == index)
        def _(out=out):
            out[...] = dot(flat(normed), w[0]).astype(bf16).reshape(out.shape)


def project_qkv(first, own, oth, tab, normed, w):
    if first:
        rows = own.shape[1]
        ins = [(own, None), (oth, None), (tab, None)]
        outs = [((2, BLOCKS, rows, D), bf16, None)]
        body = qkv_body
    else:
        rows = normed.shape[2]
        ins = [(normed, None)]
        outs = []
        body = qkv_next_body
    ins += [(w, pl.BlockSpec((1, D, HALF), lambda j: (j, 0, 0)))]
    outs += [
        ((BLOCKS, rows, HALF), bf16, None),
        ((2, BLOCKS, rows, HALF), bf16, None),
        ((2, BLOCKS, rows, HALF), bf16, None),
    ]
    return run(body, (3,), ins, outs, flops=2 * 25 * rows * D * HALF)


def by_sequence(kind, one_sequence, long_tiles):
    @pl.when(kind < 2)
    def _():
        one_sequence(kind, 4, long_tiles)
        one_sequence(jnp.where(kind == 0, 4, 0), 1, 1)

    @pl.when(kind == 2)
    def _():
        def short(i, carry):
            one_sequence(i, 1, 1)
            return carry

        lax.fori_loop(0, BLOCKS, short, 0)


def two_heads(rows, low):
    zero = jnp.zeros_like(rows)
    return jnp.concatenate([jnp.where(low, rows, zero), jnp.where(low, zero, rows)], axis=0)


def attend_body(kind, q, k, v, out):
    rows = q.shape[1]
    low = lax.broadcasted_iota(jnp.int32, (1, 128), 1) < HEAD_DIM
    scaling = HEAD_DIM ** (-0.5)

    def one_sequence(start, count, tiles):
        keys = k[:, pl.ds(start, count)].reshape(2 * count * rows, 128)
        values = v[:, pl.ds(start, count)].reshape(2 * count * rows, 128)
        size = tiles * rows
        for part in range(count // tiles):
            at = pl.ds(start + part * tiles, tiles)
            pair = two_heads((q[at].reshape(size, 128) * scaling).astype(bf16), low)
            scores = dot_cols(pair, keys)
            shifted = jnp.exp(scores - jnp.max(scores, axis=-1, keepdims=True))
            total = jnp.sum(shifted, axis=-1, keepdims=True)
            mixed = dot(shifted.astype(bf16), values) * (1.0 / total)
            out[at] = jnp.where(low, mixed[:size], mixed[size:]).astype(bf16).reshape(tiles, rows, 128)

    by_sequence(kind[0], one_sequence, 128 // rows)


def attend(kind, q, k, v):
    rows = q.shape[1]
    own = pl.BlockSpec((BLOCKS, rows, 128), lambda p, *_: (0, 0, p))
    every = pl.BlockSpec((2, BLOCKS, rows, 128), lambda p, *_: (0, 0, 0, p))
    return run(
        attend_body,
        (HALF // 128,),
        [(q, own), (k, every), (v, every)],
        [(q.shape, bf16, own)],
        scalars=(kind,),
        flops=16 * BLOCKS * rows * 8 * rows * HALF,
    )[0]


def attend_back_body(kind, q, k, v, d_out, dq, dk, dv, acc_k, acc_v):
    rows = q.shape[1]
    low = lax.broadcasted_iota(jnp.int32, (1, 128), 1) < HEAD_DIM
    scaling = HEAD_DIM ** (-0.5)

    def one_sequence(start, count, tiles):
        key_rows = 2 * count * rows
        keys = k[:, pl.ds(start, count)].reshape(key_rows, 128)
        values = v[:, pl.ds(start, count)].reshape(key_rows, 128)
        size = tiles * rows
        for part in range(count // tiles):
            at = pl.ds(start + part * tiles, tiles)
            pair = two_heads((q[at].reshape(size, 128) * scaling).astype(bf16), low)
            d_pair = two_heads(d_out[at].reshape(size, 128), low)
            scores = dot_cols(keys, pair)
            shifted = jnp.exp(scores - jnp.max(scores, axis=0, keepdims=True))
            probs = shifted * (1.0 / jnp.sum(shifted, axis=0, keepdims=True))
            d_probs = dot_cols(values, d_pair)
            row_sum = jnp.sum(probs * d_probs, axis=0, keepdims=True)
            d_scores = (probs * (d_probs - row_sum)).astype(bf16)
            add_v = dot(probs.astype(bf16), d_pair)
            add_k = dot(d_scores, pair)
            if part == 0:
                acc_v[:key_rows] = add_v
                acc_k[:key_rows] = add_k
            else:
                acc_v[:key_rows] += add_v
                acc_k[:key_rows] += add_k
            both = dot_rows(d_scores, keys) * scaling
            dq[at] = jnp.where(low, both[:size], both[size:]).astype(bf16).reshape(tiles, rows, 128)
        dk[:, pl.ds(start, count)] = acc_k[:key_rows].astype(bf16).reshape(2, count, rows, 128)
        dv[:, pl.ds(start, count)] = acc_v[:key_rows].astype(bf16).reshape(2, count, rows, 128)

    by_sequence(kind[0], one_sequence, 128 // rows)


def attend_back(kind, q, k, v, d_out):
    rows = q.shape[1]
    own = pl.BlockSpec((BLOCKS, rows, 128), lambda p, *_: (0, 0, p))
    every = pl.BlockSpec((2, BLOCKS, rows, 128), lambda p, *_: (0, 0, 0, p))
    return run(
        attend_back_body,
        (HALF // 128,),
        [(q, own), (k, every), (v, every), (d_out, own)],
        [(q.shape, bf16, own), (k.shape, bf16, every), (v.shape, bf16, every)],
        scratch=[pltpu.VMEM((8 * rows, 128), f32), pltpu.VMEM((8 * rows, 128), f32)],
        scalars=(kind,),
        flops=40 * BLOCKS * rows * 8 * rows * HALF,
    )


def gelu_parts(u):
    rate = 0.7978845608028654
    inner = rate * (u + 0.044715 * (u * u * u))
    return jnp.tanh(inner), rate


def mlp_body(
    mixed_n, mixed_r, proj_n, proj_r, own, tab, up_n, down_n, up_a, down_a, up_b, down_b,
    attn_out, middle, normed, u, mlp_out, out, acc,
):
    rows = own.shape[1]
    step = pl.program_id(0)

    @pl.when(step == 0)
    def _():
        acc[...] = dot(flat(mixed_n), proj_n[...]) + dot(flat(mixed_r), proj_r[...])
        for i in range(BLOCKS):
            attn = acc[i * rows : (i + 1) * rows]
            attn_out[i] = attn.astype(bf16)
            mid = own[i].astype(f32) + tab[i, 2:3] * attn
            middle[i] = mid
            unit, _ = unit_rows(mid)
            normed[i] = (unit * (1.0 + tab[i, 4:5]) + tab[i, 3:4]).astype(bf16)

    def hidden(up, down, first):
        pre = dot(flat(normed), up[...])
        u[0] = pre.astype(bf16)
        tanh, _ = gelu_parts(pre)
        term = dot((0.5 * pre * (1.0 + tanh)).astype(bf16), down[...])
        if first:
            acc[...] = term
        else:
            acc[...] += term

    @pl.when(step == 0)
    def _():
        hidden(up_n, down_n, True)

    @pl.when(step == 1)
    def _():
        hidden(up_n, down_n, False)

    @pl.when(step == 2)
    def _():
        hidden(up_a, down_a, False)

    @pl.when(step == 3)
    def _():
        hidden(up_b, down_b, False)
        for i in range(BLOCKS):
            term = acc[i * rows : (i + 1) * rows]
            mlp_out[i] = term.astype(bf16)
            out[i] = (middle[i] + tab[i, 5:6] * term).astype(bf16)


def halves(weights, rows_of_down):
    up, down, (up_a, down_a, at_a), (up_b, down_b, at_b) = weights
    here = lambda j: jnp.minimum(j, 1)
    return [
        (up, pl.BlockSpec((D, TILE), lambda j, *_: (0, here(j)))),
        (down, pl.BlockSpec((TILE, D), lambda j, *_: (here(j), 0))),
        (up_a, pl.BlockSpec((D, TILE), lambda j, *_: (0, at_a))),
        (down_a, pl.BlockSpec((TILE, D), lambda j, *_: (at_a, 0))),
        (up_b, pl.BlockSpec((D, TILE), lambda j, *_: (0, at_b))),
        (down_b, pl.BlockSpec((TILE, D), lambda j, *_: (at_b, 0))),
    ]


def feed_forward(mixed_n, mixed_r, proj_n, proj_r, own, tab, weights):
    rows = own.shape[1]
    total = BLOCKS * rows
    return run(
        mlp_body,
        (4,),
        [(mixed_n, None), (mixed_r, None), (proj_n, None), (proj_r, None), (own, None), (tab, None)]
        + halves(weights, None),
        [
            (own.shape, bf16, None),
            (own.shape, f32, None),
            (own.shape, bf16, None),
            ((4, total, TILE), bf16, pl.BlockSpec((1, total, TILE), lambda j: (j, 0, 0))),
            (own.shape, bf16, None),
            (own.shape, bf16, None),
        ],
        scratch=[pltpu.VMEM((total, D), f32)],
        flops=2 * total * D * (D + 8 * D),
    )


def mlp_back_body(
    part, d_out, tab, mlp_out, normed, u, up_n, down_n, up_a, down_a, up_b, down_b,
    middle, attn_out, proj_n, proj_r, mixed_n, mixed_r, order,
    g_keep, g_send, p_keep, p_send, d_middle, d_mix_n, d_mix_r, d_mod,
    d_mlp, d_mlp_t, normed_t, acc,
):
    rows = d_out.shape[1]
    step = pl.program_id(0)

    @pl.when(step == 0)
    def _():
        for i in range(BLOCKS):
            grad = d_out[i].astype(f32)
            d_mlp[i * rows : (i + 1) * rows] = (grad * tab[i, 5:6]).astype(bf16)
            d_mod[i, 3:4] = col_sum(grad * mlp_out[i].astype(f32))
        d_mlp_t[...] = dot_cols(order[...], d_mlp[...]).astype(bf16)
        normed_t[...] = dot_cols(order[...], flat(normed)).astype(bf16)

    def hidden(up, down, first):
        pre = u[0].astype(f32)
        tanh, rate = gelu_parts(pre)
        act = (0.5 * pre * (1.0 + tanh)).astype(bf16)
        slope = 0.5 * (1.0 + tanh) + (0.5 * rate) * pre * (1.0 - tanh * tanh) * (
            1.0 + (3.0 * 0.044715) * (pre * pre)
        )
        g_down = dot(d_mlp_t[...], act).astype(bf16)
        g_keep[0, :, TILE:] = g_down[:HALF]
        g_send[0, :, TILE:] = g_down[HALF:]
        d_up = (slope * dot_cols(d_mlp[...], down[...])).astype(bf16)
        g_up = dot(normed_t[...], d_up).astype(bf16)
        g_keep[0, :, :TILE] = g_up[:HALF]
        g_send[0, :, :TILE] = g_up[HALF:]
        term = dot_cols(d_up, up[...])
        if first:
            acc[...] = term
        else:
            acc[...] += term

    @pl.when(step == 0)
    def _():
        hidden(up_n, down_n, True)

    @pl.when(step == 1)
    def _():
        hidden(up_n, down_n, False)

    @pl.when(step == 2)
    def _():
        hidden(up_a, down_a, False)

    @pl.when(step == 3)
    def _():
        hidden(up_b, down_b, False)
        for i in range(BLOCKS):
            at = slice(i * rows, (i + 1) * rows)
            d_normed = acc[at]
            unit, inverse = unit_rows(middle[i])
            grad = d_out[i].astype(f32) + norm_back(d_normed, unit, inverse, tab[i, 4:5])
            d_middle[i] = grad
            d_mod[i, 0:1] = col_sum(grad * attn_out[i].astype(f32))
            d_mod[i, 1:2] = col_sum(d_normed)
            d_mod[i, 2:3] = col_sum(d_normed * unit)
            d_mlp[at] = (grad * tab[i, 2:3]).astype(bf16)
        d_mlp_t[...] = dot_cols(order[...], d_mlp[...]).astype(bf16)
        for side, mixed, proj, d_mix in (
            (0, mixed_n, proj_n, d_mix_n),
            (1, mixed_r, proj_r, d_mix_r),
        ):
            d_mix[...] = dot_cols(d_mlp[...], proj[...]).astype(bf16).reshape(d_mix.shape)
            g_proj = dot(d_mlp_t[...], flat(mixed)).astype(bf16)
            p_keep[side] = g_proj[:HALF]
            p_send[side] = g_proj[HALF:]


def feed_back(part, d_out, tab, saved, weights, proj_n, proj_r, mixed_n, mixed_r, order):
    attn_out, middle, normed, u, mlp_out = saved
    rows = d_out.shape[1]
    total = BLOCKS * rows

    def tile_of(j, part_ref):
        local = jnp.where(part_ref[0] == 0, j % 2, 1 - j % 2)
        return (j // 2, 0, jnp.where(j < 2, j % 2, local))

    grads = ((2, HALF, 4 * TILE), bf16, pl.BlockSpec((1, HALF, 2 * TILE), tile_of))
    return run(
        mlp_back_body,
        (4,),
        [
            (d_out, None),
            (tab, None),
            (mlp_out, None),
            (normed, None),
            (u, pl.BlockSpec((1, total, TILE), lambda j, *_: (j, 0, 0))),
        ]
        + halves(weights, None)
        + [
            (middle, None),
            (attn_out, None),
            (proj_n, None),
            (proj_r, None),
            (mixed_n, None),
            (mixed_r, None),
            (order, None),
        ],
        [
            grads,
            grads,
            ((2, HALF, HALF), bf16, None),
            ((2, HALF, HALF), bf16, None),
            (d_out.shape, f32, None),
            (mixed_n.shape, bf16, None),
            (mixed_n.shape, bf16, None),
            ((BLOCKS, 4, D), f32, None),
        ],
        scratch=[
            pltpu.VMEM((total, D), bf16),
            pltpu.VMEM((D, total), bf16),
            pltpu.VMEM((D, total), bf16),
            pltpu.VMEM((total, D), f32),
        ],
        scalars=(part,),
        flops=2 * total * D * (16 * D + 4 * D),
    )


def qkv_back_body(
    dq_n, dk_n, dv_n, dq_r, dk_r, dv_r, w_n, w_r, normed, order,
    g_keep, g_send, d_own, d_oth, normed_t, acc,
):
    rows = dq_n.shape[1]
    total = BLOCKS * rows
    step = pl.program_id(0)

    @pl.when(step == 0)
    def _():
        normed_t[...] = dot_cols(order[...], flat(normed)).astype(bf16)

    for index, (grad, w) in enumerate(
        ((dq_n, w_n), (dk_n, w_n), (dv_n, w_n), (dq_r, w_r), (dk_r, w_r), (dv_r, w_r))
    ):

        @pl.when(step == index)
        def _(index=index, grad=grad, w=w):
            value = flat(grad)
            term = dot_cols(value, w[0])
            if index == 0:
                acc[:total] = term
                acc[total:] = jnp.zeros((total, D), f32)
                g_w = dot(normed_t[:, :total], value).astype(bf16)
            elif index == 3:
                acc[:total] += term
                g_w = dot(normed_t[:, :total], value).astype(bf16)
            else:
                acc[...] += term
                g_w = dot(normed_t[...], value).astype(bf16)
            g_keep[0] = g_w[:HALF]
            g_send[0] = g_w[HALF:]
            if index == 5:
                d_own[...] = acc[:total]
                d_oth[...] = acc[total:].astype(bf16)


def qkv_back(grads_n, grads_r, w_n, w_r, normed, order):
    rows = normed.shape[2]
    total = BLOCKS * rows
    grads = ((2, HALF, 3 * HALF), bf16, pl.BlockSpec((1, HALF, HALF), lambda j: (j // 3, 0, j % 3)))
    return run(
        qkv_back_body,
        (6,),
        [(g, None) for g in grads_n]
        + [(g, None) for g in grads_r]
        + [
            (w_n, pl.BlockSpec((1, D, HALF), lambda j: (jnp.minimum(j, 2), 0, 0))),
            (w_r, pl.BlockSpec((1, D, HALF), lambda j: (jnp.maximum(j - 3, 0), 0, 0))),
            (normed, None),
            (order, None),
        ],
        [grads, grads, ((total, D), f32, None), ((total, D), bf16, None)],
        scratch=[pltpu.VMEM((D, 2 * total), bf16), pltpu.VMEM((2 * total, D), f32)],
        flops=2 * total * D * (20 * HALF + 2 * D),
    )


def finish_body(d_own, d_got, own, tab, d_middle, d_rows, d_mod):
    rows = own.shape[1]
    for i in range(BLOCKS):
        at = slice(i * rows, (i + 1) * rows)
        d_normed = d_own[at] + d_got[at].astype(f32)
        unit, inverse = unit_rows(own[i].astype(f32))
        grad = d_middle[i] + norm_back(d_normed, unit, inverse, tab[i, 1:2])
        d_rows[i] = grad.astype(bf16)
        d_mod[i, 0:1] = col_sum(d_normed)
        d_mod[i, 1:2] = col_sum(d_normed * unit)


def finish(d_own, d_got, own, tab, d_middle):
    return run(
        finish_body,
        (1,),
        [(d_own, None), (d_got, None), (own, None), (tab, None), (d_middle, None)],
        [(own.shape, bf16, None), ((BLOCKS, 2, D), f32, None)],
    )


def pick_body(index, own, oth, out):
    spot = lax.broadcasted_iota(jnp.int32, (1, own.shape[0]), 1)
    here = (index[...] == spot).astype(bf16)
    there = (index[...] - own.shape[0] == spot).astype(bf16)
    out[...] = (dot(here, own[...]) + dot(there, oth[...])).astype(bf16)


def pick(index, own, oth):
    count = index.shape[0]
    return run(
        pick_body,
        (1,),
        [(index, None), (own, None), (oth, None)],
        [((count, D), bf16, None)],
        flops=2 * count * GROUP * D,
    )[0]


def put_body(index_own, index_oth, own, oth, base, out):
    spot = lax.broadcasted_iota(jnp.int32, (base.shape[0], 1), 0)
    here = (index_own[...] == spot).astype(f32)
    there = (index_oth[...] == spot).astype(f32)
    hit = jnp.sum(here, axis=1, keepdims=True) + jnp.sum(there, axis=1, keepdims=True)
    put = dot(here.astype(bf16), own[...]) + dot(there.astype(bf16), oth[...])
    out[...] = jnp.where(hit > 0.5, put, base[...].astype(f32)).astype(bf16)


def put(index_own, index_oth, own, oth, base):
    return run(
        put_body,
        (1,),
        [(index_own, None), (index_oth, None), (own, None), (oth, None), (base, None)],
        [(base.shape, bf16, None)],
        flops=2 * base.shape[0] * KEEP * D,
    )[0]


def on_device(
    n_dp,
    tokens,
    conditioning,
    segment_ids,
    kept_rows,
    cotangent,
    mod_first,
    qkv_first,
    proj_first,
    up_first,
    down_first,
    mod_second,
    qkv_second,
    proj_second,
    up_second,
    down_second,
):
    dp_pos = lax.axis_index("dp")
    side = lax.axis_index("tensor")
    core = dp_pos % 2
    bits = n_dp.bit_length() - 1

    def moves(where):
        pairs = []
        for dp in range(n_dp):
            for t in range(2):
                to_dp, to_t = where(dp, t)
                pairs.append((dp * 2 + t, to_dp * 2 + to_t))
        return pairs

    across = moves(lambda dp, t: (dp, 1 - t))
    core_swap = moves(lambda dp, t: (dp ^ 1, t))
    turn = moves(lambda dp, t: (dp // 2 * 2 + t, dp % 2))
    deal = moves(lambda dp, t: (dp // 2 * 2 + 1 - t, dp % 2))
    undeal = moves(lambda dp, t: (dp // 2 * 2 + t, 1 - dp % 2))

    def send(value, pairs):
        return lax.ppermute(value, ALL, pairs)

    def to_owner(rows):
        tiles = rows.reshape(BLOCKS, SPAN // 2, D)
        even = send(tiles[0::2], turn)
        odd = send(tiles[1::2], deal)
        return jnp.where(core == 0, jnp.concatenate([even, odd]), jnp.concatenate([odd, even]))

    def from_owner(rows):
        even = send(lax.dynamic_slice_in_dim(rows, 2 * core, 3), turn)
        odd = send(lax.dynamic_slice_in_dim(rows, 3 * (1 - core), 2), undeal)
        return jnp.concatenate([even[0:1], odd[0:1], even[1:2], odd[1:2], even[2:3]]).reshape(-1, D)

    def halves_of(value, axis):
        size = value.shape[axis] // 2
        near = send(lax.dynamic_slice_in_dim(value, core * size, size, axis), across)
        return near, send(near, core_swap)

    def joined(value, axis):
        near, far = halves_of(value, axis)
        return jnp.where(
            core == 0, jnp.concatenate([near, far], axis), jnp.concatenate([far, near], axis)
        )

    def gathered(value):
        size = value.shape[0] // n_dp
        piece = send(lax.dynamic_slice_in_dim(value, dp_pos * size, size), across)
        return lax.all_gather(piece, "dp", axis=0, tiled=True)

    own = to_owner(tokens)
    oth = send(own, core_swap)
    numbers = send(jnp.concatenate([kept_rows, segment_ids[::SPAN]]), turn)
    kept, segs = numbers[:KEEP], numbers[KEEP:]
    kind = jnp.where(segs[3] == segs[0], 0, jnp.where(segs[4] == segs[1], 1, 2)).reshape(1)
    cond = send(jax.nn.silu(conditioning.astype(f32)).astype(bf16), turn)
    slot_hot = segs[:, None] == jnp.arange(SLOTS, dtype=jnp.int32)[None, :]
    cond_rows = jnp.dot(slot_hot.astype(bf16), cond, preferred_element_type=f32).astype(bf16)

    def table(mod):
        return jnp.dot(cond_rows, mod, preferred_element_type=f32).reshape(BLOCKS, 6, D)

    tab_one, tab_two = table(mod_first), table(mod_second)

    wq_one = jnp.transpose(qkv_first, (1, 0, 2))
    wq_two = jnp.transpose(qkv_second, (1, 0, 2))
    wq_one_far = joined(wq_one, 1)
    proj_one_far = joined(proj_first, 0)
    up_near, up_far = halves_of(up_first, 1)
    down_near, down_far = halves_of(down_first, 0)
    mlp_one = (up_first, down_first, (up_near, down_near, 0), (up_far, down_far, 0))
    wq_two_far = gathered(wq_two.reshape(3 * D, HALF)).reshape(3, D, HALF)
    proj_two_far = joined(proj_second, 0)
    up_two_far, down_two_far = gathered(up_second), gathered(down_second)
    mlp_two = (up_second, down_second, (up_two_far, down_two_far, 0), (up_two_far, down_two_far, 1))
    cot_own = to_owner(cotangent)
    cot_oth = send(cot_own, core_swap)

    block_of, inside = kept // SPAN, kept % SPAN
    spot = (
        jnp.where(inside // (SPAN // 2) == core, 0, GROUP // 2)
        + block_of * (SPAN // 2)
        + inside % (SPAN // 2)
    ).reshape(BLOCKS, 2, KEEP // (2 * BLOCKS))
    spot_own = lax.dynamic_slice_in_dim(spot, core, 1, 1).reshape(-1)
    spot_oth = lax.dynamic_slice_in_dim(spot, 1 - core, 1, 1).reshape(-1)
    spot_all = jnp.concatenate([spot_own, spot_oth])

    stages = [0, 1] + list(range(bits - 1, 1, -1))
    piece = D // n_dp
    row = jnp.arange(D, dtype=jnp.int32)
    turned = jnp.zeros_like(row)
    for place, bit in enumerate(stages):
        turned = turned + (((row // piece) // 2 ** (bits - 1 - place)) % 2) * 2**bit
    source = jnp.bitwise_xor(turned, dp_pos) * piece + row % piece
    order = (source[:, None] == row[None, :]).astype(bf16)

    def forward(own, oth, tab, wq, wq_far, proj, proj_far, weights):
        normed, *near = project_qkv(True, own, oth, tab, None, wq)
        mixed_n = attend(kind, *near)
        far = project_qkv(False, None, None, None, normed, wq_far)
        mixed_r = attend(kind, *far)
        *saved, out = feed_forward(mixed_n, mixed_r, proj, proj_far, own, tab, weights)
        return out, (normed, near, far, mixed_n, mixed_r, saved)

    def backward(d_out, own, tab, wq, wq_far, proj, proj_far, weights, kept_of, part):
        normed, near, far, mixed_n, mixed_r, saved = kept_of
        g_keep, g_send, p_keep, p_send, d_middle, d_mix_n, d_mix_r, d_mod = feed_back(
            part, d_out, tab, saved, weights, proj, proj_far, mixed_n, mixed_r, order
        )
        total_mlp = total(g_keep, g_send)
        total_proj = total(p_keep, p_send)
        grads_n = attend_back(kind, *near, d_mix_n)
        grads_r = attend_back(kind, *far, d_mix_r)
        q_keep, q_send, d_own, d_oth = qkv_back(grads_n, grads_r, wq, wq_far, normed, order)
        d_got = send(d_oth, core_swap)
        total_qkv = total(q_keep, q_send)
        d_rows, d_mod_a = finish(d_own, d_got, own, tab, d_middle)
        per_block = jnp.concatenate([d_mod_a, d_mod], axis=1).reshape(BLOCKS, 6 * D)
        d_table = lax.dot_general(
            slot_hot.astype(f32),
            per_block,
            (((0,), (0,)), ((), ())),
            precision=lax.Precision.HIGHEST,
        )
        return d_rows, (total_qkv, total_proj, total_mlp), d_table.astype(bf16)

    def total(keep, away):
        got = send(away, core_swap)
        other = (keep[1].astype(f32) + got[1].astype(f32)).astype(bf16)
        got_x = send(other, across)
        acc = keep[0].astype(f32) + got[0].astype(f32) + got_x.astype(f32)
        for bit in stages[1:]:
            size = acc.shape[0] // 2
            got = send(acc[size:].astype(bf16), moves(lambda dp, t, bit=bit: (dp ^ 2**bit, t)))
            acc = acc[:size] + got.astype(f32)
        return acc

    out_one, kept_one = forward(
        own, oth, tab_one, wq_one, wq_one_far, proj_first, proj_one_far, mlp_one
    )
    first_own = out_one.reshape(-1, D)
    first_oth = send(first_own, core_swap)
    first_out = from_owner(out_one)

    routed = pick(spot_all[:, None], first_own, first_oth)
    routed_own, routed_oth = routed.reshape(2, BLOCKS, KEEP // (2 * BLOCKS), D)
    cot_routed = pick(spot_own[:, None], cot_own.reshape(-1, D), cot_oth.reshape(-1, D)).reshape(
        routed_own.shape
    )
    out_two, kept_two = forward(
        routed_own, routed_oth, tab_two, wq_two, wq_two_far, proj_second, proj_two_far, mlp_two
    )
    second_own = out_two.reshape(-1, D)
    second_oth = send(second_own, core_swap)
    routed_rows = put(spot_own[None], spot_oth[None], second_own, second_oth, first_own)
    routed_out = from_owner(routed_rows.reshape(own.shape))

    d_two, grads_two, d_table_two = backward(
        cot_routed, routed_own, tab_two, wq_two, wq_two_far, proj_second, proj_two_far, mlp_two,
        kept_two, jnp.zeros((1,), jnp.int32),
    )
    d_two_own = d_two.reshape(-1, D)
    d_two_oth = send(d_two_own, core_swap)
    d_first = put(spot_own[None], spot_oth[None], d_two_own, d_two_oth, cot_own.reshape(-1, D))
    d_one, grads_one, d_table_one = backward(
        d_first.reshape(own.shape), own, tab_one, wq_one, wq_one_far, proj_first, proj_one_far,
        mlp_one, kept_one, core.reshape(1).astype(jnp.int32),
    )
    input_grad = from_owner(d_one).astype(f32)

    mod_rows = D // (n_dp * 2)
    cond_every = lax.all_gather(cond, ALL, axis=0, tiled=True)
    cond_cols = lax.dynamic_slice_in_dim(cond_every, (dp_pos * 2 + side) * mod_rows, mod_rows, 1)

    def mod_grad(d_table):
        every = lax.all_gather(d_table, ALL, axis=0, tiled=True)
        return dot_rows(cond_cols, every)

    def placed(grads):
        qkv, proj, mlp = grads
        parts = mlp.reshape(piece, 2, 2, TILE)
        up = parts[:, :, 0].reshape(piece, 2 * TILE)
        down = parts[:, :, 1].reshape(piece, 2 * TILE)
        return qkv.reshape(piece, 3, HALF), proj.T, up, down.T

    return (
        first_out,
        routed_out,
        input_grad,
        mod_grad(d_table_one),
        *placed(grads_one),
        mod_grad(d_table_two),
        *placed(grads_two),
    )


def solution(mesh):
    n_dp = mesh.shape["dp"]
    return jax.shard_map(
        functools.partial(on_device, n_dp),
        mesh=mesh,
        in_specs=(
            P(("dp", "tensor"), None),
            P("dp", None),
            P("dp"),
            P("dp"),
            P(("dp", "tensor"), None),
            P(),
            P(None, None, "tensor"),
            P("tensor", None),
            P(None, "tensor"),
            P("tensor", None),
            P(),
            P(None, None, "tensor"),
            P("tensor", None),
            P(None, "tensor"),
            P("tensor", None),
        ),
        out_specs=(
            P(("dp", "tensor"), None),
            P(("dp", "tensor"), None),
            P(("dp", "tensor"), None),
            P(("dp", "tensor"), None),
            P("dp", None, "tensor"),
            P("tensor", "dp"),
            P("dp", "tensor"),
            P("tensor", "dp"),
            P(("dp", "tensor"), None),
            P("dp", None, "tensor"),
            P("tensor", "dp"),
            P("dp", "tensor"),
            P("tensor", "dp"),
        ),
        check_vma=False,
    )
```

time: 1490 us -> 797 us (0.53)
  waiting for transfers between devices: 817 us -> 217 us
  matrix products: 301 us -> 15.3 us
  Pallas kernels: 0 us -> 239 us
  starting transfers between devices: 1.69 us -> 120 us
  other arithmetic: 129 us -> 41.2 us
  local copies, waits for them, and re-layouts: 145 us -> 64.9 us
    reduce_scatter x12 -> x0, waiting for transfers between devices: 567 us -> none  [the longest x1 79.6 us: on_device(): lax.psum_scatter(down_grad_one, 'dp', scatter_dimension=1, tiled=True)]
    dot_general x62 -> x7, matrix products: 301 us -> 15.3 us  [the longest x2 8.15 us: table(): jnp.dot(cond_rows, mod, preferred_element_type=f32).reshape(BLOCKS, 6, D)]
    pallas_call x0 -> x24, Pallas kernels: none -> 239 us  [run(): pl.pallas_call(body, grid_spec=pltpu.PrefetchScalarGridSpec(num_scalar_pr...]
    ppermute x0 -> x62, waiting for transfers between devices: none -> 217 us  [send(): return lax.ppermute(value, ALL, pairs)]
    all_gather x6 -> x5, waiting for transfers between devices: 138 us -> 0.01 us  [the longest x3 0.01 us: gathered(): return lax.all_gather(piece, 'dp', axis=0, tiled=True)]
    ppermute x0 -> x62, starting transfers between devices: none -> 119 us  [send(): return lax.ppermute(value, ALL, pairs)]
    psum x4 -> x0, waiting for transfers between devices: 111 us -> none  [the longest x3 111 us: pair_total(): lax.psum(partial_value.astype(jnp.bfloat16), 'tensor').astype(jnp.float32)]
    convert_element_type x11 -> x9, other arithmetic: 62.4 us -> 12.4 us  [the longest x6 9.59 us: total(): other = (keep[1].astype(f32) + got[1].astype(f32)).astype(bf16)]
  transfers between devices with their start and end apart: 22 -> 67, of which waited for: 19 -> 21; matrix products, arithmetic and copies ran while one was open for 11% -> 14% of each run, Pallas kernels for 0% -> 23%
where the time goes in v1:
time: 797 us; the launch traced here: 785 us
  Pallas kernels  239 us (30%)
  waiting for transfers between devices  217 us (27%)
  starting transfers between devices  120 us (15%)
  blocking collectives  69.6 us (9%)
  local copies, waits for them, and re-layouts  64.9 us (8%)
  other arithmetic  41.2 us (5%)
  between operations  17.8 us (2%)
  matrix products  15.3 us (2%)
    pallas_call x24, Pallas kernels, run(): pl.pallas_call(body, grid_spec=pltpu.PrefetchScalarGridSpec(num_scalar_pr...  239 us
    ppermute x62, waiting for transfers between devices, send(): return lax.ppermute(value, ALL, pairs)  217 us
    ppermute x62, starting transfers between devices, send(): return lax.ppermute(value, ALL, pairs)  119 us
    all_gather x1, blocking collectives, on_device(): cond_every = lax.all_gather(cond, ALL, axis=0, tiled=True)  69.6 us
    unnamed x115, local copies, waits for them, and re-layouts  22.9 us
  transfers between devices with their start and end apart: 67, of which 21 were waited for; matrix products, arithmetic and copies ran while one was open for 14% of the time, Pallas kernels for 23%

profile of v1, /device:TPU:0, one launch (start us, length us, event | category | flops | bytes accessed | tf_op | source)
XLA Modules:
  0.0 784.9 jit_solution(4775784077270559621)
XLA Ops:
  8.3 3.0 collective-permute-start.16
  11.3 3.1 collective-permute-done.16
  17.9 3.4 collective-permute-done.19
  23.9 6.0 collective-permute-start.1
  46.1 2.5 collective-permute-start.17
  51.1 24.6 %collective-permute-done.17 = bf16[192,768]{1,0:T(8,128)(2,1)} collective-permute-done((bf16[192,768]{1,0:T(8,128)(2,1)}, bf16[192,768]{1,0:T(8,128)(2,1)}, u32[]{:S(2)}, u32[]{:S(2)}) %collective-permute-start.17) | collective-permute-done | bytes 294944 | tf_op jit(solution)/shard_map/ppermute | solution.py:613
  91.6 4.1 fusion.53
  98.6 38.9 %collective-permute-start.18 = (bf16[192,768]{1,0:T(8,128)(2,1)}, bf16[192,768]{1,0:T(8,128)(2,1)}, u32[]{:S(2)}, u32[]{:S(2)}) collective-permute-start(bf16[192,768]{1,0:T(8,128)(2,1)} %collective-permute-done.17), channel_id=1, source_target_pairs={{0,2},{1,3},{2,0},{3,1},{4,6},{5,7},{6,4},{7,5},{8,10},{9,11},{10,... | collective-permute-start | bytes 884744 | tf_op jit(solution)/shard_map/ppermute | solution.py:613
  139.7 7.8 shard_map.246
  147.5 8.7 %shard_map.247.mixed_n = bf16[5,128,384]{2,1,0:T(8,128)(2,1)} custom-call(s32[1]{0:T(128)S(6)} %select_n.197.kind, bf16[5,128,384]{2,1,0:T(8,128)(2,1)} %get-tuple-element.79.q, bf16[2,5,128,384]{3,2,1,0:T(8,128)(2,1)} %get-tuple-element.80.k, bf16[2,5,128,384]{3,2,1,0:T(8,128)(2,1)} %get-tuple-element.81.v), custom_call_target="tpu_custom_call" | custom-call | flops 4026531840 | bytes 2949120 | tf_op jit(solution)/shard_map/pallas_call | solution.py:71
  156.3 3.6 maximum_select_fusion.w.w_r
  159.9 6.3 shard_map.248
  166.2 8.7 %shard_map.249.mixed_r = bf16[5,128,384]{2,1,0:T(8,128)(2,1)} custom-call(s32[1]{0:T(128)S(6)} %select_n.197.kind, bf16[5,128,384]{2,1,0:T(8,128)(2,1)} %get-tuple-element.83.q, bf16[2,5,128,384]{3,2,1,0:T(8,128)(2,1)} %get-tuple-element.84.k, bf16[2,5,128,384]{3,2,1,0:T(8,128)(2,1)} %get-tuple-element.85.v), custom_call_target="tpu_custom_call" | custom-call | flops 4026531840 | bytes 2949120 | tf_op jit(solution)/shard_map/pallas_call | solution.py:71
  175.9 17.4 %shard_map.250 = (bf16[5,128,768]{2,1,0:T(8,128)(2,1)}, f32[5,128,768]{2,1,0:T(8,128)}, bf16[5,128,768]{2,1,0:T(8,128)(2,1)}, bf16[4,640,768]{2,1,0:T(8,128)(2,1...) custom-call(bf16[5,128,384]{2,1,0:T(8,128)(2,1)} %shard_map.247.mixed_n, ...), custom_call_target="tpu_custom_call" | custom-call | flops 6794772480 | bytes 22505472 | tf_op jit(solution)/shard_map/pallas_call | solution.py:71
  195.6 4.0 fusion.54
  200.4 69.6 %all-gather = bf16[32,5,768]{2,1,0:T(8,128)(2,1)S(1)} all-gather(bf16[1,5,768]{2,1,0:T(8,128)(2,1)S(1)} %bitcast.135), channel_id=1, replica_groups=mesh['dp'=16,'tensor'=2] {'dp','tensor'}, dimensions={0}, use_global_device_ids=true | all-gather | bytes 253440 | tf_op jit(solution)/shard_map/all_gather | solution.py:764
  274.0 3.3 shard_map.258
  277.4 4.3 shard_map.251
  283.9 5.7 shard_map.252
  289.7 4.7 shard_map.253.mixed_n
  294.4 4.6 shard_map.254
  299.0 4.7 shard_map.255.mixed_r
  303.7 11.5 %shard_map.256 = (bf16[5,64,768]{2,1,0:T(8,128)(2,1)}, f32[5,64,768]{2,1,0:T(8,128)}, bf16[5,64,768]{2,1,0:T(8,128)(2,1)}, bf16[4,320,768]{2,1,0:T(8,128)(2,1)},...) custom-call(bf16[5,64,384]{2,1,0:T(8,128)(2,1)} %shard_map.253.mixed_n, ...), custom_call_target="tpu_custom_call" | custom-call | flops 3397386240 | bytes 21325824 | tf_op jit(solution)/shard_map/pallas_call | solution.py:71
  315.2 21.3 %shard_map.259 = (bf16[2,384,3072]{2,1,0:T(8,128)(2,1)}, bf16[2,384,3072]{2,1,0:T(8,128)(2,1)}, bf16[2,384,384]{2,1,0:T(8,128)(2,1)}, bf16[2,384,384]{2,1,0:T(8,...) custom-call(s32[1]{0:T(128)} %constant.156.clone.1.part, ...), custom_call_target="tpu_custom_call" | custom-call | flops 7549747200 | bytes 34166784 | tf_op jit(solution)/shard_map/pallas_call | solution.py:71
  336.4 7.5 shard_map.261
  343.9 7.1 shard_map.260
  351.0 12.7 %shard_map.262 = (bf16[2,384,1152]{2,1,0:T(8,128)(2,1)}, bf16[2,384,1152]{2,1,0:T(8,128)(2,1)}, f32[320,768]{1,0:T(8,128)}, bf16[320,768]{1,0:T(8,128)(2,1)}) custom-call(bf16[5,64,384]{2,1,0:T(8,128)(2,1)} %get-tuple-element.101.dq_n, bf16[2,5,64,384]{3,2,1,0:T(8,128)(2,1)} %get-tuple-element.102.dk_n, bf16[2,5,64,384]{3,2,1,0:T(8,128)(2,1)} %get-tuple-element.103.dv_n, ...), custom_call_target="tpu_custom_call" | custom-call | flops 4529848320 | bytes 13172736 | tf_op jit(solution)/shard_map/pallas_call | solution.py:71
  368.5 3.5 shard_map.263
  376.3 3.8 shard_map.257
  382.0 5.9 collective-permute-start.22
  393.8 3.7 shard_map.264
  397.6 31.8 %shard_map.265 = (bf16[2,384,3072]{2,1,0:T(8,128)(2,1)}, bf16[2,384,3072]{2,1,0:T(8,128)(2,1)}, bf16[2,384,384]{2,1,0:T(8,128)(2,1)}, bf16[2,384,384]{2,1,0:T(8,...) custom-call(s32[1]{0:T(128)} %bitcast.13.part, ...), custom_call_target="tpu_custom_call" | custom-call | flops 15099494400 | bytes 36329472 | tf_op jit(solution)/shard_map/pallas_call | solution.py:71
  429.3 17.8 %shard_map.267 = (bf16[5,128,384]{2,1,0:T(8,128)(2,1)}, bf16[2,5,128,384]{3,2,1,0:T(8,128)(2,1)}, bf16[2,5,128,384]{3,2,1,0:T(8,128)(2,1)}) custom-call(s32[1]{0:T(128)S(6)} %select_n.197.kind, bf16[5,128,384]{2,1,0:T(8,128)(2,1)} %get-tuple-element.83.q, bf16[2,5,128,384]{3,2,1,0:T(8,128)(2,1)} %get-tuple-element.84.k, ...), custom_call_target="tpu_custom_call" | custom-call | flops 10066329600 | bytes 5406720 | tf_op jit(solution)/shard_map/pallas_call | solution.py:71
  447.1 17.8 %shard_map.266 = (bf16[5,128,384]{2,1,0:T(8,128)(2,1)}, bf16[2,5,128,384]{3,2,1,0:T(8,128)(2,1)}, bf16[2,5,128,384]{3,2,1,0:T(8,128)(2,1)}) custom-call(s32[1]{0:T(128)S(6)} %select_n.197.kind, bf16[5,128,384]{2,1,0:T(8,128)(2,1)} %get-tuple-element.79.q, bf16[2,5,128,384]{3,2,1,0:T(8,128)(2,1)} %get-tuple-element.80.k, ...), custom_call_target="tpu_custom_call" | custom-call | flops 10066329600 | bytes 5406720 | tf_op jit(solution)/shard_map/pallas_call | solution.py:71
  464.9 19.5 %shard_map.268 = (bf16[2,384,1152]{2,1,0:T(8,128)(2,1)}, bf16[2,384,1152]{2,1,0:T(8,128)(2,1)}, f32[640,768]{1,0:T(8,128)}, bf16[640,768]{1,0:T(8,128)(2,1)}) custom-call(bf16[5,128,384]{2,1,0:T(8,128)(2,1)} %get-tuple-element.118.dq_n, bf16[2,5,128,384]{3,2,1,0:T(8,128)(2,1)} %get-tuple-element.119.dk_n, bf16[2,5,128,384]{3,2,1,0:T(8,128)(2,1)} %get-tuple-element.120.dv_n, ...), custom_call_target="tpu_custom_call" | custom-call | flops 9059696640 | bytes 18087936 | tf_op jit(solution)/shard_map/pallas_call | solution.py:71
  489.3 2.5 collective-permute-done.55
  491.8 2.8 collective-permute-start.56
  499.0 7.8 collective-permute-done.38
  508.4 5.3 shard_map.269
  515.6 5.9 collective-permute-start.30
  524.3 2.7 collective-permute-start.40
  527.1 2.6 collective-permute-done.40
  537.7 6.5 collective-permute-done.31
  546.1 16.3 %collective-permute-done.48 = bf16[384,1152]{1,0:T(8,128)(2,1)S(1)} collective-permute-done((bf16[384,1152]{1,0:T(8,128)(2,1)}, bf16[384,1152]{1,0:T(8,128)(2,1)S(1)}, u32[]{:S(2)}, u32[]{:S(2)}) %collective-permute-start.48) | collective-permute-done | bytes 884768 | tf_op jit(solution)/shard_map/ppermute | solution.py:613
  566.4 2.4 collective-permute-start.33
  568.8 3.0 collective-permute-done.49
  571.9 3.3 collective-permute-start.50
  576.6 7.9 %collective-permute-done.50 = bf16[96,1152]{1,0:T(8,128)(2,1)S(1)} collective-permute-done((bf16[96,1152]{1,0:T(8,128)(2,1)S(1)}, bf16[96,1152]{1,0:T(8,128)(2,1)S(1)}, u32[]{:S(2)}, u32[]{:S(2)}) %collective-permute-start.50) | collective-permute-done | bytes 221216 | tf_op jit(solution)/shard_map/ppermute | solution.py:613
  593.8 3.3 fusion.3
  597.1 2.4 collective-permute-start.58
  599.5 2.7 fusion.2
  602.5 3.8 collective-permute-start.35
  607.0 5.1 collective-permute-done.35
  612.3 39.4 %collective-permute-done.58 = bf16[384,3072]{1,0:T(8,128)(2,1)S(1)} collective-permute-done((bf16[384,3072]{1,0:T(8,128)(2,1)S(1)}, bf16[384,3072]{1,0:T(8,128)(2,1)S(1)}, u32[]{:S(2)}, u32[]{:S(2)}) %collective-permute-start.58) | collective-permute-done | bytes 2359328 | tf_op jit(solution)/shard_map/ppermute | solution.py:613
  651.7 2.8 bitcast_add_fusion
  655.7 41.2 %collective-permute-done.43 = bf16[384,3072]{1,0:T(8,128)(2,1)S(1)} collective-permute-done((bf16[384,3072]{1,0:T(8,128)(2,1)S(1)}, bf16[384,3072]{1,0:T(8,128)(2,1)S(1)}, u32[]{:S(2)}, u32[]{:S(2)}) %collective-permute-start.43) | collective-permute-done | bytes 2359328 | tf_op jit(solution)/shard_map/ppermute | solution.py:613
  696.9 2.8 bitcast_add_fusion.1
  709.0 2.4 slice_add_fusion
  711.4 3.5 collective-permute-start.60
  714.9 11.0 %collective-permute-done.44 = bf16[192,3072]{1,0:T(8,128)(2,1)} collective-permute-done((bf16[192,3072]{1,0:T(8,128)(2,1)}, bf16[192,3072]{1,0:T(8,128)(2,1)}, u32[]{:S(2)}, u32[]{:S(2)}) %collective-permute-start.44) | collective-permute-done | bytes 1179680 | tf_op jit(solution)/shard_map/ppermute | solution.py:613
  727.6 3.5 collective-permute-start.45
  731.1 18.1 %collective-permute-done.60 = bf16[96,3072]{1,0:T(8,128)(2,1)S(1)} collective-permute-done((bf16[96,3072]{1,0:T(8,128)(2,1)S(1)}, bf16[96,3072]{1,0:T(8,128)(2,1)S(1)}, u32[]{:S(2)}, u32[]{:S(2)}) %collective-permute-start.60) | collective-permute-done | bytes 589856 | tf_op jit(solution)/shard_map/ppermute | solution.py:613
  750.1 11.6 %collective-permute-done.45 = bf16[96,3072]{1,0:T(8,128)(2,1)S(1)} collective-permute-done((bf16[96,3072]{1,0:T(8,128)(2,1)S(1)}, bf16[96,3072]{1,0:T(8,128)(2,1)S(1)}, u32[]{:S(2)}, u32[]{:S(2)}) %collective-permute-start.45) | collective-permute-done | bytes 589856 | tf_op jit(solution)/shard_map/ppermute | solution.py:613
  762.0 6.1 collective-permute-done.61
  (327 shorter events, 135.7 us)
Async XLA Ops:
  7.2 287.1 %all-gather.9.cloned.1.call-start = ((), (), s32[]{:S(2)}) async-start(), calls=%async_computation | async-start | bytes 1880064 | tf_op jit(solution)/shard_map/all_gather | solution.py:640
  8.3 6.1 collective-permute-start.16
  15.1 288.6 %all-gather.11.cloned.1.call-start = ((), (), s32[]{:S(2)}) async-start(), calls=%async_computation.1 | async-start | bytes 2506752 | tf_op jit(solution)/shard_map/all_gather | solution.py:640
  16.1 5.2 collective-permute-start.19
  21.9 281.7 %all-gather.13.cloned.1.call-start = ((), (), s32[]{:S(2)}) async-start(), calls=%async_computation.2 | async-start | bytes 2506752 | tf_op jit(solution)/shard_map/all_gather | solution.py:640
  23.9 54.6 %collective-permute-start.1 = (bf16[3,128,768]{2,1,0:T(8,128)(2,1)}, bf16[3,128,768]{2,1,0:T(8,128)(2,1)}, u32[]{:S(2)}, u32[]{:S(2)}) collective-permute-start(bf16[3,128,768]{2,1,0:T(8,128)(2,1)} %slice.301), channel_id=1, source_target_pairs={{0,0},{1,2},{2,1},{3,3},{4,4},{5,6},{6,5},{7,7},{8,8},{9,10},{10,9... | collective-permute-start | bytes 1769480 | tf_op jit(solution)/shard_map/ppermute | solution.py:613
  30.7 10.4 %collective-permute-start = (s32[645]{0:T(1024)S(1)}, s32[645]{0:T(1024)S(1)}, u32[]{:S(2)}, u32[]{:S(2)}) collective-permute-start(s32[645]{0:T(1024)S(1)} %pad_add_fusion), channel_id=1, source_target_pairs={{0,0},{1,2},{2,1},{3,3},{4,4},{5,6},{6,5},{7,7},{8,8},{9,10},{10,9... | collective-permute-start | bytes 7748 | tf_op jit(solution)/shard_map/ppermute | solution.py:613
  31.4 11.2 %collective-permute-start.4 = (bf16[5,768]{1,0:T(8,128)(2,1)S(1)}, bf16[5,768]{1,0:T(8,128)(2,1)S(1)}, u32[]{:S(2)}, u32[]{:S(2)}) collective-permute-start(bf16[5,768]{1,0:T(8,128)(2,1)S(1)} %fusion.18), channel_id=1, source_target_pairs={{0,0},{1,2},{2,1},{3,3},{4,4},{5,6},{6,5},{7,7},{8,8},{9,10},{10,9... | collective-permute-start | bytes 23048 | tf_op jit(solution)/shard_map/ppermute | solution.py:613
  32.8 18.2 %collective-permute-start.7 = (bf16[192,768]{1,0:T(8,128)(2,1)}, bf16[192,768]{1,0:T(8,128)(2,1)}, u32[]{:S(2)}, u32[]{:S(2)}) collective-permute-start(bf16[192,768]{1,0:T(8,128)(2,1)} %constant_dynamic-slice_fusion.14), channel_id=1, source_target_pairs={{0,1},{1,0},{2,3},{3,2},{4,5},{5,4},{6,7},{7,6},{8,9},{9,8},{10,11... | collective-permute-start | bytes 884744 | tf_op jit(solution)/shard_map/ppermute | solution.py:613
  35.7 9.8 %collective-permute-start.20 = (bf16[96,768]{1,0:T(8,128)(2,1)S(1)}, bf16[96,768]{1,0:T(8,128)(2,1)S(1)}, u32[]{:S(2)}, u32[]{:S(2)}) collective-permute-start(bf16[96,768]{1,0:T(8,128)(2,1)S(1)} %constant_dynamic-slice_fusion.4), channel_id=1, source_target_pairs={{0,1},{1,0},{2,3},{3,2},{4,5},{5,4},{6,7},{7,6},{8,9},{9,8},{10,11... | collective-permute-start | bytes 442376 | tf_op jit(solution)/shard_map/ppermute | solution.py:613
  41.0 36.0 %collective-permute-start.2 = (bf16[2,128,768]{2,1,0:T(8,128)(2,1)S(1)}, bf16[2,128,768]{2,1,0:T(8,128)(2,1)S(1)}, u32[]{:S(2)}, u32[]{:S(2)}) collective-permute-start(bf16[2,128,768]{2,1,0:T(8,128)(2,1)S(1)} %slice.302), channel_id=1, source_target_pairs={{0,2},{1,0},{2,3},{3,1},{4,6},{5,4},{6,7},{7,5},{8,10},{9,8},{10,1... | collective-permute-start | bytes 1179656 | tf_op jit(solution)/shard_map/ppermute | solution.py:613
  42.5 47.1 %collective-permute-start.5 = (bf16[3,384,384]{2,1,0:T(8,128)(2,1)}, bf16[3,384,384]{2,1,0:T(8,128)(2,1)}, u32[]{:S(2)}, u32[]{:S(2)}) collective-permute-start(bf16[3,384,384]{2,1,0:T(8,128)(2,1)} %dynamic-slice_bitcast_fusion), channel_id=1, source_target_pairs={{0,1},{1,0},{2,3},{3,2},{4,5},{5,4},{6,7},{7,6},{8,9},{9,8},{10,11... | collective-permute-start | bytes 2654216 | tf_op jit(solution)/shard_map/ppermute | solution.py:613
  46.1 29.5 %collective-permute-start.17 = (bf16[192,768]{1,0:T(8,128)(2,1)}, bf16[192,768]{1,0:T(8,128)(2,1)}, u32[]{:S(2)}, u32[]{:S(2)}) collective-permute-start(bf16[192,768]{1,0:T(8,128)(2,1)} %constant_dynamic-slice_fusion.6), channel_id=1, source_target_pairs={{0,1},{1,0},{2,3},{3,2},{4,5},{5,4},{6,7},{7,6},{8,9},{9,8},{10,11... | collective-permute-start | bytes 884744 | tf_op jit(solution)/shard_map/ppermute | solution.py:613
  51.0 30.1 %collective-permute-start.25 = (bf16[2,128,768]{2,1,0:T(8,128)(2,1)S(1)}, bf16[2,128,768]{2,1,0:T(8,128)(2,1)S(1)}, u32[]{:S(2)}, u32[]{:S(2)}) collective-permute-start(bf16[2,128,768]{2,1,0:T(8,128)(2,1)S(1)} %slice.317), channel_id=1, source_target_pairs={{0,2},{1,0},{2,3},{3,1},{4,6},{5,4},{6,7},{7,5},{8,10},{9,8},{10,1... | collective-permute-start | bytes 1179656 | tf_op jit(solution)/shard_map/ppermute | solution.py:613
  75.7 11.3 %collective-permute-start.8 = (bf16[192,768]{1,0:T(8,128)(2,1)}, bf16[192,768]{1,0:T(8,128)(2,1)}, u32[]{:S(2)}, u32[]{:S(2)}) collective-permute-start(bf16[192,768]{1,0:T(8,128)(2,1)} %collective-permute-done.7), channel_id=1, source_target_pairs={{0,2},{1,3},{2,0},{3,1},{4,6},{5,7},{6,4},{7,5},{8,10},{9,11},{10,... | collective-permute-start | bytes 884744 | tf_op jit(solution)/shard_map/ppermute | solution.py:613
  77.1 62.0 %collective-permute-start.9 = (bf16[768,768]{1,0:T(8,128)(2,1)}, bf16[768,768]{1,0:T(8,128)(2,1)}, u32[]{:S(2)}, u32[]{:S(2)}) collective-permute-start(bf16[768,768]{1,0:T(8,128)(2,1)} %constant_dynamic-slice_fusion.13), channel_id=1, source_target_pairs={{0,1},{1,0},{2,3},{3,2},{4,5},{5,4},{6,7},{7,6},{8,9},{9,8},{10,11... | collective-permute-start | bytes 3538952 | tf_op jit(solution)/shard_map/ppermute | solution.py:613
  78.6 60.6 %collective-permute-start.10 = (bf16[768,768]{1,0:T(8,128)(2,1)S(1)}, bf16[768,768]{1,0:T(8,128)(2,1)}, u32[]{:S(2)}, u32[]{:S(2)}) collective-permute-start(bf16[768,768]{1,0:T(8,128)(2,1)S(1)} %constant_dynamic-slice_fusion.12), channel_id=1, source_target_pairs={{0,1},{1,0},{2,3},{3,2},{4,5},{5,4},{6,7},{7,6},{8,9},{9,8},{10,11... | collective-permute-start | bytes 3538952 | tf_op jit(solution)/shard_map/ppermute | solution.py:613
  81.1 58.5 %collective-permute-start.3 = (bf16[5,128,768]{2,1,0:T(8,128)(2,1)S(1)}, bf16[5,128,768]{2,1,0:T(8,128)(2,1)}, u32[]{:S(2)}, u32[]{:S(2)}) collective-permute-start(bf16[5,128,768]{2,1,0:T(8,128)(2,1)S(1)} %maximum_select_fusion.1.own), channel_id=1, source_target_pairs={{0,2},{1,3},{2,0},{3,1},{4,6},{5,7},{6,4},{7,5},{8,10},{9,11},{10,... | collective-permute-start | bytes 2949128 | tf_op jit(solution)/shard_map/ppermute | solution.py:613
  87.0 11.6 %collective-permute-start.24 = (bf16[3,128,768]{2,1,0:T(8,128)(2,1)S(1)}, bf16[3,128,768]{2,1,0:T(8,128)(2,1)}, u32[]{:S(2)}, u32[]{:S(2)}) collective-permute-start(bf16[3,128,768]{2,1,0:T(8,128)(2,1)S(1)} %copy-done.13), channel_id=1, source_target_pairs={{0,0},{1,2},{2,1},{3,3},{4,4},{5,6},{6,5},{7,7},{8,8},{9,10},{10,9... | collective-permute-start | bytes 1769480 | tf_op jit(solution)/shard_map/ppermute | solution.py:613
  89.4 497.6 %all-gather.17.cloned.1.call-start = ((), (), s32[]{:S(2)}) async-start(), calls=%async_computation.4 | async-start | bytes 2433024 | tf_op jit(solution)/shard_map/all_gather | solution.py:768
  89.6 66.6 %collective-permute-start.6 = (bf16[3,384,384]{2,1,0:T(8,128)(2,1)}, bf16[3,384,384]{2,1,0:T(8,128)(2,1)}, u32[]{:S(2)}, u32[]{:S(2)}) collective-permute-start(bf16[3,384,384]{2,1,0:T(8,128)(2,1)} %collective-permute-done.5), channel_id=1, source_target_pairs={{0,2},{1,3},{2,0},{3,1},{4,6},{5,7},{6,4},{7,5},{8,10},{9,11},{10,... | collective-permute-start | bytes 2654216 | tf_op jit(solution)/shard_map/ppermute | solution.py:613
  98.6 173.3 %collective-permute-start.18 = (bf16[192,768]{1,0:T(8,128)(2,1)}, bf16[192,768]{1,0:T(8,128)(2,1)}, u32[]{:S(2)}, u32[]{:S(2)}) collective-permute-start(bf16[192,768]{1,0:T(8,128)(2,1)} %collective-permute-done.17), channel_id=1, source_target_pairs={{0,2},{1,3},{2,0},{3,1},{4,6},{5,7},{6,4},{7,5},{8,10},{9,11},{10,... | collective-permute-start | bytes 884744 | tf_op jit(solution)/shard_map/ppermute | solution.py:613
  139.1 135.0 %collective-permute-start.26 = (bf16[5,128,768]{2,1,0:T(8,128)(2,1)S(1)}, bf16[5,128,768]{2,1,0:T(8,128)(2,1)}, u32[]{:S(2)}, u32[]{:S(2)}) collective-permute-start(bf16[5,128,768]{2,1,0:T(8,128)(2,1)S(1)} %maximum_select_fusion.2), channel_id=1, source_target_pairs={{0,2},{1,3},{2,0},{3,1},{4,6},{5,7},{6,4},{7,5},{8,10},{9,11},{10,... | collective-permute-start | bytes 2949128 | tf_op jit(solution)/shard_map/ppermute | solution.py:613
  139.1 35.7 %collective-permute-start.11 = (bf16[768,768]{1,0:T(8,128)(2,1)}, bf16[768,768]{1,0:T(8,128)(2,1)S(1)}, u32[]{:S(2)}, u32[]{:S(2)}) collective-permute-start(bf16[768,768]{1,0:T(8,128)(2,1)} %collective-permute-done.9.up_a), channel_id=1, source_target_pairs={{0,2},{1,3},{2,0},{3,1},{4,6},{5,7},{6,4},{7,5},{8,10},{9,11},{10,... | collective-permute-start | bytes 3538952 | tf_op jit(solution)/shard_map/ppermute | solution.py:613
  139.6 35.3 %collective-permute-start.12 = (bf16[768,768]{1,0:T(8,128)(2,1)}, bf16[768,768]{1,0:T(8,128)(2,1)}, u32[]{:S(2)}, u32[]{:S(2)}) collective-permute-start(bf16[768,768]{1,0:T(8,128)(2,1)} %collective-permute-done.10.down_a), channel_id=1, source_target_pairs={{0,2},{1,3},{2,0},{3,1},{4,6},{5,7},{6,4},{7,5},{8,10},{9,11},{10,... | collective-permute-start | bytes 3538952 | tf_op jit(solution)/shard_map/ppermute | solution.py:613
  193.3 84.1 %collective-permute-start.15 = (bf16[640,768]{1,0:T(8,128)(2,1)}, bf16[640,768]{1,0:T(8,128)(2,1)}, u32[]{:S(2)}, u32[]{:S(2)}) collective-permute-start(bf16[640,768]{1,0:T(8,128)(2,1)} %bitcast.103), channel_id=1, source_target_pairs={{0,2},{1,3},{2,0},{3,1},{4,6},{5,7},{6,4},{7,5},{8,10},{9,11},{10,... | collective-permute-start | bytes 2949128 | tf_op jit(solution)/shard_map/ppermute | solution.py:613
  194.9 82.4 %collective-permute-start.13 = (bf16[3,128,768]{2,1,0:T(8,128)(2,1)S(1)}, bf16[3,128,768]{2,1,0:T(8,128)(2,1)S(1)}, u32[]{:S(2)}, u32[]{:S(2)}) collective-permute-start(bf16[3,128,768]{2,1,0:T(8,128)(2,1)S(1)} %constant_dynamic-slice_fusion.11), channel_id=1, source_target_pairs={{0,0},{1,2},{2,1},{3,3},{4,4},{5,6},{6,5},{7,7},{8,8},{9,10},{10,9... | collective-permute-start | bytes 1769480 | tf_op jit(solution)/shard_map/ppermute | solution.py:613
  271.8 5.6 collective-permute-start.14
  365.2 8.7 %collective-permute-start.52 = (bf16[2,384,384]{2,1,0:T(8,128)(2,1)}, bf16[2,384,384]{2,1,0:T(8,128)(2,1)S(1)}, u32[]{:S(2)}, u32[]{:S(2)}) collective-permute-start(bf16[2,384,384]{2,1,0:T(8,128)(2,1)} %get-tuple-element.142), channel_id=1, source_target_pairs={{0,2},{1,3},{2,0},{3,1},{4,6},{5,7},{6,4},{7,5},{8,10},{9,11},{10,... | collective-permute-start | bytes 1769480 | tf_op jit(solution)/shard_map/ppermute | solution.py:613
  366.0 10.3 %collective-permute-start.21 = (bf16[320,768]{1,0:T(8,128)(2,1)}, bf16[320,768]{1,0:T(8,128)(2,1)}, u32[]{:S(2)}, u32[]{:S(2)}) collective-permute-start(bf16[320,768]{1,0:T(8,128)(2,1)} %bitcast.10.own), channel_id=1, source_target_pairs={{0,2},{1,3},{2,0},{3,1},{4,6},{5,7},{6,4},{7,5},{8,10},{9,11},{10,... | collective-permute-start | bytes 1474568 | tf_op jit(solution)/shard_map/ppermute | solution.py:613
  367.1 226.7 %collective-permute-start.57 = (bf16[2,384,3072]{2,1,0:T(8,128)(2,1)}, bf16[2,384,3072]{2,1,0:T(8,128)(2,1)}, u32[]{:S(2)}, u32[]{:S(2)}) collective-permute-start(bf16[2,384,3072]{2,1,0:T(8,128)(2,1)} %get-tuple-element.144), channel_id=1, source_target_pairs={{0,2},{1,3},{2,0},{3,1},{4,6},{5,7},{6,4},{7,5},{8,10},{9,11},{10,... | collective-permute-start | bytes 14155784 | tf_op jit(solution)/shard_map/ppermute | solution.py:613
  367.2 130.6 %collective-permute-start.47 = (bf16[2,384,1152]{2,1,0:T(8,128)(2,1)}, bf16[2,384,1152]{2,1,0:T(8,128)(2,1)S(1)}, u32[]{:S(2)}, u32[]{:S(2)}) collective-permute-start(bf16[2,384,1152]{2,1,0:T(8,128)(2,1)} %get-tuple-element.140), channel_id=1, source_target_pairs={{0,2},{1,3},{2,0},{3,1},{4,6},{5,7},{6,4},{7,5},{8,10},{9,11},{10,... | collective-permute-start | bytes 5308424 | tf_op jit(solution)/shard_map/ppermute | solution.py:613
  373.8 330.9 %all-gather.15.cloned.1.call-start = ((), (), s32[]{:S(2)}) async-start(), calls=%async_computation.3 | async-start | bytes 2433024 | tf_op jit(solution)/shard_map/all_gather | solution.py:768
  373.8 17.7 %collective-permute-start.28 = (bf16[320,768]{1,0:T(8,128)(2,1)}, bf16[320,768]{1,0:T(8,128)(2,1)S(1)}, u32[]{:S(2)}, u32[]{:S(2)}) collective-permute-start(bf16[320,768]{1,0:T(8,128)(2,1)} %bitcast.121), channel_id=1, source_target_pairs={{0,2},{1,3},{2,0},{3,1},{4,6},{5,7},{6,4},{7,5},{8,10},{9,11},{10,... | collective-permute-start | bytes 1474568 | tf_op jit(solution)/shard_map/ppermute | solution.py:613
  374.0 15.7 %collective-permute-start.53 = (bf16[384,384]{1,0:T(8,128)(2,1)S(1)}, bf16[384,384]{1,0:T(8,128)(2,1)S(1)}, u32[]{:S(2)}, u32[]{:S(2)}) collective-permute-start(bf16[384,384]{1,0:T(8,128)(2,1)S(1)} %fusion.8), channel_id=1, source_target_pairs={{0,1},{1,0},{2,3},{3,2},{4,5},{5,4},{6,7},{7,6},{8,9},{9,8},{10,11... | collective-permute-start | bytes 884744 | tf_op jit(solution)/shard_map/ppermute | solution.py:613
  382.0 102.8 %collective-permute-start.22 = (bf16[3,128,768]{2,1,0:T(8,128)(2,1)}, bf16[3,128,768]{2,1,0:T(8,128)(2,1)}, u32[]{:S(2)}, u32[]{:S(2)}) collective-permute-start(bf16[3,128,768]{2,1,0:T(8,128)(2,1)} %constant_dynamic-slice_fusion.3), channel_id=1, source_target_pairs={{0,0},{1,2},{2,1},{3,3},{4,4},{5,6},{6,5},{7,7},{8,8},{9,10},{10,9... | collective-permute-start | bytes 1769480 | tf_op jit(solution)/shard_map/ppermute | solution.py:613
  390.4 96.0 %collective-permute-start.23 = (bf16[2,128,768]{2,1,0:T(8,128)(2,1)}, bf16[2,128,768]{2,1,0:T(8,128)(2,1)}, u32[]{:S(2)}, u32[]{:S(2)}) collective-permute-start(bf16[2,128,768]{2,1,0:T(8,128)(2,1)} %constant_dynamic-slice_fusion.2), channel_id=1, source_target_pairs={{0,1},{1,3},{2,0},{3,2},{4,5},{5,7},{6,4},{7,6},{8,9},{9,11},{10,8... | collective-permute-start | bytes 1179656 | tf_op jit(solution)/shard_map/ppermute | solution.py:613
  391.5 92.9 %collective-permute-start.54 = (bf16[192,384]{1,0:T(8,128)(2,1)S(1)}, bf16[192,384]{1,0:T(8,128)(2,1)S(1)}, u32[]{:S(2)}, u32[]{:S(2)}) collective-permute-start(bf16[192,384]{1,0:T(8,128)(2,1)S(1)} %slice.547), channel_id=1, source_target_pairs={{0,4},{1,5},{2,6},{3,7},{4,0},{5,1},{6,2},{7,3},{8,12},{9,13},{10,... | collective-permute-start | bytes 442376 | tf_op jit(solution)/shard_map/ppermute | solution.py:613
  484.4 115.0 %collective-permute-start.42 = (bf16[2,384,3072]{2,1,0:T(8,128)(2,1)}, bf16[2,384,3072]{2,1,0:T(8,128)(2,1)}, u32[]{:S(2)}, u32[]{:S(2)}) collective-permute-start(bf16[2,384,3072]{2,1,0:T(8,128)(2,1)} %get-tuple-element.136), channel_id=1, source_target_pairs={{0,2},{1,3},{2,0},{3,1},{4,6},{5,7},{6,4},{7,5},{8,10},{9,11},{10,... | collective-permute-start | bytes 14155784 | tf_op jit(solution)/shard_map/ppermute | solution.py:613
  484.8 12.4 %collective-permute-start.37 = (bf16[2,384,384]{2,1,0:T(8,128)(2,1)}, bf16[2,384,384]{2,1,0:T(8,128)(2,1)S(1)}, u32[]{:S(2)}, u32[]{:S(2)}) collective-permute-start(bf16[2,384,384]{2,1,0:T(8,128)(2,1)} %get-tuple-element.134), channel_id=1, source_target_pairs={{0,2},{1,3},{2,0},{3,1},{4,6},{5,7},{6,4},{7,5},{8,10},{9,11},{10,... | collective-permute-start | bytes 1769480 | tf_op jit(solution)/shard_map/ppermute | solution.py:613
  486.4 5.4 collective-permute-start.55
  496.5 67.5 %collective-permute-start.32 = (bf16[2,384,1152]{2,1,0:T(8,128)(2,1)}, bf16[2,384,1152]{2,1,0:T(8,128)(2,1)}, u32[]{:S(2)}, u32[]{:S(2)}) collective-permute-start(bf16[2,384,1152]{2,1,0:T(8,128)(2,1)} %get-tuple-element.132), channel_id=1, source_target_pairs={{0,2},{1,3},{2,0},{3,1},{4,6},{5,7},{6,4},{7,5},{8,10},{9,11},{10,... | collective-permute-start | bytes 5308424 | tf_op jit(solution)/shard_map/ppermute | solution.py:613
  497.2 11.2 %collective-permute-start.29 = (bf16[640,768]{1,0:T(8,128)(2,1)S(1)}, bf16[640,768]{1,0:T(8,128)(2,1)}, u32[]{:S(2)}, u32[]{:S(2)}) collective-permute-start(bf16[640,768]{1,0:T(8,128)(2,1)S(1)} %copy-done.42), channel_id=1, source_target_pairs={{0,2},{1,3},{2,0},{3,1},{4,6},{5,7},{6,4},{7,5},{8,10},{9,11},{10,... | collective-permute-start | bytes 2949128 | tf_op jit(solution)/shard_map/ppermute | solution.py:613
  497.8 9.0 %collective-permute-start.38 = (bf16[384,384]{1,0:T(8,128)(2,1)S(1)}, bf16[384,384]{1,0:T(8,128)(2,1)S(1)}, u32[]{:S(2)}, u32[]{:S(2)}) collective-permute-start(bf16[384,384]{1,0:T(8,128)(2,1)S(1)} %fusion.7), channel_id=1, source_target_pairs={{0,1},{1,0},{2,3},{3,2},{4,5},{5,4},{6,7},{7,6},{8,9},{9,8},{10,11... | collective-permute-start | bytes 884744 | tf_op jit(solution)/shard_map/ppermute | solution.py:613
  507.6 15.7 %collective-permute-start.39 = (bf16[192,384]{1,0:T(8,128)(2,1)}, bf16[192,384]{1,0:T(8,128)(2,1)}, u32[]{:S(2)}, u32[]{:S(2)}) collective-permute-start(bf16[192,384]{1,0:T(8,128)(2,1)} %slice.548), channel_id=1, source_target_pairs={{0,4},{1,5},{2,6},{3,7},{4,0},{5,1},{6,2},{7,3},{8,12},{9,13},{10,... | collective-permute-start | bytes 442376 | tf_op jit(solution)/shard_map/ppermute | solution.py:613
  515.6 21.1 %collective-permute-start.30 = (bf16[3,128,768]{2,1,0:T(8,128)(2,1)}, bf16[3,128,768]{2,1,0:T(8,128)(2,1)}, u32[]{:S(2)}, u32[]{:S(2)}) collective-permute-start(bf16[3,128,768]{2,1,0:T(8,128)(2,1)} %constant_dynamic-slice_fusion.1), channel_id=1, source_target_pairs={{0,0},{1,2},{2,1},{3,3},{4,4},{5,6},{6,5},{7,7},{8,8},{9,10},{10,9... | collective-permute-start | bytes 1769480 | tf_op jit(solution)/shard_map/ppermute | solution.py:613
  524.3 5.4 collective-permute-start.40
  535.2 8.9 %collective-permute-start.31 = (bf16[2,128,768]{2,1,0:T(8,128)(2,1)}, bf16[2,128,768]{2,1,0:T(8,128)(2,1)S(1)}, u32[]{:S(2)}, u32[]{:S(2)}) collective-permute-start(bf16[2,128,768]{2,1,0:T(8,128)(2,1)} %constant_dynamic-slice_fusion), channel_id=1, source_target_pairs={{0,1},{1,3},{2,0},{3,2},{4,5},{5,7},{6,4},{7,6},{8,9},{9,11},{10,8... | collective-permute-start | bytes 1179656 | tf_op jit(solution)/shard_map/ppermute | solution.py:613
  536.7 25.7 %collective-permute-start.48 = (bf16[384,1152]{1,0:T(8,128)(2,1)}, bf16[384,1152]{1,0:T(8,128)(2,1)S(1)}, u32[]{:S(2)}, u32[]{:S(2)}) collective-permute-start(bf16[384,1152]{1,0:T(8,128)(2,1)} %fusion.6), channel_id=1, source_target_pairs={{0,1},{1,0},{2,3},{3,2},{4,5},{5,4},{6,7},{7,6},{8,9},{9,8},{10,11... | collective-permute-start | bytes 2654216 | tf_op jit(solution)/shard_map/ppermute | solution.py:613
  562.8 9.0 %collective-permute-start.49 = (bf16[192,1152]{1,0:T(8,128)(2,1)S(1)}, bf16[192,1152]{1,0:T(8,128)(2,1)S(1)}, u32[]{:S(2)}, u32[]{:S(2)}) collective-permute-start(bf16[192,1152]{1,0:T(8,128)(2,1)S(1)} %slice.541), channel_id=1, source_target_pairs={{0,4},{1,5},{2,6},{3,7},{4,0},{5,1},{6,2},{7,3},{8,12},{9,13},{10,... | collective-permute-start | bytes 1327112 | tf_op jit(solution)/shard_map/ppermute | solution.py:613
  566.4 24.8 %collective-permute-start.33 = (bf16[384,1152]{1,0:T(8,128)(2,1)}, bf16[384,1152]{1,0:T(8,128)(2,1)}, u32[]{:S(2)}, u32[]{:S(2)}) collective-permute-start(bf16[384,1152]{1,0:T(8,128)(2,1)} %fusion.5), channel_id=1, source_target_pairs={{0,1},{1,0},{2,3},{3,2},{4,5},{5,4},{6,7},{7,6},{8,9},{9,8},{10,11... | collective-permute-start | bytes 2654216 | tf_op jit(solution)/shard_map/ppermute | solution.py:613
  571.9 12.6 %collective-permute-start.50 = (bf16[96,1152]{1,0:T(8,128)(2,1)S(1)}, bf16[96,1152]{1,0:T(8,128)(2,1)S(1)}, u32[]{:S(2)}, u32[]{:S(2)}) collective-permute-start(bf16[96,1152]{1,0:T(8,128)(2,1)S(1)} %slice.545), channel_id=1, source_target_pairs={{0,16},{1,17},{2,18},{3,19},{4,20},{5,21},{6,22},{7,23},{8,24},{9,... | collective-permute-start | bytes 663560 | tf_op jit(solution)/shard_map/ppermute | solution.py:613
  585.3 20.9 %collective-permute-start.51 = (bf16[48,1152]{1,0:T(8,128)(2,1)S(1)}, bf16[48,1152]{1,0:T(8,128)(2,1)S(1)}, u32[]{:S(2)}, u32[]{:S(2)}) collective-permute-start(bf16[48,1152]{1,0:T(8,128)(2,1)S(1)} %slice.549), channel_id=1, source_target_pairs={{0,8},{1,9},{2,10},{3,11},{4,12},{5,13},{6,14},{7,15},{8,0},{9,1},... | collective-permute-start | bytes 331784 | tf_op jit(solution)/shard_map/ppermute | solution.py:613
  593.0 9.4 %collective-permute-start.34 = (bf16[192,1152]{1,0:T(8,128)(2,1)S(1)}, bf16[192,1152]{1,0:T(8,128)(2,1)S(1)}, u32[]{:S(2)}, u32[]{:S(2)}) collective-permute-start(bf16[192,1152]{1,0:T(8,128)(2,1)S(1)} %slice.542), channel_id=1, source_target_pairs={{0,4},{1,5},{2,6},{3,7},{4,0},{5,1},{6,2},{7,3},{8,12},{9,13},{10,... | collective-permute-start | bytes 1327112 | tf_op jit(solution)/shard_map/ppermute | solution.py:613
  597.1 54.6 %collective-permute-start.58 = (bf16[384,3072]{1,0:T(8,128)(2,1)S(1)}, bf16[384,3072]{1,0:T(8,128)(2,1)S(1)}, u32[]{:S(2)}, u32[]{:S(2)}) collective-permute-start(bf16[384,3072]{1,0:T(8,128)(2,1)S(1)} %fusion.3), channel_id=1, source_target_pairs={{0,1},{1,0},{2,3},{3,2},{4,5},{5,4},{6,7},{7,6},{8,9},{9,8},{10,11... | collective-permute-start | bytes 7077896 | tf_op jit(solution)/shard_map/ppermute | solution.py:613
  602.2 94.7 %collective-permute-start.43 = (bf16[384,3072]{1,0:T(8,128)(2,1)S(1)}, bf16[384,3072]{1,0:T(8,128)(2,1)S(1)}, u32[]{:S(2)}, u32[]{:S(2)}) collective-permute-start(bf16[384,3072]{1,0:T(8,128)(2,1)S(1)} %fusion.2), channel_id=1, source_target_pairs={{0,1},{1,0},{2,3},{3,2},{4,5},{5,4},{6,7},{7,6},{8,9},{9,8},{10,11... | collective-permute-start | bytes 7077896 | tf_op jit(solution)/shard_map/ppermute | solution.py:613
  602.5 9.7 %collective-permute-start.35 = (bf16[96,1152]{1,0:T(8,128)(2,1)S(1)}, bf16[96,1152]{1,0:T(8,128)(2,1)S(1)}, u32[]{:S(2)}, u32[]{:S(2)}) collective-permute-start(bf16[96,1152]{1,0:T(8,128)(2,1)S(1)} %slice.546), channel_id=1, source_target_pairs={{0,16},{1,17},{2,18},{3,19},{4,20},{5,21},{6,22},{7,23},{8,24},{9,... | collective-permute-start | bytes 663560 | tf_op jit(solution)/shard_map/ppermute | solution.py:613
  612.2 91.7 %collective-permute-start.36 = (bf16[48,1152]{1,0:T(8,128)(2,1)S(1)}, bf16[48,1152]{1,0:T(8,128)(2,1)S(1)}, u32[]{:S(2)}, u32[]{:S(2)}) collective-permute-start(bf16[48,1152]{1,0:T(8,128)(2,1)S(1)} %slice.550), channel_id=1, source_target_pairs={{0,8},{1,9},{2,10},{3,11},{4,12},{5,13},{6,14},{7,15},{8,0},{9,1},... | collective-permute-start | bytes 331784 | tf_op jit(solution)/shard_map/ppermute | solution.py:613
  654.6 54.3 %collective-permute-start.59 = (bf16[192,3072]{1,0:T(8,128)(2,1)S(1)}, bf16[192,3072]{1,0:T(8,128)(2,1)}, u32[]{:S(2)}, u32[]{:S(2)}) collective-permute-start(bf16[192,3072]{1,0:T(8,128)(2,1)S(1)} %slice.537), channel_id=1, source_target_pairs={{0,4},{1,5},{2,6},{3,7},{4,0},{5,1},{6,2},{7,3},{8,12},{9,13},{10,... | collective-permute-start | bytes 3538952 | tf_op jit(solution)/shard_map/ppermute | solution.py:613
  702.2 23.6 %collective-permute-start.44 = (bf16[192,3072]{1,0:T(8,128)(2,1)}, bf16[192,3072]{1,0:T(8,128)(2,1)}, u32[]{:S(2)}, u32[]{:S(2)}) collective-permute-start(bf16[192,3072]{1,0:T(8,128)(2,1)} %slice.538), channel_id=1, source_target_pairs={{0,4},{1,5},{2,6},{3,7},{4,0},{5,1},{6,2},{7,3},{8,12},{9,13},{10,... | collective-permute-start | bytes 3538952 | tf_op jit(solution)/shard_map/ppermute | solution.py:613
  711.4 37.8 %collective-permute-start.60 = (bf16[96,3072]{1,0:T(8,128)(2,1)S(1)}, bf16[96,3072]{1,0:T(8,128)(2,1)S(1)}, u32[]{:S(2)}, u32[]{:S(2)}) collective-permute-start(bf16[96,3072]{1,0:T(8,128)(2,1)S(1)} %slice.539), channel_id=1, source_target_pairs={{0,16},{1,17},{2,18},{3,19},{4,20},{5,21},{6,22},{7,23},{8,24},{9,... | collective-permute-start | bytes 1769480 | tf_op jit(solution)/shard_map/ppermute | solution.py:613
  727.6 34.1 %collective-permute-start.45 = (bf16[96,3072]{1,0:T(8,128)(2,1)S(1)}, bf16[96,3072]{1,0:T(8,128)(2,1)S(1)}, u32[]{:S(2)}, u32[]{:S(2)}) collective-permute-start(bf16[96,3072]{1,0:T(8,128)(2,1)S(1)} %slice.540), channel_id=1, source_target_pairs={{0,16},{1,17},{2,18},{3,19},{4,20},{5,21},{6,22},{7,23},{8,24},{9,... | collective-permute-start | bytes 1769480 | tf_op jit(solution)/shard_map/ppermute | solution.py:613
  749.4 18.6 %collective-permute-start.61 = (bf16[48,3072]{1,0:T(8,128)(2,1)S(1)}, bf16[48,3072]{1,0:T(8,128)(2,1)S(1)}, u32[]{:S(2)}, u32[]{:S(2)}) collective-permute-start(bf16[48,3072]{1,0:T(8,128)(2,1)S(1)} %slice.543), channel_id=1, source_target_pairs={{0,8},{1,9},{2,10},{3,11},{4,12},{5,13},{6,14},{7,15},{8,0},{9,1},... | collective-permute-start | bytes 884744 | tf_op jit(solution)/shard_map/ppermute | solution.py:613
  761.9 12.4 %collective-permute-start.46 = (bf16[48,3072]{1,0:T(8,128)(2,1)S(1)}, bf16[48,3072]{1,0:T(8,128)(2,1)S(1)}, u32[]{:S(2)}, u32[]{:S(2)}) collective-permute-start(bf16[48,3072]{1,0:T(8,128)(2,1)S(1)} %slice.544), channel_id=1, source_target_pairs={{0,8},{1,9},{2,10},{3,11},{4,12},{5,13},{6,14},{7,15},{8,0},{9,1},... | collective-permute-start | bytes 884744 | tf_op jit(solution)/shard_map/ppermute | solution.py:613
  (50 other events, 590.6 us)
Sparse Core Ops, SparseCore 0:
  15.2 41.8 all-gather.8
  59.9 40.9 all-gather.10
  103.2 42.3 all-gather.12
  373.9 60.7 all-gather.16
  534.0 59.9 all-gather.14

commit v2 on v1

v2 whole, which is shorter than its diff:
```python
import functools

import jax
import jax.numpy as jnp
from jax import lax
from jax.experimental import pallas as pl
from jax.experimental.pallas import tpu as pltpu
from jax.sharding import PartitionSpec as P

D = 768
HEAD_DIM = 64
SLOTS = 5
GROUP = 1280
KEEP = 640
BLOCKS = 5
SPAN = GROUP // BLOCKS
HALF = D // 2
TILE = 768
NORM_EPS = 1e-06
f32 = jnp.float32
bf16 = jnp.bfloat16
ALL = ("dp", "tensor")
VMEM_BYTES = 32 * 1024 * 1024
LIGHT = 2000


def dot(left, right):
    return jnp.dot(left, right, preferred_element_type=f32)


def dot_cols(left, right):
    return lax.dot_general(left, right, (((1,), (1,)), ((), ())), preferred_element_type=f32)


def dot_rows(left, right):
    return lax.dot_general(left, right, (((0,), (0,)), ((), ())), preferred_element_type=f32)


def unit_rows(rows):
    centre = rows - jnp.mean(rows, axis=-1, keepdims=True)
    inverse = lax.rsqrt(jnp.mean(centre * centre, axis=-1, keepdims=True) + NORM_EPS)
    return centre * inverse, inverse


def norm_back(d_normed, unit, inverse, scale_row):
    e = d_normed * (1.0 + scale_row)
    return inverse * (
        e
        - jnp.mean(e, axis=-1, keepdims=True)
        - unit * jnp.mean(e * unit, axis=-1, keepdims=True)
    )


def col_sum(rows):
    return jnp.sum(rows, axis=0, keepdims=True)


def flat(ref):
    value = ref[...]
    return value.reshape(-1, value.shape[-1])


def whole(shape):
    return pl.BlockSpec(shape, lambda *_: (0,) * len(shape), pipeline_mode=pl.Buffered(1))


def run(body, grid, ins, outs, scratch=(), scalars=(), flops=0, deps=()):
    in_specs = [whole(a.shape) if s is None else s for a, s in ins]
    in_specs += [pl.BlockSpec(memory_space=pl.ANY)] * len(deps)
    first, past = len(scalars) + len(ins), len(scalars) + len(ins) + len(deps)

    def step(*refs):
        body(*refs[:first], *refs[past:])

    out_specs = [whole(sh) if s is None else s for sh, _, s in outs]
    moved = sum(a.size * a.dtype.itemsize for a, _ in ins)
    moved += sum(jnp.dtype(d).itemsize * functools.reduce(lambda p, q: p * q, sh, 1) for sh, d, _ in outs)
    return pl.pallas_call(
        step,
        grid_spec=pltpu.PrefetchScalarGridSpec(
            num_scalar_prefetch=len(scalars),
            grid=grid,
            in_specs=in_specs,
            out_specs=out_specs,
            scratch_shapes=list(scratch),
        ),
        out_shape=[jax.ShapeDtypeStruct(sh, d) for sh, d, _ in outs],
        compiler_params=pltpu.CompilerParams(
            vmem_limit_bytes=VMEM_BYTES, dimension_semantics=("arbitrary",) * len(grid)
        ),
        cost_estimate=pl.CostEstimate(
            flops=1 + int(flops) // LIGHT, bytes_accessed=1 + int(moved) // LIGHT, transcendentals=0
        ),
    )(*scalars, *[a for a, _ in ins], *deps)


def qkv_body(own, oth, tab, w, normed, q, k, v):
    rows = own.shape[1]
    step = pl.program_id(0)

    @pl.when(step == 0)
    def _():
        for side, src in ((0, own), (1, oth)):
            for i in range(BLOCKS):
                unit, _ = unit_rows(src[i].astype(f32))
                normed[side, i] = (unit * (1.0 + tab[i, 1:2]) + tab[i, 0:1]).astype(bf16)

    qkv_steps(step, normed, w, q, k, v)


def qkv_next_body(normed, w, q, k, v):
    qkv_steps(pl.program_id(0), normed, w, q, k, v)


def qkv_parts_body(place, normed, w_0, w_1, w_2, w_3, w, q, k, v):
    for index, part in enumerate((w_0, w_1, w_2, w_3)):
        at = pl.multiple_of(((place[0] % 4) ^ index) * (D // 4), D // 4)
        w[0, pl.ds(at, D // 4)] = part[0]
    qkv_steps(pl.program_id(0), normed, w, q, k, v)


def block(w):
    return w[...].reshape(D, HALF)


def qkv_steps(step, normed, w, q, k, v):
    @pl.when(step == 0)
    def _():
        mine = normed[0].reshape(-1, D)
        q[...] = dot(mine, block(w)).astype(bf16).reshape(q.shape)

    for index, out in ((1, k), (2, v)):

        @pl.when(step == index)
        def _(out=out):
            out[...] = dot(flat(normed), block(w)).astype(bf16).reshape(out.shape)


def qkv_outs(rows):
    return [
        ((BLOCKS, rows, HALF), bf16, None),
        ((2, BLOCKS, rows, HALF), bf16, None),
        ((2, BLOCKS, rows, HALF), bf16, None),
    ]


BY_STEP = pl.BlockSpec((1, D, HALF), lambda j, *_: (j, 0, 0))


def block_at(w, index):
    if w.ndim == 3:
        return (w, pl.BlockSpec((1, D, HALF), lambda j, *_: (index(j), 0, 0)))
    pieces, _, rows, _ = w.shape
    return (w, pl.BlockSpec((pieces, 1, rows, HALF), lambda j, *_: (0, index(j), 0, 0)))


def project_first(own, oth, tab, w, deps=()):
    rows = own.shape[1]
    return run(
        qkv_body,
        (3,),
        [(own, None), (oth, None), (tab, None), (w, BY_STEP)],
        [((2, BLOCKS, rows, D), bf16, None)] + qkv_outs(rows),
        flops=2 * 25 * rows * D * HALF,
        deps=deps,
    )


def project_next(normed, w, deps=()):
    rows = normed.shape[2]
    ins = [(normed, None), block_at(w, lambda j: j)]
    return run(qkv_next_body, (3,), ins, qkv_outs(rows), flops=2 * 25 * rows * D * HALF, deps=deps)


def project_parts(place, normed, parts, deps=()):
    rows = normed.shape[2]
    by_step = pl.BlockSpec((1, D // 4, HALF), lambda j, *_: (j, 0, 0))
    return run(
        qkv_parts_body,
        (4,),
        [(normed, None)] + [(part, by_step) for part in parts],
        [((4, D, HALF), bf16, BY_STEP)] + qkv_outs(rows),
        scalars=(place,),
        flops=2 * 25 * rows * D * HALF,
        deps=deps,
    )


def by_sequence(kind, one_sequence, long_tiles):
    @pl.when(kind < 2)
    def _():
        one_sequence(kind, 4, long_tiles)
        one_sequence(jnp.where(kind == 0, 4, 0), 1, 1)

    @pl.when(kind == 2)
    def _():
        def short(i, carry):
            one_sequence(i, 1, 1)
            return carry

        lax.fori_loop(0, BLOCKS, short, 0)


def two_heads(rows, low):
    zero = jnp.zeros_like(rows)
    return jnp.concatenate([jnp.where(low, rows, zero), jnp.where(low, zero, rows)], axis=0)


def attend_body(kind, q, k, v, out):
    rows = q.shape[1]
    low = lax.broadcasted_iota(jnp.int32, (1, 128), 1) < HEAD_DIM
    scaling = HEAD_DIM ** (-0.5)

    def one_sequence(start, count, tiles):
        keys = k[:, pl.ds(start, count)].reshape(2 * count * rows, 128)
        values = v[:, pl.ds(start, count)].reshape(2 * count * rows, 128)
        size = tiles * rows
        for part in range(count // tiles):
            at = pl.ds(start + part * tiles, tiles)
            pair = two_heads((q[at].reshape(size, 128) * scaling).astype(bf16), low)
            scores = dot_cols(pair, keys)
            shifted = jnp.exp(scores - jnp.max(scores, axis=-1, keepdims=True))
            total = jnp.sum(shifted, axis=-1, keepdims=True)
            mixed = dot(shifted.astype(bf16), values) * (1.0 / total)
            out[at] = jnp.where(low, mixed[:size], mixed[size:]).astype(bf16).reshape(tiles, rows, 128)

    by_sequence(kind[0], one_sequence, 128 // rows)


def attend(kind, q, k, v, deps=()):
    rows = q.shape[1]
    own = pl.BlockSpec((BLOCKS, rows, 128), lambda p, *_: (0, 0, p))
    every = pl.BlockSpec((2, BLOCKS, rows, 128), lambda p, *_: (0, 0, 0, p))
    return run(
        attend_body,
        (HALF // 128,),
        [(q, own), (k, every), (v, every)],
        [(q.shape, bf16, own)],
        scalars=(kind,),
        flops=16 * BLOCKS * rows * 8 * rows * HALF,
        deps=deps,
    )[0]


def attend_back_body(kind, q, k, v, d_out, dq, dk, dv, acc_k, acc_v):
    rows = q.shape[1]
    low = lax.broadcasted_iota(jnp.int32, (1, 128), 1) < HEAD_DIM
    scaling = HEAD_DIM ** (-0.5)

    def one_sequence(start, count, tiles):
        key_rows = 2 * count * rows
        keys = k[:, pl.ds(start, count)].reshape(key_rows, 128)
        values = v[:, pl.ds(start, count)].reshape(key_rows, 128)
        size = tiles * rows
        for part in range(count // tiles):
            at = pl.ds(start + part * tiles, tiles)
            pair = two_heads((q[at].reshape(size, 128) * scaling).astype(bf16), low)
            d_pair = two_heads(d_out[at].reshape(size, 128), low)
            scores = dot_cols(keys, pair)
            shifted = jnp.exp(scores - jnp.max(scores, axis=0, keepdims=True))
            probs = shifted * (1.0 / jnp.sum(shifted, axis=0, keepdims=True))
            d_probs = dot_cols(values, d_pair)
            row_sum = jnp.sum(probs * d_probs, axis=0, keepdims=True)
            d_scores = (probs * (d_probs - row_sum)).astype(bf16)
            add_v = dot(probs.astype(bf16), d_pair)
            add_k = dot(d_scores, pair)
            if part == 0:
                acc_v[:key_rows] = add_v
                acc_k[:key_rows] = add_k
            else:
                acc_v[:key_rows] += add_v
                acc_k[:key_rows] += add_k
            both = dot_rows(d_scores, keys) * scaling
            dq[at] = jnp.where(low, both[:size], both[size:]).astype(bf16).reshape(tiles, rows, 128)
        dk[:, pl.ds(start, count)] = acc_k[:key_rows].astype(bf16).reshape(2, count, rows, 128)
        dv[:, pl.ds(start, count)] = acc_v[:key_rows].astype(bf16).reshape(2, count, rows, 128)

    by_sequence(kind[0], one_sequence, 128 // rows)


def attend_back(kind, q, k, v, d_out, deps=()):
    rows = q.shape[1]
    own = pl.BlockSpec((BLOCKS, rows, 128), lambda p, *_: (0, 0, p))
    every = pl.BlockSpec((2, BLOCKS, rows, 128), lambda p, *_: (0, 0, 0, p))
    return run(
        attend_back_body,
        (HALF // 128,),
        [(q, own), (k, every), (v, every), (d_out, own)],
        [(q.shape, bf16, own), (k.shape, bf16, every), (v.shape, bf16, every)],
        scratch=[pltpu.VMEM((8 * rows, 128), f32), pltpu.VMEM((8 * rows, 128), f32)],
        scalars=(kind,),
        flops=40 * BLOCKS * rows * 8 * rows * HALF,
        deps=deps,
    )


def gelu_parts(u):
    rate = 0.7978845608028654
    inner = rate * (u + 0.044715 * (u * u * u))
    return jnp.tanh(inner), rate


def hidden(normed, ups, downs, u, act):
    start = 0
    total = None
    ups = [far_up(up) for up in ups]
    for up, down in zip(ups, downs):
        at = slice(start, start + up.shape[1])
        start = start + up.shape[1]
        pre = dot(flat(normed), up)
        u[0, :, at] = pre.astype(bf16)
        tanh, _ = gelu_parts(pre)
        value = (0.5 * pre * (1.0 + tanh)).astype(bf16)
        act[0, :, at] = value
        term = dot(value, down[...])
        total = term if total is None else total + term
    return total


def mlp_near_body(
    mixed_n, mixed_r, proj_n, proj_r, own, tab, up, down,
    attn_out, middle, normed, u, act, acc,
):
    rows = own.shape[1]
    step = pl.program_id(0)

    @pl.when(step == 0)
    def _():
        for at in (slice(0, HALF), slice(HALF, D)):
            acc[:, at] = dot(flat(mixed_n), proj_n[:, at]) + dot(flat(mixed_r), block(proj_r)[at])
        for i in range(BLOCKS):
            attn = acc[i * rows : (i + 1) * rows]
            attn_out[i] = attn.astype(bf16)
            mid = own[i].astype(f32) + tab[i, 2:3] * attn
            middle[i] = mid
            unit, _ = unit_rows(mid)
            normed[i] = (unit * (1.0 + tab[i, 4:5]) + tab[i, 3:4]).astype(bf16)
        acc[...] = hidden(normed, [up], [down], u, act)

    @pl.when(step == 1)
    def _():
        acc[...] += hidden(normed, [up], [down], u, act)


def matching(place, down_0, down_1, down_2, down_3):
    refs = (down_0, down_1, down_2, down_3)
    if len(down_0.shape) > 2:
        return (lambda: far_downs(refs)[:2]), (lambda: far_downs(refs)[2:])
    same = (place[0] // 2 + place[0] // 4) % 2 == 0

    def first():
        return [
            jnp.where(same, down_0[...], down_2[...]),
            jnp.where(same, down_1[...], down_3[...]),
        ]

    def second():
        return [
            jnp.where(same, down_2[...], down_0[...]),
            jnp.where(same, down_3[...], down_1[...]),
        ]

    return first, second


def mlp_far_body(
    place, normed, start, middle, tab, up_0, up_1, up_2, up_3, down_0, down_1, down_2, down_3,
    u, act, mlp_out, out, acc,
):
    rows = middle.shape[1]
    step = pl.program_id(0)
    first, second = matching(place, down_0, down_1, down_2, down_3)

    @pl.when(step == 0)
    def _():
        acc[...] = start[...] + hidden(normed, [up_0, up_1], first(), u, act)

    @pl.when(step == 1)
    def _():
        acc[...] += hidden(normed, [up_2, up_3], second(), u, act)
        for i in range(BLOCKS):
            term = acc[i * rows : (i + 1) * rows]
            mlp_out[i] = term.astype(bf16)
            out[i] = (middle[i] + tab[i, 5:6] * term).astype(bf16)


def projection(w):
    return block_at(w, lambda j: 3)


def far_up(ref):
    return ref[...] if len(ref.shape) == 2 else block(ref)


def far_downs(downs):
    if len(downs[0].shape) == 2:
        return [down[...] for down in downs]
    wide = [
        jnp.concatenate([block(downs[index]), block(downs[index + 2])], axis=1) for index in range(2)
    ]
    return [wide[0][:HALF], wide[0][HALF:], wide[1][:HALF], wide[1][HALF:]]


def far_ins(ups, downs):
    if ups[0].ndim == 2:
        return [(part, None) for part in (*ups, *downs)]
    ins = []
    for index, part in enumerate((*ups, *downs)):
        pieces, _, rows, _ = part.shape
        at = pl.BlockSpec(
            (pieces, 1, rows, HALF),
            lambda *_, index=index: (0, 4 + index, 0, 0),
            pipeline_mode=pl.Buffered(1),
        )
        ins.append((part, at))
    return ins


def feed_near(mixed_n, mixed_r, proj_n, w_r, own, tab, up, down, deps=()):
    rows = own.shape[1]
    total = BLOCKS * rows
    tiles = ((2, total, TILE), bf16, pl.BlockSpec((1, total, TILE), lambda j: (j, 0, 0)))
    return run(
        mlp_near_body,
        (2,),
        [
            (mixed_n, None),
            (mixed_r, None),
            (proj_n, None),
            projection(w_r),
            (own, None),
            (tab, None),
            (up, pl.BlockSpec((D, TILE), lambda j: (0, j))),
            (down, pl.BlockSpec((TILE, D), lambda j: (j, 0))),
        ],
        [
            (own.shape, bf16, None),
            (own.shape, f32, None),
            (own.shape, bf16, None),
            tiles,
            tiles,
            ((total, D), f32, None),
        ],
        flops=2 * total * D * (D + 4 * D),
        deps=deps,
    )


def feed_far(place, normed, start, middle, tab, ups, downs, deps=()):
    total = BLOCKS * normed.shape[1]
    tiles = ((2, total, TILE), bf16, pl.BlockSpec((1, total, TILE), lambda j, *_: (j, 0, 0)))
    return run(
        mlp_far_body,
        (2,),
        [(normed, None), (start, None), (middle, None), (tab, None)]
        + far_ins(ups, downs),
        [tiles, tiles, (normed.shape, bf16, None), (normed.shape, bf16, None)],
        scratch=[pltpu.VMEM((total, D), f32)],
        scalars=(place,),
        flops=2 * total * D * (4 * D),
        deps=deps,
    )


def tile_of(j, place_ref):
    far = jnp.where(place_ref[0] // 2 % 2 == 0, j % 2, 1 - j % 2)
    return (j // 2, 0, jnp.where(j < 2, j % 2, far))


MLP_GRAD = ((2, HALF, 2 * TILE), bf16, pl.BlockSpec((1, HALF, TILE), tile_of))


def both_halves(near, far):
    size = near.shape[1]
    return [
        (near, pl.BlockSpec((1, size, TILE), lambda j, *_: (jnp.minimum(j, 1), 0, 0))),
        (far, pl.BlockSpec((1, size, TILE), lambda j, *_: (jnp.maximum(j - 2, 0), 0, 0))),
    ]


def store_grad(keep, away, at, size, value):
    there = pl.ds(at, size)
    keep[0, :, there] = value[:HALF]
    away[0, :, there] = value[HALF:]


def down_back_body(
    place, d_out, tab, mlp_out, order, act_n, act_r, g_keep, g_send, d_mlp, d_gate, d_mlp_t
):
    rows = d_out.shape[1]
    step = pl.program_id(0)
    core = place[0] % 2

    @pl.when(step == 0)
    def _():
        for i in range(BLOCKS):
            grad = d_out[i].astype(f32)
            d_mlp[i * rows : (i + 1) * rows] = (grad * tab[i, 5:6]).astype(bf16)
            d_gate[i] = col_sum(grad * mlp_out[i].astype(f32))
        d_mlp_t[...] = dot_cols(order[...], d_mlp[...]).astype(bf16)

    @pl.when(step < 2)
    def _():
        store_grad(g_keep, g_send, 0, TILE, dot(d_mlp_t[...], act_n[0]).astype(bf16))

    @pl.when(step >= 2)
    def _():
        for index in range(2):
            value = act_r[0, :, index * HALF : (index + 1) * HALF]
            at = pl.multiple_of((core if index == 0 else 1 - core) * HALF, 128)
            store_grad(g_keep, g_send, at, HALF, dot(d_mlp_t[...], value).astype(bf16))


def down_back(place, d_out, tab, mlp_out, order, act_n, act_r, deps=()):
    total = BLOCKS * d_out.shape[1]
    return run(
        down_back_body,
        (4,),
        [(d_out, None), (tab, None), (mlp_out, None), (order, None)] + both_halves(act_n, act_r),
        [MLP_GRAD, MLP_GRAD, ((total, D), bf16, None), ((BLOCKS, 1, D), f32, None)],
        scratch=[pltpu.VMEM((D, total), bf16)],
        scalars=(place,),
        flops=2 * total * D * 5 * D,
        deps=deps,
    )


def up_back_body(
    place, d_out, tab, d_mlp, normed, u_n, u_r,
    up_n, down_n, up_0, up_1, up_2, up_3, down_0, down_1, down_2, down_3,
    middle, attn_out, proj_n, proj_r, mixed_n, mixed_r, order,
    g_keep, g_send, p_keep, p_send, d_middle, d_mix_n, d_mix_r, d_mod,
    d_attn, turned, acc,
):
    rows = d_out.shape[1]
    step = pl.program_id(0)
    core = place[0] % 2

    @pl.when(step == 0)
    def _():
        turned[...] = dot_cols(order[...], flat(normed)).astype(bf16)

    def back(u, ups, downs, places):
        start = 0
        total = None
        ups = [far_up(up) for up in ups]
        for up, down, at in zip(ups, downs, places):
            size = up.shape[1]
            pre = u[0, :, start : start + size].astype(f32)
            start = start + size
            tanh, rate = gelu_parts(pre)
            slope = 0.5 * (1.0 + tanh) + (0.5 * rate) * pre * (1.0 - tanh * tanh) * (
                1.0 + (3.0 * 0.044715) * (pre * pre)
            )
            d_up = (slope * dot_cols(d_mlp[...], down[...])).astype(bf16)
            store_grad(g_keep, g_send, at, size, dot(turned[...], d_up).astype(bf16))
            term = dot_cols(d_up, up)
            total = term if total is None else total + term
        return total

    both = [pl.multiple_of(core * HALF, 128), pl.multiple_of((1 - core) * HALF, 128)]
    first, second = matching(place, down_0, down_1, down_2, down_3)

    @pl.when(step == 0)
    def _():
        acc[...] = back(u_n, [up_n], [down_n], [0])

    @pl.when(step == 1)
    def _():
        acc[...] += back(u_n, [up_n], [down_n], [0])

    @pl.when(step == 2)
    def _():
        acc[...] += back(u_r, [up_0, up_1], first(), both)

    @pl.when(step == 3)
    def _():
        acc[...] += back(u_r, [up_2, up_3], second(), both)
        for i in range(BLOCKS):
            at = slice(i * rows, (i + 1) * rows)
            d_normed = acc[at]
            unit, inverse = unit_rows(middle[i])
            grad = d_out[i].astype(f32) + norm_back(d_normed, unit, inverse, tab[i, 4:5])
            d_middle[i] = grad
            d_mod[i, 0:1] = col_sum(grad * attn_out[i].astype(f32))
            d_mod[i, 1:2] = col_sum(d_normed)
            d_mod[i, 2:3] = col_sum(d_normed * unit)
            d_attn[at] = (grad * tab[i, 2:3]).astype(bf16)
        turned[...] = dot_cols(order[...], d_attn[...]).astype(bf16)
        d_rows_n = dot_cols(d_attn[...], proj_n[...])
        far = block(proj_r)
        d_rows_r = dot_cols(d_attn[:, :HALF], far[:HALF]) + dot_cols(d_attn[:, HALF:], far[HALF:])
        for side, mixed, d_rows, d_mix in (
            (0, mixed_n, d_rows_n, d_mix_n),
            (1, mixed_r, d_rows_r, d_mix_r),
        ):
            d_mix[...] = d_rows.astype(bf16).reshape(d_mix.shape)
            g_proj = dot(turned[...], flat(mixed)).astype(bf16)
            p_keep[side] = g_proj[:HALF]
            p_send[side] = g_proj[HALF:]


def up_back(place, d_out, tab, d_mlp, saved, weights, proj_n, w_r, mixed_n, mixed_r, order, deps=()):
    attn_out, middle, normed, u_n, u_r = saved
    up, down, ups, downs = weights
    rows = d_out.shape[1]
    total = BLOCKS * rows
    here = lambda j: jnp.minimum(j, 1)
    return run(
        up_back_body,
        (4,),
        [(d_out, None), (tab, None), (d_mlp, None), (normed, None)]
        + both_halves(u_n, u_r)
        + [
            (up, pl.BlockSpec((D, TILE), lambda j, *_: (0, here(j)))),
            (down, pl.BlockSpec((TILE, D), lambda j, *_: (here(j), 0))),
        ]
        + far_ins(ups, downs)
        + [
            (middle, None),
            (attn_out, None),
            (proj_n, None),
            projection(w_r),
            (mixed_n, None),
            (mixed_r, None),
            (order, None),
        ],
        [
            MLP_GRAD,
            MLP_GRAD,
            ((2, HALF, HALF), bf16, None),
            ((2, HALF, HALF), bf16, None),
            (d_out.shape, f32, None),
            (mixed_n.shape, bf16, None),
            (mixed_n.shape, bf16, None),
            ((BLOCKS, 3, D), f32, None),
        ],
        scratch=[
            pltpu.VMEM((total, D), bf16),
            pltpu.VMEM((D, total), bf16),
            pltpu.VMEM((total, D), f32),
        ],
        scalars=(place,),
        flops=2 * total * D * (12 * D + 4 * D),
        deps=deps,
    )


def qkv_back_steps(step, grads, w, turned, p_keep, p_send, g_keep, g_send, acc, start):
    total = grads[0].shape[0] * grads[0].shape[1]

    for index, grad in enumerate(grads):

        @pl.when(step == index)
        def _(index=index, grad=grad):
            value = flat(grad)
            term = dot_cols(value, block(w))
            if index == 0:
                g_w = dot(turned[:, :total], value).astype(bf16)
                start(term)
            else:
                g_w = dot(turned[...], value).astype(bf16)
                acc[...] += term
            g_keep[...] = g_w[:HALF]
            g_send[...] = g_w[HALF:]

    @pl.when(step == 3)
    def _():
        g_keep[...] = p_keep[0]
        g_send[...] = p_send[0]


def qkv_back_body(
    dq, dk, dv, w, normed, order, p_keep, p_send, g_keep, g_send, turned, acc
):
    total = dq.shape[0] * dq.shape[1]
    step = pl.program_id(0)

    @pl.when(step == 0)
    def _():
        turned[...] = dot_cols(order[...], flat(normed)).astype(bf16)

    def start(term):
        acc[:total] = term
        acc[total:] = jnp.zeros((total, D), f32)

    qkv_back_steps(step, (dq, dk, dv), w, turned, p_keep, p_send, g_keep, g_send, acc, start)


def qkv_back_next_body(
    dq, dk, dv, w, turned, before, p_keep, p_send, g_keep, g_send, d_own, d_oth, acc
):
    total = dq.shape[0] * dq.shape[1]
    step = pl.program_id(0)

    def start(term):
        acc[...] = before[...]
        acc[:total] += term

    qkv_back_steps(step, (dq, dk, dv), w, turned, p_keep, p_send, g_keep, g_send, acc, start)

    @pl.when(step == 3)
    def _():
        d_own[...] = acc[:total]
        d_oth[...] = acc[total:].astype(bf16)


def qkv_back(first, side, grads, w, normed, order, turned, before, p_keep, p_send, deps=()):
    rows = normed.shape[2]
    total = BLOCKS * rows
    grad = ((HALF, 4 * HALF), bf16, pl.BlockSpec((HALF, HALF), lambda j: (0, j)))
    piece = pl.BlockSpec((1, HALF, HALF), lambda j: (side, 0, 0))
    ins = [(g, None) for g in grads]
    ins += [block_at(w, lambda j: jnp.minimum(j, 2))]
    ends = [(p_keep, piece), (p_send, piece)]
    flops = 2 * total * D * 10 * HALF
    if first:
        return run(
            qkv_back_body,
            (4,),
            ins + [(normed, None), (order, None)] + ends,
            [grad, grad, ((D, 2 * total), bf16, None), ((2 * total, D), f32, None)],
            flops=flops + 4 * total * D * D,
            deps=deps,
        )
    return run(
        qkv_back_next_body,
        (4,),
        ins + [(turned, None), (before, None)] + ends,
        [grad, grad, ((total, D), f32, None), ((total, D), bf16, None)],
        scratch=[pltpu.VMEM((2 * total, D), f32)],
        flops=flops,
        deps=deps,
    )


def finish_body(d_own, d_got, own, tab, d_middle, d_rows, d_mod):
    rows = own.shape[1]
    for i in range(BLOCKS):
        at = slice(i * rows, (i + 1) * rows)
        d_normed = d_own[at] + d_got[at].astype(f32)
        unit, inverse = unit_rows(own[i].astype(f32))
        grad = d_middle[i] + norm_back(d_normed, unit, inverse, tab[i, 1:2])
        d_rows[i] = grad.astype(bf16)
        d_mod[i, 0:1] = col_sum(d_normed)
        d_mod[i, 1:2] = col_sum(d_normed * unit)


def finish(d_own, d_got, own, tab, d_middle, deps=()):
    return run(
        finish_body,
        (1,),
        [(d_own, None), (d_got, None), (own, None), (tab, None), (d_middle, None)],
        [(own.shape, bf16, None), ((BLOCKS, 2, D), f32, None)],
        deps=deps,
    )


def pick_body(index, own, oth, out):
    spot = lax.broadcasted_iota(jnp.int32, (1, own.shape[0]), 1)
    here = (index[...] == spot).astype(bf16)
    there = (index[...] - own.shape[0] == spot).astype(bf16)
    out[...] = (dot(here, own[...]) + dot(there, oth[...])).astype(bf16)


def pick(index, own, oth, deps=()):
    count = index.shape[0]
    return run(
        pick_body,
        (1,),
        [(index, None), (own, None), (oth, None)],
        [((count, D), bf16, None)],
        flops=2 * count * GROUP * D,
        deps=deps,
    )[0]


def put_body(index_own, index_oth, own, oth, base, out):
    spot = lax.broadcasted_iota(jnp.int32, (base.shape[0], 1), 0)
    here = (index_own[...] == spot).astype(f32)
    there = (index_oth[...] == spot).astype(f32)
    hit = jnp.sum(here, axis=1, keepdims=True) + jnp.sum(there, axis=1, keepdims=True)
    put = dot(here.astype(bf16), own[...]) + dot(there.astype(bf16), oth[...])
    out[...] = jnp.where(hit > 0.5, put, base[...].astype(f32)).astype(bf16)


def put(index_own, index_oth, own, oth, base, deps=()):
    return run(
        put_body,
        (1,),
        [(index_own, None), (index_oth, None), (own, None), (oth, None), (base, None)],
        [(base.shape, bf16, None)],
        flops=2 * base.shape[0] * KEEP * D,
        deps=deps,
    )[0]


def on_device(
    n_dp,
    tokens,
    conditioning,
    segment_ids,
    kept_rows,
    cotangent,
    mod_first,
    qkv_first,
    proj_first,
    up_first,
    down_first,
    mod_second,
    qkv_second,
    proj_second,
    up_second,
    down_second,
):
    dp_pos = lax.axis_index("dp")
    side = lax.axis_index("tensor")
    core = dp_pos % 2
    bits = n_dp.bit_length() - 1

    def moves(where):
        pairs = []
        for dp in range(n_dp):
            for t in range(2):
                to_dp, to_t = where(dp, t)
                pairs.append((dp * 2 + t, to_dp * 2 + to_t))
        return pairs

    across = moves(lambda dp, t: (dp, 1 - t))
    core_swap = moves(lambda dp, t: (dp ^ 1, t))
    next_swap = moves(lambda dp, t: (dp ^ 2, t))
    turn = moves(lambda dp, t: (dp // 2 * 2 + t, dp % 2))
    deal = moves(lambda dp, t: (dp // 2 * 2 + 1 - t, dp % 2))
    undeal = moves(lambda dp, t: (dp // 2 * 2 + t, 1 - dp % 2))

    def send(value, pairs):
        return lax.ppermute(value, ALL, pairs)

    def after(value, *deps):
        return lax.optimization_barrier((value, *deps))[0]

    def to_owner(rows):
        tiles = rows.reshape(BLOCKS, SPAN // 2, D)
        return send(tiles[0::2], turn), send(tiles[1::2], deal)

    def owned(even, odd, *when):
        even, odd = after(even, *when), after(odd, *when)
        return jnp.where(core == 0, jnp.concatenate([even, odd]), jnp.concatenate([odd, even]))

    def from_owner(rows, begin=(), end=()):
        rows = after(rows.reshape(BLOCKS, SPAN // 2, D), *begin)
        even = after(send(lax.dynamic_slice_in_dim(rows, 2 * core, 3), turn), *end)
        odd = after(send(lax.dynamic_slice_in_dim(rows, 3 * (1 - core), 2), undeal), *end)
        shape = (3, 2, SPAN // 2, D)
        odd = jnp.pad(odd, ((0, 1), (0, 0), (0, 0)))
        even = jnp.broadcast_to(even[:, None], shape)
        odd = jnp.broadcast_to(odd[:, None], shape)
        second = lax.broadcasted_iota(jnp.int32, shape, 1) == 1
        both = jnp.where(second, odd, even).reshape(6 * SPAN // 2, D)
        return both[: BLOCKS * SPAN // 2]

    class Far:
        def __init__(self, near, bit, deps=()):
            self.swap = moves(lambda dp, t: (dp ^ 2**bit, t))
            self.first = send(after(near, *deps), across)

        def hop(self, *deps):
            first = after(self.first, *deps)
            self.third = send(first, self.swap)
            self.second = send(first, core_swap)

        def end(self, *deps):
            return self.first, self.second, self.third, send(after(self.third, *deps), core_swap)

    def part_of(value, axis, bit):
        size = value.shape[axis] // 4
        part = dp_pos // 2**bit % 2 * 2 + core
        return lax.dynamic_slice_in_dim(value, part * size, size, axis)

    numbers = send(jnp.concatenate([kept_rows, segment_ids[::SPAN]]), turn)
    cond = send(jax.nn.silu(conditioning.astype(f32)).astype(bf16), turn)
    wq_one = jnp.transpose(qkv_first, (1, 0, 2))
    wq_two = jnp.transpose(qkv_second, (1, 0, 2))
    place_ref = dp_pos.reshape(1).astype(jnp.int32)
    zero_ref = jnp.zeros((1,), jnp.int32)
    quarter_at = dp_pos // 2 % 2 * 2 + core
    proj_part = lax.dynamic_slice(
        proj_first, (quarter_at % 2 * (D // 4), quarter_at // 2 * HALF), (D // 4, HALF)
    )
    near_part = jnp.concatenate([part_of(wq_one, 1, 1), proj_part[None]])
    kept, segs = numbers[:KEEP], numbers[KEEP:]
    kind = jnp.where(segs[3] == segs[0], 0, jnp.where(segs[4] == segs[1], 1, 2)).reshape(1)
    slot_hot = segs[:, None] == jnp.arange(SLOTS, dtype=jnp.int32)[None, :]
    cond_rows = jnp.dot(slot_hot.astype(bf16), cond, preferred_element_type=f32).astype(bf16)

    def table(mod):
        return jnp.dot(cond_rows, mod, preferred_element_type=f32).reshape(BLOCKS, 6, D)

    arrived = to_owner(tokens)
    cond_rows = after(cond_rows, *arrived)
    tab_one, tab_two = table(mod_first), table(mod_second)

    block_of, inside = kept // SPAN, kept % SPAN
    spot = (
        jnp.where(inside // (SPAN // 2) == core, 0, GROUP // 2)
        + block_of * (SPAN // 2)
        + inside % (SPAN // 2)
    ).reshape(BLOCKS, 2, KEEP // (2 * BLOCKS))
    spot_own = lax.dynamic_slice_in_dim(spot, core, 1, 1).reshape(-1)
    spot_oth = lax.dynamic_slice_in_dim(spot, 1 - core, 1, 1).reshape(-1)
    spot_all = jnp.concatenate([spot_own, spot_oth])

    piece = D // n_dp
    row = jnp.arange(D, dtype=jnp.int32)
    turned = jnp.zeros_like(row)
    for bit in range(bits):
        turned = turned + (((row // piece) // 2 ** (bits - 1 - bit)) % 2) * 2**bit
    source = jnp.bitwise_xor(turned, dp_pos) * piece + row % piece
    order = (source[:, None] == row[None, :]).astype(bf16)
    pieces = min(n_dp, 16)
    deep = D // pieces
    which = dp_pos % pieces
    at = which * deep
    proj_piece = lax.dynamic_slice(
        proj_second, (at % HALF, at // HALF * HALF), (deep, HALF)
    )
    up_piece = lax.dynamic_slice_in_dim(up_second, at, deep).reshape(deep, 4, HALF)
    down_pieces = [
        lax.dynamic_slice_in_dim(down_second, row * D + at, deep).reshape(deep, 2, HALF)
        for row in range(2)
    ]
    pieces_two = jnp.concatenate(
        [
            lax.dynamic_slice_in_dim(wq_two, at, deep, 1),
            proj_piece[None],
            jnp.transpose(up_piece, (1, 0, 2)),
        ]
        + [down_pieces[row][None, :, column] for column in range(2) for row in range(2)]
    )
    w_one_parts = Far(near_part, 1, arrived)
    own = owned(*arrived, tab_one, tab_two, w_one_parts.first, order)
    piece_two = send(after(pieces_two, own), across)
    oth = send(own, core_swap)

    def add(*terms):
        return functools.reduce(lambda p, q: p + q, [t.astype(f32) for t in terms])

    quarter = HALF // 2

    class Total:
        def cores(self, keep, away):
            got = send(away, core_swap)
            self.keep_n, self.keep_r, self.got_n, self.got_r = keep[0], keep[1], got[0], got[1]
            return self

        def cores_far(self, keep, away):
            self.keep_r, self.got_r = keep, send(away, core_swap)
            return self

        def cores_near(self, keep, away):
            self.keep_n, self.got_n = keep, send(away, core_swap)
            return self

        def far(self, *when):
            away = add(self.keep_r, after(self.got_r, *when)).astype(bf16)
            self.got = send(away, across)
            return (away,)

        def chips(self, *when):
            return add(self.keep_n, self.got_n, after(self.got, *when)).astype(bf16)

        def near(self, *when):
            terms = (self.keep_n, self.got_n, after(self.got, *when))
            away = add(*[t[quarter:] for t in terms]).astype(bf16)
            self.got = send(away, next_swap)
            self.terms = tuple(t[:quarter] for t in terms)
            return (away,)

        def sum(self, *when):
            return add(*self.terms, after(self.got, *when))

    class Rest:
        def __init__(self, acc, bit=2):
            self.acc, self.got, self.bit = acc, None, bit

        def next(self, *when):
            if self.bit == bits:
                return ()
            acc = self.acc
            if self.got is not None:
                acc = acc + after(self.got, *when).astype(f32)
            self.acc = acc
            size = self.acc.shape[0] // 2
            away = self.acc[size:].astype(bf16)
            bit = self.bit
            self.got = send(away, moves(lambda dp, t: (dp ^ 2**bit, t)))
            self.acc = self.acc[:size]
            self.bit = bit + 1
            return (away,)

        def sum(self, *when):
            return self.acc + after(self.got, *when).astype(f32)

        def end(self, *when):
            while self.bit < bits:
                self.next(*when)
            return self.acc + after(self.got, *when).astype(f32)

    normed_one, *near_one = project_first(own, oth, tab_one, wq_one)
    ups_one = Far(part_of(up_first, 1, 1), 1, (normed_one,))
    downs_one = Far(part_of(down_first, 0, 2), 2, (normed_one,))
    w_one_parts.hop(own)
    mixed_one_n = attend(kind, *near_one)
    w_parts = w_one_parts.end(normed_one)
    w_two_far = lax.all_gather(
        after(piece_two, normed_one)[None],
        "dp",
        axis=0,
        tiled=True,
        axis_index_groups=[
            list(range(first, first + pieces)) for first in range(0, n_dp, pieces)
        ],
    )
    far_two_mlp = ([w_two_far] * 4, [w_two_far] * 4)
    w_one_far, *far_one = project_parts(
        place_ref, normed_one, w_parts, deps=(mixed_one_n, ups_one.first, downs_one.first)
    )
    ups_one.hop(w_one_far)
    downs_one.hop(w_one_far)
    mixed_one_r = attend(kind, *far_one)
    attn_one, middle_one, normed_mlp_one, u_one_n, act_one_n, acc = feed_near(
        mixed_one_n, mixed_one_r, proj_first, w_one_far, own, tab_one, up_first, down_first
    )
    ups_one, downs_one = ups_one.end(normed_mlp_one), downs_one.end(normed_mlp_one)
    mlp_one = (up_first, down_first, ups_one, downs_one)
    cot_parts = to_owner(after(cotangent, normed_mlp_one))
    u_one_r, act_one_r, mlp_out_one, out_one = feed_far(
        place_ref, normed_mlp_one, acc, middle_one, tab_one, ups_one, downs_one
    )
    first_own = out_one.reshape(-1, D)
    first_oth = send(first_own, core_swap)

    routed = pick(spot_all[:, None], first_own, first_oth)
    routed_own, routed_oth = routed.reshape(2, BLOCKS, KEEP // (2 * BLOCKS), D)
    normed_two, *near_two = project_first(routed_own, routed_oth, tab_two, wq_two)
    mixed_two_n = attend(kind, *near_two)
    far_two = project_next(normed_two, w_two_far, deps=(mixed_two_n,))
    mixed_two_r = attend(kind, *far_two)
    cot_own = owned(*cot_parts, mixed_two_r)
    cot_oth = send(cot_own, core_swap)
    attn_two, middle_two, normed_mlp_two, u_two_n, act_two_n, acc = feed_near(
        mixed_two_n, mixed_two_r, proj_second, w_two_far, routed_own, tab_two, up_second,
        down_second,
    )
    first_out = from_owner(out_one, (mixed_two_r,), (normed_mlp_two,))
    mlp_two = (up_second, down_second, *far_two_mlp)
    u_two_r, act_two_r, mlp_out_two, out_two = feed_far(
        zero_ref, normed_mlp_two, acc, middle_two, tab_two, *mlp_two[2:], deps=(first_out,)
    )
    second_own = out_two.reshape(-1, D)
    second_oth = send(second_own, core_swap)
    cot_routed = pick(
        spot_own[:, None], cot_own.reshape(-1, D), cot_oth.reshape(-1, D), deps=(second_own,)
    ).reshape(routed_own.shape)

    g_keep, g_send, d_mlp, d_gate_two = down_back(
        zero_ref, cot_routed, tab_two, mlp_out_two, order, act_two_n, act_two_r
    )
    down_two = Total().cores(g_keep, g_send)
    saved = (attn_two, middle_two, normed_mlp_two, u_two_n, u_two_r)
    g_keep, g_send, p_keep, p_send, d_middle, d_mix_n, d_mix_r, d_mod_two = up_back(
        zero_ref, cot_routed, tab_two, d_mlp, saved, mlp_two, proj_second, w_two_far, mixed_two_n,
        mixed_two_r, order,
    )
    up_two = Total().cores(g_keep, g_send)
    sent = down_two.far(d_mix_r)
    grads_r = attend_back(kind, *far_two, d_mix_r, deps=sent)
    sent = up_two.far(grads_r[0])
    qr_keep, qr_send, normed_t, acc = qkv_back(
        True, 1, grads_r, w_two_far, normed_two, order, None, None, p_keep, p_send, deps=sent
    )
    qkv_two = Total().cores_far(qr_keep, qr_send)
    grads_n = attend_back(kind, *near_two, d_mix_n, deps=(acc, down_two.got))
    sent = qkv_two.far(grads_n[0])
    qn_keep, qn_send, d_own, d_oth = qkv_back(
        False, 0, grads_n, wq_two, normed_two, None, normed_t, acc, p_keep, p_send, deps=sent
    )
    d_got = send(d_oth, core_swap)
    qkv_two.cores_near(qn_keep, qn_send)
    d_two, d_mod_two_a = finish(
        d_own, d_got, routed_own, tab_two, d_middle
    )
    d_two_own = d_two.reshape(-1, D)
    d_two_oth = send(d_two_own, core_swap)

    def slot_sums(*parts):
        per_block = jnp.concatenate(parts, axis=1).reshape(BLOCKS, -1)
        return lax.dot_general(
            slot_hot.astype(f32),
            per_block,
            (((0,), (0,)), ((), ())),
            precision=lax.Precision.HIGHEST,
        ).astype(bf16)

    routed_rows = put(
        spot_own[None], spot_oth[None], second_own, second_oth, first_own, deps=(d_two_own,)
    )
    d_first = put(
        spot_own[None], spot_oth[None], d_two_own, d_two_oth, cot_own.reshape(-1, D),
        deps=(routed_rows,),
    ).reshape(own.shape)
    g_keep, g_send, d_mlp, d_gate = down_back(
        place_ref, d_first, tab_one, mlp_out_one, order, act_one_n, act_one_r, deps=(up_two.got,)
    )
    down_one = Total().cores(g_keep, g_send)
    mlp_rest_two = Rest(jnp.concatenate([t.chips(d_mlp) for t in (down_two, up_two)], axis=1), 1)
    sent = mlp_rest_two.next()
    saved = (attn_one, middle_one, normed_mlp_one, u_one_n, u_one_r)
    g_keep, g_send, p_keep, p_send, d_middle, d_mix_n, d_mix_r, d_mod = up_back(
        place_ref, d_first, tab_one, d_mlp, saved, mlp_one, proj_first, w_one_far, mixed_one_n,
        mixed_one_r, order, deps=sent,
    )
    up_one = Total().cores(g_keep, g_send)
    qkv_rest_two = Rest(qkv_two.chips(d_mix_r), 1)
    sent = (*down_one.far(d_mix_r), *qkv_rest_two.next())
    early = lax.all_gather(
        jnp.concatenate(
            [cond, slot_sums(d_mod_two_a, d_mod_two, d_gate_two), slot_sums(d_mod, d_gate)], axis=1
        ),
        ALL,
        axis=0,
        tiled=True,
    )
    grads_r = attend_back(kind, *far_one, d_mix_r, deps=sent)
    rest_two = Rest(
        jnp.concatenate([t.sum(grads_r[0]) for t in (mlp_rest_two, qkv_rest_two)], axis=1)
    )
    sent = (*up_one.far(grads_r[0]), *rest_two.next())
    qr_keep, qr_send, normed_t, acc = qkv_back(
        True, 1, grads_r, w_one_far, normed_one, order, None, None, p_keep, p_send,
        deps=sent,
    )
    qkv_one = Total().cores_far(qr_keep, qr_send)
    sent = down_one.near(acc)
    grads_n = attend_back(kind, *near_one, d_mix_n, deps=sent)
    done = grads_n[0]
    sent = (*qkv_one.far(done), *up_one.near(done), *rest_two.next(done))
    qn_keep, qn_send, d_own, d_oth = qkv_back(
        False, 0, grads_n, wq_one, normed_one, None, normed_t, acc, p_keep, p_send, deps=sent
    )
    d_got = send(d_oth, core_swap)
    qkv_one.cores_near(qn_keep, qn_send)
    routed_out = from_owner(routed_rows, (grads_r[0],), (d_own,))
    mlp_rest = Rest(jnp.concatenate([down_one.sum(d_own), up_one.sum(d_own)], axis=1))
    sent = (*mlp_rest.next(), routed_out)
    d_one, d_mod_a = finish(d_own, d_got, own, tab_one, d_middle, deps=(*sent, qkv_one.got_n))

    last = qkv_one.near(d_one)
    late = after(jnp.pad(slot_sums(d_mod_a), ((0, 8 - SLOTS), (0, 0))), *last)
    late = (late.astype(f32) + send(late, core_swap).astype(f32)).astype(bf16)[None]
    sources = jnp.array([dp_pos * 2 + side])

    def doubled(late, sources, mask):
        pairs = moves(lambda dp, t: ((dp * 2 + t ^ mask) // 2, (t ^ mask) % 2))
        late = jnp.concatenate([late, send(late, pairs)])
        return late, jnp.concatenate([sources, jnp.bitwise_xor(sources, mask)])

    late, sources = doubled(late, sources, 1)
    qkv_rest = Rest(qkv_one.sum(late))
    last = qkv_rest.next()
    mlp_rest.next(*last)
    for bit in range(2, bits):
        late, sources = doubled(after(late, *last), sources, 2**bit)
        last = qkv_rest.next(late) or last
    late, sources = doubled(after(late, *last), sources, 2**bits)
    input_grad = from_owner(d_one, (), last).astype(f32)
    early = after(early, *last)
    mlp_total = mlp_rest.end(*last)
    total_two = rest_two.end(*last)
    qkv_total = qkv_rest.end(late)

    mod_rows = D // (n_dp * 2)
    mine = lax.dynamic_slice_in_dim(early[:, :D], (dp_pos * 2 + side) * mod_rows, mod_rows, 1)
    mine_late = jnp.pad(
        mine.reshape(-1, SLOTS, mod_rows)[sources], ((0, 0), (0, 8 - SLOTS), (0, 0))
    ).reshape(-1, mod_rows)
    mod_two_end = 7 * D
    mod_one = jnp.concatenate(
        [
            dot_rows(mine_late, late.reshape(-1, 2 * D)),
            dot_rows(mine, early[:, mod_two_end:]),
        ],
        axis=1,
    )
    mod_two = dot_rows(mine, early[:, D:mod_two_end])
    wide = 2 * TILE

    def placed(attention, down, up):
        qkv = attention[:, : 3 * HALF].reshape(piece, 3, HALF)
        return qkv, attention[:, 3 * HALF :].T, up, down.T

    return (
        first_out,
        routed_out,
        input_grad,
        mod_one,
        *placed(qkv_total, mlp_total[:, :wide], mlp_total[:, wide:]),
        mod_two,
        *placed(
            total_two[:, 2 * wide :].astype(f32),
            total_two[:, :wide].astype(f32),
            total_two[:, wide : 2 * wide].astype(f32),
        ),
    )


def solution(mesh):
    n_dp = mesh.shape["dp"]
    return jax.shard_map(
        functools.partial(on_device, n_dp),
        mesh=mesh,
        in_specs=(
            P(("dp", "tensor"), None),
            P("dp", None),
            P("dp"),
            P("dp"),
            P(("dp", "tensor"), None),
            P(),
            P(None, None, "tensor"),
            P("tensor", None),
            P(None, "tensor"),
            P("tensor", None),
            P(),
            P(None, None, "tensor"),
            P("tensor", None),
            P(None, "tensor"),
            P("tensor", None),
        ),
        out_specs=(
            P(("dp", "tensor"), None),
            P(("dp", "tensor"), None),
            P(("dp", "tensor"), None),
            P(("dp", "tensor"), None),
            P("dp", None, "tensor"),
            P("tensor", "dp"),
            P("dp", "tensor"),
            P("tensor", "dp"),
            P(("dp", "tensor"), None),
            P("dp", None, "tensor"),
            P("tensor", "dp"),
            P("dp", "tensor"),
            P("tensor", "dp"),
        ),
        check_vma=False,
    )
```

time: 797 us -> 542 us (0.68)
  waiting for transfers between devices: 217 us -> 90 us
  blocking collectives: 69.6 us -> 0 us
  Pallas kernels: 239 us -> 189 us
  starting transfers between devices: 120 us -> 72 us
  local copies, waits for them, and re-layouts: 64.9 us -> 109 us
    ppermute x62, waiting for transfers between devices: 217 us -> 89.9 us  [send(): return lax.ppermute(value, ALL, pairs)]
    all_gather x1 -> x0, blocking collectives: 69.6 us -> none  [on_device(): cond_every = lax.all_gather(cond, ALL, axis=0, tiled=True)]
    pallas_call x24 -> x30, Pallas kernels: 239 us -> 189 us  [run(): pl.pallas_call(step, grid_spec=pltpu.PrefetchScalarGridSpec(num_scalar_pr...]
    unnamed x115 -> x378, local copies, waits for them, and re-layouts: 22.9 us -> 71.1 us
    ppermute x62, starting transfers between devices: 119 us -> 71.4 us  [send(): return lax.ppermute(value, ALL, pairs)]
    dynamic_slice x15 -> x13, local copies, waits for them, and re-layouts: 17.4 us -> 8.68 us  [the longest x3 2.57 us: from_owner(): lax.dynamic_slice_in_dim(rows, 3 * (1 - core), 2)]
    convert_element_type x7 -> x13, other arithmetic: 11.1 us -> 19.7 us  [the longest x3 7.07 us: chips(): return add(self.keep_n, self.got_n, after(self.got, *when)).astype(bf16)]
    select_n x5, other arithmetic: 11.3 us -> 3.16 us  [the longest x2 2.83 us: owned(): jnp.where(core == 0, jnp.concatenate([even, odd]), jnp.concatenate([odd,...]
  transfers between devices with their start and end apart: 67 -> 64, of which waited for: 21 -> 16; matrix products, arithmetic and copies ran while one was open for 14% -> 16% of each run, Pallas kernels for 23% -> 34%
where the time goes in v2:
time: 542 us; the launch traced here: 533 us
  Pallas kernels  189 us (35%)
  local copies, waits for them, and re-layouts  109 us (20%)
  waiting for transfers between devices  90 us (17%)
  starting transfers between devices  72 us (13%)
  other arithmetic  39.5 us (7%)
  between operations  19.6 us (4%)
  matrix products  13.6 us (3%)
    pallas_call x30, Pallas kernels, run(): pl.pallas_call(step, grid_spec=pltpu.PrefetchScalarGridSpec(num_scalar_pr...  189 us
    ppermute x62, waiting for transfers between devices, send(): return lax.ppermute(value, ALL, pairs)  89.9 us
    ppermute x62, starting transfers between devices, send(): return lax.ppermute(value, ALL, pairs)  71.4 us
    unnamed x378, local copies, waits for them, and re-layouts  71.1 us
  transfers between devices with their start and end apart: 64, of which 16 were waited for; matrix products, arithmetic and copies ran while one was open for 16% of the time, Pallas kernels for 34%

profile of v2, /device:TPU:0, one launch (start us, length us, event | category | flops | bytes accessed | tf_op | source)
XLA Modules:
  0.0 533.4 jit_solution(15171838032380910718)
XLA Ops:
  10.1 4.3 collective-permute-start.3
  25.3 3.1 collective-permute-start.4
  28.3 4.0 fusion.65
  33.1 4.1 fusion.66
  37.2 4.3 collective-permute-done.4.refs_2_
  45.9 1.9 collective-permute-start.18
  52.4 4.0 shard_map.246
  64.3 1.8 collective-permute-start.9
  66.1 15.3 %collective-permute-done.7.refs_4_ = bf16[4,192,384]{2,1,0:T(8,128)(2,1)} collective-permute-done((bf16[4,192,384]{2,1,0:T(8,128)(2,1)}, bf16[4,192,384]{2,1,0:T(8,128)(2,1)}, u32[]{:S(2)}, u32[]{:S(2)}) %collective-permute-start.7) | collective-permute-done | bytes 589856 | tf_op jit(solution)/shard_map/ppermute | solution.py:837
  85.6 7.4 %shard_map.247.refs_6_.refs_0_.refs_21_ = bf16[5,128,384]{2,1,0:T(8,128)(2,1)S(1)} custom-call(s32[1]{0:T(128)S(6)} %select_n.250.refs_0_, bf16[5,128,384]{2,1,0:T(8,128)(2,1)S(1)} %copy-done.113, bf16[2,5,128,384]{3,2,1,0:T(8,128)(2,1)S(1)} %copy-done.52, bf16[2,5,128,384]{3,2,1,0:T(8,128)(2,1)S(1)} %copy-done.55), custom_call_target="tpu_custom_call" | custom-call | flops 2013266 | bytes 1475 | tf_op jit(solution)/shard_map/pallas_call | solution.py:78
  93.1 4.9 shard_map.248
  99.2 2.0 collective-permute-start.12
  101.7 7.4 %shard_map.249.refs_1_.refs_22_ = bf16[5,128,384]{2,1,0:T(8,128)(2,1)S(1)} custom-call(s32[1]{0:T(128)S(6)} %select_n.250.refs_0_, bf16[5,128,384]{2,1,0:T(8,128)(2,1)S(1)} %get-tuple-element.169.refs_1_, bf16[2,5,128,384]{3,2,1,0:T(8,128)(2,1)S(1)} %get-tuple-element.170.refs_2_, bf16[2,5,128,384]{3,2,1,0:T(8,128)(2,1)S(1)} %get-tuple-element.171.refs_3_), custom_call_target="tpu_custom_call" | custom-call | flops 2013266 | bytes 1475 | tf_op jit(solution)/shard_map/pallas_call | solution.py:78
  111.1 6.1 %shard_map.250 = (bf16[5,128,768]{2,1,0:T(8,128)(2,1)S(1)}, f32[5,128,768]{2,1,0:T(8,128)S(1)}, bf16[5,128,768]{2,1,0:T(8,128)(2,1)S(1)}, bf16[2,640,768]{2,1,0:...) custom-call(bf16[5,128,384]{2,1,0:T(8,128)(2,1)S(1)} %shard_map.247.refs_6_.refs_0_.refs_21_, ...), custom_call_target="tpu_custom_call" | custom-call | flops 1887437 | bytes 9779 | tf_op jit(solution)/shard_map/pallas_call | solution.py:78
  119.9 8.2 %collective-permute-done.15.refs_11_.refs_15_ = bf16[384,768]{1,0:T(8,128)(2,1)S(1)} collective-permute-done((bf16[384,768]{1,0:T(8,128)(2,1)S(1)}, bf16[384,768]{1,0:T(8,128)(2,1)S(1)}, u32[]{:S(2)}, u32[]{:S(2)}) %collective-permute-start.15) | collective-permute-done | bytes 589856 | tf_op jit(solution)/shard_map/ppermute | solution.py:837
  128.7 1.9 collective-permute-done.16.refs_12_.refs_16_
  131.4 5.6 %shard_map.251 = (bf16[2,640,768]{2,1,0:T(8,128)(2,1)S(1)}, bf16[2,640,768]{2,1,0:T(8,128)(2,1)S(1)}, bf16[5,128,768]{2,1,0:T(8,128)(2,1)S(1)}, bf16[5,128,768]{2,1,0:T(8,128)(2,1)S(1)}) custom-call(s32[1]{0:T(128)} %bitcast.refs_0_, bf16[5,128,768]{2,1,0:T(8,128)(2,1)S(1)} %get-tuple-element.173.refs_1_.refs_4_, f32[640,768]{1,0:T(8,128)S(1)} %get-tuple-element.174.refs_2_, ...), custom_call_target="tpu_custom_call" | custom-call | flops 1509950 | bytes 7813 | tf_op jit(solution)/shard_map/pallas_call | solution.py:78
  141.0 2.0 slice.277
  144.8 5.9 %collective-permute-start.22 = (bf16[3,128,768]{2,1,0:T(8,128)(2,1)}, bf16[3,128,768]{2,1,0:T(8,128)(2,1)}, u32[]{:S(2)}, u32[]{:S(2)}) collective-permute-start(bf16[3,128,768]{2,1,0:T(8,128)(2,1)} %slice.277), channel_id=1, source_target_pairs={{0,0},{1,2},{2,1},{3,3},{4,4},{5,6},{6,5},{7,7},{8,8},{9,10},{10,9... | collective-permute-start | bytes 1769480 | tf_op jit(solution)/shard_map/ppermute | solution.py:837
  154.6 2.6 shard_map.253
  157.3 3.3 shard_map.254.refs_2_.refs_0_.refs_21_
  162.9 3.1 copy-done
  166.0 2.0 shard_map.255
  168.1 3.3 shard_map.256.refs_1_.refs_22_
  171.4 2.7 maximum_select_fusion.1
  176.5 6.0 %collective-permute-start.20 = (bf16[3,128,768]{2,1,0:T(8,128)(2,1)}, bf16[3,128,768]{2,1,0:T(8,128)(2,1)}, u32[]{:S(2)}, u32[]{:S(2)}) collective-permute-start(bf16[3,128,768]{2,1,0:T(8,128)(2,1)} %constant_dynamic-slice_fusion.5), channel_id=1, source_target_pairs={{0,0},{1,2},{2,1},{3,3},{4,4},{5,6},{6,5},{7,7},{8,8},{9,10},{10,9... | collective-permute-start | bytes 1769480 | tf_op jit(solution)/shard_map/ppermute | solution.py:837
  185.2 3.0 copy-done.1
  194.5 3.6 shard_map.257
  200.6 4.3 shard_map.258
  205.0 2.7 shard_map.259
  207.7 4.9 shard_map.260
  213.2 15.5 %shard_map.261 = (bf16[2,384,1536]{2,1,0:T(8,128)(2,1)S(1)}, bf16[2,384,1536]{2,1,0:T(8,128)(2,1)S(1)}, bf16[2,384,384]{2,1,0:T(8,128)(2,1)S(1)}, bf16[2,384,384...) custom-call(s32[1]{0:T(128)} %constant.225.clone.1.refs_0_, ...), custom_call_target="tpu_custom_call" | custom-call | flops 3019899 | bytes 41554 | tf_op jit(solution)/shard_map/pallas_call | solution.py:78
  236.0 5.9 %shard_map.262 = (bf16[5,64,384]{2,1,0:T(8,128)(2,1)S(1)}, bf16[2,5,64,384]{3,2,1,0:T(8,128)(2,1)S(1)}, bf16[2,5,64,384]{3,2,1,0:T(8,128)(2,1)S(1)}) custom-call(s32[1]{0:T(128)S(6)} %select_n.250.refs_0_, bf16[5,64,384]{2,1,0:T(8,128)(2,1)S(1)} %copy-done.139, bf16[2,5,64,384]{3,2,1,0:T(8,128)(2,1)S(1)} %copy-done.120, ...), custom_call_target="tpu_custom_call" | custom-call | flops 1258292 | bytes 1352 | tf_op jit(solution)/shard_map/pallas_call | solution.py:78
  244.5 5.6 %shard_map.263 = (bf16[384,1536]{1,0:T(8,128)(2,1)S(1)}, bf16[384,1536]{1,0:T(8,128)(2,1)}, bf16[768,640]{1,0:T(8,128)(2,1)S(1)}, f32[640,768]{1,0:T(8,128)S(1)}) custom-call(bf16[5,64,384]{2,1,0:T(8,128)(2,1)S(1)} %get-tuple-element.212.refs_0_, bf16[2,5,64,384]{3,2,1,0:T(8,128)(2,1)S(1)} %get-tuple-element.213.refs_1_, ...), custom_call_target="tpu_custom_call" | custom-call | flops 1321206 | bytes 8479 | tf_op jit(solution)/shard_map/pallas_call | solution.py:78
  253.1 10.3 %collective-permute-done.27.refs_6_ = bf16[384,1536]{1,0:T(8,128)(2,1)} collective-permute-done((bf16[384,1536]{1,0:T(8,128)(2,1)}, bf16[384,1536]{1,0:T(8,128)(2,1)}, u32[]{:S(2)}, u32[]{:S(2)}) %collective-permute-start.27) | collective-permute-done | bytes 1179680 | tf_op jit(solution)/shard_map/ppermute | solution.py:837
  267.4 5.7 %shard_map.264 = (bf16[5,64,384]{2,1,0:T(8,128)(2,1)S(1)}, bf16[2,5,64,384]{3,2,1,0:T(8,128)(2,1)S(1)}, bf16[2,5,64,384]{3,2,1,0:T(8,128)(2,1)S(1)}) custom-call(s32[1]{0:T(128)S(6)} %select_n.250.refs_0_, bf16[5,64,384]{2,1,0:T(8,128)(2,1)S(1)} %copy-done.137, bf16[2,5,64,384]{3,2,1,0:T(8,128)(2,1)S(1)} %copy-done.116, ...), custom_call_target="tpu_custom_call" | custom-call | flops 1258292 | bytes 1352 | tf_op jit(solution)/shard_map/pallas_call | solution.py:78
  275.3 5.1 shard_map.265
  294.0 2.5 shard_map.267.refs_5_
  297.8 2.9 shard_map.268
  300.8 7.4 %shard_map.269 = (bf16[2,384,1536]{2,1,0:T(8,128)(2,1)S(1)}, bf16[2,384,1536]{2,1,0:T(8,128)(2,1)}, bf16[640,768]{1,0:T(8,128)(2,1)S(1)}, f32[5,1,768]{2,1,0:T(1,128)S(1)}) custom-call(s32[1]{0:T(128)} %bitcast.refs_0_, bf16[5,128,768]{2,1,0:T(8,128)(2,1)S(1)} %bitcast.168, f32[5,6,768]{2,1,0:T(8,128)S(1)} %copy-done.33, ...), custom_call_target="tpu_custom_call" | custom-call | flops 1887437 | bytes 6444 | tf_op jit(solution)/shard_map/pallas_call | solution.py:78
  308.7 2.8 fusion.4
  311.5 2.2 fusion.5
  313.9 7.7 %collective-permute-start.38 = (bf16[192,3072]{1,0:T(8,128)(2,1)S(1)}, bf16[192,3072]{1,0:T(8,128)(2,1)}, u32[]{:S(2)}, u32[]{:S(2)}) collective-permute-start(bf16[192,3072]{1,0:T(8,128)(2,1)S(1)} %fusion.14.refs_24_), channel_id=1, source_target_pairs={{0,4},{1,5},{2,6},{3,7},{4,0},{5,1},{6,2},{7,3},{8,12},{9,13},{10,... | collective-permute-start | bytes 3538952 | tf_op jit(solution)/shard_map/ppermute | solution.py:837
  323.3 24.1 %shard_map.270 = (bf16[2,384,1536]{2,1,0:T(8,128)(2,1)}, bf16[2,384,1536]{2,1,0:T(8,128)(2,1)}, bf16[2,384,384]{2,1,0:T(8,128)(2,1)S(1)}, bf16[2,384,384]{2,1,0:...) custom-call(s32[1]{0:T(128)} %bitcast.refs_0_, ...), custom_call_target="tpu_custom_call" | custom-call | flops 6039798 | bytes 16683 | tf_op jit(solution)/shard_map/pallas_call | solution.py:78
  348.7 2.1 add_convert_fusion.1
  356.7 16.6 %shard_map.271 = (bf16[5,128,384]{2,1,0:T(8,128)(2,1)S(1)}, bf16[2,5,128,384]{3,2,1,0:T(8,128)(2,1)S(1)}, bf16[2,5,128,384]{3,2,1,0:T(8,128)(2,1)S(1)}) custom-call(s32[1]{0:T(128)S(6)} %select_n.250.refs_0_, bf16[5,128,384]{2,1,0:T(8,128)(2,1)S(1)} %copy-done.103, bf16[2,5,128,384]{3,2,1,0:T(8,128)(2,1)S(1)} %copy-done.48, ...), custom_call_target="tpu_custom_call" | custom-call | flops 5033165 | bytes 2704 | tf_op jit(solution)/shard_map/pallas_call | solution.py:78
  375.4 2.0 convert_add_fusion.4
  390.9 7.7 %shard_map.272 = (bf16[384,1536]{1,0:T(8,128)(2,1)S(1)}, bf16[384,1536]{1,0:T(8,128)(2,1)S(1)}, bf16[768,1280]{1,0:T(8,128)(2,1)S(1)}, f32[1280,768]{1,0:T(8,128)S(1)}) custom-call(bf16[5,128,384]{2,1,0:T(8,128)(2,1)S(1)} %copy-done.150, bf16[2,5,128,384]{3,2,1,0:T(8,128)(2,1)S(1)} %copy-done.143, bf16[2,5,128,384]{3,2,1,0:T(8,128)(2,1)S(1)} %copy-done.145, ...), custom_call_target="tpu_custom_call" | custom-call | flops 2642412 | bytes 8700 | tf_op jit(solution)/shard_map/pallas_call | solution.py:78
  402.9 16.7 %shard_map.273 = (bf16[5,128,384]{2,1,0:T(8,128)(2,1)S(1)}, bf16[2,5,128,384]{3,2,1,0:T(8,128)(2,1)S(1)}, bf16[2,5,128,384]{3,2,1,0:T(8,128)(2,1)S(1)}) custom-call(s32[1]{0:T(128)S(6)} %select_n.250.refs_0_, bf16[5,128,384]{2,1,0:T(8,128)(2,1)S(1)} %copy-done.114, bf16[2,5,128,384]{3,2,1,0:T(8,128)(2,1)S(1)} %copy-done.53, ...), custom_call_target="tpu_custom_call" | custom-call | flops 5033165 | bytes 2704 | tf_op jit(solution)/shard_map/pallas_call | solution.py:78
  421.1 2.3 fusion.18.refs_9_
  423.4 2.1 collective-permute-start.46
  425.8 2.0 collective-permute-start.49
  427.8 6.6 %shard_map.274 = (bf16[384,1536]{1,0:T(8,128)(2,1)S(1)}, bf16[384,1536]{1,0:T(8,128)(2,1)S(1)}, f32[640,768]{1,0:T(8,128)S(1)}, bf16[640,768]{1,0:T(8,128)(2,1)S(1)}) custom-call(bf16[5,128,384]{2,1,0:T(8,128)(2,1)S(1)} %get-tuple-element.262.refs_0_, bf16[2,5,128,384]{3,2,1,0:T(8,128)(2,1)S(1)} %get-tuple-element.263.refs_1_, ...), custom_call_target="tpu_custom_call" | custom-call | flops 1887437 | bytes 8307 | tf_op jit(solution)/shard_map/pallas_call | solution.py:78
  434.5 2.7 collective-permute-start.61
  437.7 17.8 %collective-permute-done.46 = bf16[192,1536]{1,0:T(8,128)(2,1)S(1)} collective-permute-done((bf16[192,1536]{1,0:T(8,128)(2,1)S(1)}, bf16[192,1536]{1,0:T(8,128)(2,1)S(1)}, u32[]{:S(2)}, u32[]{:S(2)}) %collective-permute-start.46) | collective-permute-done | bytes 589856 | tf_op jit(solution)/shard_map/ppermute | solution.py:837
  458.2 2.0 fusion.17
  472.7 4.9 reshape.653
  477.6 3.7 collective-permute-done.50
  485.7 2.5 collective-permute-done.54
  488.2 2.6 collective-permute-start.60
  490.8 3.5 collective-permute-done.53
  496.3 5.7 %collective-permute-done.60 = bf16[48,3072]{1,0:T(8,128)(2,1)S(1)} collective-permute-done((bf16[48,3072]{1,0:T(8,128)(2,1)S(1)}, bf16[48,3072]{1,0:T(8,128)(2,1)S(1)}, u32[]{:S(2)}, u32[]{:S(2)}) %collective-permute-start.60) | collective-permute-done | bytes 294944 | tf_op jit(solution)/shard_map/ppermute | solution.py:837
  506.9 3.3 collective-permute-start.58
  511.7 12.2 %collective-permute-done.57 = bf16[8,8,1536]{2,1,0:T(8,128)(2,1)S(1)} collective-permute-done((bf16[8,8,1536]{2,1,0:T(8,128)(2,1)S(1)}, bf16[8,8,1536]{2,1,0:T(8,128)(2,1)S(1)}, u32[]{:S(2)}, u32[]{:S(2)}) %collective-permute-start.57) | collective-permute-done | bytes 196640 | tf_op jit(solution)/shard_map/ppermute | solution.py:837
  (615 shorter events, 161.5 us)
Async XLA Ops:
  7.2 155.7 %all-gather.5.cloned.1.call-start = ((), (), s32[]{:S(2)}) async-start(), calls=%async_computation | async-start | bytes 7520256 | tf_op jit(solution)/shard_map/all_gather | solution.py:1015
  8.4 16.9 %collective-permute-start.1 = (bf16[3,128,768]{2,1,0:T(8,128)(2,1)S(1)}, bf16[3,128,768]{2,1,0:T(8,128)(2,1)S(1)}, u32[]{:S(2)}, u32[]{:S(2)}) collective-permute-start(bf16[3,128,768]{2,1,0:T(8,128)(2,1)S(1)} %slice.267), channel_id=1, source_target_pairs={{0,0},{1,2},{2,1},{3,3},{4,4},{5,6},{6,5},{7,7},{8,8},{9,10},{10,9... | collective-permute-start | bytes 1769480 | tf_op jit(solution)/shard_map/ppermute | solution.py:837
  10.1 15.2 %collective-permute-start.3 = (bf16[2,128,768]{2,1,0:T(8,128)(2,1)S(1)}, bf16[2,128,768]{2,1,0:T(8,128)(2,1)S(1)}, u32[]{:S(2)}, u32[]{:S(2)}) collective-permute-start(bf16[2,128,768]{2,1,0:T(8,128)(2,1)S(1)} %slice.269), channel_id=1, source_target_pairs={{0,2},{1,0},{2,3},{3,1},{4,6},{5,4},{6,7},{7,5},{8,10},{9,8},{10,1... | collective-permute-start | bytes 1179656 | tf_op jit(solution)/shard_map/ppermute | solution.py:837
  15.2 7.5 %collective-permute-start = (s32[645]{0:T(1024)S(1)}, s32[645]{0:T(1024)S(1)}, u32[]{:S(2)}, u32[]{:S(2)}) collective-permute-start(s32[645]{0:T(1024)S(1)} %pad_add_fusion), channel_id=1, source_target_pairs={{0,0},{1,2},{2,1},{3,3},{4,4},{5,6},{6,5},{7,7},{8,8},{9,10},{10,9... | collective-permute-start | bytes 7748 | tf_op jit(solution)/shard_map/ppermute | solution.py:837
  15.9 7.4 %collective-permute-start.2 = (bf16[5,768]{1,0:T(8,128)(2,1)S(1)}, bf16[5,768]{1,0:T(8,128)(2,1)S(1)}, u32[]{:S(2)}, u32[]{:S(2)}) collective-permute-start(bf16[5,768]{1,0:T(8,128)(2,1)S(1)} %fusion.27), channel_id=1, source_target_pairs={{0,0},{1,2},{2,1},{3,3},{4,4},{5,6},{6,5},{7,7},{8,8},{9,10},{10,9... | collective-permute-start | bytes 23048 | tf_op jit(solution)/shard_map/ppermute | solution.py:837
  25.3 16.2 %collective-permute-start.4 = (bf16[4,192,384]{2,1,0:T(8,128)(2,1)S(1)}, bf16[4,192,384]{2,1,0:T(8,128)(2,1)}, u32[]{:S(2)}, u32[]{:S(2)}) collective-permute-start(bf16[4,192,384]{2,1,0:T(8,128)(2,1)S(1)} %pad_maximum_fusion.3), channel_id=1, source_target_pairs={{0,1},{1,0},{2,3},{3,2},{4,5},{5,4},{6,7},{7,6},{8,9},{9,8},{10,11... | collective-permute-start | bytes 1769480 | tf_op jit(solution)/shard_map/ppermute | solution.py:837
  41.7 6.2 %collective-permute-start.5 = (bf16[5,128,768]{2,1,0:T(8,128)(2,1)S(1)}, bf16[5,128,768]{2,1,0:T(8,128)(2,1)S(1)}, u32[]{:S(2)}, u32[]{:S(2)}) collective-permute-start(bf16[5,128,768]{2,1,0:T(8,128)(2,1)S(1)} %maximum_select_fusion.refs_0_.refs_4_.refs_2_), channel_id=1, source_target_pairs={{0,2},{1,3},{2,0},{3,1},{4,6},{5,7},{6,4},{7,5},{8,10},{9,11},{10,... | collective-permute-start | bytes 2949128 | tf_op jit(solution)/shard_map/ppermute | solution.py:837
  45.9 14.4 %collective-permute-start.18 = (bf16[12,48,384]{2,1,0:T(8,128)(2,1)S(1)}, bf16[12,48,384]{2,1,0:T(8,128)(2,1)}, u32[]{:S(2)}, u32[]{:S(2)}) collective-permute-start(bf16[12,48,384]{2,1,0:T(8,128)(2,1)S(1)} %copy.63), channel_id=1, source_target_pairs={{0,1},{1,0},{2,3},{3,2},{4,5},{5,4},{6,7},{7,6},{8,9},{9,8},{10,11... | collective-permute-start | bytes 1327112 | tf_op jit(solution)/shard_map/ppermute | solution.py:837
  60.4 412.2 %all-gather.7.cloned.1.call-start = ((), (), s32[]{:S(2)}) async-start(), calls=%async_computation.1 | async-start | bytes 4460544 | tf_op jit(solution)/shard_map/all_gather | solution.py:1126
  61.0 20.4 %collective-permute-start.7 = (bf16[4,192,384]{2,1,0:T(8,128)(2,1)}, bf16[4,192,384]{2,1,0:T(8,128)(2,1)}, u32[]{:S(2)}, u32[]{:S(2)}) collective-permute-start(bf16[4,192,384]{2,1,0:T(8,128)(2,1)} %collective-permute-done.4.refs_2_), channel_id=1, source_target_pairs={{0,4},{1,5},{2,6},{3,7},{4,0},{5,1},{6,2},{7,3},{8,12},{9,13},{10,... | collective-permute-start | bytes 1769480 | tf_op jit(solution)/shard_map/ppermute | solution.py:837
  63.9 29.1 %collective-permute-start.6 = (bf16[4,192,384]{2,1,0:T(8,128)(2,1)}, bf16[4,192,384]{2,1,0:T(8,128)(2,1)S(1)}, u32[]{:S(2)}, u32[]{:S(2)}) collective-permute-start(bf16[4,192,384]{2,1,0:T(8,128)(2,1)} %collective-permute-done.4.refs_2_), channel_id=1, source_target_pairs={{0,2},{1,3},{2,0},{3,1},{4,6},{5,7},{6,4},{7,5},{8,10},{9,11},{10,... | collective-permute-start | bytes 1769480 | tf_op jit(solution)/shard_map/ppermute | solution.py:837
  64.0 29.1 %collective-permute-start.10 = (bf16[384,768]{1,0:T(8,128)(2,1)S(1)}, bf16[384,768]{1,0:T(8,128)(2,1)S(1)}, u32[]{:S(2)}, u32[]{:S(2)}) collective-permute-start(bf16[384,768]{1,0:T(8,128)(2,1)S(1)} %constant_dynamic-slice_fusion.13), channel_id=1, source_target_pairs={{0,1},{1,0},{2,3},{3,2},{4,5},{5,4},{6,7},{7,6},{8,9},{9,8},{10,11... | collective-permute-start | bytes 1769480 | tf_op jit(solution)/shard_map/ppermute | solution.py:837
  64.3 28.8 %collective-permute-start.9 = (bf16[768,384]{1,0:T(8,128)(2,1)S(1)}, bf16[768,384]{1,0:T(8,128)(2,1)S(1)}, u32[]{:S(2)}, u32[]{:S(2)}) collective-permute-start(bf16[768,384]{1,0:T(8,128)(2,1)S(1)} %constant_dynamic-slice_fusion.14), channel_id=1, source_target_pairs={{0,1},{1,0},{2,3},{3,2},{4,5},{5,4},{6,7},{7,6},{8,9},{9,8},{10,11... | collective-permute-start | bytes 1769480 | tf_op jit(solution)/shard_map/ppermute | solution.py:837
  81.4 11.7 %collective-permute-start.8 = (bf16[4,192,384]{2,1,0:T(8,128)(2,1)}, bf16[4,192,384]{2,1,0:T(8,128)(2,1)S(1)}, u32[]{:S(2)}, u32[]{:S(2)}) collective-permute-start(bf16[4,192,384]{2,1,0:T(8,128)(2,1)} %collective-permute-done.7.refs_4_), channel_id=1, source_target_pairs={{0,2},{1,3},{2,0},{3,1},{4,6},{5,7},{6,4},{7,5},{8,10},{9,11},{10,... | collective-permute-start | bytes 1769480 | tf_op jit(solution)/shard_map/ppermute | solution.py:837
  98.0 30.1 %collective-permute-start.15 = (bf16[384,768]{1,0:T(8,128)(2,1)S(1)}, bf16[384,768]{1,0:T(8,128)(2,1)S(1)}, u32[]{:S(2)}, u32[]{:S(2)}) collective-permute-start(bf16[384,768]{1,0:T(8,128)(2,1)S(1)} %collective-permute-done.10.refs_8_.refs_9_.refs_13_), channel_id=1, source_target_pairs={{0,8},{1,9},{2,10},{3,11},{4,12},{5,13},{6,14},{7,15},{8,0},{9,1},... | collective-permute-start | bytes 1769480 | tf_op jit(solution)/shard_map/ppermute | solution.py:837
  99.2 29.0 %collective-permute-start.12 = (bf16[768,384]{1,0:T(8,128)(2,1)S(1)}, bf16[768,384]{1,0:T(8,128)(2,1)S(1)}, u32[]{:S(2)}, u32[]{:S(2)}) collective-permute-start(bf16[768,384]{1,0:T(8,128)(2,1)S(1)} %collective-permute-done.9.refs_7_.refs_5_.refs_9_), channel_id=1, source_target_pairs={{0,4},{1,5},{2,6},{3,7},{4,0},{5,1},{6,2},{7,3},{8,12},{9,13},{10,... | collective-permute-start | bytes 1769480 | tf_op jit(solution)/shard_map/ppermute | solution.py:837
  101.2 27.5 %collective-permute-start.14 = (bf16[384,768]{1,0:T(8,128)(2,1)S(1)}, bf16[384,768]{1,0:T(8,128)(2,1)S(1)}, u32[]{:S(2)}, u32[]{:S(2)}) collective-permute-start(bf16[384,768]{1,0:T(8,128)(2,1)S(1)} %collective-permute-done.10.refs_8_.refs_9_.refs_13_), channel_id=1, source_target_pairs={{0,2},{1,3},{2,0},{3,1},{4,6},{5,7},{6,4},{7,5},{8,10},{9,11},{10,... | collective-permute-start | bytes 1769480 | tf_op jit(solution)/shard_map/ppermute | solution.py:837
  101.2 27.5 %collective-permute-start.11 = (bf16[768,384]{1,0:T(8,128)(2,1)S(1)}, bf16[768,384]{1,0:T(8,128)(2,1)S(1)}, u32[]{:S(2)}, u32[]{:S(2)}) collective-permute-start(bf16[768,384]{1,0:T(8,128)(2,1)S(1)} %collective-permute-done.9.refs_7_.refs_5_.refs_9_), channel_id=1, source_target_pairs={{0,2},{1,3},{2,0},{3,1},{4,6},{5,7},{6,4},{7,5},{8,10},{9,11},{10,... | collective-permute-start | bytes 1769480 | tf_op jit(solution)/shard_map/ppermute | solution.py:837
  128.1 2.4 collective-permute-start.16
  128.2 3.2 collective-permute-start.13
  140.7 10.5 %collective-permute-start.17 = (bf16[640,768]{1,0:T(8,128)(2,1)S(1)}, bf16[640,768]{1,0:T(8,128)(2,1)S(1)}, u32[]{:S(2)}, u32[]{:S(2)}) collective-permute-start(bf16[640,768]{1,0:T(8,128)(2,1)S(1)} %bitcast.163), channel_id=1, source_target_pairs={{0,2},{1,3},{2,0},{3,1},{4,6},{5,7},{6,4},{7,5},{8,10},{9,11},{10,... | collective-permute-start | bytes 2949128 | tf_op jit(solution)/shard_map/ppermute | solution.py:837
  144.8 26.6 %collective-permute-start.22 = (bf16[3,128,768]{2,1,0:T(8,128)(2,1)}, bf16[3,128,768]{2,1,0:T(8,128)(2,1)}, u32[]{:S(2)}, u32[]{:S(2)}) collective-permute-start(bf16[3,128,768]{2,1,0:T(8,128)(2,1)} %slice.277), channel_id=1, source_target_pairs={{0,0},{1,2},{2,1},{3,3},{4,4},{5,6},{6,5},{7,7},{8,8},{9,10},{10,9... | collective-permute-start | bytes 1769480 | tf_op jit(solution)/shard_map/ppermute | solution.py:837
  150.7 20.7 %collective-permute-start.23 = (bf16[2,128,768]{2,1,0:T(8,128)(2,1)}, bf16[2,128,768]{2,1,0:T(8,128)(2,1)}, u32[]{:S(2)}, u32[]{:S(2)}) collective-permute-start(bf16[2,128,768]{2,1,0:T(8,128)(2,1)} %slice.278), channel_id=1, source_target_pairs={{0,2},{1,0},{2,3},{3,1},{4,6},{5,4},{6,7},{7,5},{8,10},{9,8},{10,1... | collective-permute-start | bytes 1179656 | tf_op jit(solution)/shard_map/ppermute | solution.py:837
  174.1 30.9 %collective-permute-start.24 = (bf16[5,128,768]{2,1,0:T(8,128)(2,1)}, bf16[5,128,768]{2,1,0:T(8,128)(2,1)}, u32[]{:S(2)}, u32[]{:S(2)}) collective-permute-start(bf16[5,128,768]{2,1,0:T(8,128)(2,1)} %maximum_select_fusion.1), channel_id=1, source_target_pairs={{0,2},{1,3},{2,0},{3,1},{4,6},{5,7},{6,4},{7,5},{8,10},{9,11},{10,... | collective-permute-start | bytes 2949128 | tf_op jit(solution)/shard_map/ppermute | solution.py:837
  176.5 22.6 %collective-permute-start.20 = (bf16[3,128,768]{2,1,0:T(8,128)(2,1)}, bf16[3,128,768]{2,1,0:T(8,128)(2,1)}, u32[]{:S(2)}, u32[]{:S(2)}) collective-permute-start(bf16[3,128,768]{2,1,0:T(8,128)(2,1)} %constant_dynamic-slice_fusion.5), channel_id=1, source_target_pairs={{0,0},{1,2},{2,1},{3,3},{4,4},{5,6},{6,5},{7,7},{8,8},{9,10},{10,9... | collective-permute-start | bytes 1769480 | tf_op jit(solution)/shard_map/ppermute | solution.py:837
  184.3 13.8 %collective-permute-start.19 = (bf16[2,128,768]{2,1,0:T(8,128)(2,1)}, bf16[2,128,768]{2,1,0:T(8,128)(2,1)}, u32[]{:S(2)}, u32[]{:S(2)}) collective-permute-start(bf16[2,128,768]{2,1,0:T(8,128)(2,1)} %constant_dynamic-slice_fusion.6), channel_id=1, source_target_pairs={{0,1},{1,3},{2,0},{3,2},{4,5},{5,7},{6,4},{7,6},{8,9},{9,11},{10,8... | collective-permute-start | bytes 1179656 | tf_op jit(solution)/shard_map/ppermute | solution.py:837
  212.6 18.7 %collective-permute-start.25 = (bf16[2,384,1536]{2,1,0:T(8,128)(2,1)S(1)}, bf16[2,384,1536]{2,1,0:T(8,128)(2,1)S(1)}, u32[]{:S(2)}, u32[]{:S(2)}) collective-permute-start(bf16[2,384,1536]{2,1,0:T(8,128)(2,1)S(1)} %get-tuple-element.210), channel_id=1, source_target_pairs={{0,2},{1,3},{2,0},{3,1},{4,6},{5,7},{6,4},{7,5},{8,10},{9,11},{10,... | collective-permute-start | bytes 7077896 | tf_op jit(solution)/shard_map/ppermute | solution.py:837
  231.0 11.0 %collective-permute-start.26 = (bf16[2,384,1536]{2,1,0:T(8,128)(2,1)S(1)}, bf16[2,384,1536]{2,1,0:T(8,128)(2,1)S(1)}, u32[]{:S(2)}, u32[]{:S(2)}) collective-permute-start(bf16[2,384,1536]{2,1,0:T(8,128)(2,1)S(1)} %get-tuple-element.218), channel_id=1, source_target_pairs={{0,2},{1,3},{2,0},{3,1},{4,6},{5,7},{6,4},{7,5},{8,10},{9,11},{10,... | collective-permute-start | bytes 7077896 | tf_op jit(solution)/shard_map/ppermute | solution.py:837
  234.3 29.1 %collective-permute-start.27 = (bf16[384,1536]{1,0:T(8,128)(2,1)}, bf16[384,1536]{1,0:T(8,128)(2,1)}, u32[]{:S(2)}, u32[]{:S(2)}) collective-permute-start(bf16[384,1536]{1,0:T(8,128)(2,1)} %fusion.3.refs_5_), channel_id=1, source_target_pairs={{0,1},{1,0},{2,3},{3,2},{4,5},{5,4},{6,7},{7,6},{8,9},{9,8},{10,11... | collective-permute-start | bytes 3538952 | tf_op jit(solution)/shard_map/ppermute | solution.py:837
  252.1 21.0 %collective-permute-start.28 = (bf16[384,1536]{1,0:T(8,128)(2,1)}, bf16[384,1536]{1,0:T(8,128)(2,1)}, u32[]{:S(2)}, u32[]{:S(2)}) collective-permute-start(bf16[384,1536]{1,0:T(8,128)(2,1)} %get-tuple-element.226), channel_id=1, source_target_pairs={{0,2},{1,3},{2,0},{3,1},{4,6},{5,7},{6,4},{7,5},{8,10},{9,11},{10,... | collective-permute-start | bytes 3538952 | tf_op jit(solution)/shard_map/ppermute | solution.py:837
  252.4 48.3 %collective-permute-start.31 = (bf16[384,1536]{1,0:T(8,128)(2,1)}, bf16[384,1536]{1,0:T(8,128)(2,1)}, u32[]{:S(2)}, u32[]{:S(2)}) collective-permute-start(bf16[384,1536]{1,0:T(8,128)(2,1)} %copy-done.39), channel_id=1, source_target_pairs={{0,1},{1,0},{2,3},{3,2},{4,5},{5,4},{6,7},{7,6},{8,9},{9,8},{10,11... | collective-permute-start | bytes 3538952 | tf_op jit(solution)/shard_map/ppermute | solution.py:837
  283.4 2.1 collective-permute-start.29
  283.7 10.3 %collective-permute-start.21 = (bf16[320,768]{1,0:T(8,128)(2,1)}, bf16[320,768]{1,0:T(8,128)(2,1)}, u32[]{:S(2)}, u32[]{:S(2)}) collective-permute-start(bf16[320,768]{1,0:T(8,128)(2,1)} %bitcast.19.refs_3_.refs_2_), channel_id=1, source_target_pairs={{0,2},{1,3},{2,0},{3,1},{4,6},{5,7},{6,4},{7,5},{8,10},{9,11},{10,... | collective-permute-start | bytes 1474568 | tf_op jit(solution)/shard_map/ppermute | solution.py:837
  292.4 5.4 %collective-permute-start.30 = (bf16[320,768]{1,0:T(8,128)(2,1)}, bf16[320,768]{1,0:T(8,128)(2,1)}, u32[]{:S(2)}, u32[]{:S(2)}) collective-permute-start(bf16[320,768]{1,0:T(8,128)(2,1)} %bitcast.28.refs_5_.refs_2_), channel_id=1, source_target_pairs={{0,2},{1,3},{2,0},{3,1},{4,6},{5,7},{6,4},{7,5},{8,10},{9,11},{10,... | collective-permute-start | bytes 1474568 | tf_op jit(solution)/shard_map/ppermute | solution.py:837
  293.3 55.4 %collective-permute-start.34 = (bf16[384,1536]{1,0:T(8,128)(2,1)S(1)}, bf16[384,1536]{1,0:T(8,128)(2,1)}, u32[]{:S(2)}, u32[]{:S(2)}) collective-permute-start(bf16[384,1536]{1,0:T(8,128)(2,1)S(1)} %copy-done.41), channel_id=1, source_target_pairs={{0,1},{1,0},{2,3},{3,2},{4,5},{5,4},{6,7},{7,6},{8,9},{9,8},{10,11... | collective-permute-start | bytes 3538952 | tf_op jit(solution)/shard_map/ppermute | solution.py:837
  293.9 54.8 %collective-permute-start.33 = (bf16[384,1536]{1,0:T(8,128)(2,1)}, bf16[384,1536]{1,0:T(8,128)(2,1)}, u32[]{:S(2)}, u32[]{:S(2)}) collective-permute-start(bf16[384,1536]{1,0:T(8,128)(2,1)} %copy-done.159), channel_id=1, source_target_pairs={{0,2},{1,3},{2,0},{3,1},{4,6},{5,7},{6,4},{7,5},{8,10},{9,11},{10,... | collective-permute-start | bytes 3538952 | tf_op jit(solution)/shard_map/ppermute | solution.py:837
  308.2 44.4 %collective-permute-start.32 = (bf16[2,384,1536]{2,1,0:T(8,128)(2,1)}, bf16[2,384,1536]{2,1,0:T(8,128)(2,1)}, u32[]{:S(2)}, u32[]{:S(2)}) collective-permute-start(bf16[2,384,1536]{2,1,0:T(8,128)(2,1)} %get-tuple-element.243), channel_id=1, source_target_pairs={{0,2},{1,3},{2,0},{3,1},{4,6},{5,7},{6,4},{7,5},{8,10},{9,11},{10,... | collective-permute-start | bytes 7077896 | tf_op jit(solution)/shard_map/ppermute | solution.py:837
  313.9 60.2 %collective-permute-start.38 = (bf16[192,3072]{1,0:T(8,128)(2,1)S(1)}, bf16[192,3072]{1,0:T(8,128)(2,1)}, u32[]{:S(2)}, u32[]{:S(2)}) collective-permute-start(bf16[192,3072]{1,0:T(8,128)(2,1)S(1)} %fusion.14.refs_24_), channel_id=1, source_target_pairs={{0,4},{1,5},{2,6},{3,7},{4,0},{5,1},{6,2},{7,3},{8,12},{9,13},{10,... | collective-permute-start | bytes 3538952 | tf_op jit(solution)/shard_map/ppermute | solution.py:837
  347.5 30.0 %collective-permute-start.37 = (bf16[2,384,1536]{2,1,0:T(8,128)(2,1)}, bf16[2,384,1536]{2,1,0:T(8,128)(2,1)S(1)}, u32[]{:S(2)}, u32[]{:S(2)}) collective-permute-start(bf16[2,384,1536]{2,1,0:T(8,128)(2,1)} %get-tuple-element.256), channel_id=1, source_target_pairs={{0,2},{1,3},{2,0},{3,1},{4,6},{5,7},{6,4},{7,5},{8,10},{9,11},{10,... | collective-permute-start | bytes 7077896 | tf_op jit(solution)/shard_map/ppermute | solution.py:837
  350.8 23.3 %collective-permute-start.39 = (bf16[192,1536]{1,0:T(8,128)(2,1)S(1)}, bf16[192,1536]{1,0:T(8,128)(2,1)S(1)}, u32[]{:S(2)}, u32[]{:S(2)}) collective-permute-start(bf16[192,1536]{1,0:T(8,128)(2,1)S(1)} %slice.354.refs_6_), channel_id=1, source_target_pairs={{0,4},{1,5},{2,6},{3,7},{4,0},{5,1},{6,2},{7,3},{8,12},{9,13},{10,... | collective-permute-start | bytes 1769480 | tf_op jit(solution)/shard_map/ppermute | solution.py:837
  355.4 44.7 %collective-permute-start.36 = (bf16[384,1536]{1,0:T(8,128)(2,1)}, bf16[384,1536]{1,0:T(8,128)(2,1)}, u32[]{:S(2)}, u32[]{:S(2)}) collective-permute-start(bf16[384,1536]{1,0:T(8,128)(2,1)} %fusion.1.refs_5_), channel_id=1, source_target_pairs={{0,1},{1,0},{2,3},{3,2},{4,5},{5,4},{6,7},{7,6},{8,9},{9,8},{10,11... | collective-permute-start | bytes 3538952 | tf_op jit(solution)/shard_map/ppermute | solution.py:837
  380.2 39.4 %collective-permute-start.42 = (bf16[96,4608]{1,0:T(8,128)(2,1)}, bf16[96,4608]{1,0:T(8,128)(2,1)}, u32[]{:S(2)}, u32[]{:S(2)}) collective-permute-start(bf16[96,4608]{1,0:T(8,128)(2,1)} %fusion.8.refs_9_), channel_id=1, source_target_pairs={{0,8},{1,9},{2,10},{3,11},{4,12},{5,13},{6,14},{7,15},{8,0},{9,1},... | collective-permute-start | bytes 2654216 | tf_op jit(solution)/shard_map/ppermute | solution.py:837
  382.3 37.4 %collective-permute-start.41 = (bf16[384,1536]{1,0:T(8,128)(2,1)}, bf16[384,1536]{1,0:T(8,128)(2,1)}, u32[]{:S(2)}, u32[]{:S(2)}) collective-permute-start(bf16[384,1536]{1,0:T(8,128)(2,1)} %fusion.refs_8_), channel_id=1, source_target_pairs={{0,1},{1,0},{2,3},{3,2},{4,5},{5,4},{6,7},{7,6},{8,9},{9,8},{10,11... | collective-permute-start | bytes 3538952 | tf_op jit(solution)/shard_map/ppermute | solution.py:837
  398.6 24.8 %collective-permute-start.40 = (bf16[384,1536]{1,0:T(8,128)(2,1)S(1)}, bf16[384,1536]{1,0:T(8,128)(2,1)S(1)}, u32[]{:S(2)}, u32[]{:S(2)}) collective-permute-start(bf16[384,1536]{1,0:T(8,128)(2,1)S(1)} %get-tuple-element.267), channel_id=1, source_target_pairs={{0,2},{1,3},{2,0},{3,1},{4,6},{5,7},{6,4},{7,5},{8,10},{9,11},{10,... | collective-permute-start | bytes 3538952 | tf_op jit(solution)/shard_map/ppermute | solution.py:837
  398.7 35.7 %collective-permute-start.35 = (bf16[2,128,768]{2,1,0:T(8,128)(2,1)S(1)}, bf16[2,128,768]{2,1,0:T(8,128)(2,1)S(1)}, u32[]{:S(2)}, u32[]{:S(2)}) collective-permute-start(bf16[2,128,768]{2,1,0:T(8,128)(2,1)S(1)} %constant_dynamic-slice_fusion.4), channel_id=1, source_target_pairs={{0,1},{1,3},{2,0},{3,2},{4,5},{5,7},{6,4},{7,6},{8,9},{9,11},{10,8... | collective-permute-start | bytes 1179656 | tf_op jit(solution)/shard_map/ppermute | solution.py:837
  400.1 37.2 %collective-permute-start.43 = (bf16[3,128,768]{2,1,0:T(8,128)(2,1)S(1)}, bf16[3,128,768]{2,1,0:T(8,128)(2,1)S(1)}, u32[]{:S(2)}, u32[]{:S(2)}) collective-permute-start(bf16[3,128,768]{2,1,0:T(8,128)(2,1)S(1)} %constant_dynamic-slice_fusion.3), channel_id=1, source_target_pairs={{0,0},{1,2},{2,1},{3,3},{4,4},{5,6},{6,5},{7,7},{8,8},{9,10},{10,9... | collective-permute-start | bytes 1769480 | tf_op jit(solution)/shard_map/ppermute | solution.py:837
  419.6 38.6 %collective-permute-start.45 = (bf16[192,1536]{1,0:T(8,128)(2,1)S(1)}, bf16[192,1536]{1,0:T(8,128)(2,1)S(1)}, u32[]{:S(2)}, u32[]{:S(2)}) collective-permute-start(bf16[192,1536]{1,0:T(8,128)(2,1)S(1)} %fusion.19.refs_5_), channel_id=1, source_target_pairs={{0,4},{1,5},{2,6},{3,7},{4,0},{5,1},{6,2},{7,3},{8,12},{9,13},{10,... | collective-permute-start | bytes 1769480 | tf_op jit(solution)/shard_map/ppermute | solution.py:837
  423.4 32.1 %collective-permute-start.46 = (bf16[192,1536]{1,0:T(8,128)(2,1)S(1)}, bf16[192,1536]{1,0:T(8,128)(2,1)S(1)}, u32[]{:S(2)}, u32[]{:S(2)}) collective-permute-start(bf16[192,1536]{1,0:T(8,128)(2,1)S(1)} %fusion.18.refs_9_), channel_id=1, source_target_pairs={{0,4},{1,5},{2,6},{3,7},{4,0},{5,1},{6,2},{7,3},{8,12},{9,13},{10,... | collective-permute-start | bytes 1769480 | tf_op jit(solution)/shard_map/ppermute | solution.py:837
  425.8 37.9 %collective-permute-start.49 = (bf16[384,1536]{1,0:T(8,128)(2,1)S(1)}, bf16[384,1536]{1,0:T(8,128)(2,1)S(1)}, u32[]{:S(2)}, u32[]{:S(2)}) collective-permute-start(bf16[384,1536]{1,0:T(8,128)(2,1)S(1)} %add_convert_fusion.refs_8_), channel_id=1, source_target_pairs={{0,1},{1,0},{2,3},{3,2},{4,5},{5,4},{6,7},{7,6},{8,9},{9,8},{10,11... | collective-permute-start | bytes 3538952 | tf_op jit(solution)/shard_map/ppermute | solution.py:837
  434.5 59.8 %collective-permute-start.61 = (bf16[48,4608]{1,0:T(8,128)(2,1)S(1)}, bf16[48,4608]{1,0:T(8,128)(2,1)}, u32[]{:S(2)}, u32[]{:S(2)}) collective-permute-start(bf16[48,4608]{1,0:T(8,128)(2,1)S(1)} %slice.470.refs_10_), channel_id=1, source_target_pairs={{0,16},{1,17},{2,18},{3,19},{4,20},{5,21},{6,22},{7,23},{8,24},{9,... | collective-permute-start | bytes 1327112 | tf_op jit(solution)/shard_map/ppermute | solution.py:837
  437.3 24.0 %collective-permute-start.47 = (bf16[384,1536]{1,0:T(8,128)(2,1)S(1)}, bf16[384,1536]{1,0:T(8,128)(2,1)S(1)}, u32[]{:S(2)}, u32[]{:S(2)}) collective-permute-start(bf16[384,1536]{1,0:T(8,128)(2,1)S(1)} %get-tuple-element.278), channel_id=1, source_target_pairs={{0,2},{1,3},{2,0},{3,1},{4,6},{5,7},{6,4},{7,5},{8,10},{9,11},{10,... | collective-permute-start | bytes 3538952 | tf_op jit(solution)/shard_map/ppermute | solution.py:837
  455.5 5.8 %collective-permute-start.44 = (bf16[640,768]{1,0:T(8,128)(2,1)S(1)}, bf16[640,768]{1,0:T(8,128)(2,1)S(1)}, u32[]{:S(2)}, u32[]{:S(2)}) collective-permute-start(bf16[640,768]{1,0:T(8,128)(2,1)S(1)} %get-tuple-element.274), channel_id=1, source_target_pairs={{0,2},{1,3},{2,0},{3,1},{4,6},{5,7},{6,4},{7,5},{8,10},{9,11},{10,... | collective-permute-start | bytes 2949128 | tf_op jit(solution)/shard_map/ppermute | solution.py:837
  461.3 22.8 %collective-permute-start.59 = (bf16[96,3072]{1,0:T(8,128)(2,1)S(1)}, bf16[96,3072]{1,0:T(8,128)(2,1)}, u32[]{:S(2)}, u32[]{:S(2)}) collective-permute-start(bf16[96,3072]{1,0:T(8,128)(2,1)S(1)} %fusion.13.refs_5_), channel_id=1, source_target_pairs={{0,8},{1,9},{2,10},{3,11},{4,12},{5,13},{6,14},{7,15},{8,0},{9,1},... | collective-permute-start | bytes 1769480 | tf_op jit(solution)/shard_map/ppermute | solution.py:837
  465.7 15.6 %collective-permute-start.50 = (bf16[192,1536]{1,0:T(8,128)(2,1)}, bf16[192,1536]{1,0:T(8,128)(2,1)}, u32[]{:S(2)}, u32[]{:S(2)}) collective-permute-start(bf16[192,1536]{1,0:T(8,128)(2,1)} %add_convert_fusion.3), channel_id=1, source_target_pairs={{0,4},{1,5},{2,6},{3,7},{4,0},{5,1},{6,2},{7,3},{8,12},{9,13},{10,... | collective-permute-start | bytes 1769480 | tf_op jit(solution)/shard_map/ppermute | solution.py:837
  465.8 1.2 collective-permute-start.51
  467.0 3.9 collective-permute-start.52
  468.3 35.3 %collective-permute-start.48 = (bf16[2,128,768]{2,1,0:T(8,128)(2,1)}, bf16[2,128,768]{2,1,0:T(8,128)(2,1)S(1)}, u32[]{:S(2)}, u32[]{:S(2)}) collective-permute-start(bf16[2,128,768]{2,1,0:T(8,128)(2,1)} %constant_dynamic-slice_fusion.2), channel_id=1, source_target_pairs={{0,1},{1,3},{2,0},{3,2},{4,5},{5,7},{6,4},{7,6},{8,9},{9,11},{10,8... | collective-permute-start | bytes 1179656 | tf_op jit(solution)/shard_map/ppermute | solution.py:837
  470.9 33.6 %collective-permute-start.55 = (bf16[3,128,768]{2,1,0:T(8,128)(2,1)}, bf16[3,128,768]{2,1,0:T(8,128)(2,1)S(1)}, u32[]{:S(2)}, u32[]{:S(2)}) collective-permute-start(bf16[3,128,768]{2,1,0:T(8,128)(2,1)} %constant_dynamic-slice_fusion.1), channel_id=1, source_target_pairs={{0,0},{1,2},{2,1},{3,3},{4,4},{5,6},{6,5},{7,7},{8,8},{9,10},{10,9... | collective-permute-start | bytes 1769480 | tf_op jit(solution)/shard_map/ppermute | solution.py:837
  483.0 11.2 %collective-permute-start.53 = (bf16[96,1536]{1,0:T(8,128)(2,1)S(1)}, bf16[96,1536]{1,0:T(8,128)(2,1)S(1)}, u32[]{:S(2)}, u32[]{:S(2)}) collective-permute-start(bf16[96,1536]{1,0:T(8,128)(2,1)S(1)} %slice.472), channel_id=1, source_target_pairs={{0,8},{1,9},{2,10},{3,11},{4,12},{5,13},{6,14},{7,15},{8,0},{9,1},... | collective-permute-start | bytes 884744 | tf_op jit(solution)/shard_map/ppermute | solution.py:837
  484.1 4.1 collective-permute-start.54
  488.2 13.8 %collective-permute-start.60 = (bf16[48,3072]{1,0:T(8,128)(2,1)S(1)}, bf16[48,3072]{1,0:T(8,128)(2,1)S(1)}, u32[]{:S(2)}, u32[]{:S(2)}) collective-permute-start(bf16[48,3072]{1,0:T(8,128)(2,1)S(1)} %slice.471), channel_id=1, source_target_pairs={{0,16},{1,17},{2,18},{3,19},{4,20},{5,21},{6,22},{7,23},{8,24},{9,... | collective-permute-start | bytes 884744 | tf_op jit(solution)/shard_map/ppermute | solution.py:837
  503.6 8.0 %collective-permute-start.56 = (bf16[4,8,1536]{2,1,0:T(8,128)(2,1)S(1)}, bf16[4,8,1536]{2,1,0:T(8,128)(2,1)S(1)}, u32[]{:S(2)}, u32[]{:S(2)}) collective-permute-start(bf16[4,8,1536]{2,1,0:T(8,128)(2,1)S(1)} %constant_dynamic-update-slice_fusion), channel_id=1, source_target_pairs={{0,8},{1,9},{2,10},{3,11},{4,12},{5,13},{6,14},{7,15},{8,0},{9,1},... | collective-permute-start | bytes 294920 | tf_op jit(solution)/shard_map/ppermute | solution.py:837
  506.9 17.1 %collective-permute-start.58 = (bf16[48,1536]{1,0:T(8,128)(2,1)S(1)}, bf16[48,1536]{1,0:T(8,128)(2,1)S(1)}, u32[]{:S(2)}, u32[]{:S(2)}) collective-permute-start(bf16[48,1536]{1,0:T(8,128)(2,1)S(1)} %slice.473), channel_id=1, source_target_pairs={{0,16},{1,17},{2,18},{3,19},{4,20},{5,21},{6,22},{7,23},{8,24},{9,... | collective-permute-start | bytes 442376 | tf_op jit(solution)/shard_map/ppermute | solution.py:837
  511.6 12.3 %collective-permute-start.57 = (bf16[8,8,1536]{2,1,0:T(8,128)(2,1)S(1)}, bf16[8,8,1536]{2,1,0:T(8,128)(2,1)S(1)}, u32[]{:S(2)}, u32[]{:S(2)}) collective-permute-start(bf16[8,8,1536]{2,1,0:T(8,128)(2,1)S(1)} %pad_maximum_fusion.5), channel_id=1, source_target_pairs={{0,16},{1,17},{2,18},{3,19},{4,20},{5,21},{6,22},{7,23},{8,24},{9,... | collective-permute-start | bytes 589832 | tf_op jit(solution)/shard_map/ppermute | solution.py:837
  (187 other events, 1271.5 us)
Sparse Core Ops, SparseCore 0:
  60.5 81.8 all-gather.4
  383.9 76.8 all-gather.6

commit v3 on v2

--- a/solution.py
+++ b/solution.py
@@ -20,7 +20,7 @@
 f32 = jnp.float32
 bf16 = jnp.bfloat16
 ALL = ("dp", "tensor")
-VMEM_BYTES = 32 * 1024 * 1024
+VMEM_BYTES = 26 * 1024 * 1024
 LIGHT = 2000
 
 
@@ -112,10 +112,10 @@
     qkv_steps(pl.program_id(0), normed, w, q, k, v)
 
 
-def qkv_parts_body(place, normed, w_0, w_1, w_2, w_3, w, q, k, v):
-    for index, part in enumerate((w_0, w_1, w_2, w_3)):
-        at = pl.multiple_of(((place[0] % 4) ^ index) * (D // 4), D // 4)
-        w[0, pl.ds(at, D // 4)] = part[0]
+def qkv_parts_body(place, normed, w_0, w_1, w, q, k, v):
+    for index, part in enumerate((w_0, w_1)):
+        at = pl.multiple_of((place[0] % 2 ^ index) * HALF, HALF)
+        w[0, pl.ds(at, HALF)] = part[0]
     qkv_steps(pl.program_id(0), normed, w, q, k, v)
 
 
@@ -174,7 +174,7 @@
 
 def project_parts(place, normed, parts, deps=()):
     rows = normed.shape[2]
-    by_step = pl.BlockSpec((1, D // 4, HALF), lambda j, *_: (j, 0, 0))
+    by_step = pl.BlockSpec((1, HALF, HALF), lambda j, *_: (j, 0, 0))
     return run(
         qkv_parts_body,
         (4,),
@@ -883,11 +883,12 @@
     wq_two = jnp.transpose(qkv_second, (1, 0, 2))
     place_ref = dp_pos.reshape(1).astype(jnp.int32)
     zero_ref = jnp.zeros((1,), jnp.int32)
-    quarter_at = dp_pos // 2 % 2 * 2 + core
-    proj_part = lax.dynamic_slice(
-        proj_first, (quarter_at % 2 * (D // 4), quarter_at // 2 * HALF), (D // 4, HALF)
-    )
-    near_part = jnp.concatenate([part_of(wq_one, 1, 1), proj_part[None]])
+    near_part = jnp.concatenate(
+        [
+            lax.dynamic_slice_in_dim(wq_one, core * HALF, HALF, 1),
+            lax.dynamic_slice_in_dim(proj_first, core * HALF, HALF, 1)[None],
+        ]
+    )
     kept, segs = numbers[:KEEP], numbers[KEEP:]
     kind = jnp.where(segs[3] == segs[0], 0, jnp.where(segs[4] == segs[1], 1, 2)).reshape(1)
     slot_hot = segs[:, None] == jnp.arange(SLOTS, dtype=jnp.int32)[None, :]
@@ -937,9 +938,9 @@
         ]
         + [down_pieces[row][None, :, column] for column in range(2) for row in range(2)]
     )
-    w_one_parts = Far(near_part, 1, arrived)
-    own = owned(*arrived, tab_one, tab_two, w_one_parts.first, order)
-    piece_two = send(after(pieces_two, own), across)
+    piece_two = send(after(pieces_two, *arrived), across)
+    w_near = send(after(near_part, *arrived), across)
+    own = owned(*arrived, tab_one, tab_two, piece_two, order)
     oth = send(own, core_swap)
 
     def add(*terms):
@@ -1007,13 +1008,12 @@
             return self.acc + after(self.got, *when).astype(f32)
 
     normed_one, *near_one = project_first(own, oth, tab_one, wq_one)
-    ups_one = Far(part_of(up_first, 1, 1), 1, (normed_one,))
-    downs_one = Far(part_of(down_first, 0, 2), 2, (normed_one,))
-    w_one_parts.hop(own)
+    ups_one = Far(part_of(up_first, 1, 1), 1, (own,))
+    downs_one = Far(part_of(down_first, 0, 2), 2, (own,))
     mixed_one_n = attend(kind, *near_one)
-    w_parts = w_one_parts.end(normed_one)
+    w_parts = (w_near, send(after(w_near, mixed_one_n), core_swap))
     w_two_far = lax.all_gather(
-        after(piece_two, normed_one)[None],
+        after(piece_two, own)[None],
         "dp",
         axis=0,
         tiled=True,
@@ -1023,11 +1023,11 @@
     )
     far_two_mlp = ([w_two_far] * 4, [w_two_far] * 4)
     w_one_far, *far_one = project_parts(
-        place_ref, normed_one, w_parts, deps=(mixed_one_n, ups_one.first, downs_one.first)
-    )
-    ups_one.hop(w_one_far)
-    downs_one.hop(w_one_far)
+        place_ref, normed_one, w_parts, deps=(mixed_one_n,)
+    )
     mixed_one_r = attend(kind, *far_one)
+    ups_one.hop(mixed_one_r)
+    downs_one.hop(mixed_one_r)
     attn_one, middle_one, normed_mlp_one, u_one_n, act_one_n, acc = feed_near(
         mixed_one_n, mixed_one_r, proj_first, w_one_far, own, tab_one, up_first, down_first
     )

time: 542 us -> 522 us (0.963)
  Pallas kernels: 189 us -> 177 us
  starting transfers between devices: 72 us -> 81.8 us
  waiting for transfers between devices: 90 us -> 80.9 us
    pallas_call x30, Pallas kernels: 189 us -> 177 us  [run(): pl.pallas_call(step, grid_spec=pltpu.PrefetchScalarGridSpec(num_scalar_pr...]
    ppermute x62 -> x60, starting transfers between devices: 71.4 us -> 81.2 us  [send(): return lax.ppermute(value, ALL, pairs)]
    ppermute x62 -> x60, waiting for transfers between devices: 89.9 us -> 80.9 us  [send(): return lax.ppermute(value, ALL, pairs)]
    unnamed x378 -> x372, local copies, waits for them, and re-layouts: 71.1 us -> 68.8 us
  transfers between devices with their start and end apart: 64 -> 62, of which waited for: 16 -> 18; matrix products, arithmetic and copies ran while one was open for 16% -> 15% of each run, Pallas kernels for 34% -> 33%
where the time goes in v3:
time: 522 us; the launch traced here: 516 us
  Pallas kernels  177 us (34%)
  local copies, waits for them, and re-layouts  105 us (20%)
  starting transfers between devices  81.8 us (16%)
  waiting for transfers between devices  80.9 us (15%)
  other arithmetic  37.6 us (7%)
  between operations  19.5 us (4%)
  matrix products  13.7 us (3%)
    pallas_call x30, Pallas kernels, run(): pl.pallas_call(step, grid_spec=pltpu.PrefetchScalarGridSpec(num_scalar_pr...  177 us
    ppermute x60, starting transfers between devices, send(): return lax.ppermute(value, ALL, pairs)  81.2 us
    ppermute x60, waiting for transfers between devices, send(): return lax.ppermute(value, ALL, pairs)  80.9 us
    unnamed x372, local copies, waits for them, and re-layouts  68.8 us
  transfers between devices with their start and end apart: 62, of which 18 were waited for; matrix products, arithmetic and copies ran while one was open for 15% of the time, Pallas kernels for 33%

profile of v3, /device:TPU:0, one launch (start us, length us, event | category | flops | bytes accessed | tf_op | source)
XLA Modules:
  0.0 515.8 jit_solution(15896856486158805016)
XLA Ops:
  10.1 4.3 collective-permute-start.3
  26.1 3.4 collective-permute-start.4
  29.5 4.0 fusion.65
  33.6 4.1 fusion.66
  37.7 1.8 collective-permute-done.4
  43.9 2.5 collective-permute-start.6
  49.7 4.0 shard_map.246
  55.0 7.0 %shard_map.247.refs_4_.refs_0_.refs_21_ = bf16[5,128,384]{2,1,0:T(8,128)(2,1)S(1)} custom-call(s32[1]{0:T(128)S(6)} %select_n.232.refs_0_, bf16[5,128,384]{2,1,0:T(8,128)(2,1)S(1)} %get-tuple-element.160.refs_1_, bf16[2,5,128,384]{3,2,1,0:T(8,128)(2,1)S(1)} %get-tuple-element.161.refs_2_, bf16[2,5,128,384]{3,2,1,0:T(8,128)(2,1)S(1)} %get-tuple-element.162.refs_3_), custom_call_target="tpu_custom_call" | custom-call | flops 2013266 | bytes 1475 | tf_op jit(solution)/shard_map/pallas_call | solution.py:78
  62.8 10.0 %collective-permute-done.6.refs_2_ = bf16[4,384,384]{2,1,0:T(8,128)(2,1)} collective-permute-done((bf16[4,384,384]{2,1,0:T(8,128)(2,1)S(1)}, bf16[4,384,384]{2,1,0:T(8,128)(2,1)}, u32[]{:S(2)}, u32[]{:S(2)}) %collective-permute-start.6) | collective-permute-done | bytes 1179680 | tf_op jit(solution)/shard_map/ppermute | solution.py:837
  77.3 4.5 shard_map.248
  81.9 7.0 %shard_map.249.refs_1_.refs_22_ = bf16[5,128,384]{2,1,0:T(8,128)(2,1)S(1)} custom-call(s32[1]{0:T(128)S(6)} %select_n.232.refs_0_, bf16[5,128,384]{2,1,0:T(8,128)(2,1)S(1)} %get-tuple-element.166.refs_1_, bf16[2,5,128,384]{3,2,1,0:T(8,128)(2,1)S(1)} %get-tuple-element.167.refs_2_, bf16[2,5,128,384]{3,2,1,0:T(8,128)(2,1)S(1)} %get-tuple-element.168.refs_3_), custom_call_target="tpu_custom_call" | custom-call | flops 2013266 | bytes 1475 | tf_op jit(solution)/shard_map/pallas_call | solution.py:78
  92.4 10.1 %collective-permute-done.8.refs_5_.refs_9_ = bf16[768,384]{1,0:T(8,128)(2,1)S(1)} collective-permute-done((bf16[768,384]{1,0:T(8,128)(2,1)S(1)}, bf16[768,384]{1,0:T(8,128)(2,1)S(1)}, u32[]{:S(2)}, u32[]{:S(2)}) %collective-permute-start.8) | collective-permute-done | bytes 589856 | tf_op jit(solution)/shard_map/ppermute | solution.py:837
  104.6 6.1 %shard_map.250 = (bf16[5,128,768]{2,1,0:T(8,128)(2,1)S(1)}, f32[5,128,768]{2,1,0:T(8,128)S(1)}, bf16[5,128,768]{2,1,0:T(8,128)(2,1)S(1)}, bf16[2,640,768]{2,1,0:...) custom-call(bf16[5,128,384]{2,1,0:T(8,128)(2,1)S(1)} %copy-done.26, ...), custom_call_target="tpu_custom_call" | custom-call | flops 1887437 | bytes 9779 | tf_op jit(solution)/shard_map/pallas_call | solution.py:78
  114.3 4.3 collective-permute-done.14.refs_11_.refs_15_
  121.4 5.6 %shard_map.251 = (bf16[2,640,768]{2,1,0:T(8,128)(2,1)S(1)}, bf16[2,640,768]{2,1,0:T(8,128)(2,1)S(1)}, bf16[5,128,768]{2,1,0:T(8,128)(2,1)S(1)}, bf16[5,128,768]{2,1,0:T(8,128)(2,1)S(1)}) custom-call(s32[1]{0:T(128)} %bitcast.refs_0_, bf16[5,128,768]{2,1,0:T(8,128)(2,1)S(1)} %get-tuple-element.170.refs_1_.refs_4_, f32[640,768]{1,0:T(8,128)S(1)} %get-tuple-element.171.refs_2_, ...), custom_call_target="tpu_custom_call" | custom-call | flops 1509950 | bytes 7813 | tf_op jit(solution)/shard_map/pallas_call | solution.py:78
  130.8 2.1 slice.277
  132.9 1.8 slice.278
  134.7 6.0 %collective-permute-start.20 = (bf16[3,128,768]{2,1,0:T(8,128)(2,1)}, bf16[3,128,768]{2,1,0:T(8,128)(2,1)}, u32[]{:S(2)}, u32[]{:S(2)}) collective-permute-start(bf16[3,128,768]{2,1,0:T(8,128)(2,1)} %slice.277), channel_id=1, source_target_pairs={{0,0},{1,2},{2,1},{3,3},{4,4},{5,6},{6,5},{7,7},{8,8},{9,10},{10,9... | collective-permute-start | bytes 1769480 | tf_op jit(solution)/shard_map/ppermute | solution.py:837
  141.1 1.8 shard_map.252
  144.4 2.6 shard_map.253
  147.1 5.9 %shard_map.254.refs_2_.refs_0_.refs_21_ = bf16[5,64,384]{2,1,0:T(8,128)(2,1)S(1)} custom-call(s32[1]{0:T(128)S(6)} %select_n.232.refs_0_, bf16[5,64,384]{2,1,0:T(8,128)(2,1)S(1)} %get-tuple-element.182.refs_1_, bf16[2,5,64,384]{3,2,1,0:T(8,128)(2,1)S(1)} %get-tuple-element.183.refs_2_, bf16[2,5,64,384]{3,2,1,0:T(8,128)(2,1)S(1)} %get-tuple-element.184.refs_3_), custom_call_target="tpu_custom_call" | custom-call | flops 503317 | bytes 738 | tf_op jit(solution)/shard_map/pallas_call | solution.py:78
  155.2 3.1 copy-done
  158.3 2.0 shard_map.255
  160.4 5.9 %shard_map.256.refs_1_.refs_22_ = bf16[5,64,384]{2,1,0:T(8,128)(2,1)S(1)} custom-call(s32[1]{0:T(128)S(6)} %select_n.232.refs_0_, bf16[5,64,384]{2,1,0:T(8,128)(2,1)S(1)} %get-tuple-element.185.refs_1_, bf16[2,5,64,384]{3,2,1,0:T(8,128)(2,1)S(1)} %get-tuple-element.186.refs_2_, bf16[2,5,64,384]{3,2,1,0:T(8,128)(2,1)S(1)} %get-tuple-element.187.refs_3_), custom_call_target="tpu_custom_call" | custom-call | flops 503317 | bytes 738 | tf_op jit(solution)/shard_map/pallas_call | solution.py:78
  166.4 2.7 maximum_select_fusion.1
  171.4 6.0 %collective-permute-start.18 = (bf16[3,128,768]{2,1,0:T(8,128)(2,1)}, bf16[3,128,768]{2,1,0:T(8,128)(2,1)}, u32[]{:S(2)}, u32[]{:S(2)}) collective-permute-start(bf16[3,128,768]{2,1,0:T(8,128)(2,1)} %constant_dynamic-slice_fusion.5), channel_id=1, source_target_pairs={{0,0},{1,2},{2,1},{3,3},{4,4},{5,6},{6,5},{7,7},{8,8},{9,10},{10,9... | collective-permute-start | bytes 1769480 | tf_op jit(solution)/shard_map/ppermute | solution.py:837
  180.0 3.0 copy-done.1
  189.3 3.6 shard_map.257
  195.5 3.6 shard_map.258
  199.1 2.7 shard_map.259
  201.9 4.9 shard_map.260
  207.4 13.6 %shard_map.261 = (bf16[2,384,1536]{2,1,0:T(8,128)(2,1)S(1)}, bf16[2,384,1536]{2,1,0:T(8,128)(2,1)S(1)}, bf16[2,384,384]{2,1,0:T(8,128)(2,1)S(1)}, bf16[2,384,384...) custom-call(s32[1]{0:T(128)} %constant.205.clone.1.refs_0_, ...), custom_call_target="tpu_custom_call" | custom-call | flops 3019899 | bytes 41554 | tf_op jit(solution)/shard_map/pallas_call | solution.py:78
  225.5 7.4 %shard_map.262 = (bf16[5,64,384]{2,1,0:T(8,128)(2,1)S(1)}, bf16[2,5,64,384]{3,2,1,0:T(8,128)(2,1)S(1)}, bf16[2,5,64,384]{3,2,1,0:T(8,128)(2,1)S(1)}) custom-call(s32[1]{0:T(128)S(6)} %select_n.232.refs_0_, bf16[5,64,384]{2,1,0:T(8,128)(2,1)S(1)} %copy-done.140, bf16[2,5,64,384]{3,2,1,0:T(8,128)(2,1)S(1)} %copy-done.121, ...), custom_call_target="tpu_custom_call" | custom-call | flops 1258292 | bytes 1352 | tf_op jit(solution)/shard_map/pallas_call | solution.py:78
  235.5 5.6 %shard_map.263 = (bf16[384,1536]{1,0:T(8,128)(2,1)S(1)}, bf16[384,1536]{1,0:T(8,128)(2,1)}, bf16[768,640]{1,0:T(8,128)(2,1)S(1)}, f32[640,768]{1,0:T(8,128)S(1)}) custom-call(bf16[5,64,384]{2,1,0:T(8,128)(2,1)S(1)} %get-tuple-element.210.refs_0_, bf16[2,5,64,384]{3,2,1,0:T(8,128)(2,1)S(1)} %get-tuple-element.211.refs_1_, ...), custom_call_target="tpu_custom_call" | custom-call | flops 1321206 | bytes 8479 | tf_op jit(solution)/shard_map/pallas_call | solution.py:78
  244.8 8.9 %collective-permute-done.25.refs_6_ = bf16[384,1536]{1,0:T(8,128)(2,1)} collective-permute-done((bf16[384,1536]{1,0:T(8,128)(2,1)}, bf16[384,1536]{1,0:T(8,128)(2,1)}, u32[]{:S(2)}, u32[]{:S(2)}) %collective-permute-start.25) | collective-permute-done | bytes 1179680 | tf_op jit(solution)/shard_map/ppermute | solution.py:837
  259.3 7.2 %shard_map.264 = (bf16[5,64,384]{2,1,0:T(8,128)(2,1)S(1)}, bf16[2,5,64,384]{3,2,1,0:T(8,128)(2,1)S(1)}, bf16[2,5,64,384]{3,2,1,0:T(8,128)(2,1)S(1)}) custom-call(s32[1]{0:T(128)S(6)} %select_n.232.refs_0_, bf16[5,64,384]{2,1,0:T(8,128)(2,1)S(1)} %copy-done.138, bf16[2,5,64,384]{3,2,1,0:T(8,128)(2,1)S(1)} %copy-done.117, ...), custom_call_target="tpu_custom_call" | custom-call | flops 1258292 | bytes 1352 | tf_op jit(solution)/shard_map/pallas_call | solution.py:78
  268.7 4.3 shard_map.265
  285.2 2.4 shard_map.267.refs_5_
  289.0 2.7 shard_map.268
  291.9 6.7 %shard_map.269 = (bf16[2,384,1536]{2,1,0:T(8,128)(2,1)S(1)}, bf16[2,384,1536]{2,1,0:T(8,128)(2,1)S(1)}, bf16[640,768]{1,0:T(8,128)(2,1)S(1)}, f32[5,1,768]{2,1,0:T(1,128)S(1)}) custom-call(s32[1]{0:T(128)} %bitcast.refs_0_, bf16[5,128,768]{2,1,0:T(8,128)(2,1)S(1)} %bitcast.166, f32[5,6,768]{2,1,0:T(8,128)S(1)} %copy-done.36, ...), custom_call_target="tpu_custom_call" | custom-call | flops 1887437 | bytes 6444 | tf_op jit(solution)/shard_map/pallas_call | solution.py:78
  298.8 2.7 fusion.4
  301.6 1.8 fusion.5
  303.6 2.8 collective-permute-start.36
  308.1 23.6 %shard_map.270 = (bf16[2,384,1536]{2,1,0:T(8,128)(2,1)S(1)}, bf16[2,384,1536]{2,1,0:T(8,128)(2,1)S(1)}, bf16[2,384,384]{2,1,0:T(8,128)(2,1)S(1)}, bf16[2,384,384...) custom-call(s32[1]{0:T(128)} %bitcast.refs_0_, ...), custom_call_target="tpu_custom_call" | custom-call | flops 6039798 | bytes 16683 | tf_op jit(solution)/shard_map/pallas_call | solution.py:78
  334.1 2.2 add_convert_fusion.1
  336.4 1.8 collective-permute-start.37
  341.7 9.5 %shard_map.271 = (bf16[5,128,384]{2,1,0:T(8,128)(2,1)S(1)}, bf16[2,5,128,384]{3,2,1,0:T(8,128)(2,1)S(1)}, bf16[2,5,128,384]{3,2,1,0:T(8,128)(2,1)S(1)}) custom-call(s32[1]{0:T(128)S(6)} %select_n.232.refs_0_, bf16[5,128,384]{2,1,0:T(8,128)(2,1)S(1)} %copy-done.103, bf16[2,5,128,384]{3,2,1,0:T(8,128)(2,1)S(1)} %copy-done.46, ...), custom_call_target="tpu_custom_call" | custom-call | flops 5033165 | bytes 2704 | tf_op jit(solution)/shard_map/pallas_call | solution.py:78
  358.0 8.4 %collective-permute-start.39 = (bf16[384,1536]{1,0:T(8,128)(2,1)}, bf16[384,1536]{1,0:T(8,128)(2,1)}, u32[]{:S(2)}, u32[]{:S(2)}) collective-permute-start(bf16[384,1536]{1,0:T(8,128)(2,1)} %fusion.refs_8_), channel_id=1, source_target_pairs={{0,1},{1,0},{2,3},{3,2},{4,5},{5,4},{6,7},{7,6},{8,9},{9,8},{10,11... | collective-permute-start | bytes 3538952 | tf_op jit(solution)/shard_map/ppermute | solution.py:837
  374.3 7.7 %shard_map.272 = (bf16[384,1536]{1,0:T(8,128)(2,1)S(1)}, bf16[384,1536]{1,0:T(8,128)(2,1)S(1)}, bf16[768,1280]{1,0:T(8,128)(2,1)S(1)}, f32[1280,768]{1,0:T(8,128)S(1)}) custom-call(bf16[5,128,384]{2,1,0:T(8,128)(2,1)S(1)} %copy-done.149, bf16[2,5,128,384]{3,2,1,0:T(8,128)(2,1)S(1)} %copy-done.142, bf16[2,5,128,384]{3,2,1,0:T(8,128)(2,1)S(1)} %copy-done.144, ...), custom_call_target="tpu_custom_call" | custom-call | flops 2642412 | bytes 8700 | tf_op jit(solution)/shard_map/pallas_call | solution.py:78
  385.0 9.7 %shard_map.273 = (bf16[5,128,384]{2,1,0:T(8,128)(2,1)S(1)}, bf16[2,5,128,384]{3,2,1,0:T(8,128)(2,1)S(1)}, bf16[2,5,128,384]{3,2,1,0:T(8,128)(2,1)S(1)}) custom-call(s32[1]{0:T(128)S(6)} %select_n.232.refs_0_, bf16[5,128,384]{2,1,0:T(8,128)(2,1)S(1)} %copy-done.113, bf16[2,5,128,384]{3,2,1,0:T(8,128)(2,1)S(1)} %copy-done.50, ...), custom_call_target="tpu_custom_call" | custom-call | flops 5033165 | bytes 2704 | tf_op jit(solution)/shard_map/pallas_call | solution.py:78
  394.7 8.8 %collective-permute-start.43 = (bf16[192,1536]{1,0:T(8,128)(2,1)S(1)}, bf16[192,1536]{1,0:T(8,128)(2,1)S(1)}, u32[]{:S(2)}, u32[]{:S(2)}) collective-permute-start(bf16[192,1536]{1,0:T(8,128)(2,1)S(1)} %fusion.19.refs_5_), channel_id=1, source_target_pairs={{0,4},{1,5},{2,6},{3,7},{4,0},{5,1},{6,2},{7,3},{8,12},{9,13},{10,... | collective-permute-start | bytes 1769480 | tf_op jit(solution)/shard_map/ppermute | solution.py:837
  408.3 3.6 collective-permute-start.47
  411.9 6.6 %shard_map.274 = (bf16[384,1536]{1,0:T(8,128)(2,1)S(1)}, bf16[384,1536]{1,0:T(8,128)(2,1)S(1)}, f32[640,768]{1,0:T(8,128)S(1)}, bf16[640,768]{1,0:T(8,128)(2,1)S(1)}) custom-call(bf16[5,128,384]{2,1,0:T(8,128)(2,1)S(1)} %get-tuple-element.260.refs_0_, bf16[2,5,128,384]{3,2,1,0:T(8,128)(2,1)S(1)} %get-tuple-element.261.refs_1_, ...), custom_call_target="tpu_custom_call" | custom-call | flops 1887437 | bytes 8307 | tf_op jit(solution)/shard_map/pallas_call | solution.py:78
  418.6 2.5 collective-permute-start.59
  421.5 15.5 %collective-permute-done.44 = bf16[192,1536]{1,0:T(8,128)(2,1)S(1)} collective-permute-done((bf16[192,1536]{1,0:T(8,128)(2,1)S(1)}, bf16[192,1536]{1,0:T(8,128)(2,1)S(1)}, u32[]{:S(2)}, u32[]{:S(2)}) %collective-permute-start.44) | collective-permute-done | bytes 589856 | tf_op jit(solution)/shard_map/ppermute | solution.py:837
  439.6 2.0 fusion.17
  447.6 2.0 collective-permute-start.48
  451.7 2.0 collective-permute-start.46
  456.5 4.9 reshape.653
  470.0 2.7 collective-permute-start.58
  472.6 3.5 collective-permute-done.51
  478.2 6.2 %collective-permute-done.58 = bf16[48,3072]{1,0:T(8,128)(2,1)S(1)} collective-permute-done((bf16[48,3072]{1,0:T(8,128)(2,1)S(1)}, bf16[48,3072]{1,0:T(8,128)(2,1)S(1)}, u32[]{:S(2)}, u32[]{:S(2)}) %collective-permute-start.58) | collective-permute-done | bytes 294944 | tf_op jit(solution)/shard_map/ppermute | solution.py:837
  489.2 3.3 collective-permute-start.56
  494.0 12.3 %collective-permute-done.55 = bf16[8,8,1536]{2,1,0:T(8,128)(2,1)S(1)} collective-permute-done((bf16[8,8,1536]{2,1,0:T(8,128)(2,1)S(1)}, bf16[8,8,1536]{2,1,0:T(8,128)(2,1)S(1)}, u32[]{:S(2)}, u32[]{:S(2)}) %collective-permute-start.55) | collective-permute-done | bytes 196640 | tf_op jit(solution)/shard_map/ppermute | solution.py:837
  (604 shorter events, 155.2 us)
Async XLA Ops:
  7.2 148.0 %all-gather.5.cloned.1.call-start = ((), (), s32[]{:S(2)}) async-start(), calls=%async_computation | async-start | bytes 7520256 | tf_op jit(solution)/shard_map/all_gather | solution.py:1015
  8.4 16.9 %collective-permute-start.1 = (bf16[3,128,768]{2,1,0:T(8,128)(2,1)S(1)}, bf16[3,128,768]{2,1,0:T(8,128)(2,1)S(1)}, u32[]{:S(2)}, u32[]{:S(2)}) collective-permute-start(bf16[3,128,768]{2,1,0:T(8,128)(2,1)S(1)} %slice.267), channel_id=1, source_target_pairs={{0,0},{1,2},{2,1},{3,3},{4,4},{5,6},{6,5},{7,7},{8,8},{9,10},{10,9... | collective-permute-start | bytes 1769480 | tf_op jit(solution)/shard_map/ppermute | solution.py:837
  10.1 15.2 %collective-permute-start.3 = (bf16[2,128,768]{2,1,0:T(8,128)(2,1)S(1)}, bf16[2,128,768]{2,1,0:T(8,128)(2,1)S(1)}, u32[]{:S(2)}, u32[]{:S(2)}) collective-permute-start(bf16[2,128,768]{2,1,0:T(8,128)(2,1)S(1)} %slice.269), channel_id=1, source_target_pairs={{0,2},{1,0},{2,3},{3,1},{4,6},{5,4},{6,7},{7,5},{8,10},{9,8},{10,1... | collective-permute-start | bytes 1179656 | tf_op jit(solution)/shard_map/ppermute | solution.py:837
  15.2 7.9 %collective-permute-start = (s32[645]{0:T(1024)S(1)}, s32[645]{0:T(1024)S(1)}, u32[]{:S(2)}, u32[]{:S(2)}) collective-permute-start(s32[645]{0:T(1024)S(1)} %pad_add_fusion), channel_id=1, source_target_pairs={{0,0},{1,2},{2,1},{3,3},{4,4},{5,6},{6,5},{7,7},{8,8},{9,10},{10,9... | collective-permute-start | bytes 7748 | tf_op jit(solution)/shard_map/ppermute | solution.py:837
  15.9 7.7 %collective-permute-start.2 = (bf16[5,768]{1,0:T(8,128)(2,1)S(1)}, bf16[5,768]{1,0:T(8,128)(2,1)S(1)}, u32[]{:S(2)}, u32[]{:S(2)}) collective-permute-start(bf16[5,768]{1,0:T(8,128)(2,1)S(1)} %fusion.27), channel_id=1, source_target_pairs={{0,0},{1,2},{2,1},{3,3},{4,4},{5,6},{6,5},{7,7},{8,8},{9,10},{10,9... | collective-permute-start | bytes 23048 | tf_op jit(solution)/shard_map/ppermute | solution.py:837
  26.1 13.4 %collective-permute-start.4 = (bf16[12,48,384]{2,1,0:T(8,128)(2,1)S(1)}, bf16[12,48,384]{2,1,0:T(8,128)(2,1)S(1)}, u32[]{:S(2)}, u32[]{:S(2)}) collective-permute-start(bf16[12,48,384]{2,1,0:T(8,128)(2,1)S(1)} %copy.62), channel_id=1, source_target_pairs={{0,1},{1,0},{2,3},{3,2},{4,5},{5,4},{6,7},{7,6},{8,9},{9,8},{10,11... | collective-permute-start | bytes 1327112 | tf_op jit(solution)/shard_map/ppermute | solution.py:837
  42.0 62.5 %copy-start.6 = (bf16[5,128,768]{2,1,0:T(8,128)(2,1)}, bf16[5,128,768]{2,1,0:T(8,128)(2,1)S(1)}, u32[]{:S(2)}) copy-start(bf16[5,128,768]{2,1,0:T(8,128)(2,1)S(1)} %maximum_select_fusion.refs_0_.refs_4_.refs_2_) | copy-start | bytes 2949124
  42.1 414.4 %all-gather.7.cloned.1.call-start = ((), (), s32[]{:S(2)}) async-start(), calls=%async_computation.1 | async-start | bytes 4460544 | tf_op jit(solution)/shard_map/all_gather | solution.py:1126
  43.9 28.9 %collective-permute-start.6 = (bf16[4,384,384]{2,1,0:T(8,128)(2,1)S(1)}, bf16[4,384,384]{2,1,0:T(8,128)(2,1)}, u32[]{:S(2)}, u32[]{:S(2)}) collective-permute-start(bf16[4,384,384]{2,1,0:T(8,128)(2,1)S(1)} %pad_maximum_fusion.3), channel_id=1, source_target_pairs={{0,1},{1,0},{2,3},{3,2},{4,5},{5,4},{6,7},{7,6},{8,9},{9,8},{10,11... | collective-permute-start | bytes 3538952 | tf_op jit(solution)/shard_map/ppermute | solution.py:837
  46.5 3.2 collective-permute-start.5
  72.8 3.5 collective-permute-start.7
  74.1 16.7 %collective-permute-start.12 = (bf16[384,768]{1,0:T(8,128)(2,1)S(1)}, bf16[384,768]{1,0:T(8,128)(2,1)S(1)}, u32[]{:S(2)}, u32[]{:S(2)}) collective-permute-start(bf16[384,768]{1,0:T(8,128)(2,1)S(1)} %constant_dynamic-slice_fusion.9), channel_id=1, source_target_pairs={{0,1},{1,0},{2,3},{3,2},{4,5},{5,4},{6,7},{7,6},{8,9},{9,8},{10,11... | collective-permute-start | bytes 1769480 | tf_op jit(solution)/shard_map/ppermute | solution.py:837
  75.4 27.1 %collective-permute-start.8 = (bf16[768,384]{1,0:T(8,128)(2,1)S(1)}, bf16[768,384]{1,0:T(8,128)(2,1)S(1)}, u32[]{:S(2)}, u32[]{:S(2)}) collective-permute-start(bf16[768,384]{1,0:T(8,128)(2,1)S(1)} %constant_dynamic-slice_fusion.10), channel_id=1, source_target_pairs={{0,1},{1,0},{2,3},{3,2},{4,5},{5,4},{6,7},{7,6},{8,9},{9,8},{10,11... | collective-permute-start | bytes 1769480 | tf_op jit(solution)/shard_map/ppermute | solution.py:837
  90.8 27.8 %collective-permute-start.14 = (bf16[384,768]{1,0:T(8,128)(2,1)S(1)}, bf16[384,768]{1,0:T(8,128)(2,1)S(1)}, u32[]{:S(2)}, u32[]{:S(2)}) collective-permute-start(bf16[384,768]{1,0:T(8,128)(2,1)S(1)} %collective-permute-done.12.refs_9_.refs_13_), channel_id=1, source_target_pairs={{0,8},{1,9},{2,10},{3,11},{4,12},{5,13},{6,14},{7,15},{8,0},{9,1},... | collective-permute-start | bytes 1769480 | tf_op jit(solution)/shard_map/ppermute | solution.py:837
  102.5 16.0 %collective-permute-start.10 = (bf16[768,384]{1,0:T(8,128)(2,1)S(1)}, bf16[768,384]{1,0:T(8,128)(2,1)S(1)}, u32[]{:S(2)}, u32[]{:S(2)}) collective-permute-start(bf16[768,384]{1,0:T(8,128)(2,1)S(1)} %collective-permute-done.8.refs_5_.refs_9_), channel_id=1, source_target_pairs={{0,4},{1,5},{2,6},{3,7},{4,0},{5,1},{6,2},{7,3},{8,12},{9,13},{10,... | collective-permute-start | bytes 1769480 | tf_op jit(solution)/shard_map/ppermute | solution.py:837
  104.0 15.1 %collective-permute-start.13 = (bf16[384,768]{1,0:T(8,128)(2,1)S(1)}, bf16[384,768]{1,0:T(8,128)(2,1)S(1)}, u32[]{:S(2)}, u32[]{:S(2)}) collective-permute-start(bf16[384,768]{1,0:T(8,128)(2,1)S(1)} %collective-permute-done.12.refs_9_.refs_13_), channel_id=1, source_target_pairs={{0,2},{1,3},{2,0},{3,1},{4,6},{5,7},{6,4},{7,5},{8,10},{9,11},{10,... | collective-permute-start | bytes 1769480 | tf_op jit(solution)/shard_map/ppermute | solution.py:837
  104.1 15.1 %collective-permute-start.9 = (bf16[768,384]{1,0:T(8,128)(2,1)S(1)}, bf16[768,384]{1,0:T(8,128)(2,1)S(1)}, u32[]{:S(2)}, u32[]{:S(2)}) collective-permute-start(bf16[768,384]{1,0:T(8,128)(2,1)S(1)} %collective-permute-done.8.refs_5_.refs_9_), channel_id=1, source_target_pairs={{0,2},{1,3},{2,0},{3,1},{4,6},{5,7},{6,4},{7,5},{8,10},{9,11},{10,... | collective-permute-start | bytes 1769480 | tf_op jit(solution)/shard_map/ppermute | solution.py:837
  118.6 2.0 collective-permute-start.15
  118.6 2.8 collective-permute-start.11
  130.7 10.5 %collective-permute-start.16 = (bf16[640,768]{1,0:T(8,128)(2,1)S(1)}, bf16[640,768]{1,0:T(8,128)(2,1)S(1)}, u32[]{:S(2)}, u32[]{:S(2)}) collective-permute-start(bf16[640,768]{1,0:T(8,128)(2,1)S(1)} %bitcast.161), channel_id=1, source_target_pairs={{0,2},{1,3},{2,0},{3,1},{4,6},{5,7},{6,4},{7,5},{8,10},{9,11},{10,... | collective-permute-start | bytes 2949128 | tf_op jit(solution)/shard_map/ppermute | solution.py:837
  134.7 31.6 %collective-permute-start.20 = (bf16[3,128,768]{2,1,0:T(8,128)(2,1)}, bf16[3,128,768]{2,1,0:T(8,128)(2,1)}, u32[]{:S(2)}, u32[]{:S(2)}) collective-permute-start(bf16[3,128,768]{2,1,0:T(8,128)(2,1)} %slice.277), channel_id=1, source_target_pairs={{0,0},{1,2},{2,1},{3,3},{4,4},{5,6},{6,5},{7,7},{8,8},{9,10},{10,9... | collective-permute-start | bytes 1769480 | tf_op jit(solution)/shard_map/ppermute | solution.py:837
  140.7 25.7 %collective-permute-start.21 = (bf16[2,128,768]{2,1,0:T(8,128)(2,1)}, bf16[2,128,768]{2,1,0:T(8,128)(2,1)}, u32[]{:S(2)}, u32[]{:S(2)}) collective-permute-start(bf16[2,128,768]{2,1,0:T(8,128)(2,1)} %slice.278), channel_id=1, source_target_pairs={{0,2},{1,0},{2,3},{3,1},{4,6},{5,4},{6,7},{7,5},{8,10},{9,8},{10,1... | collective-permute-start | bytes 1179656 | tf_op jit(solution)/shard_map/ppermute | solution.py:837
  169.0 30.1 %collective-permute-start.22 = (bf16[5,128,768]{2,1,0:T(8,128)(2,1)}, bf16[5,128,768]{2,1,0:T(8,128)(2,1)}, u32[]{:S(2)}, u32[]{:S(2)}) collective-permute-start(bf16[5,128,768]{2,1,0:T(8,128)(2,1)} %maximum_select_fusion.1), channel_id=1, source_target_pairs={{0,2},{1,3},{2,0},{3,1},{4,6},{5,7},{6,4},{7,5},{8,10},{9,11},{10,... | collective-permute-start | bytes 2949128 | tf_op jit(solution)/shard_map/ppermute | solution.py:837
  171.4 22.7 %collective-permute-start.18 = (bf16[3,128,768]{2,1,0:T(8,128)(2,1)}, bf16[3,128,768]{2,1,0:T(8,128)(2,1)}, u32[]{:S(2)}, u32[]{:S(2)}) collective-permute-start(bf16[3,128,768]{2,1,0:T(8,128)(2,1)} %constant_dynamic-slice_fusion.5), channel_id=1, source_target_pairs={{0,0},{1,2},{2,1},{3,3},{4,4},{5,6},{6,5},{7,7},{8,8},{9,10},{10,9... | collective-permute-start | bytes 1769480 | tf_op jit(solution)/shard_map/ppermute | solution.py:837
  179.1 13.9 %collective-permute-start.17 = (bf16[2,128,768]{2,1,0:T(8,128)(2,1)}, bf16[2,128,768]{2,1,0:T(8,128)(2,1)}, u32[]{:S(2)}, u32[]{:S(2)}) collective-permute-start(bf16[2,128,768]{2,1,0:T(8,128)(2,1)} %constant_dynamic-slice_fusion.6), channel_id=1, source_target_pairs={{0,1},{1,3},{2,0},{3,2},{4,5},{5,7},{6,4},{7,6},{8,9},{9,11},{10,8... | collective-permute-start | bytes 1179656 | tf_op jit(solution)/shard_map/ppermute | solution.py:837
  206.8 16.5 %collective-permute-start.23 = (bf16[2,384,1536]{2,1,0:T(8,128)(2,1)S(1)}, bf16[2,384,1536]{2,1,0:T(8,128)(2,1)S(1)}, u32[]{:S(2)}, u32[]{:S(2)}) collective-permute-start(bf16[2,384,1536]{2,1,0:T(8,128)(2,1)S(1)} %get-tuple-element.208), channel_id=1, source_target_pairs={{0,2},{1,3},{2,0},{3,1},{4,6},{5,7},{6,4},{7,5},{8,10},{9,11},{10,... | collective-permute-start | bytes 7077896 | tf_op jit(solution)/shard_map/ppermute | solution.py:837
  223.2 9.7 %collective-permute-start.24 = (bf16[2,384,1536]{2,1,0:T(8,128)(2,1)S(1)}, bf16[2,384,1536]{2,1,0:T(8,128)(2,1)S(1)}, u32[]{:S(2)}, u32[]{:S(2)}) collective-permute-start(bf16[2,384,1536]{2,1,0:T(8,128)(2,1)S(1)} %get-tuple-element.216), channel_id=1, source_target_pairs={{0,2},{1,3},{2,0},{3,1},{4,6},{5,7},{6,4},{7,5},{8,10},{9,11},{10,... | collective-permute-start | bytes 7077896 | tf_op jit(solution)/shard_map/ppermute | solution.py:837
  224.7 29.1 %collective-permute-start.25 = (bf16[384,1536]{1,0:T(8,128)(2,1)}, bf16[384,1536]{1,0:T(8,128)(2,1)}, u32[]{:S(2)}, u32[]{:S(2)}) collective-permute-start(bf16[384,1536]{1,0:T(8,128)(2,1)} %fusion.3.refs_5_), channel_id=1, source_target_pairs={{0,1},{1,0},{2,3},{3,2},{4,5},{5,4},{6,7},{7,6},{8,9},{9,8},{10,11... | collective-permute-start | bytes 3538952 | tf_op jit(solution)/shard_map/ppermute | solution.py:837
  244.4 22.2 %collective-permute-start.26 = (bf16[384,1536]{1,0:T(8,128)(2,1)}, bf16[384,1536]{1,0:T(8,128)(2,1)S(1)}, u32[]{:S(2)}, u32[]{:S(2)}) collective-permute-start(bf16[384,1536]{1,0:T(8,128)(2,1)} %get-tuple-element.224), channel_id=1, source_target_pairs={{0,2},{1,3},{2,0},{3,1},{4,6},{5,7},{6,4},{7,5},{8,10},{9,11},{10,... | collective-permute-start | bytes 3538952 | tf_op jit(solution)/shard_map/ppermute | solution.py:837
  244.8 47.0 %collective-permute-start.29 = (bf16[384,1536]{1,0:T(8,128)(2,1)}, bf16[384,1536]{1,0:T(8,128)(2,1)S(1)}, u32[]{:S(2)}, u32[]{:S(2)}) collective-permute-start(bf16[384,1536]{1,0:T(8,128)(2,1)} %copy-done.38), channel_id=1, source_target_pairs={{0,1},{1,0},{2,3},{3,2},{4,5},{5,4},{6,7},{7,6},{8,9},{9,8},{10,11... | collective-permute-start | bytes 3538952 | tf_op jit(solution)/shard_map/ppermute | solution.py:837
  276.2 1.9 collective-permute-start.27
  276.4 8.8 %collective-permute-start.19 = (bf16[320,768]{1,0:T(8,128)(2,1)S(1)}, bf16[320,768]{1,0:T(8,128)(2,1)}, u32[]{:S(2)}, u32[]{:S(2)}) collective-permute-start(bf16[320,768]{1,0:T(8,128)(2,1)S(1)} %bitcast.176), channel_id=1, source_target_pairs={{0,2},{1,3},{2,0},{3,1},{4,6},{5,7},{6,4},{7,5},{8,10},{9,11},{10,... | collective-permute-start | bytes 1474568 | tf_op jit(solution)/shard_map/ppermute | solution.py:837
  283.9 5.2 collective-permute-start.28
  284.8 49.3 %collective-permute-start.32 = (bf16[384,1536]{1,0:T(8,128)(2,1)}, bf16[384,1536]{1,0:T(8,128)(2,1)}, u32[]{:S(2)}, u32[]{:S(2)}) collective-permute-start(bf16[384,1536]{1,0:T(8,128)(2,1)} %copy-done.39), channel_id=1, source_target_pairs={{0,1},{1,0},{2,3},{3,2},{4,5},{5,4},{6,7},{7,6},{8,9},{9,8},{10,11... | collective-permute-start | bytes 3538952 | tf_op jit(solution)/shard_map/ppermute | solution.py:837
  284.8 49.3 %collective-permute-start.31 = (bf16[384,1536]{1,0:T(8,128)(2,1)}, bf16[384,1536]{1,0:T(8,128)(2,1)}, u32[]{:S(2)}, u32[]{:S(2)}) collective-permute-start(bf16[384,1536]{1,0:T(8,128)(2,1)} %copy-done.158), channel_id=1, source_target_pairs={{0,2},{1,3},{2,0},{3,1},{4,6},{5,7},{6,4},{7,5},{8,10},{9,11},{10,... | collective-permute-start | bytes 3538952 | tf_op jit(solution)/shard_map/ppermute | solution.py:837
  298.6 41.0 %copy-start.89 = (bf16[2,384,1536]{2,1,0:T(8,128)(2,1)}, bf16[2,384,1536]{2,1,0:T(8,128)(2,1)S(1)}, u32[]{:S(2)}) copy-start(bf16[2,384,1536]{2,1,0:T(8,128)(2,1)S(1)} %get-tuple-element.240) | copy-start | bytes 7077892
  298.6 39.6 %collective-permute-start.30 = (bf16[2,384,1536]{2,1,0:T(8,128)(2,1)S(1)}, bf16[2,384,1536]{2,1,0:T(8,128)(2,1)}, u32[]{:S(2)}, u32[]{:S(2)}) collective-permute-start(bf16[2,384,1536]{2,1,0:T(8,128)(2,1)S(1)} %get-tuple-element.241), channel_id=1, source_target_pairs={{0,2},{1,3},{2,0},{3,1},{4,6},{5,7},{6,4},{7,5},{8,10},{9,11},{10,... | collective-permute-start | bytes 7077896 | tf_op jit(solution)/shard_map/ppermute | solution.py:837
  303.6 48.4 %collective-permute-start.36 = (bf16[192,3072]{1,0:T(8,128)(2,1)S(1)}, bf16[192,3072]{1,0:T(8,128)(2,1)S(1)}, u32[]{:S(2)}, u32[]{:S(2)}) collective-permute-start(bf16[192,3072]{1,0:T(8,128)(2,1)S(1)} %fusion.14.refs_24_), channel_id=1, source_target_pairs={{0,4},{1,5},{2,6},{3,7},{4,0},{5,1},{6,2},{7,3},{8,12},{9,13},{10,... | collective-permute-start | bytes 3538952 | tf_op jit(solution)/shard_map/ppermute | solution.py:837
  333.0 20.6 %collective-permute-start.35 = (bf16[2,384,1536]{2,1,0:T(8,128)(2,1)S(1)}, bf16[2,384,1536]{2,1,0:T(8,128)(2,1)S(1)}, u32[]{:S(2)}, u32[]{:S(2)}) collective-permute-start(bf16[2,384,1536]{2,1,0:T(8,128)(2,1)S(1)} %get-tuple-element.254), channel_id=1, source_target_pairs={{0,2},{1,3},{2,0},{3,1},{4,6},{5,7},{6,4},{7,5},{8,10},{9,11},{10,... | collective-permute-start | bytes 7077896 | tf_op jit(solution)/shard_map/ppermute | solution.py:837
  336.4 15.6 %collective-permute-start.37 = (bf16[192,1536]{1,0:T(8,128)(2,1)S(1)}, bf16[192,1536]{1,0:T(8,128)(2,1)S(1)}, u32[]{:S(2)}, u32[]{:S(2)}) collective-permute-start(bf16[192,1536]{1,0:T(8,128)(2,1)S(1)} %slice.354.refs_6_), channel_id=1, source_target_pairs={{0,4},{1,5},{2,6},{3,7},{4,0},{5,1},{6,2},{7,3},{8,12},{9,13},{10,... | collective-permute-start | bytes 1769480 | tf_op jit(solution)/shard_map/ppermute | solution.py:837
  341.0 41.2 %collective-permute-start.34 = (bf16[384,1536]{1,0:T(8,128)(2,1)}, bf16[384,1536]{1,0:T(8,128)(2,1)}, u32[]{:S(2)}, u32[]{:S(2)}) collective-permute-start(bf16[384,1536]{1,0:T(8,128)(2,1)} %fusion.1.refs_5_), channel_id=1, source_target_pairs={{0,1},{1,0},{2,3},{3,2},{4,5},{5,4},{6,7},{7,6},{8,9},{9,8},{10,11... | collective-permute-start | bytes 3538952 | tf_op jit(solution)/shard_map/ppermute | solution.py:837
  356.1 38.6 %collective-permute-start.40 = (bf16[96,4608]{1,0:T(8,128)(2,1)}, bf16[96,4608]{1,0:T(8,128)(2,1)}, u32[]{:S(2)}, u32[]{:S(2)}) collective-permute-start(bf16[96,4608]{1,0:T(8,128)(2,1)} %fusion.8.refs_9_), channel_id=1, source_target_pairs={{0,8},{1,9},{2,10},{3,11},{4,12},{5,13},{6,14},{7,15},{8,0},{9,1},... | collective-permute-start | bytes 2654216 | tf_op jit(solution)/shard_map/ppermute | solution.py:837
  358.0 45.5 %collective-permute-start.39 = (bf16[384,1536]{1,0:T(8,128)(2,1)}, bf16[384,1536]{1,0:T(8,128)(2,1)}, u32[]{:S(2)}, u32[]{:S(2)}) collective-permute-start(bf16[384,1536]{1,0:T(8,128)(2,1)} %fusion.refs_8_), channel_id=1, source_target_pairs={{0,1},{1,0},{2,3},{3,2},{4,5},{5,4},{6,7},{7,6},{8,9},{9,8},{10,11... | collective-permute-start | bytes 3538952 | tf_op jit(solution)/shard_map/ppermute | solution.py:837
  382.0 25.9 %collective-permute-start.38 = (bf16[384,1536]{1,0:T(8,128)(2,1)S(1)}, bf16[384,1536]{1,0:T(8,128)(2,1)S(1)}, u32[]{:S(2)}, u32[]{:S(2)}) collective-permute-start(bf16[384,1536]{1,0:T(8,128)(2,1)S(1)} %get-tuple-element.265), channel_id=1, source_target_pairs={{0,2},{1,3},{2,0},{3,1},{4,6},{5,7},{6,4},{7,5},{8,10},{9,11},{10,... | collective-permute-start | bytes 3538952 | tf_op jit(solution)/shard_map/ppermute | solution.py:837
  382.1 36.4 %collective-permute-start.33 = (bf16[2,128,768]{2,1,0:T(8,128)(2,1)S(1)}, bf16[2,128,768]{2,1,0:T(8,128)(2,1)S(1)}, u32[]{:S(2)}, u32[]{:S(2)}) collective-permute-start(bf16[2,128,768]{2,1,0:T(8,128)(2,1)S(1)} %constant_dynamic-slice_fusion.4), channel_id=1, source_target_pairs={{0,1},{1,3},{2,0},{3,2},{4,5},{5,7},{6,4},{7,6},{8,9},{9,11},{10,8... | collective-permute-start | bytes 1179656 | tf_op jit(solution)/shard_map/ppermute | solution.py:837
  382.2 38.9 %collective-permute-start.41 = (bf16[3,128,768]{2,1,0:T(8,128)(2,1)S(1)}, bf16[3,128,768]{2,1,0:T(8,128)(2,1)S(1)}, u32[]{:S(2)}, u32[]{:S(2)}) collective-permute-start(bf16[3,128,768]{2,1,0:T(8,128)(2,1)S(1)} %constant_dynamic-slice_fusion.3), channel_id=1, source_target_pairs={{0,0},{1,2},{2,1},{3,3},{4,4},{5,6},{6,5},{7,7},{8,8},{9,10},{10,9... | collective-permute-start | bytes 1769480 | tf_op jit(solution)/shard_map/ppermute | solution.py:837
  394.7 44.9 %collective-permute-start.43 = (bf16[192,1536]{1,0:T(8,128)(2,1)S(1)}, bf16[192,1536]{1,0:T(8,128)(2,1)S(1)}, u32[]{:S(2)}, u32[]{:S(2)}) collective-permute-start(bf16[192,1536]{1,0:T(8,128)(2,1)S(1)} %fusion.19.refs_5_), channel_id=1, source_target_pairs={{0,4},{1,5},{2,6},{3,7},{4,0},{5,1},{6,2},{7,3},{8,12},{9,13},{10,... | collective-permute-start | bytes 1769480 | tf_op jit(solution)/shard_map/ppermute | solution.py:837
  407.9 29.1 %collective-permute-start.44 = (bf16[192,1536]{1,0:T(8,128)(2,1)S(1)}, bf16[192,1536]{1,0:T(8,128)(2,1)S(1)}, u32[]{:S(2)}, u32[]{:S(2)}) collective-permute-start(bf16[192,1536]{1,0:T(8,128)(2,1)S(1)} %fusion.18.refs_9_), channel_id=1, source_target_pairs={{0,4},{1,5},{2,6},{3,7},{4,0},{5,1},{6,2},{7,3},{8,12},{9,13},{10,... | collective-permute-start | bytes 1769480 | tf_op jit(solution)/shard_map/ppermute | solution.py:837
  408.3 37.2 %collective-permute-start.47 = (bf16[384,1536]{1,0:T(8,128)(2,1)S(1)}, bf16[384,1536]{1,0:T(8,128)(2,1)S(1)}, u32[]{:S(2)}, u32[]{:S(2)}) collective-permute-start(bf16[384,1536]{1,0:T(8,128)(2,1)S(1)} %add_convert_fusion.refs_8_), channel_id=1, source_target_pairs={{0,1},{1,0},{2,3},{3,2},{4,5},{5,4},{6,7},{7,6},{8,9},{9,8},{10,11... | collective-permute-start | bytes 3538952 | tf_op jit(solution)/shard_map/ppermute | solution.py:837
  418.6 57.6 %collective-permute-start.59 = (bf16[48,4608]{1,0:T(8,128)(2,1)S(1)}, bf16[48,4608]{1,0:T(8,128)(2,1)}, u32[]{:S(2)}, u32[]{:S(2)}) collective-permute-start(bf16[48,4608]{1,0:T(8,128)(2,1)S(1)} %slice.470.refs_10_), channel_id=1, source_target_pairs={{0,16},{1,17},{2,18},{3,19},{4,20},{5,21},{6,22},{7,23},{8,24},{9,... | collective-permute-start | bytes 1327112 | tf_op jit(solution)/shard_map/ppermute | solution.py:837
  421.1 22.8 %collective-permute-start.45 = (bf16[384,1536]{1,0:T(8,128)(2,1)S(1)}, bf16[384,1536]{1,0:T(8,128)(2,1)S(1)}, u32[]{:S(2)}, u32[]{:S(2)}) collective-permute-start(bf16[384,1536]{1,0:T(8,128)(2,1)S(1)} %get-tuple-element.276), channel_id=1, source_target_pairs={{0,2},{1,3},{2,0},{3,1},{4,6},{5,7},{6,4},{7,5},{8,10},{9,11},{10,... | collective-permute-start | bytes 3538952 | tf_op jit(solution)/shard_map/ppermute | solution.py:837
  437.0 6.9 %collective-permute-start.42 = (bf16[640,768]{1,0:T(8,128)(2,1)S(1)}, bf16[640,768]{1,0:T(8,128)(2,1)S(1)}, u32[]{:S(2)}, u32[]{:S(2)}) collective-permute-start(bf16[640,768]{1,0:T(8,128)(2,1)S(1)} %get-tuple-element.272), channel_id=1, source_target_pairs={{0,2},{1,3},{2,0},{3,1},{4,6},{5,7},{6,4},{7,5},{8,10},{9,11},{10,... | collective-permute-start | bytes 2949128 | tf_op jit(solution)/shard_map/ppermute | solution.py:837
  442.7 23.2 %collective-permute-start.57 = (bf16[96,3072]{1,0:T(8,128)(2,1)S(1)}, bf16[96,3072]{1,0:T(8,128)(2,1)}, u32[]{:S(2)}, u32[]{:S(2)}) collective-permute-start(bf16[96,3072]{1,0:T(8,128)(2,1)S(1)} %fusion.13.refs_5_), channel_id=1, source_target_pairs={{0,8},{1,9},{2,10},{3,11},{4,12},{5,13},{6,14},{7,15},{8,0},{9,1},... | collective-permute-start | bytes 1769480 | tf_op jit(solution)/shard_map/ppermute | solution.py:837
  447.6 15.5 %collective-permute-start.48 = (bf16[192,1536]{1,0:T(8,128)(2,1)}, bf16[192,1536]{1,0:T(8,128)(2,1)}, u32[]{:S(2)}, u32[]{:S(2)}) collective-permute-start(bf16[192,1536]{1,0:T(8,128)(2,1)} %add_convert_fusion.3), channel_id=1, source_target_pairs={{0,4},{1,5},{2,6},{3,7},{4,0},{5,1},{6,2},{7,3},{8,12},{9,13},{10,... | collective-permute-start | bytes 1769480 | tf_op jit(solution)/shard_map/ppermute | solution.py:837
  449.6 1.2 collective-permute-start.49
  450.8 3.9 collective-permute-start.50
  451.7 34.3 %collective-permute-start.46 = (bf16[2,128,768]{2,1,0:T(8,128)(2,1)}, bf16[2,128,768]{2,1,0:T(8,128)(2,1)S(1)}, u32[]{:S(2)}, u32[]{:S(2)}) collective-permute-start(bf16[2,128,768]{2,1,0:T(8,128)(2,1)} %constant_dynamic-slice_fusion.2), channel_id=1, source_target_pairs={{0,1},{1,3},{2,0},{3,2},{4,5},{5,7},{6,4},{7,6},{8,9},{9,11},{10,8... | collective-permute-start | bytes 1179656 | tf_op jit(solution)/shard_map/ppermute | solution.py:837
  454.8 32.1 %collective-permute-start.53 = (bf16[3,128,768]{2,1,0:T(8,128)(2,1)}, bf16[3,128,768]{2,1,0:T(8,128)(2,1)S(1)}, u32[]{:S(2)}, u32[]{:S(2)}) collective-permute-start(bf16[3,128,768]{2,1,0:T(8,128)(2,1)} %constant_dynamic-slice_fusion.1), channel_id=1, source_target_pairs={{0,0},{1,2},{2,1},{3,3},{4,4},{5,6},{6,5},{7,7},{8,8},{9,10},{10,9... | collective-permute-start | bytes 1769480 | tf_op jit(solution)/shard_map/ppermute | solution.py:837
  464.9 11.2 %collective-permute-start.51 = (bf16[96,1536]{1,0:T(8,128)(2,1)S(1)}, bf16[96,1536]{1,0:T(8,128)(2,1)S(1)}, u32[]{:S(2)}, u32[]{:S(2)}) collective-permute-start(bf16[96,1536]{1,0:T(8,128)(2,1)S(1)} %slice.472), channel_id=1, source_target_pairs={{0,8},{1,9},{2,10},{3,11},{4,12},{5,13},{6,14},{7,15},{8,0},{9,1},... | collective-permute-start | bytes 884744 | tf_op jit(solution)/shard_map/ppermute | solution.py:837
  465.9 4.1 collective-permute-start.52
  470.0 14.4 %collective-permute-start.58 = (bf16[48,3072]{1,0:T(8,128)(2,1)S(1)}, bf16[48,3072]{1,0:T(8,128)(2,1)S(1)}, u32[]{:S(2)}, u32[]{:S(2)}) collective-permute-start(bf16[48,3072]{1,0:T(8,128)(2,1)S(1)} %slice.471), channel_id=1, source_target_pairs={{0,16},{1,17},{2,18},{3,19},{4,20},{5,21},{6,22},{7,23},{8,24},{9,... | collective-permute-start | bytes 884744 | tf_op jit(solution)/shard_map/ppermute | solution.py:837
  485.9 8.0 %collective-permute-start.54 = (bf16[4,8,1536]{2,1,0:T(8,128)(2,1)S(1)}, bf16[4,8,1536]{2,1,0:T(8,128)(2,1)S(1)}, u32[]{:S(2)}, u32[]{:S(2)}) collective-permute-start(bf16[4,8,1536]{2,1,0:T(8,128)(2,1)S(1)} %constant_dynamic-update-slice_fusion), channel_id=1, source_target_pairs={{0,8},{1,9},{2,10},{3,11},{4,12},{5,13},{6,14},{7,15},{8,0},{9,1},... | collective-permute-start | bytes 294920 | tf_op jit(solution)/shard_map/ppermute | solution.py:837
  489.2 17.1 %collective-permute-start.56 = (bf16[48,1536]{1,0:T(8,128)(2,1)S(1)}, bf16[48,1536]{1,0:T(8,128)(2,1)S(1)}, u32[]{:S(2)}, u32[]{:S(2)}) collective-permute-start(bf16[48,1536]{1,0:T(8,128)(2,1)S(1)} %slice.473), channel_id=1, source_target_pairs={{0,16},{1,17},{2,18},{3,19},{4,20},{5,21},{6,22},{7,23},{8,24},{9,... | collective-permute-start | bytes 442376 | tf_op jit(solution)/shard_map/ppermute | solution.py:837
  493.9 12.4 %collective-permute-start.55 = (bf16[8,8,1536]{2,1,0:T(8,128)(2,1)S(1)}, bf16[8,8,1536]{2,1,0:T(8,128)(2,1)S(1)}, u32[]{:S(2)}, u32[]{:S(2)}) collective-permute-start(bf16[8,8,1536]{2,1,0:T(8,128)(2,1)S(1)} %pad_maximum_fusion.5), channel_id=1, source_target_pairs={{0,16},{1,17},{2,18},{3,19},{4,20},{5,21},{6,22},{7,23},{8,24},{9,... | collective-permute-start | bytes 589832 | tf_op jit(solution)/shard_map/ppermute | solution.py:837
  (182 other events, 1075.4 us)
Sparse Core Ops, SparseCore 0:
  42.2 74.3 all-gather.4
  367.2 76.9 all-gather.6

commit v4 on v3

--- a/solution.py
+++ b/solution.py
@@ -20,7 +20,8 @@
 f32 = jnp.float32
 bf16 = jnp.bfloat16
 ALL = ("dp", "tensor")
-VMEM_BYTES = 26 * 1024 * 1024
+VMEM_BYTES = 24 * 1024 * 1024
+CHUNK = 1024
 LIGHT = 2000
 
 
@@ -206,7 +207,7 @@
     return jnp.concatenate([jnp.where(low, rows, zero), jnp.where(low, zero, rows)], axis=0)
 
 
-def attend_body(kind, q, k, v, out):
+def attend_body(kind, q, k, v, out, log_total):
     rows = q.shape[1]
     low = lax.broadcasted_iota(jnp.int32, (1, 128), 1) < HEAD_DIM
     scaling = HEAD_DIM ** (-0.5)
@@ -219,8 +220,12 @@
             at = pl.ds(start + part * tiles, tiles)
             pair = two_heads((q[at].reshape(size, 128) * scaling).astype(bf16), low)
             scores = dot_cols(pair, keys)
-            shifted = jnp.exp(scores - jnp.max(scores, axis=-1, keepdims=True))
+            highest = jnp.max(scores, axis=-1, keepdims=True)
+            shifted = jnp.exp(scores - highest)
             total = jnp.sum(shifted, axis=-1, keepdims=True)
+            log_rows = highest + jnp.log(total)
+            log_both = jnp.where(low, log_rows[:size], log_rows[size:])
+            log_total[at] = log_both.reshape(tiles, rows, 128)
             mixed = dot(shifted.astype(bf16), values) * (1.0 / total)
             out[at] = jnp.where(low, mixed[:size], mixed[size:]).astype(bf16).reshape(tiles, rows, 128)
 
@@ -235,42 +240,59 @@
         attend_body,
         (HALF // 128,),
         [(q, own), (k, every), (v, every)],
-        [(q.shape, bf16, own)],
+        [(q.shape, bf16, own), (q.shape, f32, own)],
         scalars=(kind,),
         flops=16 * BLOCKS * rows * 8 * rows * HALF,
         deps=deps,
-    )[0]
-
-
-def attend_back_body(kind, q, k, v, d_out, dq, dk, dv, acc_k, acc_v):
+    )
+
+
+def attend_back_body(kind, q, k, v, d_out, mixed, log_total, dq, dk, dv, acc_k, acc_v):
     rows = q.shape[1]
     low = lax.broadcasted_iota(jnp.int32, (1, 128), 1) < HEAD_DIM
     scaling = HEAD_DIM ** (-0.5)
+    head = lax.broadcasted_iota(jnp.int32, (8, 128), 0)
+    lane = lax.broadcasted_iota(jnp.int32, (8, 128), 1)
+    first_lane = (lane == head * HEAD_DIM).astype(f32)
+    own_lanes = (lane // HEAD_DIM == head).astype(f32)
+
+    def as_row(pick_lanes, value):
+        both = lax.dot_general(
+            pick_lanes, value, (((1,), (1,)), ((), ())), precision=lax.Precision.HIGHEST
+        )
+        return jnp.concatenate([both[0:1], both[1:2]], axis=1)
 
     def one_sequence(start, count, tiles):
         key_rows = 2 * count * rows
         keys = k[:, pl.ds(start, count)].reshape(key_rows, 128)
         values = v[:, pl.ds(start, count)].reshape(key_rows, 128)
         size = tiles * rows
+        chunk = min(key_rows, CHUNK)
         for part in range(count // tiles):
             at = pl.ds(start + part * tiles, tiles)
             pair = two_heads((q[at].reshape(size, 128) * scaling).astype(bf16), low)
-            d_pair = two_heads(d_out[at].reshape(size, 128), low)
-            scores = dot_cols(keys, pair)
-            shifted = jnp.exp(scores - jnp.max(scores, axis=0, keepdims=True))
-            probs = shifted * (1.0 / jnp.sum(shifted, axis=0, keepdims=True))
-            d_probs = dot_cols(values, d_pair)
-            row_sum = jnp.sum(probs * d_probs, axis=0, keepdims=True)
-            d_scores = (probs * (d_probs - row_sum)).astype(bf16)
-            add_v = dot(probs.astype(bf16), d_pair)
-            add_k = dot(d_scores, pair)
-            if part == 0:
-                acc_v[:key_rows] = add_v
-                acc_k[:key_rows] = add_k
-            else:
-                acc_v[:key_rows] += add_v
-                acc_k[:key_rows] += add_k
-            both = dot_rows(d_scores, keys) * scaling
+            d_rows = d_out[at].reshape(size, 128)
+            d_pair = two_heads(d_rows, low)
+            log_row = as_row(first_lane, log_total[at].reshape(size, 128))
+            product = d_rows.astype(f32) * mixed[at].reshape(size, 128).astype(f32)
+            row_sum = as_row(own_lanes, product)
+            both = None
+            for begin in range(0, key_rows, chunk):
+                here = slice(begin, begin + chunk)
+                probs = jnp.exp(dot_cols(keys[here], pair) - log_row)
+                d_probs = dot_cols(values[here], d_pair)
+                d_scores = (probs * (d_probs - row_sum)).astype(bf16)
+                add_v = dot(probs.astype(bf16), d_pair)
+                add_k = dot(d_scores, pair)
+                if part == 0:
+                    acc_v[here] = add_v
+                    acc_k[here] = add_k
+                else:
+                    acc_v[here] += add_v
+                    acc_k[here] += add_k
+                term = dot_rows(d_scores, keys[here])
+                both = term if both is None else both + term
+            both = both * scaling
             dq[at] = jnp.where(low, both[:size], both[size:]).astype(bf16).reshape(tiles, rows, 128)
         dk[:, pl.ds(start, count)] = acc_k[:key_rows].astype(bf16).reshape(2, count, rows, 128)
         dv[:, pl.ds(start, count)] = acc_v[:key_rows].astype(bf16).reshape(2, count, rows, 128)
@@ -278,14 +300,21 @@
     by_sequence(kind[0], one_sequence, 128 // rows)
 
 
-def attend_back(kind, q, k, v, d_out, deps=()):
+def attend_back(kind, q, k, v, d_out, mixed, log_total, deps=()):
     rows = q.shape[1]
     own = pl.BlockSpec((BLOCKS, rows, 128), lambda p, *_: (0, 0, p))
     every = pl.BlockSpec((2, BLOCKS, rows, 128), lambda p, *_: (0, 0, 0, p))
     return run(
         attend_back_body,
         (HALF // 128,),
-        [(q, own), (k, every), (v, every), (d_out, own)],
+        [
+            (q, own),
+            (k, every),
+            (v, every),
+            (d_out, own),
+            (mixed, own),
+            (log_total, own),
+        ],
         [(q.shape, bf16, own), (k.shape, bf16, every), (v.shape, bf16, every)],
         scratch=[pltpu.VMEM((8 * rows, 128), f32), pltpu.VMEM((8 * rows, 128), f32)],
         scalars=(kind,),
@@ -1010,7 +1039,7 @@
     normed_one, *near_one = project_first(own, oth, tab_one, wq_one)
     ups_one = Far(part_of(up_first, 1, 1), 1, (own,))
     downs_one = Far(part_of(down_first, 0, 2), 2, (own,))
-    mixed_one_n = attend(kind, *near_one)
+    mixed_one_n, log_one_n = attend(kind, *near_one)
     w_parts = (w_near, send(after(w_near, mixed_one_n), core_swap))
     w_two_far = lax.all_gather(
         after(piece_two, own)[None],
@@ -1025,7 +1054,7 @@
     w_one_far, *far_one = project_parts(
         place_ref, normed_one, w_parts, deps=(mixed_one_n,)
     )
-    mixed_one_r = attend(kind, *far_one)
+    mixed_one_r, log_one_r = attend(kind, *far_one)
     ups_one.hop(mixed_one_r)
     downs_one.hop(mixed_one_r)
     attn_one, middle_one, normed_mlp_one, u_one_n, act_one_n, acc = feed_near(
@@ -1043,9 +1072,9 @@
     routed = pick(spot_all[:, None], first_own, first_oth)
     routed_own, routed_oth = routed.reshape(2, BLOCKS, KEEP // (2 * BLOCKS), D)
     normed_two, *near_two = project_first(routed_own, routed_oth, tab_two, wq_two)
-    mixed_two_n = attend(kind, *near_two)
+    mixed_two_n, log_two_n = attend(kind, *near_two)
     far_two = project_next(normed_two, w_two_far, deps=(mixed_two_n,))
-    mixed_two_r = attend(kind, *far_two)
+    mixed_two_r, log_two_r = attend(kind, *far_two)
     cot_own = owned(*cot_parts, mixed_two_r)
     cot_oth = send(cot_own, core_swap)
     attn_two, middle_two, normed_mlp_two, u_two_n, act_two_n, acc = feed_near(
@@ -1074,13 +1103,13 @@
     )
     up_two = Total().cores(g_keep, g_send)
     sent = down_two.far(d_mix_r)
-    grads_r = attend_back(kind, *far_two, d_mix_r, deps=sent)
+    grads_r = attend_back(kind, *far_two, d_mix_r, mixed_two_r, log_two_r, deps=sent)
     sent = up_two.far(grads_r[0])
     qr_keep, qr_send, normed_t, acc = qkv_back(
         True, 1, grads_r, w_two_far, normed_two, order, None, None, p_keep, p_send, deps=sent
     )
     qkv_two = Total().cores_far(qr_keep, qr_send)
-    grads_n = attend_back(kind, *near_two, d_mix_n, deps=(acc, down_two.got))
+    grads_n = attend_back(kind, *near_two, d_mix_n, mixed_two_n, log_two_n, deps=(acc, down_two.got))
     sent = qkv_two.far(grads_n[0])
     qn_keep, qn_send, d_own, d_oth = qkv_back(
         False, 0, grads_n, wq_two, normed_two, None, normed_t, acc, p_keep, p_send, deps=sent
@@ -1131,7 +1160,7 @@
         axis=0,
         tiled=True,
     )
-    grads_r = attend_back(kind, *far_one, d_mix_r, deps=sent)
+    grads_r = attend_back(kind, *far_one, d_mix_r, mixed_one_r, log_one_r, deps=sent)
     rest_two = Rest(
         jnp.concatenate([t.sum(grads_r[0]) for t in (mlp_rest_two, qkv_rest_two)], axis=1)
     )
@@ -1142,7 +1171,7 @@
     )
     qkv_one = Total().cores_far(qr_keep, qr_send)
     sent = down_one.near(acc)
-    grads_n = attend_back(kind, *near_one, d_mix_n, deps=sent)
+    grads_n = attend_back(kind, *near_one, d_mix_n, mixed_one_n, log_one_n, deps=sent)
     done = grads_n[0]
     sent = (*qkv_one.far(done), *up_one.near(done), *rest_two.next(done))
     qn_keep, qn_send, d_own, d_oth = qkv_back(

time: 522 us -> 521 us (level)
  starting transfers between devices: 81.8 us -> 66.2 us
  Pallas kernels: 177 us -> 184 us
    ppermute x60, starting transfers between devices: 81.2 us -> 65.6 us  [send(): return lax.ppermute(value, ALL, pairs)]
    pallas_call x30, Pallas kernels: 177 us -> 184 us  [run(): pl.pallas_call(step, grid_spec=pltpu.PrefetchScalarGridSpec(num_scalar_pr...]
    unnamed x372 -> x392, local copies, waits for them, and re-layouts: 68.8 us -> 73.9 us
  transfers between devices with their start and end apart: 62 -> 62, of which waited for: 18 -> 19; matrix products, arithmetic and copies ran while one was open for 15% -> 15% of each run, Pallas kernels for 33% -> 34%
where the time goes in v4:
time: 521 us; the launch traced here: 514 us
  Pallas kernels  184 us (35%)
  local copies, waits for them, and re-layouts  110 us (21%)
  waiting for transfers between devices  84.1 us (16%)
  starting transfers between devices  66.2 us (13%)
  other arithmetic  37.1 us (7%)
  between operations  19.5 us (4%)
  matrix products  13.4 us (3%)
    pallas_call x30, Pallas kernels, run(): pl.pallas_call(step, grid_spec=pltpu.PrefetchScalarGridSpec(num_scalar_pr...  184 us
    ppermute x60, waiting for transfers between devices, send(): return lax.ppermute(value, ALL, pairs)  84 us
    unnamed x392, local copies, waits for them, and re-layouts  73.9 us
    ppermute x60, starting transfers between devices, send(): return lax.ppermute(value, ALL, pairs)  65.6 us
  transfers between devices with their start and end apart: 62, of which 19 were waited for; matrix products, arithmetic and copies ran while one was open for 15% of the time, Pallas kernels for 34%

profile of v4, /device:TPU:0, one launch (start us, length us, event | category | flops | bytes accessed | tf_op | source)
XLA Modules:
  0.0 513.9 jit_solution(13115797853715095771)
XLA Ops:
  10.1 4.3 collective-permute-start.3
  26.1 3.3 collective-permute-start.4
  29.4 4.0 fusion.65
  33.5 4.1 fusion.66
  37.6 1.8 collective-permute-done.4
  40.2 1.8 maximum_select_fusion.refs_0_.refs_4_.refs_2_
  43.8 2.5 collective-permute-start.6
  49.6 4.0 shard_map.246
  54.9 7.0 %shard_map.247 = (bf16[5,128,384]{2,1,0:T(8,128)(2,1)S(1)}, f32[5,128,384]{2,1,0:T(8,128)S(1)}) custom-call(s32[1]{0:T(128)S(6)} %select_n.232.refs_0_, bf16[5,128,384]{2,1,0:T(8,128)(2,1)S(1)} %get-tuple-element.168.refs_1_, bf16[2,5,128,384]{3,2,1,0:T(8,128)(2,1)S(1)} %get-tuple-element.169.refs_2_, bf16[2,5,128,384]{3,2,1,0:T(8,128)(2,1)S(1)} %get-tuple-element.170.refs_3_), custom_call_target="tpu_custom_call" | custom-call | flops 2013266 | bytes 1967 | tf_op jit(solution)/shard_map/pallas_call | solution.py:79
  63.8 8.9 %collective-permute-done.6.refs_2_ = bf16[4,384,384]{2,1,0:T(8,128)(2,1)} collective-permute-done((bf16[4,384,384]{2,1,0:T(8,128)(2,1)S(1)}, bf16[4,384,384]{2,1,0:T(8,128)(2,1)}, u32[]{:S(2)}, u32[]{:S(2)}) %collective-permute-start.6) | collective-permute-done | bytes 1179680 | tf_op jit(solution)/shard_map/ppermute | solution.py:866
  77.2 4.5 shard_map.248
  81.8 7.0 %shard_map.249 = (bf16[5,128,384]{2,1,0:T(8,128)(2,1)S(1)}, f32[5,128,384]{2,1,0:T(8,128)S(1)}) custom-call(s32[1]{0:T(128)S(6)} %select_n.232.refs_0_, bf16[5,128,384]{2,1,0:T(8,128)(2,1)S(1)} %get-tuple-element.175.refs_1_, bf16[2,5,128,384]{3,2,1,0:T(8,128)(2,1)S(1)} %get-tuple-element.176.refs_2_, bf16[2,5,128,384]{3,2,1,0:T(8,128)(2,1)S(1)} %get-tuple-element.177.refs_3_), custom_call_target="tpu_custom_call" | custom-call | flops 2013266 | bytes 1967 | tf_op jit(solution)/shard_map/pallas_call | solution.py:79
  92.6 2.1 collective-permute-start.14
  94.7 7.7 %collective-permute-done.8.refs_5_.refs_9_ = bf16[768,384]{1,0:T(8,128)(2,1)S(1)} collective-permute-done((bf16[768,384]{1,0:T(8,128)(2,1)S(1)}, bf16[768,384]{1,0:T(8,128)(2,1)S(1)}, u32[]{:S(2)}, u32[]{:S(2)}) %collective-permute-start.8) | collective-permute-done | bytes 589856 | tf_op jit(solution)/shard_map/ppermute | solution.py:866
  104.5 6.1 %shard_map.250 = (bf16[5,128,768]{2,1,0:T(8,128)(2,1)S(1)}, f32[5,128,768]{2,1,0:T(8,128)S(1)}, bf16[5,128,768]{2,1,0:T(8,128)(2,1)S(1)}, bf16[2,640,768]{2,1,0:...) custom-call(bf16[5,128,384]{2,1,0:T(8,128)(2,1)S(1)} %copy-done.31, ...), custom_call_target="tpu_custom_call" | custom-call | flops 1887437 | bytes 9779 | tf_op jit(solution)/shard_map/pallas_call | solution.py:79
  114.2 4.9 collective-permute-done.14.refs_11_.refs_15_
  122.0 5.6 %shard_map.251 = (bf16[2,640,768]{2,1,0:T(8,128)(2,1)S(1)}, bf16[2,640,768]{2,1,0:T(8,128)(2,1)S(1)}, bf16[5,128,768]{2,1,0:T(8,128)(2,1)S(1)}, bf16[5,128,768]{2,1,0:T(8,128)(2,1)S(1)}) custom-call(s32[1]{0:T(128)} %bitcast.refs_0_, bf16[5,128,768]{2,1,0:T(8,128)(2,1)S(1)} %get-tuple-element.180.refs_1_.refs_4_, f32[640,768]{1,0:T(8,128)S(1)} %get-tuple-element.181.refs_2_, ...), custom_call_target="tpu_custom_call" | custom-call | flops 1509950 | bytes 7813 | tf_op jit(solution)/shard_map/pallas_call | solution.py:79
  131.3 2.1 slice.277
  133.4 1.8 slice.278
  135.2 6.0 %collective-permute-start.20 = (bf16[3,128,768]{2,1,0:T(8,128)(2,1)}, bf16[3,128,768]{2,1,0:T(8,128)(2,1)}, u32[]{:S(2)}, u32[]{:S(2)}) collective-permute-start(bf16[3,128,768]{2,1,0:T(8,128)(2,1)} %slice.277), channel_id=1, source_target_pairs={{0,0},{1,2},{2,1},{3,3},{4,4},{5,6},{6,5},{7,7},{8,8},{9,10},{10,9... | collective-permute-start | bytes 1769480 | tf_op jit(solution)/shard_map/ppermute | solution.py:866
  141.7 1.8 shard_map.252
  144.9 2.6 shard_map.253
  147.6 5.9 %shard_map.254 = (bf16[5,64,384]{2,1,0:T(8,128)(2,1)S(1)}, f32[5,64,384]{2,1,0:T(8,128)S(1)}) custom-call(s32[1]{0:T(128)S(6)} %select_n.232.refs_0_, bf16[5,64,384]{2,1,0:T(8,128)(2,1)S(1)} %get-tuple-element.192.refs_1_, bf16[2,5,64,384]{3,2,1,0:T(8,128)(2,1)S(1)} %get-tuple-element.193.refs_2_, bf16[2,5,64,384]{3,2,1,0:T(8,128)(2,1)S(1)} %get-tuple-element.194.refs_3_), custom_call_target="tpu_custom_call" | custom-call | flops 503317 | bytes 984 | tf_op jit(solution)/shard_map/pallas_call | solution.py:79
  156.5 3.1 copy-done
  159.6 2.0 shard_map.255
  161.7 5.9 %shard_map.256 = (bf16[5,64,384]{2,1,0:T(8,128)(2,1)S(1)}, f32[5,64,384]{2,1,0:T(8,128)S(1)}) custom-call(s32[1]{0:T(128)S(6)} %select_n.232.refs_0_, bf16[5,64,384]{2,1,0:T(8,128)(2,1)S(1)} %get-tuple-element.196.refs_1_, bf16[2,5,64,384]{3,2,1,0:T(8,128)(2,1)S(1)} %get-tuple-element.197.refs_2_, bf16[2,5,64,384]{3,2,1,0:T(8,128)(2,1)S(1)} %get-tuple-element.198.refs_3_), custom_call_target="tpu_custom_call" | custom-call | flops 503317 | bytes 984 | tf_op jit(solution)/shard_map/pallas_call | solution.py:79
  167.7 2.9 maximum_select_fusion.1
  172.9 6.0 %collective-permute-start.18 = (bf16[3,128,768]{2,1,0:T(8,128)(2,1)}, bf16[3,128,768]{2,1,0:T(8,128)(2,1)}, u32[]{:S(2)}, u32[]{:S(2)}) collective-permute-start(bf16[3,128,768]{2,1,0:T(8,128)(2,1)} %constant_dynamic-slice_fusion.5), channel_id=1, source_target_pairs={{0,0},{1,2},{2,1},{3,3},{4,4},{5,6},{6,5},{7,7},{8,8},{9,10},{10,9... | collective-permute-start | bytes 1769480 | tf_op jit(solution)/shard_map/ppermute | solution.py:866
  178.9 1.8 constant_dynamic-slice_fusion.6
  181.6 3.0 copy-done.1
  190.9 3.6 shard_map.257
  197.0 3.6 shard_map.258
  200.7 2.7 shard_map.259
  203.4 4.9 shard_map.260
  208.9 13.6 %shard_map.261 = (bf16[2,384,1536]{2,1,0:T(8,128)(2,1)S(1)}, bf16[2,384,1536]{2,1,0:T(8,128)(2,1)S(1)}, bf16[2,384,384]{2,1,0:T(8,128)(2,1)S(1)}, bf16[2,384,384...) custom-call(s32[1]{0:T(128)} %constant.205.clone.1.refs_0_, ...), custom_call_target="tpu_custom_call" | custom-call | flops 3019899 | bytes 41554 | tf_op jit(solution)/shard_map/pallas_call | solution.py:79
  227.6 8.4 %shard_map.262 = (bf16[5,64,384]{2,1,0:T(8,128)(2,1)S(1)}, bf16[2,5,64,384]{3,2,1,0:T(8,128)(2,1)S(1)}, bf16[2,5,64,384]{3,2,1,0:T(8,128)(2,1)S(1)}) custom-call(s32[1]{0:T(128)S(6)} %select_n.232.refs_0_, bf16[5,64,384]{2,1,0:T(8,128)(2,1)S(1)} %copy-done.147, bf16[2,5,64,384]{3,2,1,0:T(8,128)(2,1)S(1)} %copy-done.118, ...), custom_call_target="tpu_custom_call" | custom-call | flops 1258292 | bytes 1721 | tf_op jit(solution)/shard_map/pallas_call | solution.py:79
  238.6 5.6 %shard_map.263 = (bf16[384,1536]{1,0:T(8,128)(2,1)S(1)}, bf16[384,1536]{1,0:T(8,128)(2,1)}, bf16[768,640]{1,0:T(8,128)(2,1)S(1)}, f32[640,768]{1,0:T(8,128)S(1)}) custom-call(bf16[5,64,384]{2,1,0:T(8,128)(2,1)S(1)} %get-tuple-element.224.refs_0_, bf16[2,5,64,384]{3,2,1,0:T(8,128)(2,1)S(1)} %get-tuple-element.225.refs_1_, ...), custom_call_target="tpu_custom_call" | custom-call | flops 1321206 | bytes 8479 | tf_op jit(solution)/shard_map/pallas_call | solution.py:79
  248.5 6.8 %collective-permute-done.25.refs_8_ = bf16[384,1536]{1,0:T(8,128)(2,1)} collective-permute-done((bf16[384,1536]{1,0:T(8,128)(2,1)}, bf16[384,1536]{1,0:T(8,128)(2,1)}, u32[]{:S(2)}, u32[]{:S(2)}) %collective-permute-start.25) | collective-permute-done | bytes 1179680 | tf_op jit(solution)/shard_map/ppermute | solution.py:866
  262.9 8.2 %shard_map.264 = (bf16[5,64,384]{2,1,0:T(8,128)(2,1)S(1)}, bf16[2,5,64,384]{3,2,1,0:T(8,128)(2,1)S(1)}, bf16[2,5,64,384]{3,2,1,0:T(8,128)(2,1)S(1)}) custom-call(s32[1]{0:T(128)S(6)} %select_n.232.refs_0_, bf16[5,64,384]{2,1,0:T(8,128)(2,1)S(1)} %copy-done.145, bf16[2,5,64,384]{3,2,1,0:T(8,128)(2,1)S(1)} %copy-done.124, ...), custom_call_target="tpu_custom_call" | custom-call | flops 1258292 | bytes 1721 | tf_op jit(solution)/shard_map/pallas_call | solution.py:79
  273.2 4.3 shard_map.265
  290.5 2.4 shard_map.267.refs_5_
  294.3 2.8 shard_map.268
  297.2 7.4 %shard_map.269 = (bf16[2,384,1536]{2,1,0:T(8,128)(2,1)S(1)}, bf16[2,384,1536]{2,1,0:T(8,128)(2,1)}, bf16[640,768]{1,0:T(8,128)(2,1)S(1)}, f32[5,1,768]{2,1,0:T(1,128)S(1)}) custom-call(s32[1]{0:T(128)} %bitcast.refs_0_, bf16[5,128,768]{2,1,0:T(8,128)(2,1)S(1)} %bitcast.166, f32[5,6,768]{2,1,0:T(8,128)S(1)} %copy-done.38, ...), custom_call_target="tpu_custom_call" | custom-call | flops 1887437 | bytes 6444 | tf_op jit(solution)/shard_map/pallas_call | solution.py:79
  305.1 2.1 fusion.4
  307.3 2.2 fusion.5
  311.6 23.2 %shard_map.270 = (bf16[2,384,1536]{2,1,0:T(8,128)(2,1)S(1)}, bf16[2,384,1536]{2,1,0:T(8,128)(2,1)S(1)}, bf16[2,384,384]{2,1,0:T(8,128)(2,1)S(1)}, bf16[2,384,384...) custom-call(s32[1]{0:T(128)} %bitcast.refs_0_, ...), custom_call_target="tpu_custom_call" | custom-call | flops 6039798 | bytes 16683 | tf_op jit(solution)/shard_map/pallas_call | solution.py:79
  338.3 2.1 add_convert_fusion.1
  344.9 11.5 %shard_map.271 = (bf16[5,128,384]{2,1,0:T(8,128)(2,1)S(1)}, bf16[2,5,128,384]{3,2,1,0:T(8,128)(2,1)S(1)}, bf16[2,5,128,384]{3,2,1,0:T(8,128)(2,1)S(1)}) custom-call(s32[1]{0:T(128)S(6)} %select_n.232.refs_0_, bf16[5,128,384]{2,1,0:T(8,128)(2,1)S(1)} %copy-done.114, bf16[2,5,128,384]{3,2,1,0:T(8,128)(2,1)S(1)} %copy-done.49, ...), custom_call_target="tpu_custom_call" | custom-call | flops 5033165 | bytes 3441 | tf_op jit(solution)/shard_map/pallas_call | solution.py:79
  371.4 7.7 %shard_map.272 = (bf16[384,1536]{1,0:T(8,128)(2,1)S(1)}, bf16[384,1536]{1,0:T(8,128)(2,1)S(1)}, bf16[768,1280]{1,0:T(8,128)(2,1)S(1)}, f32[1280,768]{1,0:T(8,128)S(1)}) custom-call(bf16[5,128,384]{2,1,0:T(8,128)(2,1)S(1)} %copy-done.158, bf16[2,5,128,384]{3,2,1,0:T(8,128)(2,1)S(1)} %copy-done.149, bf16[2,5,128,384]{3,2,1,0:T(8,128)(2,1)S(1)} %copy-done.151, ...), custom_call_target="tpu_custom_call" | custom-call | flops 2642412 | bytes 8700 | tf_op jit(solution)/shard_map/pallas_call | solution.py:79
  383.1 11.6 %shard_map.273 = (bf16[5,128,384]{2,1,0:T(8,128)(2,1)S(1)}, bf16[2,5,128,384]{3,2,1,0:T(8,128)(2,1)S(1)}, bf16[2,5,128,384]{3,2,1,0:T(8,128)(2,1)S(1)}) custom-call(s32[1]{0:T(128)S(6)} %select_n.232.refs_0_, bf16[5,128,384]{2,1,0:T(8,128)(2,1)S(1)} %copy-done.122, bf16[2,5,128,384]{3,2,1,0:T(8,128)(2,1)S(1)} %copy-done.53, ...), custom_call_target="tpu_custom_call" | custom-call | flops 5033165 | bytes 3441 | tf_op jit(solution)/shard_map/pallas_call | solution.py:79
  394.8 3.2 collective-permute-start.43
  397.9 4.6 collective-permute-done.39
  405.7 2.1 collective-permute-start.44
  409.5 6.6 %shard_map.274 = (bf16[384,1536]{1,0:T(8,128)(2,1)S(1)}, bf16[384,1536]{1,0:T(8,128)(2,1)S(1)}, f32[640,768]{1,0:T(8,128)S(1)}, bf16[640,768]{1,0:T(8,128)(2,1)S(1)}) custom-call(bf16[5,128,384]{2,1,0:T(8,128)(2,1)S(1)} %get-tuple-element.276.refs_0_, bf16[2,5,128,384]{3,2,1,0:T(8,128)(2,1)S(1)} %get-tuple-element.277.refs_1_, ...), custom_call_target="tpu_custom_call" | custom-call | flops 1887437 | bytes 8307 | tf_op jit(solution)/shard_map/pallas_call | solution.py:79
  416.7 14.8 %collective-permute-done.44 = bf16[192,1536]{1,0:T(8,128)(2,1)S(1)} collective-permute-done((bf16[192,1536]{1,0:T(8,128)(2,1)S(1)}, bf16[192,1536]{1,0:T(8,128)(2,1)S(1)}, u32[]{:S(2)}, u32[]{:S(2)}) %collective-permute-start.44) | collective-permute-done | bytes 589856 | tf_op jit(solution)/shard_map/ppermute | solution.py:866
  434.1 2.0 fusion.17
  437.1 4.6 collective-permute-start.57
  447.1 1.7 collective-permute-start.48
  455.7 4.9 reshape.653
  463.6 1.7 collective-permute-start.52
  467.7 6.0 %collective-permute-done.51 = bf16[96,1536]{1,0:T(8,128)(2,1)S(1)} collective-permute-done((bf16[96,1536]{1,0:T(8,128)(2,1)S(1)}, bf16[96,1536]{1,0:T(8,128)(2,1)S(1)}, u32[]{:S(2)}, u32[]{:S(2)}) %collective-permute-start.51) | collective-permute-done | bytes 294944 | tf_op jit(solution)/shard_map/ppermute | solution.py:866
  475.8 6.8 %collective-permute-done.58 = bf16[48,3072]{1,0:T(8,128)(2,1)S(1)} collective-permute-done((bf16[48,3072]{1,0:T(8,128)(2,1)S(1)}, bf16[48,3072]{1,0:T(8,128)(2,1)S(1)}, u32[]{:S(2)}, u32[]{:S(2)}) %collective-permute-start.58) | collective-permute-done | bytes 294944 | tf_op jit(solution)/shard_map/ppermute | solution.py:866
  487.4 2.2 collective-permute-start.56
  492.0 12.4 %collective-permute-done.55 = bf16[8,8,1536]{2,1,0:T(8,128)(2,1)S(1)} collective-permute-done((bf16[8,8,1536]{2,1,0:T(8,128)(2,1)S(1)}, bf16[8,8,1536]{2,1,0:T(8,128)(2,1)S(1)}, u32[]{:S(2)}, u32[]{:S(2)}) %collective-permute-start.55) | collective-permute-done | bytes 196640 | tf_op jit(solution)/shard_map/ppermute | solution.py:866
  (624 shorter events, 161.7 us)
Async XLA Ops:
  7.2 149.3 %all-gather.5.cloned.1.call-start = ((), (), s32[]{:S(2)}) async-start(), calls=%async_computation | async-start | bytes 7520256 | tf_op jit(solution)/shard_map/all_gather | solution.py:1044
  8.4 16.9 %collective-permute-start.1 = (bf16[3,128,768]{2,1,0:T(8,128)(2,1)S(1)}, bf16[3,128,768]{2,1,0:T(8,128)(2,1)S(1)}, u32[]{:S(2)}, u32[]{:S(2)}) collective-permute-start(bf16[3,128,768]{2,1,0:T(8,128)(2,1)S(1)} %slice.267), channel_id=1, source_target_pairs={{0,0},{1,2},{2,1},{3,3},{4,4},{5,6},{6,5},{7,7},{8,8},{9,10},{10,9... | collective-permute-start | bytes 1769480 | tf_op jit(solution)/shard_map/ppermute | solution.py:866
  10.1 15.2 %collective-permute-start.3 = (bf16[2,128,768]{2,1,0:T(8,128)(2,1)S(1)}, bf16[2,128,768]{2,1,0:T(8,128)(2,1)S(1)}, u32[]{:S(2)}, u32[]{:S(2)}) collective-permute-start(bf16[2,128,768]{2,1,0:T(8,128)(2,1)S(1)} %slice.269), channel_id=1, source_target_pairs={{0,2},{1,0},{2,3},{3,1},{4,6},{5,4},{6,7},{7,5},{8,10},{9,8},{10,1... | collective-permute-start | bytes 1179656 | tf_op jit(solution)/shard_map/ppermute | solution.py:866
  15.2 7.9 %collective-permute-start = (s32[645]{0:T(1024)S(1)}, s32[645]{0:T(1024)S(1)}, u32[]{:S(2)}, u32[]{:S(2)}) collective-permute-start(s32[645]{0:T(1024)S(1)} %pad_add_fusion), channel_id=1, source_target_pairs={{0,0},{1,2},{2,1},{3,3},{4,4},{5,6},{6,5},{7,7},{8,8},{9,10},{10,9... | collective-permute-start | bytes 7748 | tf_op jit(solution)/shard_map/ppermute | solution.py:866
  15.9 7.7 %collective-permute-start.2 = (bf16[5,768]{1,0:T(8,128)(2,1)S(1)}, bf16[5,768]{1,0:T(8,128)(2,1)S(1)}, u32[]{:S(2)}, u32[]{:S(2)}) collective-permute-start(bf16[5,768]{1,0:T(8,128)(2,1)S(1)} %fusion.27), channel_id=1, source_target_pairs={{0,0},{1,2},{2,1},{3,3},{4,4},{5,6},{6,5},{7,7},{8,8},{9,10},{10,9... | collective-permute-start | bytes 23048 | tf_op jit(solution)/shard_map/ppermute | solution.py:866
  26.1 13.3 %collective-permute-start.4 = (bf16[12,48,384]{2,1,0:T(8,128)(2,1)S(1)}, bf16[12,48,384]{2,1,0:T(8,128)(2,1)S(1)}, u32[]{:S(2)}, u32[]{:S(2)}) collective-permute-start(bf16[12,48,384]{2,1,0:T(8,128)(2,1)S(1)} %copy.62), channel_id=1, source_target_pairs={{0,1},{1,0},{2,3},{3,2},{4,5},{5,4},{6,7},{7,6},{8,9},{9,8},{10,11... | collective-permute-start | bytes 1327112 | tf_op jit(solution)/shard_map/ppermute | solution.py:866
  41.9 62.5 %copy-start.6 = (bf16[5,128,768]{2,1,0:T(8,128)(2,1)}, bf16[5,128,768]{2,1,0:T(8,128)(2,1)S(1)}, u32[]{:S(2)}) copy-start(bf16[5,128,768]{2,1,0:T(8,128)(2,1)S(1)} %maximum_select_fusion.refs_0_.refs_4_.refs_2_) | copy-start | bytes 2949124
  42.0 413.7 %all-gather.7.cloned.1.call-start = ((), (), s32[]{:S(2)}) async-start(), calls=%async_computation.1 | async-start | bytes 4460544 | tf_op jit(solution)/shard_map/all_gather | solution.py:1155
  43.8 28.9 %collective-permute-start.6 = (bf16[4,384,384]{2,1,0:T(8,128)(2,1)S(1)}, bf16[4,384,384]{2,1,0:T(8,128)(2,1)}, u32[]{:S(2)}, u32[]{:S(2)}) collective-permute-start(bf16[4,384,384]{2,1,0:T(8,128)(2,1)S(1)} %pad_maximum_fusion.3), channel_id=1, source_target_pairs={{0,1},{1,0},{2,3},{3,2},{4,5},{5,4},{6,7},{7,6},{8,9},{9,8},{10,11... | collective-permute-start | bytes 3538952 | tf_op jit(solution)/shard_map/ppermute | solution.py:866
  46.4 3.2 collective-permute-start.5
  72.7 3.5 collective-permute-start.7
  74.0 18.6 %collective-permute-start.12 = (bf16[384,768]{1,0:T(8,128)(2,1)S(1)}, bf16[384,768]{1,0:T(8,128)(2,1)S(1)}, u32[]{:S(2)}, u32[]{:S(2)}) collective-permute-start(bf16[384,768]{1,0:T(8,128)(2,1)S(1)} %constant_dynamic-slice_fusion.9), channel_id=1, source_target_pairs={{0,1},{1,0},{2,3},{3,2},{4,5},{5,4},{6,7},{7,6},{8,9},{9,8},{10,11... | collective-permute-start | bytes 1769480 | tf_op jit(solution)/shard_map/ppermute | solution.py:866
  75.3 27.1 %collective-permute-start.8 = (bf16[768,384]{1,0:T(8,128)(2,1)S(1)}, bf16[768,384]{1,0:T(8,128)(2,1)S(1)}, u32[]{:S(2)}, u32[]{:S(2)}) collective-permute-start(bf16[768,384]{1,0:T(8,128)(2,1)S(1)} %constant_dynamic-slice_fusion.10), channel_id=1, source_target_pairs={{0,1},{1,0},{2,3},{3,2},{4,5},{5,4},{6,7},{7,6},{8,9},{9,8},{10,11... | collective-permute-start | bytes 1769480 | tf_op jit(solution)/shard_map/ppermute | solution.py:866
  92.6 26.5 %collective-permute-start.14 = (bf16[384,768]{1,0:T(8,128)(2,1)S(1)}, bf16[384,768]{1,0:T(8,128)(2,1)S(1)}, u32[]{:S(2)}, u32[]{:S(2)}) collective-permute-start(bf16[384,768]{1,0:T(8,128)(2,1)S(1)} %collective-permute-done.12.refs_9_.refs_13_), channel_id=1, source_target_pairs={{0,8},{1,9},{2,10},{3,11},{4,12},{5,13},{6,14},{7,15},{8,0},{9,1},... | collective-permute-start | bytes 1769480 | tf_op jit(solution)/shard_map/ppermute | solution.py:866
  102.4 16.7 %collective-permute-start.10 = (bf16[768,384]{1,0:T(8,128)(2,1)S(1)}, bf16[768,384]{1,0:T(8,128)(2,1)S(1)}, u32[]{:S(2)}, u32[]{:S(2)}) collective-permute-start(bf16[768,384]{1,0:T(8,128)(2,1)S(1)} %collective-permute-done.8.refs_5_.refs_9_), channel_id=1, source_target_pairs={{0,4},{1,5},{2,6},{3,7},{4,0},{5,1},{6,2},{7,3},{8,12},{9,13},{10,... | collective-permute-start | bytes 1769480 | tf_op jit(solution)/shard_map/ppermute | solution.py:866
  103.9 15.7 %collective-permute-start.13 = (bf16[384,768]{1,0:T(8,128)(2,1)S(1)}, bf16[384,768]{1,0:T(8,128)(2,1)S(1)}, u32[]{:S(2)}, u32[]{:S(2)}) collective-permute-start(bf16[384,768]{1,0:T(8,128)(2,1)S(1)} %collective-permute-done.12.refs_9_.refs_13_), channel_id=1, source_target_pairs={{0,2},{1,3},{2,0},{3,1},{4,6},{5,7},{6,4},{7,5},{8,10},{9,11},{10,... | collective-permute-start | bytes 1769480 | tf_op jit(solution)/shard_map/ppermute | solution.py:866
  103.9 15.7 %collective-permute-start.9 = (bf16[768,384]{1,0:T(8,128)(2,1)S(1)}, bf16[768,384]{1,0:T(8,128)(2,1)S(1)}, u32[]{:S(2)}, u32[]{:S(2)}) collective-permute-start(bf16[768,384]{1,0:T(8,128)(2,1)S(1)} %collective-permute-done.8.refs_5_.refs_9_), channel_id=1, source_target_pairs={{0,2},{1,3},{2,0},{3,1},{4,6},{5,7},{6,4},{7,5},{8,10},{9,11},{10,... | collective-permute-start | bytes 1769480 | tf_op jit(solution)/shard_map/ppermute | solution.py:866
  119.1 2.0 collective-permute-start.15
  119.1 2.8 collective-permute-start.11
  131.2 10.5 %collective-permute-start.16 = (bf16[640,768]{1,0:T(8,128)(2,1)S(1)}, bf16[640,768]{1,0:T(8,128)(2,1)S(1)}, u32[]{:S(2)}, u32[]{:S(2)}) collective-permute-start(bf16[640,768]{1,0:T(8,128)(2,1)S(1)} %bitcast.161), channel_id=1, source_target_pairs={{0,2},{1,3},{2,0},{3,1},{4,6},{5,7},{6,4},{7,5},{8,10},{9,11},{10,... | collective-permute-start | bytes 2949128 | tf_op jit(solution)/shard_map/ppermute | solution.py:866
  135.2 32.5 %collective-permute-start.20 = (bf16[3,128,768]{2,1,0:T(8,128)(2,1)}, bf16[3,128,768]{2,1,0:T(8,128)(2,1)}, u32[]{:S(2)}, u32[]{:S(2)}) collective-permute-start(bf16[3,128,768]{2,1,0:T(8,128)(2,1)} %slice.277), channel_id=1, source_target_pairs={{0,0},{1,2},{2,1},{3,3},{4,4},{5,6},{6,5},{7,7},{8,8},{9,10},{10,9... | collective-permute-start | bytes 1769480 | tf_op jit(solution)/shard_map/ppermute | solution.py:866
  141.2 26.5 %collective-permute-start.21 = (bf16[2,128,768]{2,1,0:T(8,128)(2,1)}, bf16[2,128,768]{2,1,0:T(8,128)(2,1)}, u32[]{:S(2)}, u32[]{:S(2)}) collective-permute-start(bf16[2,128,768]{2,1,0:T(8,128)(2,1)} %slice.278), channel_id=1, source_target_pairs={{0,2},{1,0},{2,3},{3,1},{4,6},{5,4},{6,7},{7,5},{8,10},{9,8},{10,1... | collective-permute-start | bytes 1179656 | tf_op jit(solution)/shard_map/ppermute | solution.py:866
  170.6 30.1 %collective-permute-start.22 = (bf16[5,128,768]{2,1,0:T(8,128)(2,1)}, bf16[5,128,768]{2,1,0:T(8,128)(2,1)}, u32[]{:S(2)}, u32[]{:S(2)}) collective-permute-start(bf16[5,128,768]{2,1,0:T(8,128)(2,1)} %maximum_select_fusion.1), channel_id=1, source_target_pairs={{0,2},{1,3},{2,0},{3,1},{4,6},{5,7},{6,4},{7,5},{8,10},{9,11},{10,... | collective-permute-start | bytes 2949128 | tf_op jit(solution)/shard_map/ppermute | solution.py:866
  172.9 22.7 %collective-permute-start.18 = (bf16[3,128,768]{2,1,0:T(8,128)(2,1)}, bf16[3,128,768]{2,1,0:T(8,128)(2,1)}, u32[]{:S(2)}, u32[]{:S(2)}) collective-permute-start(bf16[3,128,768]{2,1,0:T(8,128)(2,1)} %constant_dynamic-slice_fusion.5), channel_id=1, source_target_pairs={{0,0},{1,2},{2,1},{3,3},{4,4},{5,6},{6,5},{7,7},{8,8},{9,10},{10,9... | collective-permute-start | bytes 1769480 | tf_op jit(solution)/shard_map/ppermute | solution.py:866
  180.6 13.9 %collective-permute-start.17 = (bf16[2,128,768]{2,1,0:T(8,128)(2,1)}, bf16[2,128,768]{2,1,0:T(8,128)(2,1)}, u32[]{:S(2)}, u32[]{:S(2)}) collective-permute-start(bf16[2,128,768]{2,1,0:T(8,128)(2,1)} %constant_dynamic-slice_fusion.6), channel_id=1, source_target_pairs={{0,1},{1,3},{2,0},{3,2},{4,5},{5,7},{6,4},{7,6},{8,9},{9,11},{10,8... | collective-permute-start | bytes 1179656 | tf_op jit(solution)/shard_map/ppermute | solution.py:866
  208.3 16.5 %collective-permute-start.23 = (bf16[2,384,1536]{2,1,0:T(8,128)(2,1)S(1)}, bf16[2,384,1536]{2,1,0:T(8,128)(2,1)S(1)}, u32[]{:S(2)}, u32[]{:S(2)}) collective-permute-start(bf16[2,384,1536]{2,1,0:T(8,128)(2,1)S(1)} %get-tuple-element.222), channel_id=1, source_target_pairs={{0,2},{1,3},{2,0},{3,1},{4,6},{5,7},{6,4},{7,5},{8,10},{9,11},{10,... | collective-permute-start | bytes 7077896 | tf_op jit(solution)/shard_map/ppermute | solution.py:866
  224.8 11.2 %collective-permute-start.24 = (bf16[2,384,1536]{2,1,0:T(8,128)(2,1)S(1)}, bf16[2,384,1536]{2,1,0:T(8,128)(2,1)S(1)}, u32[]{:S(2)}, u32[]{:S(2)}) collective-permute-start(bf16[2,384,1536]{2,1,0:T(8,128)(2,1)S(1)} %get-tuple-element.230), channel_id=1, source_target_pairs={{0,2},{1,3},{2,0},{3,1},{4,6},{5,7},{6,4},{7,5},{8,10},{9,11},{10,... | collective-permute-start | bytes 7077896 | tf_op jit(solution)/shard_map/ppermute | solution.py:866
  226.3 29.1 %collective-permute-start.25 = (bf16[384,1536]{1,0:T(8,128)(2,1)}, bf16[384,1536]{1,0:T(8,128)(2,1)}, u32[]{:S(2)}, u32[]{:S(2)}) collective-permute-start(bf16[384,1536]{1,0:T(8,128)(2,1)} %fusion.3.refs_7_), channel_id=1, source_target_pairs={{0,1},{1,0},{2,3},{3,2},{4,5},{5,4},{6,7},{7,6},{8,9},{9,8},{10,11... | collective-permute-start | bytes 3538952 | tf_op jit(solution)/shard_map/ppermute | solution.py:866
  247.4 23.6 %collective-permute-start.26 = (bf16[384,1536]{1,0:T(8,128)(2,1)}, bf16[384,1536]{1,0:T(8,128)(2,1)S(1)}, u32[]{:S(2)}, u32[]{:S(2)}) collective-permute-start(bf16[384,1536]{1,0:T(8,128)(2,1)} %get-tuple-element.238), channel_id=1, source_target_pairs={{0,2},{1,3},{2,0},{3,1},{4,6},{5,7},{6,4},{7,5},{8,10},{9,11},{10,... | collective-permute-start | bytes 3538952 | tf_op jit(solution)/shard_map/ppermute | solution.py:866
  247.9 49.2 %collective-permute-start.29 = (bf16[384,1536]{1,0:T(8,128)(2,1)}, bf16[384,1536]{1,0:T(8,128)(2,1)S(1)}, u32[]{:S(2)}, u32[]{:S(2)}) collective-permute-start(bf16[384,1536]{1,0:T(8,128)(2,1)} %copy-done.40), channel_id=1, source_target_pairs={{0,1},{1,0},{2,3},{3,2},{4,5},{5,4},{6,7},{7,6},{8,9},{9,8},{10,11... | collective-permute-start | bytes 3538952 | tf_op jit(solution)/shard_map/ppermute | solution.py:866
  280.7 1.9 collective-permute-start.27
  280.9 9.6 %collective-permute-start.19 = (bf16[320,768]{1,0:T(8,128)(2,1)S(1)}, bf16[320,768]{1,0:T(8,128)(2,1)}, u32[]{:S(2)}, u32[]{:S(2)}) collective-permute-start(bf16[320,768]{1,0:T(8,128)(2,1)S(1)} %bitcast.176), channel_id=1, source_target_pairs={{0,2},{1,3},{2,0},{3,1},{4,6},{5,7},{6,4},{7,5},{8,10},{9,11},{10,... | collective-permute-start | bytes 1474568 | tf_op jit(solution)/shard_map/ppermute | solution.py:866
  288.4 5.9 %collective-permute-start.28 = (bf16[320,768]{1,0:T(8,128)(2,1)}, bf16[320,768]{1,0:T(8,128)(2,1)S(1)}, u32[]{:S(2)}, u32[]{:S(2)}) collective-permute-start(bf16[320,768]{1,0:T(8,128)(2,1)} %bitcast.28.refs_5_.refs_2_), channel_id=1, source_target_pairs={{0,2},{1,3},{2,0},{3,1},{4,6},{5,7},{6,4},{7,5},{8,10},{9,11},{10,... | collective-permute-start | bytes 1474568 | tf_op jit(solution)/shard_map/ppermute | solution.py:866
  289.3 49.0 %collective-permute-start.32 = (bf16[384,1536]{1,0:T(8,128)(2,1)}, bf16[384,1536]{1,0:T(8,128)(2,1)}, u32[]{:S(2)}, u32[]{:S(2)}) collective-permute-start(bf16[384,1536]{1,0:T(8,128)(2,1)} %copy-done.41), channel_id=1, source_target_pairs={{0,1},{1,0},{2,3},{3,2},{4,5},{5,4},{6,7},{7,6},{8,9},{9,8},{10,11... | collective-permute-start | bytes 3538952 | tf_op jit(solution)/shard_map/ppermute | solution.py:866
  290.5 47.8 %collective-permute-start.31 = (bf16[384,1536]{1,0:T(8,128)(2,1)}, bf16[384,1536]{1,0:T(8,128)(2,1)}, u32[]{:S(2)}, u32[]{:S(2)}) collective-permute-start(bf16[384,1536]{1,0:T(8,128)(2,1)} %copy-done.169), channel_id=1, source_target_pairs={{0,2},{1,3},{2,0},{3,1},{4,6},{5,7},{6,4},{7,5},{8,10},{9,11},{10,... | collective-permute-start | bytes 3538952 | tf_op jit(solution)/shard_map/ppermute | solution.py:866
  304.6 37.3 %copy-start.92 = (bf16[2,384,1536]{2,1,0:T(8,128)(2,1)}, bf16[2,384,1536]{2,1,0:T(8,128)(2,1)S(1)}, u32[]{:S(2)}) copy-start(bf16[2,384,1536]{2,1,0:T(8,128)(2,1)S(1)} %get-tuple-element.255) | copy-start | bytes 7077892
  304.6 36.0 %collective-permute-start.30 = (bf16[2,384,1536]{2,1,0:T(8,128)(2,1)}, bf16[2,384,1536]{2,1,0:T(8,128)(2,1)}, u32[]{:S(2)}, u32[]{:S(2)}) collective-permute-start(bf16[2,384,1536]{2,1,0:T(8,128)(2,1)} %get-tuple-element.256), channel_id=1, source_target_pairs={{0,2},{1,3},{2,0},{3,1},{4,6},{5,7},{6,4},{7,5},{8,10},{9,11},{10,... | collective-permute-start | bytes 7077896 | tf_op jit(solution)/shard_map/ppermute | solution.py:866
  309.6 47.5 %collective-permute-start.36 = (bf16[192,3072]{1,0:T(8,128)(2,1)S(1)}, bf16[192,3072]{1,0:T(8,128)(2,1)S(1)}, u32[]{:S(2)}, u32[]{:S(2)}) collective-permute-start(bf16[192,3072]{1,0:T(8,128)(2,1)S(1)} %fusion.14.refs_24_), channel_id=1, source_target_pairs={{0,4},{1,5},{2,6},{3,7},{4,0},{5,1},{6,2},{7,3},{8,12},{9,13},{10,... | collective-permute-start | bytes 3538952 | tf_op jit(solution)/shard_map/ppermute | solution.py:866
  336.9 22.0 %collective-permute-start.35 = (bf16[2,384,1536]{2,1,0:T(8,128)(2,1)S(1)}, bf16[2,384,1536]{2,1,0:T(8,128)(2,1)S(1)}, u32[]{:S(2)}, u32[]{:S(2)}) collective-permute-start(bf16[2,384,1536]{2,1,0:T(8,128)(2,1)S(1)} %get-tuple-element.270), channel_id=1, source_target_pairs={{0,2},{1,3},{2,0},{3,1},{4,6},{5,7},{6,4},{7,5},{8,10},{9,11},{10,... | collective-permute-start | bytes 7077896 | tf_op jit(solution)/shard_map/ppermute | solution.py:866
  340.4 16.7 %collective-permute-start.37 = (bf16[192,1536]{1,0:T(8,128)(2,1)S(1)}, bf16[192,1536]{1,0:T(8,128)(2,1)S(1)}, u32[]{:S(2)}, u32[]{:S(2)}) collective-permute-start(bf16[192,1536]{1,0:T(8,128)(2,1)S(1)} %slice.354.refs_8_), channel_id=1, source_target_pairs={{0,4},{1,5},{2,6},{3,7},{4,0},{5,1},{6,2},{7,3},{8,12},{9,13},{10,... | collective-permute-start | bytes 1769480 | tf_op jit(solution)/shard_map/ppermute | solution.py:866
  343.3 37.1 %collective-permute-start.34 = (bf16[384,1536]{1,0:T(8,128)(2,1)}, bf16[384,1536]{1,0:T(8,128)(2,1)}, u32[]{:S(2)}, u32[]{:S(2)}) collective-permute-start(bf16[384,1536]{1,0:T(8,128)(2,1)} %fusion.1.refs_7_), channel_id=1, source_target_pairs={{0,1},{1,0},{2,3},{3,2},{4,5},{5,4},{6,7},{7,6},{8,9},{9,8},{10,11... | collective-permute-start | bytes 3538952 | tf_op jit(solution)/shard_map/ppermute | solution.py:866
  361.3 33.5 %collective-permute-start.40 = (bf16[96,4608]{1,0:T(8,128)(2,1)}, bf16[96,4608]{1,0:T(8,128)(2,1)}, u32[]{:S(2)}, u32[]{:S(2)}) collective-permute-start(bf16[96,4608]{1,0:T(8,128)(2,1)} %fusion.8.refs_9_), channel_id=1, source_target_pairs={{0,8},{1,9},{2,10},{3,11},{4,12},{5,13},{6,14},{7,15},{8,0},{9,1},... | collective-permute-start | bytes 2654216 | tf_op jit(solution)/shard_map/ppermute | solution.py:866
  362.6 39.9 %collective-permute-start.39 = (bf16[384,1536]{1,0:T(8,128)(2,1)}, bf16[384,1536]{1,0:T(8,128)(2,1)}, u32[]{:S(2)}, u32[]{:S(2)}) collective-permute-start(bf16[384,1536]{1,0:T(8,128)(2,1)} %fusion.refs_8_), channel_id=1, source_target_pairs={{0,1},{1,0},{2,3},{3,2},{4,5},{5,4},{6,7},{7,6},{8,9},{9,8},{10,11... | collective-permute-start | bytes 3538952 | tf_op jit(solution)/shard_map/ppermute | solution.py:866
  379.1 26.6 %collective-permute-start.38 = (bf16[384,1536]{1,0:T(8,128)(2,1)S(1)}, bf16[384,1536]{1,0:T(8,128)(2,1)S(1)}, u32[]{:S(2)}, u32[]{:S(2)}) collective-permute-start(bf16[384,1536]{1,0:T(8,128)(2,1)S(1)} %get-tuple-element.281), channel_id=1, source_target_pairs={{0,2},{1,3},{2,0},{3,1},{4,6},{5,7},{6,4},{7,5},{8,10},{9,11},{10,... | collective-permute-start | bytes 3538952 | tf_op jit(solution)/shard_map/ppermute | solution.py:866
  379.3 36.9 %collective-permute-start.33 = (bf16[2,128,768]{2,1,0:T(8,128)(2,1)S(1)}, bf16[2,128,768]{2,1,0:T(8,128)(2,1)S(1)}, u32[]{:S(2)}, u32[]{:S(2)}) collective-permute-start(bf16[2,128,768]{2,1,0:T(8,128)(2,1)S(1)} %constant_dynamic-slice_fusion.4), channel_id=1, source_target_pairs={{0,1},{1,3},{2,0},{3,2},{4,5},{5,7},{6,4},{7,6},{8,9},{9,11},{10,8... | collective-permute-start | bytes 1179656 | tf_op jit(solution)/shard_map/ppermute | solution.py:866
  380.4 35.9 %collective-permute-start.41 = (bf16[3,128,768]{2,1,0:T(8,128)(2,1)S(1)}, bf16[3,128,768]{2,1,0:T(8,128)(2,1)S(1)}, u32[]{:S(2)}, u32[]{:S(2)}) collective-permute-start(bf16[3,128,768]{2,1,0:T(8,128)(2,1)S(1)} %constant_dynamic-slice_fusion.3), channel_id=1, source_target_pairs={{0,0},{1,2},{2,1},{3,3},{4,4},{5,6},{6,5},{7,7},{8,8},{9,10},{10,9... | collective-permute-start | bytes 1769480 | tf_op jit(solution)/shard_map/ppermute | solution.py:866
  394.8 39.3 %collective-permute-start.43 = (bf16[192,1536]{1,0:T(8,128)(2,1)S(1)}, bf16[192,1536]{1,0:T(8,128)(2,1)S(1)}, u32[]{:S(2)}, u32[]{:S(2)}) collective-permute-start(bf16[192,1536]{1,0:T(8,128)(2,1)S(1)} %fusion.19.refs_7_), channel_id=1, source_target_pairs={{0,4},{1,5},{2,6},{3,7},{4,0},{5,1},{6,2},{7,3},{8,12},{9,13},{10,... | collective-permute-start | bytes 1769480 | tf_op jit(solution)/shard_map/ppermute | solution.py:866
  405.7 25.8 %collective-permute-start.44 = (bf16[192,1536]{1,0:T(8,128)(2,1)S(1)}, bf16[192,1536]{1,0:T(8,128)(2,1)S(1)}, u32[]{:S(2)}, u32[]{:S(2)}) collective-permute-start(bf16[192,1536]{1,0:T(8,128)(2,1)S(1)} %fusion.18.refs_9_), channel_id=1, source_target_pairs={{0,4},{1,5},{2,6},{3,7},{4,0},{5,1},{6,2},{7,3},{8,12},{9,13},{10,... | collective-permute-start | bytes 1769480 | tf_op jit(solution)/shard_map/ppermute | solution.py:866
  408.1 37.1 %collective-permute-start.47 = (bf16[384,1536]{1,0:T(8,128)(2,1)S(1)}, bf16[384,1536]{1,0:T(8,128)(2,1)S(1)}, u32[]{:S(2)}, u32[]{:S(2)}) collective-permute-start(bf16[384,1536]{1,0:T(8,128)(2,1)S(1)} %add_convert_fusion.refs_8_), channel_id=1, source_target_pairs={{0,1},{1,0},{2,3},{3,2},{4,5},{5,4},{6,7},{7,6},{8,9},{9,8},{10,11... | collective-permute-start | bytes 3538952 | tf_op jit(solution)/shard_map/ppermute | solution.py:866
  416.2 57.7 %collective-permute-start.59 = (bf16[48,4608]{1,0:T(8,128)(2,1)S(1)}, bf16[48,4608]{1,0:T(8,128)(2,1)}, u32[]{:S(2)}, u32[]{:S(2)}) collective-permute-start(bf16[48,4608]{1,0:T(8,128)(2,1)S(1)} %slice.470.refs_10_), channel_id=1, source_target_pairs={{0,16},{1,17},{2,18},{3,19},{4,20},{5,21},{6,22},{7,23},{8,24},{9,... | collective-permute-start | bytes 1327112 | tf_op jit(solution)/shard_map/ppermute | solution.py:866
  416.3 25.5 %collective-permute-start.45 = (bf16[384,1536]{1,0:T(8,128)(2,1)S(1)}, bf16[384,1536]{1,0:T(8,128)(2,1)S(1)}, u32[]{:S(2)}, u32[]{:S(2)}) collective-permute-start(bf16[384,1536]{1,0:T(8,128)(2,1)S(1)} %get-tuple-element.292), channel_id=1, source_target_pairs={{0,2},{1,3},{2,0},{3,1},{4,6},{5,7},{6,4},{7,5},{8,10},{9,11},{10,... | collective-permute-start | bytes 3538952 | tf_op jit(solution)/shard_map/ppermute | solution.py:866
  431.5 10.3 %collective-permute-start.42 = (bf16[640,768]{1,0:T(8,128)(2,1)S(1)}, bf16[640,768]{1,0:T(8,128)(2,1)S(1)}, u32[]{:S(2)}, u32[]{:S(2)}) collective-permute-start(bf16[640,768]{1,0:T(8,128)(2,1)S(1)} %get-tuple-element.288), channel_id=1, source_target_pairs={{0,2},{1,3},{2,0},{3,1},{4,6},{5,7},{6,4},{7,5},{8,10},{9,11},{10,... | collective-permute-start | bytes 2949128 | tf_op jit(solution)/shard_map/ppermute | solution.py:866
  437.1 26.5 %collective-permute-start.57 = (bf16[96,3072]{1,0:T(8,128)(2,1)S(1)}, bf16[96,3072]{1,0:T(8,128)(2,1)}, u32[]{:S(2)}, u32[]{:S(2)}) collective-permute-start(bf16[96,3072]{1,0:T(8,128)(2,1)S(1)} %fusion.13.refs_5_), channel_id=1, source_target_pairs={{0,8},{1,9},{2,10},{3,11},{4,12},{5,13},{6,14},{7,15},{8,0},{9,1},... | collective-permute-start | bytes 1769480 | tf_op jit(solution)/shard_map/ppermute | solution.py:866
  447.1 14.6 %collective-permute-start.48 = (bf16[192,1536]{1,0:T(8,128)(2,1)}, bf16[192,1536]{1,0:T(8,128)(2,1)}, u32[]{:S(2)}, u32[]{:S(2)}) collective-permute-start(bf16[192,1536]{1,0:T(8,128)(2,1)} %add_convert_fusion.3), channel_id=1, source_target_pairs={{0,4},{1,5},{2,6},{3,7},{4,0},{5,1},{6,2},{7,3},{8,12},{9,13},{10,... | collective-permute-start | bytes 1769480 | tf_op jit(solution)/shard_map/ppermute | solution.py:866
  448.8 1.2 collective-permute-start.49
  450.0 3.9 collective-permute-start.50
  451.4 32.9 %collective-permute-start.46 = (bf16[2,128,768]{2,1,0:T(8,128)(2,1)}, bf16[2,128,768]{2,1,0:T(8,128)(2,1)S(1)}, u32[]{:S(2)}, u32[]{:S(2)}) collective-permute-start(bf16[2,128,768]{2,1,0:T(8,128)(2,1)} %constant_dynamic-slice_fusion.2), channel_id=1, source_target_pairs={{0,1},{1,3},{2,0},{3,2},{4,5},{5,7},{6,4},{7,6},{8,9},{9,11},{10,8... | collective-permute-start | bytes 1179656 | tf_op jit(solution)/shard_map/ppermute | solution.py:866
  453.9 31.2 %collective-permute-start.53 = (bf16[3,128,768]{2,1,0:T(8,128)(2,1)}, bf16[3,128,768]{2,1,0:T(8,128)(2,1)S(1)}, u32[]{:S(2)}, u32[]{:S(2)}) collective-permute-start(bf16[3,128,768]{2,1,0:T(8,128)(2,1)} %constant_dynamic-slice_fusion.1), channel_id=1, source_target_pairs={{0,0},{1,2},{2,1},{3,3},{4,4},{5,6},{6,5},{7,7},{8,8},{9,10},{10,9... | collective-permute-start | bytes 1769480 | tf_op jit(solution)/shard_map/ppermute | solution.py:866
  463.4 10.3 %collective-permute-start.51 = (bf16[96,1536]{1,0:T(8,128)(2,1)S(1)}, bf16[96,1536]{1,0:T(8,128)(2,1)S(1)}, u32[]{:S(2)}, u32[]{:S(2)}) collective-permute-start(bf16[96,1536]{1,0:T(8,128)(2,1)S(1)} %slice.472), channel_id=1, source_target_pairs={{0,8},{1,9},{2,10},{3,11},{4,12},{5,13},{6,14},{7,15},{8,0},{9,1},... | collective-permute-start | bytes 884744 | tf_op jit(solution)/shard_map/ppermute | solution.py:866
  463.6 4.1 collective-permute-start.52
  467.7 14.9 %collective-permute-start.58 = (bf16[48,3072]{1,0:T(8,128)(2,1)S(1)}, bf16[48,3072]{1,0:T(8,128)(2,1)S(1)}, u32[]{:S(2)}, u32[]{:S(2)}) collective-permute-start(bf16[48,3072]{1,0:T(8,128)(2,1)S(1)} %slice.471), channel_id=1, source_target_pairs={{0,16},{1,17},{2,18},{3,19},{4,20},{5,21},{6,22},{7,23},{8,24},{9,... | collective-permute-start | bytes 884744 | tf_op jit(solution)/shard_map/ppermute | solution.py:866
  484.2 6.9 %collective-permute-start.54 = (bf16[4,8,1536]{2,1,0:T(8,128)(2,1)S(1)}, bf16[4,8,1536]{2,1,0:T(8,128)(2,1)S(1)}, u32[]{:S(2)}, u32[]{:S(2)}) collective-permute-start(bf16[4,8,1536]{2,1,0:T(8,128)(2,1)S(1)} %constant_dynamic-update-slice_fusion), channel_id=1, source_target_pairs={{0,8},{1,9},{2,10},{3,11},{4,12},{5,13},{6,14},{7,15},{8,0},{9,1},... | collective-permute-start | bytes 294920 | tf_op jit(solution)/shard_map/ppermute | solution.py:866
  487.4 16.9 %collective-permute-start.56 = (bf16[48,1536]{1,0:T(8,128)(2,1)S(1)}, bf16[48,1536]{1,0:T(8,128)(2,1)S(1)}, u32[]{:S(2)}, u32[]{:S(2)}) collective-permute-start(bf16[48,1536]{1,0:T(8,128)(2,1)S(1)} %slice.473), channel_id=1, source_target_pairs={{0,16},{1,17},{2,18},{3,19},{4,20},{5,21},{6,22},{7,23},{8,24},{9,... | collective-permute-start | bytes 442376 | tf_op jit(solution)/shard_map/ppermute | solution.py:866
  491.1 13.2 %collective-permute-start.55 = (bf16[8,8,1536]{2,1,0:T(8,128)(2,1)S(1)}, bf16[8,8,1536]{2,1,0:T(8,128)(2,1)S(1)}, u32[]{:S(2)}, u32[]{:S(2)}) collective-permute-start(bf16[8,8,1536]{2,1,0:T(8,128)(2,1)S(1)} %pad_maximum_fusion.5), channel_id=1, source_target_pairs={{0,16},{1,17},{2,18},{3,19},{4,20},{5,21},{6,22},{7,23},{8,24},{9,... | collective-permute-start | bytes 589832 | tf_op jit(solution)/shard_map/ppermute | solution.py:866
  (192 other events, 1117.8 us)
Sparse Core Ops, SparseCore 0:
  42.1 74.1 all-gather.4
  364.4 78.2 all-gather.6

commit v5 on v3

--- a/solution.py
+++ b/solution.py
@@ -20,7 +20,7 @@
 f32 = jnp.float32
 bf16 = jnp.bfloat16
 ALL = ("dp", "tensor")
-VMEM_BYTES = 26 * 1024 * 1024
+VMEM_BYTES = 24 * 1024 * 1024
 LIGHT = 2000
 
 

time: 522 us -> 520 us (level)
  starting transfers between devices: 81.8 us -> 70.7 us
  Pallas kernels: 177 us -> 185 us
    ppermute x60, starting transfers between devices: 81.2 us -> 70.1 us  [send(): return lax.ppermute(value, ALL, pairs)]
    pallas_call x30, Pallas kernels: 177 us -> 185 us  [run(): pl.pallas_call(step, grid_spec=pltpu.PrefetchScalarGridSpec(num_scalar_pr...]
  transfers between devices with their start and end apart: 62 -> 62, of which waited for: 18 -> 17; matrix products, arithmetic and copies ran while one was open for 15% -> 15% of each run, Pallas kernels for 33% -> 34%
where the time goes in v5:
time: 520 us; the launch traced here: 514 us
  Pallas kernels  185 us (36%)
  local copies, waits for them, and re-layouts  103 us (20%)
  waiting for transfers between devices  85 us (16%)
  starting transfers between devices  70.7 us (14%)
  other arithmetic  37.4 us (7%)
  between operations  19.4 us (4%)
  matrix products  13.7 us (3%)
    pallas_call x30, Pallas kernels, run(): pl.pallas_call(step, grid_spec=pltpu.PrefetchScalarGridSpec(num_scalar_pr...  185 us
    ppermute x60, waiting for transfers between devices, send(): return lax.ppermute(value, ALL, pairs)  85 us
    ppermute x60, starting transfers between devices, send(): return lax.ppermute(value, ALL, pairs)  70.1 us
    unnamed x372, local copies, waits for them, and re-layouts  67.1 us
  transfers between devices with their start and end apart: 62, of which 17 were waited for; matrix products, arithmetic and copies ran while one was open for 15% of the time, Pallas kernels for 34%

profile of v5, /device:TPU:0, one launch (start us, length us, event | category | flops | bytes accessed | tf_op | source)
XLA Modules:
  0.0 514.1 jit_solution(1140787762824988418)
XLA Ops:
  10.1 4.3 collective-permute-start.3
  26.1 3.5 collective-permute-start.4
  29.6 4.0 fusion.65
  33.7 4.1 fusion.66
  37.8 1.8 collective-permute-done.4
  40.3 1.8 maximum_select_fusion.refs_0_.refs_4_.refs_2_
  44.0 2.5 collective-permute-start.6
  49.7 4.0 shard_map.246
  55.1 7.4 %shard_map.247.refs_4_.refs_0_.refs_21_ = bf16[5,128,384]{2,1,0:T(8,128)(2,1)S(1)} custom-call(s32[1]{0:T(128)S(6)} %select_n.232.refs_0_, bf16[5,128,384]{2,1,0:T(8,128)(2,1)S(1)} %get-tuple-element.160.refs_1_, bf16[2,5,128,384]{3,2,1,0:T(8,128)(2,1)S(1)} %get-tuple-element.161.refs_2_, bf16[2,5,128,384]{3,2,1,0:T(8,128)(2,1)S(1)} %get-tuple-element.162.refs_3_), custom_call_target="tpu_custom_call" | custom-call | flops 2013266 | bytes 1475 | tf_op jit(solution)/shard_map/pallas_call | solution.py:78
  63.4 9.5 %collective-permute-done.6.refs_2_ = bf16[4,384,384]{2,1,0:T(8,128)(2,1)} collective-permute-done((bf16[4,384,384]{2,1,0:T(8,128)(2,1)S(1)}, bf16[4,384,384]{2,1,0:T(8,128)(2,1)}, u32[]{:S(2)}, u32[]{:S(2)}) %collective-permute-start.6) | collective-permute-done | bytes 1179680 | tf_op jit(solution)/shard_map/ppermute | solution.py:837
  77.4 4.5 shard_map.248
  82.0 7.4 %shard_map.249.refs_1_.refs_22_ = bf16[5,128,384]{2,1,0:T(8,128)(2,1)S(1)} custom-call(s32[1]{0:T(128)S(6)} %select_n.232.refs_0_, bf16[5,128,384]{2,1,0:T(8,128)(2,1)S(1)} %get-tuple-element.166.refs_1_, bf16[2,5,128,384]{3,2,1,0:T(8,128)(2,1)S(1)} %get-tuple-element.167.refs_2_, bf16[2,5,128,384]{3,2,1,0:T(8,128)(2,1)S(1)} %get-tuple-element.168.refs_3_), custom_call_target="tpu_custom_call" | custom-call | flops 2013266 | bytes 1475 | tf_op jit(solution)/shard_map/pallas_call | solution.py:78
  92.9 9.7 %collective-permute-done.8.refs_5_.refs_9_ = bf16[768,384]{1,0:T(8,128)(2,1)S(1)} collective-permute-done((bf16[768,384]{1,0:T(8,128)(2,1)S(1)}, bf16[768,384]{1,0:T(8,128)(2,1)S(1)}, u32[]{:S(2)}, u32[]{:S(2)}) %collective-permute-start.8) | collective-permute-done | bytes 589856 | tf_op jit(solution)/shard_map/ppermute | solution.py:837
  104.6 6.1 %shard_map.250 = (bf16[5,128,768]{2,1,0:T(8,128)(2,1)S(1)}, f32[5,128,768]{2,1,0:T(8,128)S(1)}, bf16[5,128,768]{2,1,0:T(8,128)(2,1)S(1)}, bf16[2,640,768]{2,1,0:...) custom-call(bf16[5,128,384]{2,1,0:T(8,128)(2,1)S(1)} %copy-done.27, ...), custom_call_target="tpu_custom_call" | custom-call | flops 1887437 | bytes 9779 | tf_op jit(solution)/shard_map/pallas_call | solution.py:78
  114.4 4.2 collective-permute-done.14.refs_11_.refs_15_
  121.5 5.6 %shard_map.251 = (bf16[2,640,768]{2,1,0:T(8,128)(2,1)S(1)}, bf16[2,640,768]{2,1,0:T(8,128)(2,1)S(1)}, bf16[5,128,768]{2,1,0:T(8,128)(2,1)S(1)}, bf16[5,128,768]{2,1,0:T(8,128)(2,1)S(1)}) custom-call(s32[1]{0:T(128)} %bitcast.refs_0_, bf16[5,128,768]{2,1,0:T(8,128)(2,1)S(1)} %get-tuple-element.170.refs_1_.refs_4_, f32[640,768]{1,0:T(8,128)S(1)} %get-tuple-element.171.refs_2_, ...), custom_call_target="tpu_custom_call" | custom-call | flops 1509950 | bytes 7813 | tf_op jit(solution)/shard_map/pallas_call | solution.py:78
  130.9 2.1 slice.277
  133.0 1.8 slice.278
  134.8 6.0 %collective-permute-start.20 = (bf16[3,128,768]{2,1,0:T(8,128)(2,1)}, bf16[3,128,768]{2,1,0:T(8,128)(2,1)}, u32[]{:S(2)}, u32[]{:S(2)}) collective-permute-start(bf16[3,128,768]{2,1,0:T(8,128)(2,1)} %slice.277), channel_id=1, source_target_pairs={{0,0},{1,2},{2,1},{3,3},{4,4},{5,6},{6,5},{7,7},{8,8},{9,10},{10,9... | collective-permute-start | bytes 1769480 | tf_op jit(solution)/shard_map/ppermute | solution.py:837
  141.2 1.8 shard_map.252
  144.5 2.6 shard_map.253
  147.1 3.3 shard_map.254.refs_2_.refs_0_.refs_21_
  152.7 3.1 copy-done
  155.8 2.0 shard_map.255
  157.9 3.3 shard_map.256.refs_1_.refs_22_
  161.2 2.7 maximum_select_fusion.1
  166.3 6.0 %collective-permute-start.18 = (bf16[3,128,768]{2,1,0:T(8,128)(2,1)}, bf16[3,128,768]{2,1,0:T(8,128)(2,1)}, u32[]{:S(2)}, u32[]{:S(2)}) collective-permute-start(bf16[3,128,768]{2,1,0:T(8,128)(2,1)} %constant_dynamic-slice_fusion.5), channel_id=1, source_target_pairs={{0,0},{1,2},{2,1},{3,3},{4,4},{5,6},{6,5},{7,7},{8,8},{9,10},{10,9... | collective-permute-start | bytes 1769480 | tf_op jit(solution)/shard_map/ppermute | solution.py:837
  172.2 1.8 constant_dynamic-slice_fusion.6
  174.9 3.0 copy-done.1
  184.2 3.6 shard_map.257
  190.4 3.6 shard_map.258
  194.1 2.7 shard_map.259
  196.8 4.9 shard_map.260
  202.3 13.6 %shard_map.261 = (bf16[2,384,1536]{2,1,0:T(8,128)(2,1)S(1)}, bf16[2,384,1536]{2,1,0:T(8,128)(2,1)S(1)}, bf16[2,384,384]{2,1,0:T(8,128)(2,1)S(1)}, bf16[2,384,384...) custom-call(s32[1]{0:T(128)} %constant.205.clone.1.refs_0_, ...), custom_call_target="tpu_custom_call" | custom-call | flops 3019899 | bytes 41554 | tf_op jit(solution)/shard_map/pallas_call | solution.py:78
  220.8 5.9 %shard_map.262 = (bf16[5,64,384]{2,1,0:T(8,128)(2,1)S(1)}, bf16[2,5,64,384]{3,2,1,0:T(8,128)(2,1)S(1)}, bf16[2,5,64,384]{3,2,1,0:T(8,128)(2,1)S(1)}) custom-call(s32[1]{0:T(128)S(6)} %select_n.232.refs_0_, bf16[5,64,384]{2,1,0:T(8,128)(2,1)S(1)} %copy-done.141, bf16[2,5,64,384]{3,2,1,0:T(8,128)(2,1)S(1)} %copy-done.122, ...), custom_call_target="tpu_custom_call" | custom-call | flops 1258292 | bytes 1352 | tf_op jit(solution)/shard_map/pallas_call | solution.py:78
  229.3 5.6 %shard_map.263 = (bf16[384,1536]{1,0:T(8,128)(2,1)S(1)}, bf16[384,1536]{1,0:T(8,128)(2,1)}, bf16[768,640]{1,0:T(8,128)(2,1)S(1)}, f32[640,768]{1,0:T(8,128)S(1)}) custom-call(bf16[5,64,384]{2,1,0:T(8,128)(2,1)S(1)} %get-tuple-element.210.refs_0_, bf16[2,5,64,384]{3,2,1,0:T(8,128)(2,1)S(1)} %get-tuple-element.211.refs_1_, ...), custom_call_target="tpu_custom_call" | custom-call | flops 1321206 | bytes 8479 | tf_op jit(solution)/shard_map/pallas_call | solution.py:78
  239.3 9.4 %collective-permute-done.25.refs_6_ = bf16[384,1536]{1,0:T(8,128)(2,1)} collective-permute-done((bf16[384,1536]{1,0:T(8,128)(2,1)}, bf16[384,1536]{1,0:T(8,128)(2,1)}, u32[]{:S(2)}, u32[]{:S(2)}) %collective-permute-start.25) | collective-permute-done | bytes 1179680 | tf_op jit(solution)/shard_map/ppermute | solution.py:837
  254.3 5.7 %shard_map.264 = (bf16[5,64,384]{2,1,0:T(8,128)(2,1)S(1)}, bf16[2,5,64,384]{3,2,1,0:T(8,128)(2,1)S(1)}, bf16[2,5,64,384]{3,2,1,0:T(8,128)(2,1)S(1)}) custom-call(s32[1]{0:T(128)S(6)} %select_n.232.refs_0_, bf16[5,64,384]{2,1,0:T(8,128)(2,1)S(1)} %copy-done.139, bf16[2,5,64,384]{3,2,1,0:T(8,128)(2,1)S(1)} %copy-done.118, ...), custom_call_target="tpu_custom_call" | custom-call | flops 1258292 | bytes 1352 | tf_op jit(solution)/shard_map/pallas_call | solution.py:78
  262.2 4.3 shard_map.265
  279.5 2.4 shard_map.267.refs_5_
  283.3 2.8 shard_map.268
  286.2 7.4 %shard_map.269 = (bf16[2,384,1536]{2,1,0:T(8,128)(2,1)S(1)}, bf16[2,384,1536]{2,1,0:T(8,128)(2,1)}, bf16[640,768]{1,0:T(8,128)(2,1)S(1)}, f32[5,1,768]{2,1,0:T(1,128)S(1)}) custom-call(s32[1]{0:T(128)} %bitcast.refs_0_, bf16[5,128,768]{2,1,0:T(8,128)(2,1)S(1)} %bitcast.166, f32[5,6,768]{2,1,0:T(8,128)S(1)} %copy-done.37, ...), custom_call_target="tpu_custom_call" | custom-call | flops 1887437 | bytes 6444 | tf_op jit(solution)/shard_map/pallas_call | solution.py:78
  294.0 2.1 fusion.4
  296.2 2.2 fusion.5
  300.5 23.2 %shard_map.270 = (bf16[2,384,1536]{2,1,0:T(8,128)(2,1)S(1)}, bf16[2,384,1536]{2,1,0:T(8,128)(2,1)S(1)}, bf16[2,384,384]{2,1,0:T(8,128)(2,1)S(1)}, bf16[2,384,384...) custom-call(s32[1]{0:T(128)} %bitcast.refs_0_, ...), custom_call_target="tpu_custom_call" | custom-call | flops 6039798 | bytes 16683 | tf_op jit(solution)/shard_map/pallas_call | solution.py:78
  326.6 2.1 add_convert_fusion.1
  333.9 16.6 %shard_map.271 = (bf16[5,128,384]{2,1,0:T(8,128)(2,1)S(1)}, bf16[2,5,128,384]{3,2,1,0:T(8,128)(2,1)S(1)}, bf16[2,5,128,384]{3,2,1,0:T(8,128)(2,1)S(1)}) custom-call(s32[1]{0:T(128)S(6)} %select_n.232.refs_0_, bf16[5,128,384]{2,1,0:T(8,128)(2,1)S(1)} %copy-done.104, bf16[2,5,128,384]{3,2,1,0:T(8,128)(2,1)S(1)} %copy-done.47, ...), custom_call_target="tpu_custom_call" | custom-call | flops 5033165 | bytes 2704 | tf_op jit(solution)/shard_map/pallas_call | solution.py:78
  355.4 7.0 %collective-permute-start.40 = (bf16[96,4608]{1,0:T(8,128)(2,1)}, bf16[96,4608]{1,0:T(8,128)(2,1)}, u32[]{:S(2)}, u32[]{:S(2)}) collective-permute-start(bf16[96,4608]{1,0:T(8,128)(2,1)} %fusion.8.refs_9_), channel_id=1, source_target_pairs={{0,8},{1,9},{2,10},{3,11},{4,12},{5,13},{6,14},{7,15},{8,0},{9,1},... | collective-permute-start | bytes 2654216 | tf_op jit(solution)/shard_map/ppermute | solution.py:837
  373.0 7.7 %shard_map.272 = (bf16[384,1536]{1,0:T(8,128)(2,1)S(1)}, bf16[384,1536]{1,0:T(8,128)(2,1)S(1)}, bf16[768,1280]{1,0:T(8,128)(2,1)S(1)}, f32[1280,768]{1,0:T(8,128)S(1)}) custom-call(bf16[5,128,384]{2,1,0:T(8,128)(2,1)S(1)} %copy-done.150, bf16[2,5,128,384]{3,2,1,0:T(8,128)(2,1)S(1)} %copy-done.143, bf16[2,5,128,384]{3,2,1,0:T(8,128)(2,1)S(1)} %copy-done.145, ...), custom_call_target="tpu_custom_call" | custom-call | flops 2642412 | bytes 8700 | tf_op jit(solution)/shard_map/pallas_call | solution.py:78
  384.4 16.7 %shard_map.273 = (bf16[5,128,384]{2,1,0:T(8,128)(2,1)S(1)}, bf16[2,5,128,384]{3,2,1,0:T(8,128)(2,1)S(1)}, bf16[2,5,128,384]{3,2,1,0:T(8,128)(2,1)S(1)}) custom-call(s32[1]{0:T(128)S(6)} %select_n.232.refs_0_, bf16[5,128,384]{2,1,0:T(8,128)(2,1)S(1)} %copy-done.114, bf16[2,5,128,384]{3,2,1,0:T(8,128)(2,1)S(1)} %copy-done.51, ...), custom_call_target="tpu_custom_call" | custom-call | flops 5033165 | bytes 2704 | tf_op jit(solution)/shard_map/pallas_call | solution.py:78
  405.7 2.0 collective-permute-start.44
  408.0 2.6 collective-permute-start.47
  410.7 6.6 %shard_map.274 = (bf16[384,1536]{1,0:T(8,128)(2,1)S(1)}, bf16[384,1536]{1,0:T(8,128)(2,1)S(1)}, f32[640,768]{1,0:T(8,128)S(1)}, bf16[640,768]{1,0:T(8,128)(2,1)S(1)}) custom-call(bf16[5,128,384]{2,1,0:T(8,128)(2,1)S(1)} %get-tuple-element.260.refs_0_, bf16[2,5,128,384]{3,2,1,0:T(8,128)(2,1)S(1)} %get-tuple-element.261.refs_1_, ...), custom_call_target="tpu_custom_call" | custom-call | flops 1887437 | bytes 8307 | tf_op jit(solution)/shard_map/pallas_call | solution.py:78
  419.6 17.5 %collective-permute-done.44 = bf16[192,1536]{1,0:T(8,128)(2,1)S(1)} collective-permute-done((bf16[192,1536]{1,0:T(8,128)(2,1)S(1)}, bf16[192,1536]{1,0:T(8,128)(2,1)S(1)}, u32[]{:S(2)}, u32[]{:S(2)}) %collective-permute-start.44) | collective-permute-done | bytes 589856 | tf_op jit(solution)/shard_map/ppermute | solution.py:837
  439.4 2.0 fusion.17
  449.5 1.7 collective-permute-start.46
  454.0 4.9 reshape.653
  458.9 3.5 collective-permute-done.48
  466.9 2.5 collective-permute-done.52
  469.4 1.9 collective-permute-start.58
  471.3 4.3 collective-permute-done.51
  477.7 5.2 %collective-permute-done.58 = bf16[48,3072]{1,0:T(8,128)(2,1)S(1)} collective-permute-done((bf16[48,3072]{1,0:T(8,128)(2,1)S(1)}, bf16[48,3072]{1,0:T(8,128)(2,1)S(1)}, u32[]{:S(2)}, u32[]{:S(2)}) %collective-permute-start.58) | collective-permute-done | bytes 294944 | tf_op jit(solution)/shard_map/ppermute | solution.py:837
  487.8 3.2 collective-permute-start.56
  492.5 12.0 %collective-permute-done.55 = bf16[8,8,1536]{2,1,0:T(8,128)(2,1)S(1)} collective-permute-done((bf16[8,8,1536]{2,1,0:T(8,128)(2,1)S(1)}, bf16[8,8,1536]{2,1,0:T(8,128)(2,1)S(1)}, u32[]{:S(2)}, u32[]{:S(2)}) %collective-permute-start.55) | collective-permute-done | bytes 196640 | tf_op jit(solution)/shard_map/ppermute | solution.py:837
  (604 shorter events, 155.2 us)
Async XLA Ops:
  7.2 145.5 %all-gather.5.cloned.1.call-start = ((), (), s32[]{:S(2)}) async-start(), calls=%async_computation | async-start | bytes 7520256 | tf_op jit(solution)/shard_map/all_gather | solution.py:1015
  8.4 16.9 %collective-permute-start.1 = (bf16[3,128,768]{2,1,0:T(8,128)(2,1)S(1)}, bf16[3,128,768]{2,1,0:T(8,128)(2,1)S(1)}, u32[]{:S(2)}, u32[]{:S(2)}) collective-permute-start(bf16[3,128,768]{2,1,0:T(8,128)(2,1)S(1)} %slice.267), channel_id=1, source_target_pairs={{0,0},{1,2},{2,1},{3,3},{4,4},{5,6},{6,5},{7,7},{8,8},{9,10},{10,9... | collective-permute-start | bytes 1769480 | tf_op jit(solution)/shard_map/ppermute | solution.py:837
  10.1 15.2 %collective-permute-start.3 = (bf16[2,128,768]{2,1,0:T(8,128)(2,1)S(1)}, bf16[2,128,768]{2,1,0:T(8,128)(2,1)S(1)}, u32[]{:S(2)}, u32[]{:S(2)}) collective-permute-start(bf16[2,128,768]{2,1,0:T(8,128)(2,1)S(1)} %slice.269), channel_id=1, source_target_pairs={{0,2},{1,0},{2,3},{3,1},{4,6},{5,4},{6,7},{7,5},{8,10},{9,8},{10,1... | collective-permute-start | bytes 1179656 | tf_op jit(solution)/shard_map/ppermute | solution.py:837
  15.2 7.9 %collective-permute-start = (s32[645]{0:T(1024)S(1)}, s32[645]{0:T(1024)S(1)}, u32[]{:S(2)}, u32[]{:S(2)}) collective-permute-start(s32[645]{0:T(1024)S(1)} %pad_add_fusion), channel_id=1, source_target_pairs={{0,0},{1,2},{2,1},{3,3},{4,4},{5,6},{6,5},{7,7},{8,8},{9,10},{10,9... | collective-permute-start | bytes 7748 | tf_op jit(solution)/shard_map/ppermute | solution.py:837
  15.9 7.8 %collective-permute-start.2 = (bf16[5,768]{1,0:T(8,128)(2,1)S(1)}, bf16[5,768]{1,0:T(8,128)(2,1)S(1)}, u32[]{:S(2)}, u32[]{:S(2)}) collective-permute-start(bf16[5,768]{1,0:T(8,128)(2,1)S(1)} %fusion.27), channel_id=1, source_target_pairs={{0,0},{1,2},{2,1},{3,3},{4,4},{5,6},{6,5},{7,7},{8,8},{9,10},{10,9... | collective-permute-start | bytes 23048 | tf_op jit(solution)/shard_map/ppermute | solution.py:837
  26.1 13.5 %collective-permute-start.4 = (bf16[12,48,384]{2,1,0:T(8,128)(2,1)S(1)}, bf16[12,48,384]{2,1,0:T(8,128)(2,1)S(1)}, u32[]{:S(2)}, u32[]{:S(2)}) collective-permute-start(bf16[12,48,384]{2,1,0:T(8,128)(2,1)S(1)} %copy.62), channel_id=1, source_target_pairs={{0,1},{1,0},{2,3},{3,2},{4,5},{5,4},{6,7},{7,6},{8,9},{9,8},{10,11... | collective-permute-start | bytes 1327112 | tf_op jit(solution)/shard_map/ppermute | solution.py:837
  42.1 62.5 %copy-start.6 = (bf16[5,128,768]{2,1,0:T(8,128)(2,1)}, bf16[5,128,768]{2,1,0:T(8,128)(2,1)S(1)}, u32[]{:S(2)}) copy-start(bf16[5,128,768]{2,1,0:T(8,128)(2,1)S(1)} %maximum_select_fusion.refs_0_.refs_4_.refs_2_) | copy-start | bytes 2949124
  42.1 411.9 %all-gather.7.cloned.1.call-start = ((), (), s32[]{:S(2)}) async-start(), calls=%async_computation.1 | async-start | bytes 4460544 | tf_op jit(solution)/shard_map/all_gather | solution.py:1126
  44.0 28.9 %collective-permute-start.6 = (bf16[4,384,384]{2,1,0:T(8,128)(2,1)S(1)}, bf16[4,384,384]{2,1,0:T(8,128)(2,1)}, u32[]{:S(2)}, u32[]{:S(2)}) collective-permute-start(bf16[4,384,384]{2,1,0:T(8,128)(2,1)S(1)} %pad_maximum_fusion.3), channel_id=1, source_target_pairs={{0,1},{1,0},{2,3},{3,2},{4,5},{5,4},{6,7},{7,6},{8,9},{9,8},{10,11... | collective-permute-start | bytes 3538952 | tf_op jit(solution)/shard_map/ppermute | solution.py:837
  46.5 3.2 collective-permute-start.5
  72.9 3.5 collective-permute-start.7
  74.1 17.2 %collective-permute-start.12 = (bf16[384,768]{1,0:T(8,128)(2,1)S(1)}, bf16[384,768]{1,0:T(8,128)(2,1)S(1)}, u32[]{:S(2)}, u32[]{:S(2)}) collective-permute-start(bf16[384,768]{1,0:T(8,128)(2,1)S(1)} %constant_dynamic-slice_fusion.9), channel_id=1, source_target_pairs={{0,1},{1,0},{2,3},{3,2},{4,5},{5,4},{6,7},{7,6},{8,9},{9,8},{10,11... | collective-permute-start | bytes 1769480 | tf_op jit(solution)/shard_map/ppermute | solution.py:837
  75.5 27.1 %collective-permute-start.8 = (bf16[768,384]{1,0:T(8,128)(2,1)S(1)}, bf16[768,384]{1,0:T(8,128)(2,1)S(1)}, u32[]{:S(2)}, u32[]{:S(2)}) collective-permute-start(bf16[768,384]{1,0:T(8,128)(2,1)S(1)} %constant_dynamic-slice_fusion.10), channel_id=1, source_target_pairs={{0,1},{1,0},{2,3},{3,2},{4,5},{5,4},{6,7},{7,6},{8,9},{9,8},{10,11... | collective-permute-start | bytes 1769480 | tf_op jit(solution)/shard_map/ppermute | solution.py:837
  91.3 27.3 %collective-permute-start.14 = (bf16[384,768]{1,0:T(8,128)(2,1)S(1)}, bf16[384,768]{1,0:T(8,128)(2,1)S(1)}, u32[]{:S(2)}, u32[]{:S(2)}) collective-permute-start(bf16[384,768]{1,0:T(8,128)(2,1)S(1)} %collective-permute-done.12.refs_9_.refs_13_), channel_id=1, source_target_pairs={{0,8},{1,9},{2,10},{3,11},{4,12},{5,13},{6,14},{7,15},{8,0},{9,1},... | collective-permute-start | bytes 1769480 | tf_op jit(solution)/shard_map/ppermute | solution.py:837
  102.6 16.0 %collective-permute-start.10 = (bf16[768,384]{1,0:T(8,128)(2,1)S(1)}, bf16[768,384]{1,0:T(8,128)(2,1)S(1)}, u32[]{:S(2)}, u32[]{:S(2)}) collective-permute-start(bf16[768,384]{1,0:T(8,128)(2,1)S(1)} %collective-permute-done.8.refs_5_.refs_9_), channel_id=1, source_target_pairs={{0,4},{1,5},{2,6},{3,7},{4,0},{5,1},{6,2},{7,3},{8,12},{9,13},{10,... | collective-permute-start | bytes 1769480 | tf_op jit(solution)/shard_map/ppermute | solution.py:837
  104.1 15.1 %collective-permute-start.13 = (bf16[384,768]{1,0:T(8,128)(2,1)S(1)}, bf16[384,768]{1,0:T(8,128)(2,1)S(1)}, u32[]{:S(2)}, u32[]{:S(2)}) collective-permute-start(bf16[384,768]{1,0:T(8,128)(2,1)S(1)} %collective-permute-done.12.refs_9_.refs_13_), channel_id=1, source_target_pairs={{0,2},{1,3},{2,0},{3,1},{4,6},{5,7},{6,4},{7,5},{8,10},{9,11},{10,... | collective-permute-start | bytes 1769480 | tf_op jit(solution)/shard_map/ppermute | solution.py:837
  104.1 15.1 %collective-permute-start.9 = (bf16[768,384]{1,0:T(8,128)(2,1)S(1)}, bf16[768,384]{1,0:T(8,128)(2,1)S(1)}, u32[]{:S(2)}, u32[]{:S(2)}) collective-permute-start(bf16[768,384]{1,0:T(8,128)(2,1)S(1)} %collective-permute-done.8.refs_5_.refs_9_), channel_id=1, source_target_pairs={{0,2},{1,3},{2,0},{3,1},{4,6},{5,7},{6,4},{7,5},{8,10},{9,11},{10,... | collective-permute-start | bytes 1769480 | tf_op jit(solution)/shard_map/ppermute | solution.py:837
  118.6 2.0 collective-permute-start.15
  118.7 2.8 collective-permute-start.11
  130.7 10.5 %collective-permute-start.16 = (bf16[640,768]{1,0:T(8,128)(2,1)S(1)}, bf16[640,768]{1,0:T(8,128)(2,1)S(1)}, u32[]{:S(2)}, u32[]{:S(2)}) collective-permute-start(bf16[640,768]{1,0:T(8,128)(2,1)S(1)} %bitcast.161), channel_id=1, source_target_pairs={{0,2},{1,3},{2,0},{3,1},{4,6},{5,7},{6,4},{7,5},{8,10},{9,11},{10,... | collective-permute-start | bytes 2949128 | tf_op jit(solution)/shard_map/ppermute | solution.py:837
  134.8 26.5 %collective-permute-start.20 = (bf16[3,128,768]{2,1,0:T(8,128)(2,1)}, bf16[3,128,768]{2,1,0:T(8,128)(2,1)}, u32[]{:S(2)}, u32[]{:S(2)}) collective-permute-start(bf16[3,128,768]{2,1,0:T(8,128)(2,1)} %slice.277), channel_id=1, source_target_pairs={{0,0},{1,2},{2,1},{3,3},{4,4},{5,6},{6,5},{7,7},{8,8},{9,10},{10,9... | collective-permute-start | bytes 1769480 | tf_op jit(solution)/shard_map/ppermute | solution.py:837
  140.7 20.5 %collective-permute-start.21 = (bf16[2,128,768]{2,1,0:T(8,128)(2,1)}, bf16[2,128,768]{2,1,0:T(8,128)(2,1)}, u32[]{:S(2)}, u32[]{:S(2)}) collective-permute-start(bf16[2,128,768]{2,1,0:T(8,128)(2,1)} %slice.278), channel_id=1, source_target_pairs={{0,2},{1,0},{2,3},{3,1},{4,6},{5,4},{6,7},{7,5},{8,10},{9,8},{10,1... | collective-permute-start | bytes 1179656 | tf_op jit(solution)/shard_map/ppermute | solution.py:837
  164.0 30.1 %collective-permute-start.22 = (bf16[5,128,768]{2,1,0:T(8,128)(2,1)}, bf16[5,128,768]{2,1,0:T(8,128)(2,1)}, u32[]{:S(2)}, u32[]{:S(2)}) collective-permute-start(bf16[5,128,768]{2,1,0:T(8,128)(2,1)} %maximum_select_fusion.1), channel_id=1, source_target_pairs={{0,2},{1,3},{2,0},{3,1},{4,6},{5,7},{6,4},{7,5},{8,10},{9,11},{10,... | collective-permute-start | bytes 2949128 | tf_op jit(solution)/shard_map/ppermute | solution.py:837
  166.3 22.6 %collective-permute-start.18 = (bf16[3,128,768]{2,1,0:T(8,128)(2,1)}, bf16[3,128,768]{2,1,0:T(8,128)(2,1)}, u32[]{:S(2)}, u32[]{:S(2)}) collective-permute-start(bf16[3,128,768]{2,1,0:T(8,128)(2,1)} %constant_dynamic-slice_fusion.5), channel_id=1, source_target_pairs={{0,0},{1,2},{2,1},{3,3},{4,4},{5,6},{6,5},{7,7},{8,8},{9,10},{10,9... | collective-permute-start | bytes 1769480 | tf_op jit(solution)/shard_map/ppermute | solution.py:837
  174.0 13.9 %collective-permute-start.17 = (bf16[2,128,768]{2,1,0:T(8,128)(2,1)}, bf16[2,128,768]{2,1,0:T(8,128)(2,1)}, u32[]{:S(2)}, u32[]{:S(2)}) collective-permute-start(bf16[2,128,768]{2,1,0:T(8,128)(2,1)} %constant_dynamic-slice_fusion.6), channel_id=1, source_target_pairs={{0,1},{1,3},{2,0},{3,2},{4,5},{5,7},{6,4},{7,6},{8,9},{9,11},{10,8... | collective-permute-start | bytes 1179656 | tf_op jit(solution)/shard_map/ppermute | solution.py:837
  201.7 16.5 %collective-permute-start.23 = (bf16[2,384,1536]{2,1,0:T(8,128)(2,1)S(1)}, bf16[2,384,1536]{2,1,0:T(8,128)(2,1)S(1)}, u32[]{:S(2)}, u32[]{:S(2)}) collective-permute-start(bf16[2,384,1536]{2,1,0:T(8,128)(2,1)S(1)} %get-tuple-element.208), channel_id=1, source_target_pairs={{0,2},{1,3},{2,0},{3,1},{4,6},{5,7},{6,4},{7,5},{8,10},{9,11},{10,... | collective-permute-start | bytes 7077896 | tf_op jit(solution)/shard_map/ppermute | solution.py:837
  218.2 8.5 %collective-permute-start.24 = (bf16[2,384,1536]{2,1,0:T(8,128)(2,1)S(1)}, bf16[2,384,1536]{2,1,0:T(8,128)(2,1)S(1)}, u32[]{:S(2)}, u32[]{:S(2)}) collective-permute-start(bf16[2,384,1536]{2,1,0:T(8,128)(2,1)S(1)} %get-tuple-element.216), channel_id=1, source_target_pairs={{0,2},{1,3},{2,0},{3,1},{4,6},{5,7},{6,4},{7,5},{8,10},{9,11},{10,... | collective-permute-start | bytes 7077896 | tf_op jit(solution)/shard_map/ppermute | solution.py:837
  219.7 29.1 %collective-permute-start.25 = (bf16[384,1536]{1,0:T(8,128)(2,1)}, bf16[384,1536]{1,0:T(8,128)(2,1)}, u32[]{:S(2)}, u32[]{:S(2)}) collective-permute-start(bf16[384,1536]{1,0:T(8,128)(2,1)} %fusion.3.refs_5_), channel_id=1, source_target_pairs={{0,1},{1,0},{2,3},{3,2},{4,5},{5,4},{6,7},{7,6},{8,9},{9,8},{10,11... | collective-permute-start | bytes 3538952 | tf_op jit(solution)/shard_map/ppermute | solution.py:837
  238.2 21.8 %collective-permute-start.26 = (bf16[384,1536]{1,0:T(8,128)(2,1)}, bf16[384,1536]{1,0:T(8,128)(2,1)S(1)}, u32[]{:S(2)}, u32[]{:S(2)}) collective-permute-start(bf16[384,1536]{1,0:T(8,128)(2,1)} %get-tuple-element.224), channel_id=1, source_target_pairs={{0,2},{1,3},{2,0},{3,1},{4,6},{5,7},{6,4},{7,5},{8,10},{9,11},{10,... | collective-permute-start | bytes 3538952 | tf_op jit(solution)/shard_map/ppermute | solution.py:837
  238.3 47.8 %collective-permute-start.29 = (bf16[384,1536]{1,0:T(8,128)(2,1)}, bf16[384,1536]{1,0:T(8,128)(2,1)S(1)}, u32[]{:S(2)}, u32[]{:S(2)}) collective-permute-start(bf16[384,1536]{1,0:T(8,128)(2,1)} %copy-done.39), channel_id=1, source_target_pairs={{0,1},{1,0},{2,3},{3,2},{4,5},{5,4},{6,7},{7,6},{8,9},{9,8},{10,11... | collective-permute-start | bytes 3538952 | tf_op jit(solution)/shard_map/ppermute | solution.py:837
  269.6 1.9 collective-permute-start.27
  269.8 9.6 %collective-permute-start.19 = (bf16[320,768]{1,0:T(8,128)(2,1)S(1)}, bf16[320,768]{1,0:T(8,128)(2,1)}, u32[]{:S(2)}, u32[]{:S(2)}) collective-permute-start(bf16[320,768]{1,0:T(8,128)(2,1)S(1)} %bitcast.176), channel_id=1, source_target_pairs={{0,2},{1,3},{2,0},{3,1},{4,6},{5,7},{6,4},{7,5},{8,10},{9,11},{10,... | collective-permute-start | bytes 1474568 | tf_op jit(solution)/shard_map/ppermute | solution.py:837
  277.3 6.0 %collective-permute-start.28 = (bf16[320,768]{1,0:T(8,128)(2,1)}, bf16[320,768]{1,0:T(8,128)(2,1)S(1)}, u32[]{:S(2)}, u32[]{:S(2)}) collective-permute-start(bf16[320,768]{1,0:T(8,128)(2,1)} %bitcast.28.refs_5_.refs_2_), channel_id=1, source_target_pairs={{0,2},{1,3},{2,0},{3,1},{4,6},{5,7},{6,4},{7,5},{8,10},{9,11},{10,... | collective-permute-start | bytes 1474568 | tf_op jit(solution)/shard_map/ppermute | solution.py:837
  278.2 48.4 %collective-permute-start.32 = (bf16[384,1536]{1,0:T(8,128)(2,1)}, bf16[384,1536]{1,0:T(8,128)(2,1)}, u32[]{:S(2)}, u32[]{:S(2)}) collective-permute-start(bf16[384,1536]{1,0:T(8,128)(2,1)} %copy-done.40), channel_id=1, source_target_pairs={{0,1},{1,0},{2,3},{3,2},{4,5},{5,4},{6,7},{7,6},{8,9},{9,8},{10,11... | collective-permute-start | bytes 3538952 | tf_op jit(solution)/shard_map/ppermute | solution.py:837
  279.4 47.3 %collective-permute-start.31 = (bf16[384,1536]{1,0:T(8,128)(2,1)}, bf16[384,1536]{1,0:T(8,128)(2,1)}, u32[]{:S(2)}, u32[]{:S(2)}) collective-permute-start(bf16[384,1536]{1,0:T(8,128)(2,1)} %copy-done.159), channel_id=1, source_target_pairs={{0,2},{1,3},{2,0},{3,1},{4,6},{5,7},{6,4},{7,5},{8,10},{9,11},{10,... | collective-permute-start | bytes 3538952 | tf_op jit(solution)/shard_map/ppermute | solution.py:837
  293.6 38.1 %copy-start.90 = (bf16[2,384,1536]{2,1,0:T(8,128)(2,1)}, bf16[2,384,1536]{2,1,0:T(8,128)(2,1)S(1)}, u32[]{:S(2)}) copy-start(bf16[2,384,1536]{2,1,0:T(8,128)(2,1)S(1)} %get-tuple-element.240) | copy-start | bytes 7077892
  293.6 36.7 %collective-permute-start.30 = (bf16[2,384,1536]{2,1,0:T(8,128)(2,1)}, bf16[2,384,1536]{2,1,0:T(8,128)(2,1)}, u32[]{:S(2)}, u32[]{:S(2)}) collective-permute-start(bf16[2,384,1536]{2,1,0:T(8,128)(2,1)} %get-tuple-element.241), channel_id=1, source_target_pairs={{0,2},{1,3},{2,0},{3,1},{4,6},{5,7},{6,4},{7,5},{8,10},{9,11},{10,... | collective-permute-start | bytes 7077896 | tf_op jit(solution)/shard_map/ppermute | solution.py:837
  298.6 52.6 %collective-permute-start.36 = (bf16[192,3072]{1,0:T(8,128)(2,1)S(1)}, bf16[192,3072]{1,0:T(8,128)(2,1)S(1)}, u32[]{:S(2)}, u32[]{:S(2)}) collective-permute-start(bf16[192,3072]{1,0:T(8,128)(2,1)S(1)} %fusion.14.refs_24_), channel_id=1, source_target_pairs={{0,4},{1,5},{2,6},{3,7},{4,0},{5,1},{6,2},{7,3},{8,12},{9,13},{10,... | collective-permute-start | bytes 3538952 | tf_op jit(solution)/shard_map/ppermute | solution.py:837
  325.1 27.8 %collective-permute-start.35 = (bf16[2,384,1536]{2,1,0:T(8,128)(2,1)S(1)}, bf16[2,384,1536]{2,1,0:T(8,128)(2,1)S(1)}, u32[]{:S(2)}, u32[]{:S(2)}) collective-permute-start(bf16[2,384,1536]{2,1,0:T(8,128)(2,1)S(1)} %get-tuple-element.254), channel_id=1, source_target_pairs={{0,2},{1,3},{2,0},{3,1},{4,6},{5,7},{6,4},{7,5},{8,10},{9,11},{10,... | collective-permute-start | bytes 7077896 | tf_op jit(solution)/shard_map/ppermute | solution.py:837
  328.8 22.5 %collective-permute-start.37 = (bf16[192,1536]{1,0:T(8,128)(2,1)S(1)}, bf16[192,1536]{1,0:T(8,128)(2,1)S(1)}, u32[]{:S(2)}, u32[]{:S(2)}) collective-permute-start(bf16[192,1536]{1,0:T(8,128)(2,1)S(1)} %slice.354.refs_6_), channel_id=1, source_target_pairs={{0,4},{1,5},{2,6},{3,7},{4,0},{5,1},{6,2},{7,3},{8,12},{9,13},{10,... | collective-permute-start | bytes 1769480 | tf_op jit(solution)/shard_map/ppermute | solution.py:837
  333.0 48.6 %collective-permute-start.34 = (bf16[384,1536]{1,0:T(8,128)(2,1)}, bf16[384,1536]{1,0:T(8,128)(2,1)}, u32[]{:S(2)}, u32[]{:S(2)}) collective-permute-start(bf16[384,1536]{1,0:T(8,128)(2,1)} %fusion.1.refs_5_), channel_id=1, source_target_pairs={{0,1},{1,0},{2,3},{3,2},{4,5},{5,4},{6,7},{7,6},{8,9},{9,8},{10,11... | collective-permute-start | bytes 3538952 | tf_op jit(solution)/shard_map/ppermute | solution.py:837
  355.4 45.8 %collective-permute-start.40 = (bf16[96,4608]{1,0:T(8,128)(2,1)}, bf16[96,4608]{1,0:T(8,128)(2,1)}, u32[]{:S(2)}, u32[]{:S(2)}) collective-permute-start(bf16[96,4608]{1,0:T(8,128)(2,1)} %fusion.8.refs_9_), channel_id=1, source_target_pairs={{0,8},{1,9},{2,10},{3,11},{4,12},{5,13},{6,14},{7,15},{8,0},{9,1},... | collective-permute-start | bytes 2654216 | tf_op jit(solution)/shard_map/ppermute | solution.py:837
  363.8 37.4 %collective-permute-start.39 = (bf16[384,1536]{1,0:T(8,128)(2,1)}, bf16[384,1536]{1,0:T(8,128)(2,1)}, u32[]{:S(2)}, u32[]{:S(2)}) collective-permute-start(bf16[384,1536]{1,0:T(8,128)(2,1)} %fusion.refs_8_), channel_id=1, source_target_pairs={{0,1},{1,0},{2,3},{3,2},{4,5},{5,4},{6,7},{7,6},{8,9},{9,8},{10,11... | collective-permute-start | bytes 3538952 | tf_op jit(solution)/shard_map/ppermute | solution.py:837
  380.7 24.9 %collective-permute-start.38 = (bf16[384,1536]{1,0:T(8,128)(2,1)S(1)}, bf16[384,1536]{1,0:T(8,128)(2,1)S(1)}, u32[]{:S(2)}, u32[]{:S(2)}) collective-permute-start(bf16[384,1536]{1,0:T(8,128)(2,1)S(1)} %get-tuple-element.265), channel_id=1, source_target_pairs={{0,2},{1,3},{2,0},{3,1},{4,6},{5,7},{6,4},{7,5},{8,10},{9,11},{10,... | collective-permute-start | bytes 3538952 | tf_op jit(solution)/shard_map/ppermute | solution.py:837
  380.9 36.4 %collective-permute-start.33 = (bf16[2,128,768]{2,1,0:T(8,128)(2,1)S(1)}, bf16[2,128,768]{2,1,0:T(8,128)(2,1)S(1)}, u32[]{:S(2)}, u32[]{:S(2)}) collective-permute-start(bf16[2,128,768]{2,1,0:T(8,128)(2,1)S(1)} %constant_dynamic-slice_fusion.4), channel_id=1, source_target_pairs={{0,1},{1,3},{2,0},{3,2},{4,5},{5,7},{6,4},{7,6},{8,9},{9,11},{10,8... | collective-permute-start | bytes 1179656 | tf_op jit(solution)/shard_map/ppermute | solution.py:837
  381.6 37.2 %collective-permute-start.41 = (bf16[3,128,768]{2,1,0:T(8,128)(2,1)S(1)}, bf16[3,128,768]{2,1,0:T(8,128)(2,1)S(1)}, u32[]{:S(2)}, u32[]{:S(2)}) collective-permute-start(bf16[3,128,768]{2,1,0:T(8,128)(2,1)S(1)} %constant_dynamic-slice_fusion.3), channel_id=1, source_target_pairs={{0,0},{1,2},{2,1},{3,3},{4,4},{5,6},{6,5},{7,7},{8,8},{9,10},{10,9... | collective-permute-start | bytes 1769480 | tf_op jit(solution)/shard_map/ppermute | solution.py:837
  401.1 38.3 %collective-permute-start.43 = (bf16[192,1536]{1,0:T(8,128)(2,1)S(1)}, bf16[192,1536]{1,0:T(8,128)(2,1)S(1)}, u32[]{:S(2)}, u32[]{:S(2)}) collective-permute-start(bf16[192,1536]{1,0:T(8,128)(2,1)S(1)} %fusion.19.refs_5_), channel_id=1, source_target_pairs={{0,4},{1,5},{2,6},{3,7},{4,0},{5,1},{6,2},{7,3},{8,12},{9,13},{10,... | collective-permute-start | bytes 1769480 | tf_op jit(solution)/shard_map/ppermute | solution.py:837
  405.7 31.4 %collective-permute-start.44 = (bf16[192,1536]{1,0:T(8,128)(2,1)S(1)}, bf16[192,1536]{1,0:T(8,128)(2,1)S(1)}, u32[]{:S(2)}, u32[]{:S(2)}) collective-permute-start(bf16[192,1536]{1,0:T(8,128)(2,1)S(1)} %fusion.18.refs_9_), channel_id=1, source_target_pairs={{0,4},{1,5},{2,6},{3,7},{4,0},{5,1},{6,2},{7,3},{8,12},{9,13},{10,... | collective-permute-start | bytes 1769480 | tf_op jit(solution)/shard_map/ppermute | solution.py:837
  408.0 36.8 %collective-permute-start.47 = (bf16[384,1536]{1,0:T(8,128)(2,1)S(1)}, bf16[384,1536]{1,0:T(8,128)(2,1)S(1)}, u32[]{:S(2)}, u32[]{:S(2)}) collective-permute-start(bf16[384,1536]{1,0:T(8,128)(2,1)S(1)} %add_convert_fusion.refs_8_), channel_id=1, source_target_pairs={{0,1},{1,0},{2,3},{3,2},{4,5},{5,4},{6,7},{7,6},{8,9},{9,8},{10,11... | collective-permute-start | bytes 3538952 | tf_op jit(solution)/shard_map/ppermute | solution.py:837
  417.3 58.4 %collective-permute-start.59 = (bf16[48,4608]{1,0:T(8,128)(2,1)S(1)}, bf16[48,4608]{1,0:T(8,128)(2,1)}, u32[]{:S(2)}, u32[]{:S(2)}) collective-permute-start(bf16[48,4608]{1,0:T(8,128)(2,1)S(1)} %slice.470.refs_10_), channel_id=1, source_target_pairs={{0,16},{1,17},{2,18},{3,19},{4,20},{5,21},{6,22},{7,23},{8,24},{9,... | collective-permute-start | bytes 1327112 | tf_op jit(solution)/shard_map/ppermute | solution.py:837
  418.8 23.7 %collective-permute-start.45 = (bf16[384,1536]{1,0:T(8,128)(2,1)S(1)}, bf16[384,1536]{1,0:T(8,128)(2,1)S(1)}, u32[]{:S(2)}, u32[]{:S(2)}) collective-permute-start(bf16[384,1536]{1,0:T(8,128)(2,1)S(1)} %get-tuple-element.276), channel_id=1, source_target_pairs={{0,2},{1,3},{2,0},{3,1},{4,6},{5,7},{6,4},{7,5},{8,10},{9,11},{10,... | collective-permute-start | bytes 3538952 | tf_op jit(solution)/shard_map/ppermute | solution.py:837
  437.1 5.4 %collective-permute-start.42 = (bf16[640,768]{1,0:T(8,128)(2,1)S(1)}, bf16[640,768]{1,0:T(8,128)(2,1)S(1)}, u32[]{:S(2)}, u32[]{:S(2)}) collective-permute-start(bf16[640,768]{1,0:T(8,128)(2,1)S(1)} %get-tuple-element.272), channel_id=1, source_target_pairs={{0,2},{1,3},{2,0},{3,1},{4,6},{5,7},{6,4},{7,5},{8,10},{9,11},{10,... | collective-permute-start | bytes 2949128 | tf_op jit(solution)/shard_map/ppermute | solution.py:837
  442.5 22.8 %collective-permute-start.57 = (bf16[96,3072]{1,0:T(8,128)(2,1)S(1)}, bf16[96,3072]{1,0:T(8,128)(2,1)}, u32[]{:S(2)}, u32[]{:S(2)}) collective-permute-start(bf16[96,3072]{1,0:T(8,128)(2,1)S(1)} %fusion.13.refs_5_), channel_id=1, source_target_pairs={{0,8},{1,9},{2,10},{3,11},{4,12},{5,13},{6,14},{7,15},{8,0},{9,1},... | collective-permute-start | bytes 1769480 | tf_op jit(solution)/shard_map/ppermute | solution.py:837
  446.9 15.5 %collective-permute-start.48 = (bf16[192,1536]{1,0:T(8,128)(2,1)}, bf16[192,1536]{1,0:T(8,128)(2,1)}, u32[]{:S(2)}, u32[]{:S(2)}) collective-permute-start(bf16[192,1536]{1,0:T(8,128)(2,1)} %add_convert_fusion.3), channel_id=1, source_target_pairs={{0,4},{1,5},{2,6},{3,7},{4,0},{5,1},{6,2},{7,3},{8,12},{9,13},{10,... | collective-permute-start | bytes 1769480 | tf_op jit(solution)/shard_map/ppermute | solution.py:837
  447.2 1.2 collective-permute-start.49
  448.4 3.9 collective-permute-start.50
  449.5 35.0 %collective-permute-start.46 = (bf16[2,128,768]{2,1,0:T(8,128)(2,1)}, bf16[2,128,768]{2,1,0:T(8,128)(2,1)S(1)}, u32[]{:S(2)}, u32[]{:S(2)}) collective-permute-start(bf16[2,128,768]{2,1,0:T(8,128)(2,1)} %constant_dynamic-slice_fusion.2), channel_id=1, source_target_pairs={{0,1},{1,3},{2,0},{3,2},{4,5},{5,7},{6,4},{7,6},{8,9},{9,11},{10,8... | collective-permute-start | bytes 1179656 | tf_op jit(solution)/shard_map/ppermute | solution.py:837
  452.3 33.2 %collective-permute-start.53 = (bf16[3,128,768]{2,1,0:T(8,128)(2,1)}, bf16[3,128,768]{2,1,0:T(8,128)(2,1)S(1)}, u32[]{:S(2)}, u32[]{:S(2)}) collective-permute-start(bf16[3,128,768]{2,1,0:T(8,128)(2,1)} %constant_dynamic-slice_fusion.1), channel_id=1, source_target_pairs={{0,0},{1,2},{2,1},{3,3},{4,4},{5,6},{6,5},{7,7},{8,8},{9,10},{10,9... | collective-permute-start | bytes 1769480 | tf_op jit(solution)/shard_map/ppermute | solution.py:837
  464.1 11.5 %collective-permute-start.51 = (bf16[96,1536]{1,0:T(8,128)(2,1)S(1)}, bf16[96,1536]{1,0:T(8,128)(2,1)S(1)}, u32[]{:S(2)}, u32[]{:S(2)}) collective-permute-start(bf16[96,1536]{1,0:T(8,128)(2,1)S(1)} %slice.472), channel_id=1, source_target_pairs={{0,8},{1,9},{2,10},{3,11},{4,12},{5,13},{6,14},{7,15},{8,0},{9,1},... | collective-permute-start | bytes 884744 | tf_op jit(solution)/shard_map/ppermute | solution.py:837
  465.3 4.1 collective-permute-start.52
  469.4 13.5 %collective-permute-start.58 = (bf16[48,3072]{1,0:T(8,128)(2,1)S(1)}, bf16[48,3072]{1,0:T(8,128)(2,1)S(1)}, u32[]{:S(2)}, u32[]{:S(2)}) collective-permute-start(bf16[48,3072]{1,0:T(8,128)(2,1)S(1)} %slice.471), channel_id=1, source_target_pairs={{0,16},{1,17},{2,18},{3,19},{4,20},{5,21},{6,22},{7,23},{8,24},{9,... | collective-permute-start | bytes 884744 | tf_op jit(solution)/shard_map/ppermute | solution.py:837
  484.5 7.9 %collective-permute-start.54 = (bf16[4,8,1536]{2,1,0:T(8,128)(2,1)S(1)}, bf16[4,8,1536]{2,1,0:T(8,128)(2,1)S(1)}, u32[]{:S(2)}, u32[]{:S(2)}) collective-permute-start(bf16[4,8,1536]{2,1,0:T(8,128)(2,1)S(1)} %constant_dynamic-update-slice_fusion), channel_id=1, source_target_pairs={{0,8},{1,9},{2,10},{3,11},{4,12},{5,13},{6,14},{7,15},{8,0},{9,1},... | collective-permute-start | bytes 294920 | tf_op jit(solution)/shard_map/ppermute | solution.py:837
  487.8 16.8 %collective-permute-start.56 = (bf16[48,1536]{1,0:T(8,128)(2,1)S(1)}, bf16[48,1536]{1,0:T(8,128)(2,1)S(1)}, u32[]{:S(2)}, u32[]{:S(2)}) collective-permute-start(bf16[48,1536]{1,0:T(8,128)(2,1)S(1)} %slice.473), channel_id=1, source_target_pairs={{0,16},{1,17},{2,18},{3,19},{4,20},{5,21},{6,22},{7,23},{8,24},{9,... | collective-permute-start | bytes 442376 | tf_op jit(solution)/shard_map/ppermute | solution.py:837
  492.4 12.1 %collective-permute-start.55 = (bf16[8,8,1536]{2,1,0:T(8,128)(2,1)S(1)}, bf16[8,8,1536]{2,1,0:T(8,128)(2,1)S(1)}, u32[]{:S(2)}, u32[]{:S(2)}) collective-permute-start(bf16[8,8,1536]{2,1,0:T(8,128)(2,1)S(1)} %pad_maximum_fusion.5), channel_id=1, source_target_pairs={{0,16},{1,17},{2,18},{3,19},{4,20},{5,21},{6,22},{7,23},{8,24},{9,... | collective-permute-start | bytes 589832 | tf_op jit(solution)/shard_map/ppermute | solution.py:837
  (182 other events, 1068.8 us)
Sparse Core Ops, SparseCore 0:
  42.3 74.2 all-gather.4
  366.0 76.7 all-gather.6
